TPU v7x, 128 devices: a whole 4x4x4 slice. The times are simulated.
128 devices in a mesh: seg: 32 (over z, x, y_hi), span: 4 (over y_lo, core).
Axes of the slice: x: 4, y: 4 (y_hi: 2, y_lo: 2; y = y_hi * 2 + y_lo), z: 4, core: 2. Of those that a mesh axis runs over, the one named last changes fastest.
Arguments:
- inputs: bfloat16 [16384, 2048], P(('seg', 'span')), may hold values from -6 to 6
- cotangent: bfloat16 [16384, 2048], P(('seg', 'span')), may hold values from -6 to 6
- states: float32 [32, 32, 64, 64], P('seg', 'span'), may hold values from -4 to 4
- vectors: bfloat16 [16, 2048], P(None, ('seg', 'span')), may hold values from -7.5 to 1.3, as said below
- time_mix_weight: bfloat16 [4, 2048, 2048], P(None, 'seg', 'span'), may hold values from -0.125 to 0.125
- output_weight: bfloat16 [2048, 2048], P('span', 'seg'), may hold values from -0.125 to 0.125
- channel_receptance_weight: bfloat16 [2048, 2048], P(('seg', 'span')), may hold values from -0.125 to 0.125
- rank_down_weight: bfloat16 [2048, 224], P(('seg', 'span')), may hold values from -0.125 to 0.125
- rank_up_weight: bfloat16 [224, 2048], P(None, ('seg', 'span')), may hold values from -0.35 to 0.35
- channel_key_weight: bfloat16 [2048, 7168], P('seg', 'span'), may hold values from -0.125 to 0.125
- channel_value_weight: bfloat16 [7168, 2048], P('span', 'seg'), may hold values from -0.0625 to 0.0625
Outputs:
- output: bfloat16 [16384, 2048], P(('seg', 'span'))
- x_grad: float32 [16384, 2048], P(('seg', 'span'))
- state_grad: float32 [32, 32, 64, 64], P('seg', 'span')
- vectors_grad: float32 [16, 2048], P(None, ('seg', 'span'))
- time_proj_grad: float32 [4, 2048, 2048], P(None, 'seg', 'span')
- out_proj_grad: float32 [2048, 2048], P('span', 'seg')
- cm_recept_grad: float32 [2048, 2048], P(('seg', 'span'))
- lora_down_grad: float32 [2048, 224], P(('seg', 'span'))
- lora_up_grad: float32 [224, 2048], P(None, ('seg', 'span'))
- cm_key_grad: float32 [2048, 7168], P('seg', 'span')
- cm_value_grad: float32 [7168, 2048], P('span', 'seg')
Inputs may be any that keep to these rules, and one draw needn't show every extreme that they name: `vectors`: rows 0, 10, 12 are gains in [0.7, 1.3]; rows 1, 11, 13 offsets in [-0.2, 0.2]; rows 2 to 7, 14, 15 blend weights in [0, 1]; row 8 decay exponents of at most -1; row 9 bonuses in [-1, 1].
All inputs are finite; a program needn't handle non-finite values.
Results may differ from a plain program's by a relative error of at most 0.033.
Values may be sent and summed in bfloat16 or wider, within the bound.
No kernel may reach another device: no remote copies, remote signals or barrier semaphores. Data moves between devices by JAX's collectives and lax.ppermute only.
A program may use at most 384 MiB of HBM per device.

v0:
```python
import jax
import jax.numpy as jnp
from jax import lax
from jax.sharding import PartitionSpec as P

GROUP_DIMENSION = 64
SHIFT_RANK = 32


maximal_accuracy = lax.Precision.HIGHEST
ln_eps = 1e-05
gn_eps = 0.00064


def side_by_side(arrays, axis, dim, along):
    widths = [a.shape[along] for a in arrays]
    both = jnp.concatenate(arrays, axis=along)
    result = lax.all_gather(both, axis, axis=dim, tiled=True)
    return tuple(jnp.split(result, [sum(widths[:k]) for k in range(1, len(widths))], axis=along))


def rows_first(arrays, axis, dims):
    turned = [jnp.moveaxis(a, dim, 0) for a, dim in zip(arrays, dims)]
    both = jnp.concatenate([t.reshape(len(t), -1) for t in turned], axis=1)
    result, at, done = (lax.all_gather(both, axis, axis=0, tiled=True), 0, [])
    for t, dim in zip(turned, dims):
        slab = result[:, at : at + t[0].size].reshape(-1, *t.shape[1:])
        done.append(jnp.moveaxis(slab, 0, dim))
        at += t[0].size
    return tuple(done)


def split_up(shard, dim, size):
    before, after = (shard.shape[:dim], shard.shape[dim + 1 :])
    return jnp.moveaxis(shard.reshape(*before, size, -1, *after), dim, 0)


def sent_and_summed(shard, axis, dim):
    pieces = split_up(shard, dim, lax.axis_size(axis))
    arrived = lax.all_to_all(pieces, axis, split_axis=0, concat_axis=0, tiled=True)
    return arrived.astype(jnp.float32).sum(axis=0)


def from_everyone(shard, axis):
    copies = jnp.broadcast_to(shard, (lax.axis_size(axis), *shard.shape))
    return lax.all_to_all(copies, axis, split_axis=0, concat_axis=0, tiled=True)


def joined_along(pieces, dim):
    lengths = list(pieces.shape[1:])
    lengths[dim] *= pieces.shape[0]
    return jnp.moveaxis(pieces, 0, dim).reshape(lengths)


def gather_directly(shard, axis, dim):
    pieces = from_everyone(shard, axis)
    return joined_along(pieces, dim)


def from_behind(block, axis, distance):
    devices = range(lax.axis_size(axis))
    route = [(i - distance, i) for i in devices if i - distance in devices]
    return lax.ppermute(block, axis, route)


def sum_packed(arrays, axis, dims):
    size = lax.axis_size(axis)
    pieces = [split_up(a, dim, size) for a, dim in zip(arrays, dims)]
    lines = jnp.concatenate([b.reshape(size, -1) for b in pieces], axis=1)
    rows = max(16, -(-lines.shape[1] // 1024) * 8)
    lines = jnp.pad(lines, ((0, 0), (0, rows * 128 - lines.shape[1]))).reshape(-1, 128)
    vector, at, done = (lax.psum_scatter(lines, axis, tiled=True).reshape(-1), 0, [])
    for b in pieces:
        part = b[0]
        done.append(vector[at : at + part.size].reshape(part.shape))
        at += part.size
    return tuple(done)


def in_one_piece(arrays, axis, dim, along):
    ends, at = ([], 0)
    for a in arrays[:-1]:
        at += a.shape[along]
        ends.append(at)
    both = jnp.concatenate(arrays, axis=along)
    return tuple(
        jnp.split(lax.psum_scatter(both, axis, scatter_dimension=dim, tiled=True), ends, axis=along)
    )


def product_lower(left_arg, right_arg):
    return jnp.dot(left_arg, right_arg, preferred_element_type=jnp.float32)


def outer_sum(left_arg, right_arg):
    return jnp.einsum("td,te->de", left_arg, right_arg, preferred_element_type=jnp.float32)


def backward_product(gradient, weights):
    return jnp.einsum("te,de->td", gradient, weights, preferred_element_type=jnp.float32)


def norm_rows(values, gain_vec, offset):
    centre = values - jnp.mean(values, -1, keepdims=True)
    row_rstd = lax.rsqrt(jnp.mean(centre * centre, -1, keepdims=True) + ln_eps)
    unit_rows = centre * row_rstd
    return (unit_rows * gain_vec + offset, unit_rows, row_rstd)


def norm_back(gradient, unit_rows, row_rstd, gain_vec):
    scaled = gradient * gain_vec
    return row_rstd * (
        scaled
        - jnp.mean(scaled, -1, keepdims=True)
        - unit_rows * jnp.mean(scaled * unit_rows, -1, keepdims=True)
    )


def weighted_kv_local(
    acceptance_lines, address_mapped, content_mapped, logged_fading, reward_array, start_state
):
    token_rows, group_count, head_size = acceptance_lines.shape
    block_len = min(64, token_rows)
    block_count = token_rows // block_len

    def to_blocks(input_tensor):
        return input_tensor.reshape(block_count, block_len, group_count, head_size)

    acceptance_tile = to_blocks(acceptance_lines)
    address_tile = to_blocks(address_mapped)
    content_tile = to_blocks(content_mapped)
    dec_blk = to_blocks(logged_fading)
    running = jnp.cumsum(dec_blk, axis=1)
    rec_scaled = acceptance_tile * jnp.exp(running - dec_blk)
    key_scaled = address_tile * jnp.exp(-running)
    scores = jnp.einsum("bthk,bihk->bhti", rec_scaled, key_scaled, precision=maximal_accuracy)
    lower_mask = jnp.arange(block_len)[:, None] > jnp.arange(block_len)[None, :]
    scores = jnp.where(lower_mask, scores, 0.0)
    intra_out = jnp.einsum("bhti,bihv->bthv", scores, content_tile, precision=maximal_accuracy)
    diagonal_term = (
        jnp.sum(acceptance_tile * reward_array * address_tile, axis=-1, keepdims=True)
        * content_tile
    )
    block_total = running[:, -1]
    key_end = address_tile * jnp.exp(block_total[:, None] - running)
    block_state = jnp.einsum("bihk,bihv->bhkv", key_end, content_tile, precision=maximal_accuracy)

    def pass_state(transported_memory, block_item):
        return (
            jnp.exp(block_item[0])[..., None] * transported_memory + block_item[1],
            transported_memory,
        )

    final_state, start_states = lax.scan(pass_state, start_state, (block_total, block_state))
    inter_out = jnp.einsum("bthk,bhkv->bthv", rec_scaled, start_states, precision=maximal_accuracy)
    return (intra_out + diagonal_term + inter_out).reshape(token_rows, group_count, head_size)


def shards(
    inputs,
    cotangent,
    states,
    vectors,
    time_mix_weight,
    output_weight,
    channel_receptance_weight,
    rank_down_weight,
    rank_up_weight,
    channel_key_weight,
    channel_value_weight,
):
    gathered = side_by_side(
        (vectors.T, channel_receptance_weight, rank_down_weight, rank_up_weight.T),
        ("seg", "span"),
        0,
        1,
    )
    parameter_array_list = gathered[0].T.astype(jnp.float32)
    recept_w = gathered[1]
    down_weight = gathered[2]
    up_weight = gathered[3].T
    proj_all, out_w, key_w, value_w = rows_first(
        (time_mix_weight, output_weight, channel_key_weight, channel_value_weight),
        "seg",
        (1, 1, 0, 1),
    )
    token_rows, embedding_dimension = inputs.shape
    rank_columns = 5 * SHIFT_RANK
    col_count = proj_all.shape[2]
    local_heads = col_count // GROUP_DIMENSION
    col_start = lax.axis_index("span") * col_count
    position = lax.axis_index("span") * token_rows

    def own_cols(line):
        return lax.dynamic_slice_in_dim(line, col_start, col_count, 0)

    def own_rows(values):
        return lax.dynamic_slice_in_dim(values, position, token_rows, 0)

    def place_cols(values):
        blank = jnp.zeros(values.shape[:-1] + (embedding_dimension,), jnp.float32)
        return lax.dynamic_update_slice_in_dim(blank, values, col_start, values.ndim - 1)

    x_in = inputs.astype(jnp.float32)
    normed_own, unit_one, rstd_one = norm_rows(
        x_in, parameter_array_list[0], parameter_array_list[1]
    )
    seg_normed = lax.all_gather(normed_own.astype(jnp.bfloat16), "span", axis=0, tiled=True).astype(
        normed_own.dtype
    )
    seg_rows = seg_normed.shape[0]
    head_shape = (seg_rows, local_heads, GROUP_DIMENSION)
    shifted = (
        jnp.concatenate([jnp.zeros((1, embedding_dimension), jnp.float32), seg_normed[:-1]], axis=0)
        - seg_normed
    )
    mixed_input = (seg_normed + shifted * parameter_array_list[2]).astype(jnp.bfloat16)
    squash_values = jnp.tanh(product_lower(mixed_input, down_weight[:, :rank_columns]))
    squash_low = squash_values.astype(jnp.bfloat16).reshape(seg_rows, 5, SHIFT_RANK)
    up_modulations = up_weight[:rank_columns].reshape(5, SHIFT_RANK, embedding_dimension)
    modulation_terms = jnp.einsum(
        "spi,pif->psf", squash_low, up_modulations, preferred_element_type=jnp.float32
    )
    coeffs = [
        parameter_array_list[3 + group_id] + modulation_terms[group_id] for group_id in range(5)
    ]
    shift_mixes = [
        (seg_normed + shifted * coeffs[group_id]).astype(jnp.bfloat16) for group_id in range(5)
    ]
    acceptance_lines = product_lower(shift_mixes[3], proj_all[0])
    address_mapped = product_lower(shift_mixes[1], proj_all[1])
    content_mapped = product_lower(shift_mixes[2], proj_all[2])
    gate_pre = product_lower(shift_mixes[4], proj_all[3])
    gate_act = jax.nn.silu(gate_pre)
    decay_hyperbolic = jnp.tanh(product_lower(shift_mixes[0], down_weight[:, rank_columns:]))
    decay_low_rank = decay_hyperbolic.astype(jnp.bfloat16)
    up_decay_own = lax.dynamic_slice_in_dim(up_weight[rank_columns:], col_start, col_count, 1)
    logged_fading = -jnp.exp(
        own_cols(parameter_array_list[8]) + product_lower(decay_low_rank, up_decay_own)
    )
    reward_array = own_cols(parameter_array_list[9]).reshape(local_heads, GROUP_DIMENSION)
    weighted_kv, wkv_pullback = jax.vjp(
        weighted_kv_local,
        acceptance_lines.reshape(head_shape),
        address_mapped.reshape(head_shape),
        content_mapped.reshape(head_shape),
        logged_fading.reshape(head_shape),
        reward_array,
        states[0],
    )
    centre = weighted_kv - jnp.mean(weighted_kv, -1, keepdims=True)
    gn_rstd = lax.rsqrt(jnp.mean(centre * centre, -1, keepdims=True) + gn_eps)
    gn_unit = centre * gn_rstd
    grouped = gn_unit.reshape(seg_rows, col_count) * own_cols(parameter_array_list[10]) + own_cols(
        parameter_array_list[11]
    )
    mixed = (grouped * gate_act).astype(jnp.bfloat16)
    att_out = sent_and_summed(product_lower(mixed, out_w).astype(jnp.bfloat16), "span", 0)
    resid = x_in + att_out
    normed_two, unit_two, rstd_two = norm_rows(
        resid, parameter_array_list[12], parameter_array_list[13]
    )
    span_rows = lax.all_gather(normed_two.astype(jnp.bfloat16), "span", axis=0, tiled=True).astype(
        normed_two.dtype
    )
    whole_rows = span_rows.shape[0]
    shifted_all = (
        jnp.concatenate([jnp.zeros((1, embedding_dimension), jnp.float32), span_rows[:-1]], axis=0)
        - span_rows
    )
    key_in = (span_rows + shifted_all * parameter_array_list[14]).astype(jnp.bfloat16)
    shifted_own_two = own_rows(shifted_all)
    rec_in = (normed_two + shifted_own_two * parameter_array_list[15]).astype(jnp.bfloat16)
    hidden_two = product_lower(key_in, key_w)
    active = jax.nn.relu(hidden_two)
    squared = (active * active).astype(jnp.bfloat16)
    value_out = sent_and_summed(product_lower(squared, value_w).astype(jnp.bfloat16), "span", 0)
    rec_gate = jax.nn.sigmoid(product_lower(rec_in, recept_w))
    output = (resid + rec_gate * value_out).astype(jnp.bfloat16)
    grad_out = cotangent.astype(jnp.float32)
    grad_value = (grad_out * rec_gate).astype(jnp.bfloat16)
    grad_rec_pre = (grad_out * value_out * rec_gate * (1.0 - rec_gate)).astype(jnp.bfloat16)
    recept_grad_local = outer_sum(rec_in, grad_rec_pre)
    grad_rec_in = backward_product(grad_rec_pre, recept_w)
    grad_value_all = gather_directly(grad_value, "span", 0)
    value_grad_local = outer_sum(squared, grad_value_all)
    grad_squared = backward_product(grad_value_all, value_w)
    grad_hidden_two = (grad_squared * 2.0 * active).astype(jnp.bfloat16)
    key_grad_local = outer_sum(key_in, grad_hidden_two)
    grad_key_in = backward_product(grad_hidden_two, key_w)
    grad_rec_all = lax.dynamic_update_slice_in_dim(
        jnp.zeros((whole_rows, embedding_dimension), jnp.float32), grad_rec_in, position, 0
    )
    grad_shift_all = (
        grad_key_in * parameter_array_list[14] + grad_rec_all * parameter_array_list[15]
    )
    grad_rows_all = (
        grad_key_in
        + grad_rec_all
        - grad_shift_all
        + jnp.concatenate(
            [grad_shift_all[1:], jnp.zeros((1, embedding_dimension), jnp.float32)], axis=0
        )
    )
    vec_fourteen = jnp.sum(grad_key_in * shifted_all, axis=0)
    vec_fifteen = jnp.sum(grad_rec_in * shifted_own_two, axis=0)
    grad_normed_two = sent_and_summed(grad_rows_all.astype(jnp.bfloat16), "span", 0)
    vec_twelve = jnp.sum(grad_normed_two * unit_two, axis=0)
    vec_thirteen = jnp.sum(grad_normed_two, axis=0)
    grad_resid = grad_out + norm_back(grad_normed_two, unit_two, rstd_two, parameter_array_list[12])
    grad_att = grad_resid.astype(jnp.bfloat16)
    seg_grad_att = gather_directly(grad_att, "span", 0)
    out_grad_local = outer_sum(mixed, seg_grad_att)
    grad_mixed = backward_product(seg_grad_att, out_w)
    grad_grouped = grad_mixed * gate_act
    gate_sig = jax.nn.sigmoid(gate_pre)
    grad_gate_pre = (grad_mixed * grouped * gate_sig * (1.0 + gate_pre * (1.0 - gate_sig))).astype(
        jnp.bfloat16
    )
    vec_ten = jnp.sum(grad_grouped * gn_unit.reshape(seg_rows, col_count), axis=0)
    vec_eleven = jnp.sum(grad_grouped, axis=0)
    grad_unit = (grad_grouped * own_cols(parameter_array_list[10])).reshape(head_shape)
    weighted_kv_gradient = gn_rstd * (
        grad_unit
        - jnp.mean(grad_unit, -1, keepdims=True)
        - gn_unit * jnp.mean(grad_unit * gn_unit, -1, keepdims=True)
    )
    (
        receptance_head_gradient,
        key_head_gradient,
        value_head_gradient,
        decay_head_gradient,
        reward_derivative,
        start_gradient,
    ) = wkv_pullback(weighted_kv_gradient)
    state_grad = start_gradient[None]
    grad_recept = receptance_head_gradient.reshape(seg_rows, col_count).astype(jnp.bfloat16)
    grad_key = key_head_gradient.reshape(seg_rows, col_count).astype(jnp.bfloat16)
    grad_val = value_head_gradient.reshape(seg_rows, col_count).astype(jnp.bfloat16)
    grad_decay_in = decay_head_gradient.reshape(seg_rows, col_count) * logged_fading
    vec_eight = jnp.sum(grad_decay_in, axis=0)
    decay_rank_gradient = grad_decay_in.astype(jnp.bfloat16)
    up_decay_grad = outer_sum(decay_low_rank, decay_rank_gradient)
    decay_hyper_partial = backward_product(decay_rank_gradient, up_decay_own)
    proj_grad_local = jnp.stack(
        [
            outer_sum(shift_mixes[3], grad_recept),
            outer_sum(shift_mixes[1], grad_key),
            outer_sum(shift_mixes[2], grad_val),
            outer_sum(shift_mixes[4], grad_gate_pre),
        ]
    )
    mix_partials = jnp.stack(
        [
            backward_product(grad_key, proj_all[1]),
            backward_product(grad_val, proj_all[2]),
            backward_product(grad_recept, proj_all[0]),
            backward_product(grad_gate_pre, proj_all[3]),
        ]
    )
    mix_own, decay_hyper_own = (
        lax.psum_scatter(
            mix_partials.astype(jnp.bfloat16), "span", scatter_dimension=1, tiled=True
        ).astype(jnp.float32),
        lax.psum_scatter(
            decay_hyper_partial.astype(jnp.bfloat16), "span", scatter_dimension=0, tiled=True
        ).astype(jnp.float32),
    )
    shifted_own = own_rows(shifted)
    squash_own = own_rows(squash_values)
    squash_low_own = squash_own.astype(jnp.bfloat16).reshape(token_rows, 5, SHIFT_RANK)
    decay_hyper_rows = own_rows(decay_hyperbolic)
    decay_preact_gradient = (decay_hyper_own * (1.0 - decay_hyper_rows * decay_hyper_rows)).astype(
        jnp.bfloat16
    )
    down_decay_grad = outer_sum(own_rows(shift_mixes[0]), decay_preact_gradient)
    grad_mix = [
        backward_product(decay_preact_gradient, down_weight[:, rank_columns:]),
        mix_own[0],
        mix_own[1],
        mix_own[2],
        mix_own[3],
    ]
    vec_mixes = [jnp.sum(grad_mix[group_id] * shifted_own, axis=0) for group_id in range(5)]
    grad_mods = jnp.stack([grad_mix[group_id] * shifted_own for group_id in range(5)]).astype(
        jnp.bfloat16
    )
    up_mods_grad = jnp.einsum(
        "tgj,gtd->gjd", squash_low_own, grad_mods, preferred_element_type=jnp.float32
    ).reshape(rank_columns, embedding_dimension)
    grad_squash = jnp.einsum(
        "gtd,gjd->tgj", grad_mods, up_modulations, preferred_element_type=jnp.float32
    ).reshape(token_rows, rank_columns)
    hidden_gradient = (grad_squash * (1.0 - squash_own * squash_own)).astype(jnp.bfloat16)
    down_mods_grad = outer_sum(own_rows(mixed_input), hidden_gradient)
    mixed_input_gradient = backward_product(hidden_gradient, down_weight[:, :rank_columns])
    vec_two = jnp.sum(mixed_input_gradient * shifted_own, axis=0)
    grad_shifted = mixed_input_gradient * parameter_array_list[2]
    grad_normed = mixed_input_gradient
    for group_id in range(5):
        grad_shifted = grad_shifted + grad_mix[group_id] * own_rows(coeffs[group_id])
        grad_normed = grad_normed + grad_mix[group_id]
    back_edge = from_behind(grad_shifted[:1], "span", -1)
    grad_normed = (
        grad_normed - grad_shifted + jnp.concatenate([grad_shifted[1:], back_edge], axis=0)
    )
    vec_zero = jnp.sum(grad_normed * unit_one, axis=0)
    vec_one = jnp.sum(grad_normed, axis=0)
    x_grad = grad_resid + norm_back(grad_normed, unit_one, rstd_one, parameter_array_list[0])
    vec_grad_local = jnp.stack(
        [
            vec_zero,
            vec_one,
            vec_two,
            vec_mixes[0],
            vec_mixes[1],
            vec_mixes[2],
            vec_mixes[3],
            vec_mixes[4],
            place_cols(vec_eight),
            place_cols(reward_derivative.reshape(col_count)),
            place_cols(vec_ten),
            place_cols(vec_eleven),
            vec_twelve,
            vec_thirteen,
            vec_fourteen,
            vec_fifteen,
        ]
    )
    down_grad_local = jnp.concatenate([down_mods_grad, down_decay_grad], axis=1)
    up_grad_local = jnp.concatenate([up_mods_grad, place_cols(up_decay_grad)], axis=0)
    proj_grad, out_grad, key_grad, value_grad = tuple(
        (
            part.astype(jnp.float32)
            for part in sum_packed(
                (
                    proj_grad_local.astype(jnp.bfloat16),
                    out_grad_local.astype(jnp.bfloat16),
                    key_grad_local.astype(jnp.bfloat16),
                    value_grad_local.astype(jnp.bfloat16),
                ),
                "seg",
                (1, 1, 0, 1),
            )
        )
    )
    vec_grad_turned, recept_grad, down_grad, up_grad_turned = in_one_piece(
        (vec_grad_local.T, recept_grad_local, down_grad_local, up_grad_local.T),
        ("seg", "span"),
        0,
        1,
    )
    vec_grad = vec_grad_turned.T
    up_grad = up_grad_turned.T
    return (
        output,
        x_grad,
        state_grad,
        vec_grad,
        proj_grad,
        out_grad,
        recept_grad,
        down_grad,
        up_grad,
        key_grad,
        value_grad,
    )


def solution(mesh):
    placed = (
        P(("seg", "span"), None),
        P(("seg", "span"), None),
        P("seg", "span", None, None),
        P(None, ("seg", "span")),
        P(None, "seg", "span"),
        P("span", "seg"),
        P(("seg", "span"), None),
        P(("seg", "span"), None),
        P(None, ("seg", "span")),
        P("seg", "span"),
        P("span", "seg"),
    )
    return jax.shard_map(
        shards,
        mesh=mesh,
        in_specs=placed,
        out_specs=(
            P(("seg", "span"), None),
            P(("seg", "span"), None),
            P("seg", "span", None, None),
            P(None, ("seg", "span")),
            P(None, "seg", "span"),
            P("span", "seg"),
            P(("seg", "span"), None),
            P(("seg", "span"), None),
            P(None, ("seg", "span")),
            P("seg", "span"),
            P("span", "seg"),
        ),
        check_vma=False,
    )
```

profile of v0, /device:TPU:1, one launch (start us, length us, event | category | flops | bytes accessed | tf_op | source)
XLA Modules:
  0.0 1977.9 jit_solution(4544245851336987160)
XLA Ops:
  12.2 74.8 %all-gather.5.cloned.1.call-done = bf16[2048,2512]{1,0:T(8,128)(2,1)} async-done(((bf16[16,2512]{1,0:T(8,128)(2,1)}), bf16[2048,2512]{1,0:T(8,128)(2,1)}) %all-gather.5.cloned.1.call-update) | async-done | bytes 10289168 | tf_op jit(solution)/shard_map/all_gather | solution.py:18
  88.1 8.5 fusion.186
  104.7 20.7 %all-gather.7.cloned.1.call-done = bf16[512,2048]{1,0:T(8,128)(2,1)} async-done(((bf16[128,2048]{1,0:T(8,128)(2,1)}), bf16[512,2048]{1,0:T(8,128)(2,1)}) %all-gather.7.cloned.1.call-update) | async-done | bytes 2097168 | tf_op jit(solution)/shard_map/all_gather | solution.py:208
  135.0 9.0 fusion.190
  144.0 20.4 %fusion.21 = (bf16[512,2048]{1,0:T(8,128)(2,1)}, f32[512,2048]{1,0:T(8,128)}, bf16[512,2048]{1,0:T(8,128)(2,1)}, f32[512,2048]{1,0:T(8,128)}, bf16[512,2048]{1,0...) fusion(bf16[512,2048]{1,0:T(8,128)(2,1)S(1)} %copy-done.10, ...), kind=kLoop, calls=%fused_computation.45 | loop fusion | flops 23068672 | bytes 58753024 | tf_op jit(solution)/shard_map/convert_element_type | solution.py:228
  172.9 162.8 %all-gather.9.cloned.1.call-done = bf16[2048,6144]{1,0:T(8,128)(2,1)} async-done(((bf16[64,6144]{1,0:T(8,128)(2,1)}), bf16[2048,6144]{1,0:T(8,128)(2,1)}) %all-gather.9.cloned.1.call-update) | async-done | bytes 25165840 | tf_op jit(solution)/shard_map/all_gather | solution.py:25
  335.7 8.3 slice.214
  343.9 12.8 copy.154
  377.1 19.8 %while.35 = (s32[]{:T(128)}, f32[8,64,64]{2,1,0:T(8,128)S(1)}, f32[8,8,64,64]{3,2,1,0:T(8,128)}, f32[8,8,64]{2,1,0:T(8,128)S(1)}, f32[8,8,64,1]{2,1,3,0:T(8,128)...) while((s32[]{:T(128)}, f32[8,64,64]{2,1,0:T(8,128)S(1)}, f32[8,8,64,64]{3,2,1,0:T(8,128)}, ...), condition=%wide.region_5.6_spmd, body=%wide.region_4.5_spmd.sunk | while | flops 65538 | bytes 807021 | solution.py:154
  424.1 28.2 %all_to_all.25 = bf16[4,128,2048]{2,1,0:T(8,128)(2,1)S(1)} all-to-all(bf16[4,128,2048]{2,1,0:T(8,128)(2,1)S(1)} %bitcast.473), channel_id=1, replica_groups=mesh['seg'=32,'span'=4] {'span'}, dimensions={0} | all-to-all | bytes 4194304 | tf_op jit(solution)/shard_map/all_to_all | solution.py:40
  454.9 27.8 %all-gather.11.cloned.1.call-done = bf16[512,2048]{1,0:T(8,128)(2,1)} async-done(((bf16[128,2048]{1,0:T(8,128)(2,1)}), bf16[512,2048]{1,0:T(8,128)(2,1)}) %all-gather.11.cloned.1.call-update) | async-done | bytes 2097168 | tf_op jit(solution)/shard_map/all_gather | solution.py:263
  496.5 9.7 fusion.29
  513.0 22.6 %all-to-all-done.1 = bf16[4,128,2048]{2,1,0:T(8,128)(2,1)} async-done(((bf16[4,128,2048]{2,1,0:T(8,128)(2,1)}), bf16[4,128,2048]{2,1,0:T(8,128)(2,1)}, u32[]{:S(2)}, u32[]{:S(2)}) %all-to-all-start.1) | async-done | bytes 2097184 | tf_op jit(solution)/shard_map/all_to_all | solution.py:40
  545.6 28.4 %all_to_all.26 = bf16[4,128,2048]{2,1,0:T(8,128)(2,1)S(1)} all-to-all(bf16[4,128,2048]{2,1,0:T(8,128)(2,1)S(1)} %broadcast_in_dim.80), channel_id=1, replica_groups=mesh['seg'=32,'span'=4] {'span'}, dimensions={0} | all-to-all | bytes 4194304 | tf_op jit(solution)/shard_map/all_to_all | solution.py:46
  592.7 7.7 multiply_reduce_fusion.5
  608.9 28.6 %all_to_all.27 = bf16[4,128,2048]{2,1,0:T(8,128)(2,1)S(1)} all-to-all(bf16[4,128,2048]{2,1,0:T(8,128)(2,1)S(1)} %bitcast.461), channel_id=1, replica_groups=mesh['seg'=32,'span'=4] {'span'}, dimensions={0} | all-to-all | bytes 4194304 | tf_op jit(solution)/shard_map/all_to_all | solution.py:40
  662.8 9.6 convolution_convert_fusion
  672.4 10.1 copy.134
  682.5 13.9 copy.135
  696.5 14.2 reshape.339
  710.7 9.1 convolution_convert_fusion.1
  719.8 8.3 reshape_reshape.10
  764.7 27.2 %while.36 = (s32[]{:T(128)}, f32[8,64,64]{2,1,0:T(8,128)S(1)}, f32[8,8,64]{2,1,0:T(8,128)S(1)}, f32[8,8,64,64]{3,2,1,0:T(8,128)}, f32[8,8,64,64]{3,2,1,0:T(8,128...) while((s32[]{:T(128)}, f32[8,64,64]{2,1,0:T(8,128)S(1)}, ...), condition=%wide.region_19.20_spmd.clone, body=%wide.region_17.19_spmd.clone.sunk | while | flops 196612 | bytes 936092 | solution.py:154
  806.6 7.8 multiply_reduce_fusion.1
  891.8 7.8 copy.131
  899.6 11.4 copy.169
  911.5 38.5 %pad_maximum_fusion = bf16[32,393216]{1,0:T(8,128)(2,1)} fusion(bf16[32,114688]{1,0:T(8,128)(2,1)} %reshape.339, bf16[32,114688]{1,0:T(8,128)(2,1)} %reshape_reshape.10, bf16[32,32768]{1,0:T(8,128)(2,1)S(1)} %reshape.337, bf16[32,131072]{1,0:T(8,128)(2,1)} %bitcast.451), kind=kLoop, calls=%fused_computation.13 | loop fusion | flops 100663296 | bytes 50331648 | tf_op jit(solution)/shard_map/concatenate | solution.py:69
  950.0 33.2 %reshape.340 = bf16[98304,128]{1,0:T(8,128)(2,1)} reshape(bf16[32,393216]{1,0:T(8,128)(2,1)} %pad_maximum_fusion) | data formatting | bytes 50331648 | tf_op jit(solution)/shard_map/reshape | solution.py:71
  1008.9 9.3 convolution_dynamic-update-slice_fusion
  1025.3 20.2 %copy.160 = f32[2048,2512]{1,0:T(8,128)} copy(f32[2048,2512]{0,1:T(8,128)} %fusion.89) | data formatting | bytes 41156608
  1048.1 252.4 %reduce-scatter.11.cloned.1.call-done = bf16[3072,128]{1,0:T(8,128)(2,1)} async-done(((bf16[98304,128]{1,0:T(8,128)(2,1)}), bf16[3072,128]{1,0:T(8,128)(2,1)}) %reduce-scatter.11.cloned.1.call-update) | async-done | bytes 786448 | tf_op jit(solution)/shard_map/reduce_scatter | solution.py:72
  1306.3 660.1 %reduce-scatter.15.cloned.1.call-done = f32[16,2512]{1,0:T(8,128)} async-done(((f32[2048,2512]{1,0:T(8,128)}), f32[16,2512]{1,0:T(8,128)}) %reduce-scatter.15.cloned.1.call-update) | async-done | bytes 160784
  (480 shorter events, 385.5 us)
Async XLA Ops:
  7.2 79.8 %all-gather.5.cloned.1.call-start = ((), (), s32[]{:S(2)}) async-start(), calls=%async_computation.9 | async-start | bytes 10567680 | tf_op jit(solution)/shard_map/all_gather | solution.py:18
  9.6 115.7 %all-gather.7.cloned.1.call-start = ((), (), s32[]{:S(2)}) async-start(), calls=%async_computation.10 | async-start | bytes 2621440 | tf_op jit(solution)/shard_map/all_gather | solution.py:208
  10.9 85.8 %copy-start.99 = (f32[128]{0:T(128)}, f32[128]{0:T(128)S(1)}, u32[]{:S(2)}) copy-start(f32[128]{0:T(128)S(1)} %broadcast_multiply_fusion.9) | copy-start | bytes 1540
  12.2 84.5 %copy-start.104 = (f32[128]{0:T(128)}, f32[128]{0:T(128)S(1)}, u32[]{:S(2)}) copy-start(f32[128]{0:T(128)S(1)} %add_rsqrt_fusion.2) | copy-start | bytes 1540
  88.1 8.6 copy-start.23
  88.1 9.9 copy-start.81
  96.7 31.0 %copy-start.91 = (f32[2048]{0:T(1024)}, f32[2048]{0:T(1024)S(1)}, u32[]{:S(2)}) copy-start(f32[2048]{0:T(1024)S(1)} %get-tuple-element.401) | copy-start | bytes 24580
  97.9 237.7 %all-gather.9.cloned.1.call-start = ((), (), s32[]{:S(2)}) async-start(), calls=%async_computation.11 | async-start | bytes 25952256 | tf_op jit(solution)/shard_map/all_gather | solution.py:25
  99.0 383.7 %all-gather.11.cloned.1.call-start = ((), (), s32[]{:S(2)}) async-start(), calls=%async_computation.12 | async-start | bytes 2621440 | tf_op jit(solution)/shard_map/all_gather | solution.py:263
  99.4 307.6 %copy-start.84 = (pred[64,64]{1,0:T(8,128)(4,1)}, pred[64,64]{1,0:T(8,128)(4,1)S(1)}, u32[]{:S(2)}) copy-start(pred[64,64]{1,0:T(8,128)(4,1)S(1)} %iota_compare_fusion) | copy-start | bytes 12292
  101.5 66.0 %copy-start.68 = (bf16[64,2048]{0,1:T(8,128)(2,1)}, bf16[64,2048]{0,1:T(8,128)(2,1)S(1)}, u32[]{:S(2)}) copy-start(bf16[64,2048]{0,1:T(8,128)(2,1)S(1)} %slice.223) | copy-start | bytes 786436
  102.0 33.0 %copy-start.48 = (bf16[160,2048]{1,0:T(8,128)(2,1)}, bf16[160,2048]{1,0:T(8,128)(2,1)S(1)}, u32[]{:S(2)}) copy-start(bf16[160,2048]{1,0:T(8,128)(2,1)S(1)} %copy.96) | copy-start | bytes 1966084
  103.5 261.8 %copy-start.97 = (f32[8,64]{1,0:T(8,128)}, f32[8,64]{1,0:T(8,128)S(1)}, u32[]{:S(2)}) copy-start(f32[8,64]{1,0:T(8,128)S(1)} %mul.487) | copy-start | bytes 6148
  130.9 13.1 copy-start.36
  172.9 224.1 %copy-start = (f32[8,64,8,64]{3,2,1,0:T(8,128)}, f32[8,64,8,64]{3,2,1,0:T(8,128)S(1)}, u32[]{:S(2)}) copy-start(f32[8,64,8,64]{3,2,1,0:T(8,128)S(1)} %fusion.189) | copy-start | bytes 3145732
  370.3 36.7 %copy-start.88 = (f32[8,64,8]{1,2,0:T(8,128)}, f32[8,64,8]{1,2,0:T(8,128)S(1)}, u32[]{:S(2)}) copy-start(f32[8,64,8]{1,2,0:T(8,128)S(1)} %get-tuple-element.390) | copy-start | bytes 49156
  496.5 9.7 copy-start.106
  506.2 29.4 %all-to-all-start.1 = ((bf16[4,128,2048]{2,1,0:T(8,128)(2,1)}), bf16[4,128,2048]{2,1,0:T(8,128)(2,1)}, u32[]{:S(2)}, u32[]{:S(2)}) async-start(bf16[4,128,2048]{2,1,0:T(8,128)(2,1)} %bitcast.472), calls=%async_computation.1 | async-start | bytes 4194304 | tf_op jit(solution)/shard_map/all_to_all | solution.py:40
  545.4 45.6 %copy-start.70 = (bf16[128,2048]{1,0:T(8,128)(2,1)}, bf16[128,2048]{1,0:T(8,128)(2,1)S(1)}, u32[]{:S(2)}) copy-start(bf16[128,2048]{1,0:T(8,128)(2,1)S(1)} %get-tuple-element.388) | copy-start | bytes 1572868
  545.6 29.8 %copy-start.107 = (f32[512,1792]{1,0:T(8,128)S(1)}, f32[512,1792]{1,0:T(8,128)}, u32[]{:S(2)}) copy-start(f32[512,1792]{1,0:T(8,128)} %copy-done.106) | copy-start | bytes 11010052
  642.8 85.3 %all-to-all-start.4 = ((bf16[4,128,2048]{2,1,0:T(8,128)(2,1)}), bf16[4,128,2048]{2,1,0:T(8,128)(2,1)}, u32[]{:S(2)}, u32[]{:S(2)}) async-start(bf16[4,128,2048]{2,1,0:T(8,128)(2,1)} %broadcast_in_dim.82), calls=%async_computation.4 | async-start | bytes 4194304 | tf_op jit(solution)/shard_map/all_to_all | solution.py:46
  648.3 337.9 %reduce-scatter.13.cloned.1.call-start = ((), (), s32[]{:S(2)}) async-start(), calls=%async_computation.15 | async-start | bytes 163840
  719.8 8.4 copy-start.40
  741.2 9.8 copy-start.4
  760.4 31.5 %copy-start.1 = (f32[8,64,8,64]{3,2,1,0:T(8,128)S(1)}, f32[8,64,8,64]{3,2,1,0:T(8,128)}, u32[]{:S(2)}) copy-start(f32[8,64,8,64]{3,2,1,0:T(8,128)} %copy-done) | copy-start | bytes 3145732
  764.7 27.2 %copy-start.67 = (f32[8,8,64]{2,1,0:T(8,128)S(1)}, f32[8,8,64]{2,1,0:T(8,128)}, u32[]{:S(2)}) copy-start(f32[8,8,64]{2,1,0:T(8,128)} %copy-done.66) | copy-start | bytes 49156
  806.6 7.8 copy-start.29
  806.6 7.8 copy-start.46
  856.2 135.1 %reduce-scatter.9.cloned.1.call-start = ((), (), s32[]{:S(2)}) async-start(), calls=%async_computation.13 | async-start | bytes 10485760 | tf_op jit(solution)/shard_map/reduce_scatter | solution.py:362
  911.1 389.4 %reduce-scatter.11.cloned.1.call-start = ((), (), s32[]{:S(2)}) async-start(), calls=%async_computation.14 | async-start | bytes 25952256 | tf_op jit(solution)/shard_map/reduce_scatter | solution.py:72
  983.3 983.1 %reduce-scatter.15.cloned.1.call-start = ((), (), s32[]{:S(2)}) async-start(), calls=%async_computation.16 | async-start | bytes 21135360
  1002.0 5.0 collective-permute-start
  (88 other events, 299.6 us)
Sparse Core Ops, SparseCore 0:
  11.7 75.2 all-gather.4
  98.1 27.2 all-gather.6
  128.3 207.3 all-gather.8
  455.0 27.6 all-gather.10
  856.4 18.1 reduce-scatter.12
  911.2 80.1 reduce-scatter.8
  998.1 302.3 reduce-scatter.10
  1303.0 663.3 reduce-scatter.14
where the time goes:
time: 1990 us; the launch traced here: 1980 us
  waiting for transfers between devices  1220 us (61%)
  local copies, waits for them, and re-layouts  265 us (13%)
  matrix products  224 us (11%)
  other arithmetic  151 us (8%)
  blocking collectives  85.2 us (4%)
    unnamed x10, waiting for transfers between devices  660 us
    reduce_scatter x1, waiting for transfers between devices, sum_packed(): lax.psum_scatter(lines, axis, tiled=True).reshape(-1)  252 us
    all_gather x1, waiting for transfers between devices, rows_first(): result, at, done = (lax.all_gather(both, axis, axis=0, tiled=True), 0, [])  163 us
    all_gather x1, waiting for transfers between devices, side_by_side(): result = lax.all_gather(both, axis, axis=dim, tiled=True)  74.8 us
    all_to_all x2, blocking collectives, sent_and_summed(): lax.all_to_all(pieces, axis, split_axis=0, concat_axis=0, tiled=True)  56.8 us
    dot_general x11, matrix products, backward_product(): jnp.einsum('te,de->td', gradient, weights, preferred_element_type=jnp.flo...  52.8 us
    unnamed x228, local copies, waits for them, and re-layouts  51.1 us
    dot_general x11, matrix products, outer_sum(): jnp.einsum('td,te->de', left_arg, right_arg, preferred_element_type=jnp.f...  49.9 us
  transfers between devices with their start and end apart: 11, of which 9 were waited for; matrix products, arithmetic and copies ran while one was open for 16% of the time, Pallas kernels for 0%

commit v1 on v0

v1 whole, which is shorter than its diff:
```python
import jax
import jax.numpy as jnp
from jax import lax
from jax.sharding import PartitionSpec as P

GROUP_DIMENSION = 64
SHIFT_RANK = 32
ALL = ("seg", "span")

maximal_accuracy = lax.Precision.HIGHEST
ln_eps = 1e-05
gn_eps = 0.00064


def swap(block, bit):
    count = lax.axis_size("seg") * lax.axis_size("span")
    return lax.ppermute(block, ALL, [(i, i ^ bit) for i in range(count)])


def swap_core(block):
    return swap(block, 1)


def swap_low(block):
    return swap(block, 2)


def swap_high(block):
    return swap(block, 4)


def plane_groups():
    half = lax.axis_size("seg") // 2
    return [[2 * j + h for j in range(half)] for h in range(2)]


def in_order(own, other, second):
    return jnp.where(second, other, own), jnp.where(second, own, other)


def span_gather(block):
    place = lax.axis_index("span")
    low, core = place // 2, place % 2
    p0, p1 = in_order(block, swap_low(block), low == 1)
    q = swap_core(jnp.stack([p0, p1]))
    a0, a1 = in_order(p0, q[0], core == 1)
    b0, b1 = in_order(p1, q[1], core == 1)
    return jnp.concatenate([a0, a1, b0, b1], axis=0)


def span_reduce(part):
    place = lax.axis_index("span")
    low, core = place // 2, place % 2
    rows = part.shape[0] // 4
    b = part.reshape(2, 2, rows, part.shape[1])
    keep = jnp.where(core == 1, b[:, 1], b[:, 0])
    send = jnp.where(core == 1, b[:, 0], b[:, 1]).astype(jnp.bfloat16)
    got = swap_core(send)
    both = keep.astype(jnp.float32) + got.astype(jnp.float32)
    mine = jnp.where(low == 1, both[1], both[0])
    send = jnp.where(low == 1, both[0], both[1]).astype(jnp.bfloat16)
    return mine + swap_low(send).astype(jnp.float32)


def plane_gather(block):
    high = lax.axis_index("seg") % 2
    first, second = in_order(block, swap_high(block), high == 1)
    return lax.all_gather(
        jnp.concatenate([first, second], axis=0),
        "seg",
        axis=0,
        tiled=True,
        axis_index_groups=plane_groups(),
    )


def plane_reduce(part):
    high = lax.axis_index("seg") % 2
    pair = lax.psum_scatter(
        part, "seg", scatter_dimension=0, tiled=True, axis_index_groups=plane_groups()
    )
    rows = pair.shape[0] // 2
    mine = jnp.where(high == 1, pair[rows:], pair[:rows])
    send = jnp.where(high == 1, pair[:rows], pair[rows:])
    return mine.astype(jnp.float32) + swap_high(send).astype(jnp.float32)


def split_columns(block):
    place = lax.axis_index("span")
    n = block.shape[1] // 4

    def columns(at):
        return lax.dynamic_slice_in_dim(block, at * n, n, 1)

    pieces = [columns(place)] + [swap(columns(place ^ bit), bit) for bit in (1, 2, 3)]
    result = jnp.zeros((4, block.shape[0], n), block.dtype)
    for bit, piece in enumerate(pieces):
        result = lax.dynamic_update_index_in_dim(result, piece, place ^ bit, 0)
    return result.reshape(4 * block.shape[0], n)


def join_columns(block):
    place = lax.axis_index("span")
    r, n = block.shape[0] // 4, block.shape[1]

    def rows(at):
        return lax.dynamic_slice_in_dim(block, at * r, r, 0)

    result = jnp.zeros((r, 4 * n), block.dtype)
    for bit in range(4):
        piece = rows(place ^ bit)
        if bit:
            piece = swap(piece, bit)
        result = lax.dynamic_update_slice_in_dim(result, piece, (place ^ bit) * n, 1)
    return result


def product_lower(left_arg, right_arg):
    return jnp.dot(left_arg, right_arg, preferred_element_type=jnp.float32)


def outer_sum(left_arg, right_arg):
    return jnp.einsum("td,te->de", left_arg, right_arg, preferred_element_type=jnp.float32)


def backward_product(gradient, weights):
    return jnp.einsum("te,de->td", gradient, weights, preferred_element_type=jnp.float32)


def norm_rows(values, gain_vec, offset):
    centre = values - jnp.mean(values, -1, keepdims=True)
    row_rstd = lax.rsqrt(jnp.mean(centre * centre, -1, keepdims=True) + ln_eps)
    unit_rows = centre * row_rstd
    return (unit_rows * gain_vec + offset, unit_rows, row_rstd)


def norm_back(gradient, unit_rows, row_rstd, gain_vec):
    scaled = gradient * gain_vec
    return row_rstd * (
        scaled
        - jnp.mean(scaled, -1, keepdims=True)
        - unit_rows * jnp.mean(scaled * unit_rows, -1, keepdims=True)
    )


def prior_rows(values):
    return jnp.concatenate([jnp.zeros_like(values[:1]), values[:-1]], axis=0)


def next_rows(values):
    return jnp.concatenate([values[1:], jnp.zeros_like(values[:1])], axis=0)


def gather_small(block):
    return lax.all_gather(block, ALL, axis=0, tiled=True)


def reduce_small(part):
    count = lax.axis_size("seg") * lax.axis_size("span")
    rows, width = part.shape[0] // count, part.shape[1]
    pieces = part.astype(jnp.bfloat16).reshape(count, rows, width)
    arrived = lax.all_to_all(pieces, ALL, split_axis=0, concat_axis=0, tiled=True)
    return arrived.astype(jnp.float32).sum(axis=0)


def weighted_kv_local(
    acceptance_lines, address_mapped, content_mapped, logged_fading, reward_array, start_state
):
    token_rows, group_count, head_size = acceptance_lines.shape
    block_len = min(64, token_rows)
    block_count = token_rows // block_len

    def to_blocks(input_tensor):
        return input_tensor.reshape(block_count, block_len, group_count, head_size)

    acceptance_tile = to_blocks(acceptance_lines)
    address_tile = to_blocks(address_mapped)
    content_tile = to_blocks(content_mapped)
    dec_blk = to_blocks(logged_fading)
    running = jnp.cumsum(dec_blk, axis=1)
    rec_scaled = acceptance_tile * jnp.exp(running - dec_blk)
    key_scaled = address_tile * jnp.exp(-running)
    scores = jnp.einsum("bthk,bihk->bhti", rec_scaled, key_scaled, precision=maximal_accuracy)
    lower_mask = jnp.arange(block_len)[:, None] > jnp.arange(block_len)[None, :]
    scores = jnp.where(lower_mask, scores, 0.0)
    intra_out = jnp.einsum("bhti,bihv->bthv", scores, content_tile, precision=maximal_accuracy)
    diagonal_term = (
        jnp.sum(acceptance_tile * reward_array * address_tile, axis=-1, keepdims=True)
        * content_tile
    )
    block_total = running[:, -1]
    key_end = address_tile * jnp.exp(block_total[:, None] - running)
    block_state = jnp.einsum("bihk,bihv->bhkv", key_end, content_tile, precision=maximal_accuracy)

    def pass_state(transported_memory, block_item):
        return (
            jnp.exp(block_item[0])[..., None] * transported_memory + block_item[1],
            transported_memory,
        )

    final_state, start_states = lax.scan(pass_state, start_state, (block_total, block_state))
    inter_out = jnp.einsum("bthk,bhkv->bthv", rec_scaled, start_states, precision=maximal_accuracy)
    return (intra_out + diagonal_term + inter_out).reshape(token_rows, group_count, head_size)


def shards(
    inputs,
    cotangent,
    states,
    vectors,
    time_mix_weight,
    output_weight,
    channel_receptance_weight,
    rank_down_weight,
    rank_up_weight,
    channel_key_weight,
    channel_value_weight,
):
    token_rows, width = inputs.shape
    ranks = 5 * SHIFT_RANK
    own_width = time_mix_weight.shape[2]
    hidden = channel_key_weight.shape[1]
    local_heads = own_width // GROUP_DIMENSION
    col_start = lax.axis_index("span") * own_width
    position = lax.axis_index("span") * token_rows

    proj_w = plane_gather(jnp.moveaxis(time_mix_weight, 0, 1).reshape(-1, 4 * own_width))
    key_all = plane_gather(jnp.concatenate([output_weight.T, channel_key_weight], axis=1))
    value_all = plane_gather(
        jnp.concatenate([split_columns(channel_receptance_weight), channel_value_weight.T], axis=1)
    )
    down_weight = gather_small(rank_down_weight)
    up_turned = gather_small(jnp.concatenate([rank_up_weight.T, vectors.T], axis=1))
    up_weight = up_turned[:, : ranks + 64].T
    vec = up_turned[:, ranks + 64 :].T.astype(jnp.float32)

    def own_cols(line):
        return lax.dynamic_slice_in_dim(line, col_start, own_width, line.ndim - 1)

    def own_rows(values):
        return lax.dynamic_slice_in_dim(values, position, token_rows, 0)

    def place_cols(values):
        blank = jnp.zeros(values.shape[:-1] + (width,), jnp.float32)
        return lax.dynamic_update_slice_in_dim(blank, values, col_start, values.ndim - 1)

    def w_proj(g):
        return proj_w[:, g * own_width : (g + 1) * own_width]

    out_w, key_w = key_all[:, :own_width], key_all[:, own_width:]
    recept_w, value_w = value_all[:, :own_width], value_all[:, own_width:]

    x_in = inputs.astype(jnp.float32)
    x_seg = span_gather(inputs).astype(jnp.float32)
    normed, unit_one, _ = norm_rows(x_seg, vec[0], vec[1])
    seg_rows = normed.shape[0]
    head_shape = (seg_rows, local_heads, GROUP_DIMENSION)
    shifted = prior_rows(normed) - normed
    mix_in = (normed + shifted * vec[2]).astype(jnp.bfloat16)
    squash = jnp.tanh(product_lower(mix_in, down_weight[:, :ranks]))
    squash_low = squash.astype(jnp.bfloat16).reshape(seg_rows, 5, SHIFT_RANK)
    up_mods = up_weight[:ranks].reshape(5, SHIFT_RANK, width)
    mods = jnp.einsum("spi,pif->psf", squash_low, up_mods, preferred_element_type=jnp.float32)
    coeffs = [vec[3 + g] + mods[g] for g in range(5)]
    mixes = [(normed + shifted * coeffs[g]).astype(jnp.bfloat16) for g in range(5)]
    recept = product_lower(mixes[3], w_proj(0))
    key_proj = product_lower(mixes[1], w_proj(1))
    val_proj = product_lower(mixes[2], w_proj(2))
    gate_pre = product_lower(mixes[4], w_proj(3))
    gate_act = jax.nn.silu(gate_pre)
    decay_tanh = jnp.tanh(product_lower(mixes[0], down_weight[:, ranks:]))
    decay_low = decay_tanh.astype(jnp.bfloat16)
    up_decay_own = own_cols(up_weight[ranks:])
    log_decay = -jnp.exp(own_cols(vec[8]) + product_lower(decay_low, up_decay_own))
    reward = own_cols(vec[9]).reshape(local_heads, GROUP_DIMENSION)
    wkv, wkv_pullback = jax.vjp(
        weighted_kv_local,
        recept.reshape(head_shape),
        key_proj.reshape(head_shape),
        val_proj.reshape(head_shape),
        log_decay.reshape(head_shape),
        reward,
        states[0],
    )
    centre = wkv - jnp.mean(wkv, -1, keepdims=True)
    gn_rstd = lax.rsqrt(jnp.mean(centre * centre, -1, keepdims=True) + gn_eps)
    gn_unit = centre * gn_rstd
    grouped = gn_unit.reshape(seg_rows, own_width) * own_cols(vec[10]) + own_cols(vec[11])
    mixed = (grouped * gate_act).astype(jnp.bfloat16)
    resid = x_in + span_reduce(backward_product(mixed, out_w).astype(jnp.bfloat16))

    normed_two, unit_two, rstd_two = norm_rows(resid, vec[12], vec[13])
    n2 = span_gather(normed_two.astype(jnp.bfloat16)).astype(jnp.float32)
    shifted_two = prior_rows(n2) - n2
    key_in = (n2 + shifted_two * vec[14]).astype(jnp.bfloat16)
    rec_in = (n2 + shifted_two * vec[15]).astype(jnp.bfloat16)
    hidden_two = product_lower(key_in, key_w)
    active = jax.nn.relu(hidden_two)
    squared = (active * active).astype(jnp.bfloat16)
    value_out = span_reduce(backward_product(squared, value_w).astype(jnp.bfloat16))
    rec_pre = join_columns(product_lower(rec_in, recept_w).astype(jnp.bfloat16))
    rec_gate = jax.nn.sigmoid(rec_pre.astype(jnp.float32))
    output = (resid + rec_gate * value_out).astype(jnp.bfloat16)

    grad_out = cotangent.astype(jnp.float32)
    g_value = (grad_out * rec_gate).astype(jnp.bfloat16)
    g_rec = (grad_out * value_out * rec_gate * (1.0 - rec_gate)).astype(jnp.bfloat16)
    g_value_all = span_gather(g_value)
    g_rec_own = split_columns(g_rec)
    value_part = outer_sum(g_value_all, squared).astype(jnp.bfloat16)
    rec_part = outer_sum(rec_in, g_rec_own).astype(jnp.bfloat16)
    g_hid = (product_lower(g_value_all, value_w) * 2.0 * active).astype(jnp.bfloat16)
    key_part = outer_sum(key_in, g_hid).astype(jnp.bfloat16)
    cm_grad = plane_reduce(jnp.concatenate([rec_part, value_part, key_part], axis=1))
    g_key_in = backward_product(g_hid, key_w)
    g_rec_in = backward_product(g_rec_own, recept_w)
    vec_fourteen = jnp.sum(g_key_in * shifted_two, axis=0)
    vec_fifteen = jnp.sum(g_rec_in * shifted_two, axis=0)
    g_shift_two = g_key_in * vec[14] + g_rec_in * vec[15]
    g_n2_part = g_key_in + g_rec_in - g_shift_two + next_rows(g_shift_two)
    g_n2 = span_reduce(g_n2_part.astype(jnp.bfloat16))
    vec_twelve = jnp.sum(g_n2 * unit_two, axis=0)
    vec_thirteen = jnp.sum(g_n2, axis=0)
    g_resid = grad_out + norm_back(g_n2, unit_two, rstd_two, vec[12])

    g_att = span_gather(g_resid.astype(jnp.bfloat16))
    out_part = outer_sum(g_att, mixed).astype(jnp.bfloat16)
    g_mixed = product_lower(g_att, out_w)
    g_grouped = g_mixed * gate_act
    gate_sig = jax.nn.sigmoid(gate_pre)
    g_gate = (g_mixed * grouped * gate_sig * (1.0 + gate_pre * (1.0 - gate_sig))).astype(jnp.bfloat16)
    vec_ten = jnp.sum(g_grouped * gn_unit.reshape(seg_rows, own_width), axis=0)
    vec_eleven = jnp.sum(g_grouped, axis=0)
    g_unit = (g_grouped * own_cols(vec[10])).reshape(head_shape)
    g_wkv = gn_rstd * (
        g_unit
        - jnp.mean(g_unit, -1, keepdims=True)
        - gn_unit * jnp.mean(g_unit * gn_unit, -1, keepdims=True)
    )
    g_r, g_k, g_v, g_w, g_u, g_start = wkv_pullback(g_wkv)
    state_grad = g_start[None]
    g_recept = g_r.reshape(seg_rows, own_width).astype(jnp.bfloat16)
    g_key = g_k.reshape(seg_rows, own_width).astype(jnp.bfloat16)
    g_val = g_v.reshape(seg_rows, own_width).astype(jnp.bfloat16)
    g_expo = g_w.reshape(seg_rows, own_width) * log_decay
    vec_eight = jnp.sum(g_expo, axis=0)
    g_ww = g_expo.astype(jnp.bfloat16)
    proj_parts = [
        outer_sum(mixes[3], g_recept).astype(jnp.bfloat16),
        outer_sum(mixes[1], g_key).astype(jnp.bfloat16),
        outer_sum(mixes[2], g_val).astype(jnp.bfloat16),
        outer_sum(mixes[4], g_gate).astype(jnp.bfloat16),
    ]
    tm_grad = plane_reduce(jnp.concatenate([out_part] + proj_parts, axis=1))

    up_decay_grad = outer_sum(decay_low, g_ww)
    g_decay_hidden = (
        backward_product(g_ww, up_decay_own) * (1.0 - decay_tanh * decay_tanh)
    ).astype(jnp.bfloat16)
    down_decay_grad = outer_sum(mixes[0], g_decay_hidden)
    g_mix = [
        backward_product(g_decay_hidden, down_weight[:, ranks:]),
        backward_product(g_key, w_proj(1)),
        backward_product(g_val, w_proj(2)),
        backward_product(g_recept, w_proj(0)),
        backward_product(g_gate, w_proj(3)),
    ]
    g_times = [g * shifted for g in g_mix]
    vec_mixes = [jnp.sum(g, axis=0) for g in g_times]
    g_mods = jnp.stack(g_times).astype(jnp.bfloat16)
    up_mods_grad = jnp.einsum(
        "tgj,gtd->gjd", squash_low, g_mods, preferred_element_type=jnp.float32
    ).reshape(ranks, width)
    g_squash = jnp.einsum(
        "gtd,gjd->tgj", g_mods, up_mods, preferred_element_type=jnp.float32
    ).reshape(seg_rows, ranks)
    g_hidden = (g_squash * (1.0 - squash * squash)).astype(jnp.bfloat16)
    down_mods_grad = outer_sum(mix_in, g_hidden)
    g_mix_in = backward_product(g_hidden, down_weight[:, :ranks])
    vec_two = jnp.sum(g_mix_in * shifted, axis=0)
    g_shifted = g_mix_in * vec[2]
    g_normed = g_mix_in
    for g in range(5):
        g_shifted = g_shifted + g_mix[g] * coeffs[g]
        g_normed = g_normed + g_mix[g]
    g_normed = g_normed - g_shifted + next_rows(g_shifted)
    vec_zero = jnp.sum(g_normed * unit_one, axis=0)
    vec_one = jnp.sum(g_normed, axis=0)
    g_n1 = span_reduce(g_normed.astype(jnp.bfloat16))
    _, unit_own, rstd_own = norm_rows(x_in, vec[0], vec[1])
    x_grad = g_resid + norm_back(g_n1, unit_own, rstd_own, vec[0])
    vec_part = jnp.stack(
        [vec_zero, vec_one, vec_two]
        + vec_mixes
        + [
            place_cols(vec_eight),
            place_cols(g_u.reshape(own_width)),
            place_cols(vec_ten),
            place_cols(vec_eleven),
            vec_twelve,
            vec_thirteen,
            vec_fourteen,
            vec_fifteen,
        ]
    )
    up_part = jnp.concatenate([up_mods_grad, place_cols(up_decay_grad)], axis=0)
    small = reduce_small(
        jnp.concatenate([down_mods_grad, down_decay_grad, up_part.T, vec_part.T], axis=1)
    )
    rank_all = ranks + 64
    down_grad, up_grad, vec_grad = (
        small[:, :rank_all],
        small[:, rank_all : 2 * rank_all].T,
        small[:, 2 * rank_all :].T,
    )
    rec_grad = join_columns(cm_grad[:, :own_width])
    value_grad = cm_grad[:, own_width : own_width + hidden].T
    key_grad = cm_grad[:, own_width + hidden :]
    out_grad = tm_grad[:, :own_width].T
    proj_grad = jnp.moveaxis(tm_grad[:, own_width:].reshape(-1, 4, own_width), 1, 0)
    return (
        output,
        x_grad,
        state_grad,
        vec_grad,
        proj_grad,
        out_grad,
        rec_grad,
        down_grad,
        up_grad,
        key_grad,
        value_grad,
    )


def solution(mesh):
    rows, columns = P(ALL, None), P(None, ALL)
    state = P("seg", "span", None, None)
    time_mix = P(None, "seg", "span")
    turned, straight = P("span", "seg"), P("seg", "span")
    return jax.shard_map(
        shards,
        mesh=mesh,
        in_specs=(
            rows, rows, state, columns, time_mix, turned, rows, rows, columns, straight, turned
        ),
        out_specs=(
            rows, rows, state, columns, time_mix, turned, rows, rows, columns, straight, turned
        ),
        check_vma=False,
    )
```

time: 1990 us -> 855 us (0.43)
  waiting for transfers between devices: 1220 us -> 175 us
  local copies, waits for them, and re-layouts: 265 us -> 167 us
  starting transfers between devices: 13.7 us -> 45.5 us
    unnamed x10 -> x7, waiting for transfers between devices: 660 us -> 10.2 us
    all_gather x4 -> x3, waiting for transfers between devices: 286 us -> 0.02 us  [plane_gather(): lax.all_gather(jnp.concatenate([first, second], axis=0), 'seg', axis=0, t...]
    reduce_scatter x2 -> x0, waiting for transfers between devices: 254 us -> none  [the longest x1 252 us: sum_packed(): lax.psum_scatter(lines, axis, tiled=True).reshape(-1)]
    ppermute x1 -> x33, waiting for transfers between devices: 0.81 us -> 158 us  [swap(): return lax.ppermute(block, ALL, [(i, i ^ bit) for i in range(count)])]
    all_to_all x3 -> x0, blocking collectives: 85.2 us -> none  [the longest x2 56.8 us: sent_and_summed(): lax.all_to_all(pieces, axis, split_axis=0, concat_axis=0, tiled=True)]
    all_gather x0 -> x2, blocking collectives: none -> 80.7 us  [gather_small(): return lax.all_gather(block, ALL, axis=0, tiled=True)]
    reshape x7 -> x5, local copies, waits for them, and re-layouts: 68.4 us -> 7.37 us  [the longest x1 2.23 us: shards(): g_expo = g_w.reshape(seg_rows, own_width) * log_decay]
    ppermute x1 -> x33, starting transfers between devices: 2.48 us -> 37.2 us  [swap(): return lax.ppermute(block, ALL, [(i, i ^ bit) for i in range(count)])]
  transfers between devices with their start and end apart: 11 -> 39, of which waited for: 9 -> 22; matrix products, arithmetic and copies ran while one was open for 16% -> 38% of each run, Pallas kernels for 0% -> 0%
where the time goes in v1:
time: 855 us; the launch traced here: 845 us
  matrix products  214 us (25%)
  waiting for transfers between devices  175 us (20%)
  local copies, waits for them, and re-layouts  167 us (20%)
  other arithmetic  146 us (17%)
  blocking collectives  80.7 us (9%)
  starting transfers between devices  45.5 us (5%)
  between operations  16.7 us (2%)
    ppermute x33, waiting for transfers between devices, swap(): return lax.ppermute(block, ALL, [(i, i ^ bit) for i in range(count)])  158 us
    all_gather x2, blocking collectives, gather_small(): return lax.all_gather(block, ALL, axis=0, tiled=True)  80.7 us
    unnamed x382, local copies, waits for them, and re-layouts  68 us
    dot_general x11, matrix products, backward_product(): jnp.einsum('te,de->td', gradient, weights, preferred_element_type=jnp.flo...  64.6 us
    dot_general x11, matrix products, product_lower(): return jnp.dot(left_arg, right_arg, preferred_element_type=jnp.float32)  37.6 us
    ppermute x33, starting transfers between devices, swap(): return lax.ppermute(block, ALL, [(i, i ^ bit) for i in range(count)])  37.2 us
    dot_general x11, matrix products, outer_sum(): jnp.einsum('td,te->de', left_arg, right_arg, preferred_element_type=jnp.f...  32.5 us
    convert_element_type x3, other arithmetic, shards(): (normed + shifted * coeffs[g]).astype(jnp.bfloat16)  21.3 us
  transfers between devices with their start and end apart: 39, of which 22 were waited for; matrix products, arithmetic and copies ran while one was open for 38% of the time, Pallas kernels for 0%

profile of v1, /device:TPU:1, one launch (start us, length us, event | category | flops | bytes accessed | tf_op | source)
XLA Modules:
  0.0 844.9 jit_solution(14277213705387288029)
XLA Ops:
  34.8 45.4 %all_gather.15 = bf16[2048,240]{1,0:T(8,128)(2,1)S(1)} all-gather(bf16[16,240]{1,0:T(8,128)(2,1)S(1)} %pad_maximum_fusion.20), channel_id=1, replica_groups=mesh['seg'=32,'span'=4] {'seg','span'}, dimensions={0}, use_global_device_ids=true | all-gather | bytes 990720 | tf_op jit(solution)/shard_map/all_gather | solution.py:155
  80.4 9.4 %fusion.170 = (f32[1,2048]{0,1:T(8,128)}, f32[1,2048]{0,1:T(8,128)}, f32[2048]{0:T(1024)S(1)}, f32[2048]{0:T(1024)S(1)}, f32[2048]{0:T(1024)S(1)}, /*index=5*/f3...) fusion(f32[16,2048]{0,1:T(8,128)S(1)} %convert_bitcast_fusion), kind=kLoop, calls=%fused_computation.419 | loop fusion | bytes 262144 | tf_op jit(solution)/shard_map/slice | solution.py:288
  89.8 35.3 %all_gather.16 = bf16[2048,224]{1,0:T(8,128)(2,1)S(1)} all-gather(bf16[16,224]{1,0:T(8,128)(2,1)S(1)} %copy-done.166), channel_id=1, replica_groups=mesh['seg'=32,'span'=4] {'seg','span'}, dimensions={0}, use_global_device_ids=true | all-gather | bytes 924672 | tf_op jit(solution)/shard_map/all_gather | solution.py:155
  137.5 6.4 collective-permute-done.11
  159.2 6.7 add_convert_fusion.6
  176.7 6.3 add_convert_fusion.7
  183.1 8.2 add_convert_fusion.3
  204.8 7.7 fusion.141
  224.8 19.9 %while.35 = (s32[]{:T(128)}, f32[8,64,64]{2,1,0:T(8,128)S(1)}, f32[8,8,64,64]{3,2,1,0:T(8,128)}, f32[8,8,64]{2,1,0:T(8,128)S(1)}, f32[8,8,64,1]{2,1,3,0:T(8,128)...) while((s32[]{:T(128)}, f32[8,64,64]{2,1,0:T(8,128)S(1)}, f32[8,8,64,64]{3,2,1,0:T(8,128)}, ...), condition=%wide.region_5.6_spmd, body=%wide.region_4.5_spmd.sunk | while | flops 65538 | bytes 807021 | solution.py:201
  280.0 12.6 %collective-permute-done.5 = bf16[128,2048]{1,0:T(8,128)(2,1)S(1)} collective-permute-done((bf16[128,2048]{1,0:T(8,128)(2,1)S(1)}, bf16[128,2048]{1,0:T(8,128)(2,1)S(1)}, u32[]{:S(2)}, u32[]{:S(2)}) %collective-permute-start.5) | collective-permute-done | bytes 524320 | tf_op jit(solution)/shard_map/ppermute | solution.py:17
  294.6 11.9 %collective-permute-done.6 = bf16[128,2048]{1,0:T(8,128)(2,1)S(1)} collective-permute-done((bf16[128,2048]{1,0:T(8,128)(2,1)S(1)}, bf16[128,2048]{1,0:T(8,128)(2,1)S(1)}, u32[]{:S(2)}, u32[]{:S(2)}) %collective-permute-start.6) | collective-permute-done | bytes 524320 | tf_op jit(solution)/shard_map/ppermute | solution.py:17
  324.7 8.2 fusion.26
  344.0 13.5 %collective-permute-done.13 = bf16[128,512]{1,0:T(8,128)(2,1)S(1)} collective-permute-done((bf16[128,512]{1,0:T(8,128)(2,1)S(1)}, bf16[128,512]{1,0:T(8,128)(2,1)S(1)}, u32[]{:S(2)}, u32[]{:S(2)}) %collective-permute-start.13) | collective-permute-done | bytes 131104 | tf_op jit(solution)/shard_map/ppermute | solution.py:17
  362.4 13.0 %collective-permute-done.17 = bf16[128,2048]{1,0:T(8,128)(2,1)S(1)} collective-permute-done((bf16[128,2048]{1,0:T(8,128)(2,1)S(1)}, bf16[128,2048]{1,0:T(8,128)(2,1)S(1)}, u32[]{:S(2)}, u32[]{:S(2)}) %collective-permute-start.17) | collective-permute-done | bytes 524320 | tf_op jit(solution)/shard_map/ppermute | solution.py:17
  392.0 6.9 fusion.8
  409.4 13.0 %collective-permute-done.23 = bf16[128,2048]{1,0:T(8,128)(2,1)S(1)} collective-permute-done((bf16[128,2048]{1,0:T(8,128)(2,1)S(1)}, bf16[128,2048]{1,0:T(8,128)(2,1)S(1)}, u32[]{:S(2)}, u32[]{:S(2)}) %collective-permute-start.23) | collective-permute-done | bytes 524320 | tf_op jit(solution)/shard_map/ppermute | solution.py:17
  425.4 12.1 %collective-permute-done.24 = bf16[128,2048]{1,0:T(8,128)(2,1)S(1)} collective-permute-done((bf16[128,2048]{1,0:T(8,128)(2,1)S(1)}, bf16[128,2048]{1,0:T(8,128)(2,1)S(1)}, u32[]{:S(2)}, u32[]{:S(2)}) %collective-permute-start.24) | collective-permute-done | bytes 524320 | tf_op jit(solution)/shard_map/ppermute | solution.py:17
  479.1 27.3 %while.36 = (s32[]{:T(128)}, f32[8,64,64]{2,1,0:T(8,128)S(1)}, f32[8,8,64]{2,1,0:T(8,128)S(1)}, f32[8,8,64,64]{3,2,1,0:T(8,128)}, f32[8,8,64,64]{3,2,1,0:T(8,128...) while((s32[]{:T(128)}, f32[8,64,64]{2,1,0:T(8,128)S(1)}, ...), condition=%wide.region_18.19_spmd.clone, body=%wide.region_16.18_spmd.clone.sunk | while | flops 196612 | bytes 936092 | solution.py:201
  506.4 7.0 fusion.100
  525.0 7.5 fusion.38
  534.6 6.9 fusion.34
  560.3 13.6 %copy.215 = bf16[2048,2560]{1,0:T(8,128)(2,1)} copy(bf16[2048,2560]{0,1:T(8,128)(2,1)} %fusion.29) | data formatting | bytes 20971520
  590.2 9.1 %pad_maximum_fusion = bf16[2048,4096]{0,1:T(8,128)(2,1)} fusion(bf16[2048,1792]{0,1:T(8,128)(2,1)S(1)} %convolution_convert_fusion, bf16[2048,1792]{0,1:T(8,128)(2,1)S(1)} %convolution_convert_fusion.1, bf16[2048,512]{0,1:T(8,128)(2,1)} %convolution_convert_fusion.4), kind=kLoop, calls=%fused_computation.13 | loop fusion | flops 50331648 | bytes 33554432 | tf_op jit(solution)/shard_map/concatenate | solution.py:314
  599.3 21.4 %copy.217 = bf16[2048,4096]{1,0:T(8,128)(2,1)} copy(bf16[2048,4096]{0,1:T(8,128)(2,1)} %pad_maximum_fusion) | data formatting | bytes 33554432
  662.1 20.8 %multiply_reduce_fusion.6 = (bf16[2048]{0:T(1024)(128)(2,1)S(1)}, bf16[2048]{0:T(1024)(128)(2,1)S(1)}, bf16[2048]{0:T(1024)(128)(2,1)S(1)}, bf16[2048]{0:T(1024)...) fusion(f32[512,2048]{1,0:T(8,128)} %get-tuple-element.471, ...), kind=kOutput, calls=%fused_computation.167 | convolution fusion | flops 364892160 | bytes 55681024 | tf_op jit(solution)/shard_map/te,de->td/dot_general | solution.py:127
  687.2 13.0 %fusion.161 = (bf16[2048]{0:T(1024)(128)(2,1)S(1)}, bf16[2048]{0:T(1024)(128)(2,1)S(1)}, bf16[512,2048]{1,0:T(8,128)(2,1)S(1)}) fusion(f32[512]{0:T(512)S(1)} %copy-done.140, f32[512]{0:T(512)S(1)} %copy-done.138, bf16[128,2048]{1,0:T(8,128)(2,1)S(1)} %copy-done.21, bf16[128,2048]{1,0:T(8,128)(2,1)S(1)} %copy-done.24, bf16[128,2048]{1,0:T(8,128)(2,1)S(1)} %copy-done.18, ...), kind=kLoop, calls=%fused_computation.413 | loop fusion | flops 22016000 | bytes 37752832 | tf_op jit(solution)/shard_map/reduce_sum | solution.py:388
  707.8 6.6 convolution_convert_fusion.10
  723.9 8.0 all-to-all-start
  736.9 24.7 %collective-permute-done.27 = bf16[128,2048]{1,0:T(8,128)(2,1)S(1)} collective-permute-done((bf16[128,2048]{1,0:T(8,128)(2,1)S(1)}, bf16[128,2048]{1,0:T(8,128)(2,1)S(1)}, u32[]{:S(2)}, u32[]{:S(2)}) %collective-permute-start.27) | collective-permute-done | bytes 524320 | tf_op jit(solution)/shard_map/ppermute | solution.py:17
  765.0 7.0 all-to-all-done
  777.8 8.5 %collective-permute-done.28 = bf16[64,2560]{1,0:T(8,128)(2,1)S(1)} collective-permute-done((bf16[64,2560]{1,0:T(8,128)(2,1)S(1)}, bf16[64,2560]{1,0:T(8,128)(2,1)S(1)}, u32[]{:S(2)}, u32[]{:S(2)}) %collective-permute-start.28) | collective-permute-done | bytes 327712 | tf_op jit(solution)/shard_map/ppermute | solution.py:17
  787.4 10.1 %reduce-scatter.9.cloned.1.call-done = bf16[128,4096]{1,0:T(8,128)(2,1)} async-done(((bf16[2048,4096]{1,0:T(8,128)(2,1)}), bf16[128,4096]{1,0:T(8,128)(2,1)}) %reduce-scatter.9.cloned.1.call-update) | async-done | bytes 1048592
  (751 shorter events, 447.0 us)
Async XLA Ops:
  7.2 184.2 %all-gather.4.cloned.1.call-start = ((), (), s32[]{:S(2)}) async-start(), calls=%async_computation.3 | async-start | bytes 8912896 | tf_op jit(solution)/shard_map/all_gather | solution.py:68
  8.3 9.6 %collective-permute-start.2 = (bf16[64,2048]{1,0:T(8,128)(2,1)S(1)}, bf16[64,2048]{1,0:T(8,128)(2,1)S(1)}, u32[]{:S(2)}, u32[]{:S(2)}) collective-permute-start(bf16[64,2048]{1,0:T(8,128)(2,1)S(1)} %bitcast.518), channel_id=1, source_target_pairs={{0,4},{1,5},{2,6},{3,7},{4,0},{5,1},{6,2},{7,3},{8,12},{9,13},{10,... | collective-permute-start | bytes 786440 | tf_op jit(solution)/shard_map/ppermute | solution.py:17
  18.8 253.3 %all-gather.6.cloned.1.call-start = ((), (), s32[]{:S(2)}) async-start(), calls=%async_computation.4 | async-start | bytes 10027008 | tf_op jit(solution)/shard_map/all_gather | solution.py:68
  18.9 8.6 %collective-permute-start.3 = (bf16[64,2304]{1,0:T(8,128)(2,1)S(1)}, bf16[64,2304]{1,0:T(8,128)(2,1)S(1)}, u32[]{:S(2)}, u32[]{:S(2)}) collective-permute-start(bf16[64,2304]{1,0:T(8,128)(2,1)S(1)} %pad_maximum_fusion.18), channel_id=1, source_target_pairs={{0,4},{1,5},{2,6},{3,7},{4,0},{5,1},{6,2},{7,3},{8,12},{9,13},{10,... | collective-permute-start | bytes 884744 | tf_op jit(solution)/shard_map/ppermute | solution.py:17
  28.5 296.2 %all-gather.8.cloned.1.call-start = ((), (), s32[]{:S(2)}) async-start(), calls=%async_computation.5 | async-start | bytes 10027008 | tf_op jit(solution)/shard_map/all_gather | solution.py:68
  29.2 102.4 %collective-permute-start.8 = (bf16[16,512]{1,0:T(8,128)(2,1)}, bf16[16,512]{1,0:T(8,128)(2,1)}, u32[]{:S(2)}, u32[]{:S(2)}) collective-permute-start(bf16[16,512]{1,0:T(8,128)(2,1)} %get-tuple-element.449), channel_id=1, source_target_pairs={{0,1},{1,0},{2,3},{3,2},{4,5},{5,4},{6,7},{7,6},{8,9},{9,8},{10,11... | collective-permute-start | bytes 49160 | tf_op jit(solution)/shard_map/ppermute | solution.py:17
  31.6 100.7 %collective-permute-start.9 = (bf16[16,512]{1,0:T(8,128)(2,1)S(1)}, bf16[16,512]{1,0:T(8,128)(2,1)}, u32[]{:S(2)}, u32[]{:S(2)}) collective-permute-start(bf16[16,512]{1,0:T(8,128)(2,1)S(1)} %get-tuple-element.450), channel_id=1, source_target_pairs={{0,2},{1,3},{2,0},{3,1},{4,6},{5,7},{6,4},{7,5},{8,10},{9,11},{10,... | collective-permute-start | bytes 49160 | tf_op jit(solution)/shard_map/ppermute | solution.py:17
  32.9 100.1 %collective-permute-start.10 = (bf16[16,512]{1,0:T(8,128)(2,1)S(1)}, bf16[16,512]{1,0:T(8,128)(2,1)}, u32[]{:S(2)}, u32[]{:S(2)}) collective-permute-start(bf16[16,512]{1,0:T(8,128)(2,1)S(1)} %get-tuple-element.448), channel_id=1, source_target_pairs={{0,3},{1,2},{2,1},{3,0},{4,7},{5,6},{6,5},{7,4},{8,11},{9,10},{10,... | collective-permute-start | bytes 49160 | tf_op jit(solution)/shard_map/ppermute | solution.py:17
  33.3 102.7 %collective-permute-start = (bf16[128,2048]{1,0:T(8,128)(2,1)S(1)}, bf16[128,2048]{1,0:T(8,128)(2,1)S(1)}, u32[]{:S(2)}, u32[]{:S(2)}) collective-permute-start(bf16[128,2048]{1,0:T(8,128)(2,1)S(1)} %copy-done.47), channel_id=1, source_target_pairs={{0,2},{1,3},{2,0},{3,1},{4,6},{5,7},{6,4},{7,5},{8,10},{9,11},{10,... | collective-permute-start | bytes 1572872 | tf_op jit(solution)/shard_map/ppermute | solution.py:17
  133.8 10.0 %collective-permute-start.11 = (bf16[64,2304]{1,0:T(8,128)(2,1)S(1)}, bf16[64,2304]{1,0:T(8,128)(2,1)S(1)}, u32[]{:S(2)}, u32[]{:S(2)}) collective-permute-start(bf16[64,2304]{1,0:T(8,128)(2,1)S(1)} %pad_maximum_fusion.19), channel_id=1, source_target_pairs={{0,4},{1,5},{2,6},{3,7},{4,0},{5,1},{6,2},{7,3},{8,12},{9,13},{10,... | collective-permute-start | bytes 884744 | tf_op jit(solution)/shard_map/ppermute | solution.py:17
  137.0 8.0 collective-permute-start.1
  144.9 629.1 %reduce-scatter.7.cloned.1.call-start = ((), (), s32[]{:S(2)}) async-start(), calls=%async_computation.6 | async-start | bytes 11141120
  279.4 13.2 %collective-permute-start.5 = (bf16[128,2048]{1,0:T(8,128)(2,1)S(1)}, bf16[128,2048]{1,0:T(8,128)(2,1)S(1)}, u32[]{:S(2)}, u32[]{:S(2)}) collective-permute-start(bf16[128,2048]{1,0:T(8,128)(2,1)S(1)} %fusion.132), channel_id=1, source_target_pairs={{0,2},{1,3},{2,0},{3,1},{4,6},{5,7},{6,4},{7,5},{8,10},{9,11},{10,... | collective-permute-start | bytes 1572872 | tf_op jit(solution)/shard_map/ppermute | solution.py:17
  294.2 12.3 %collective-permute-start.6 = (bf16[128,2048]{1,0:T(8,128)(2,1)S(1)}, bf16[128,2048]{1,0:T(8,128)(2,1)S(1)}, u32[]{:S(2)}, u32[]{:S(2)}) collective-permute-start(bf16[128,2048]{1,0:T(8,128)(2,1)S(1)} %add_convert_fusion.10), channel_id=1, source_target_pairs={{0,2},{1,3},{2,0},{3,1},{4,6},{5,7},{6,4},{7,5},{8,10},{9,11},{10,... | collective-permute-start | bytes 1572872 | tf_op jit(solution)/shard_map/ppermute | solution.py:17
  341.2 19.4 %collective-permute-start.16 = (bf16[128,2048]{1,0:T(8,128)(2,1)S(1)}, bf16[128,2048]{1,0:T(8,128)(2,1)S(1)}, u32[]{:S(2)}, u32[]{:S(2)}) collective-permute-start(bf16[128,2048]{1,0:T(8,128)(2,1)S(1)} %fusion.133), channel_id=1, source_target_pairs={{0,2},{1,3},{2,0},{3,1},{4,6},{5,7},{6,4},{7,5},{8,10},{9,11},{10,... | collective-permute-start | bytes 1572872 | tf_op jit(solution)/shard_map/ppermute | solution.py:17
  342.3 15.2 %collective-permute-start.13 = (bf16[128,512]{1,0:T(8,128)(2,1)S(1)}, bf16[128,512]{1,0:T(8,128)(2,1)S(1)}, u32[]{:S(2)}, u32[]{:S(2)}) collective-permute-start(bf16[128,512]{1,0:T(8,128)(2,1)S(1)} %get-tuple-element.439), channel_id=1, source_target_pairs={{0,2},{1,3},{2,0},{3,1},{4,6},{5,7},{6,4},{7,5},{8,10},{9,11},{10,... | collective-permute-start | bytes 393224 | tf_op jit(solution)/shard_map/ppermute | solution.py:17
  343.4 17.2 %collective-permute-start.14 = (bf16[128,512]{1,0:T(8,128)(2,1)S(1)}, bf16[128,512]{1,0:T(8,128)(2,1)S(1)}, u32[]{:S(2)}, u32[]{:S(2)}) collective-permute-start(bf16[128,512]{1,0:T(8,128)(2,1)S(1)} %get-tuple-element.438), channel_id=1, source_target_pairs={{0,3},{1,2},{2,1},{3,0},{4,7},{5,6},{6,5},{7,4},{8,11},{9,10},{10,... | collective-permute-start | bytes 393224 | tf_op jit(solution)/shard_map/ppermute | solution.py:17
  362.1 13.4 %collective-permute-start.17 = (bf16[128,2048]{1,0:T(8,128)(2,1)S(1)}, bf16[128,2048]{1,0:T(8,128)(2,1)S(1)}, u32[]{:S(2)}, u32[]{:S(2)}) collective-permute-start(bf16[128,2048]{1,0:T(8,128)(2,1)S(1)} %get-tuple-element.403), channel_id=1, source_target_pairs={{0,2},{1,3},{2,0},{3,1},{4,6},{5,7},{6,4},{7,5},{8,10},{9,11},{10,... | collective-permute-start | bytes 1572872 | tf_op jit(solution)/shard_map/ppermute | solution.py:17
  375.7 9.3 %collective-permute-start.18 = (bf16[2,128,2048]{2,1,0:T(8,128)(2,1)S(1)}, bf16[2,128,2048]{2,1,0:T(8,128)(2,1)S(1)}, u32[]{:S(2)}, u32[]{:S(2)}) collective-permute-start(bf16[2,128,2048]{2,1,0:T(8,128)(2,1)S(1)} %pad_maximum_fusion.8), channel_id=1, source_target_pairs={{0,1},{1,0},{2,3},{3,2},{4,5},{5,4},{6,7},{7,6},{8,9},{9,8},{10,11... | collective-permute-start | bytes 3145736 | tf_op jit(solution)/shard_map/ppermute | solution.py:17
  377.3 7.7 collective-permute-start.21
  408.9 13.5 %collective-permute-start.23 = (bf16[128,2048]{1,0:T(8,128)(2,1)S(1)}, bf16[128,2048]{1,0:T(8,128)(2,1)S(1)}, u32[]{:S(2)}, u32[]{:S(2)}) collective-permute-start(bf16[128,2048]{1,0:T(8,128)(2,1)S(1)} %fusion.134), channel_id=1, source_target_pairs={{0,2},{1,3},{2,0},{3,1},{4,6},{5,7},{6,4},{7,5},{8,10},{9,11},{10,... | collective-permute-start | bytes 1572872 | tf_op jit(solution)/shard_map/ppermute | solution.py:17
  425.0 12.5 %collective-permute-start.24 = (bf16[128,2048]{1,0:T(8,128)(2,1)S(1)}, bf16[128,2048]{1,0:T(8,128)(2,1)S(1)}, u32[]{:S(2)}, u32[]{:S(2)}) collective-permute-start(bf16[128,2048]{1,0:T(8,128)(2,1)S(1)} %get-tuple-element.346), channel_id=1, source_target_pairs={{0,2},{1,3},{2,0},{3,1},{4,6},{5,7},{6,4},{7,5},{8,10},{9,11},{10,... | collective-permute-start | bytes 1572872 | tf_op jit(solution)/shard_map/ppermute | solution.py:17
  438.7 5.0 collective-permute-start.25
  573.9 223.6 %reduce-scatter.9.cloned.1.call-start = ((), (), s32[]{:S(2)}) async-start(), calls=%async_computation.7 | async-start | bytes 17825792
  702.6 29.4 %collective-permute-start.26 = (bf16[2,128,2048]{2,1,0:T(8,128)(2,1)}, bf16[2,128,2048]{2,1,0:T(8,128)(2,1)}, u32[]{:S(2)}, u32[]{:S(2)}) collective-permute-start(bf16[2,128,2048]{2,1,0:T(8,128)(2,1)} %select_bitcast_fusion), channel_id=1, source_target_pairs={{0,1},{1,0},{2,3},{3,2},{4,5},{5,4},{6,7},{7,6},{8,9},{9,8},{10,11... | collective-permute-start | bytes 3145736 | tf_op jit(solution)/shard_map/ppermute | solution.py:17
  723.9 48.1 %all-to-all-start = ((bf16[128,16,464]{2,1,0:T(8,128)(2,1)}), bf16[128,16,464]{2,1,0:T(8,128)(2,1)}, u32[]{:S(2)}, u32[]{:S(2)}) async-start(bf16[128,16,464]{2,1,0:T(8,128)(2,1)} %pad_maximum_fusion.5), calls=%async_computation | async-start | bytes 4194304 | tf_op jit(solution)/shard_map/all_to_all | solution.py:162
  735.2 26.4 %collective-permute-start.27 = (bf16[128,2048]{1,0:T(8,128)(2,1)S(1)}, bf16[128,2048]{1,0:T(8,128)(2,1)S(1)}, u32[]{:S(2)}, u32[]{:S(2)}) collective-permute-start(bf16[128,2048]{1,0:T(8,128)(2,1)S(1)} %fusion.135), channel_id=1, source_target_pairs={{0,2},{1,3},{2,0},{3,1},{4,6},{5,7},{6,4},{7,5},{8,10},{9,11},{10,... | collective-permute-start | bytes 1572872 | tf_op jit(solution)/shard_map/ppermute | solution.py:17
  776.1 10.2 %collective-permute-start.28 = (bf16[64,2560]{1,0:T(8,128)(2,1)S(1)}, bf16[64,2560]{1,0:T(8,128)(2,1)S(1)}, u32[]{:S(2)}, u32[]{:S(2)}) collective-permute-start(bf16[64,2560]{1,0:T(8,128)(2,1)S(1)} %copy.190), channel_id=1, source_target_pairs={{0,4},{1,5},{2,6},{3,7},{4,0},{5,1},{6,2},{7,3},{8,12},{9,13},{10,... | collective-permute-start | bytes 983048 | tf_op jit(solution)/shard_map/ppermute | solution.py:17
  805.0 14.2 %collective-permute-start.29 = (bf16[64,4096]{1,0:T(8,128)(2,1)}, bf16[64,4096]{1,0:T(8,128)(2,1)}, u32[]{:S(2)}, u32[]{:S(2)}) collective-permute-start(bf16[64,4096]{1,0:T(8,128)(2,1)} %copy.193), channel_id=1, source_target_pairs={{0,4},{1,5},{2,6},{3,7},{4,0},{5,1},{6,2},{7,3},{8,12},{9,13},{10,... | collective-permute-start | bytes 1572872 | tf_op jit(solution)/shard_map/ppermute | solution.py:17
  821.7 6.6 collective-permute-start.30
  823.7 7.9 collective-permute-start.31
  824.9 12.5 %collective-permute-start.32 = (f32[16,512]{0,1:T(8,128)S(1)}, f32[16,512]{0,1:T(8,128)S(1)}, u32[]{:S(2)}, u32[]{:S(2)}) collective-permute-start(f32[16,512]{0,1:T(8,128)S(1)} %get-tuple-element.444), channel_id=1, source_target_pairs={{0,3},{1,2},{2,1},{3,0},{4,7},{5,6},{6,5},{7,4},{8,11},{9,10},{10,... | collective-permute-start | bytes 98312 | tf_op jit(solution)/shard_map/ppermute | solution.py:17
  (192 other events, 1982.6 us)
Sparse Core Ops, SparseCore 0:
  18.9 76.7 all-gather.3
  97.9 75.9 all-gather.5
  176.0 75.4 all-gather.7
  574.1 87.2 reduce-scatter.6
  664.6 132.8 reduce-scatter.8

commit v2 on v1

v2 whole, which is shorter than its diff:
```python
import jax
import jax.numpy as jnp
from jax import lax
from jax.experimental import pallas as pl
from jax.experimental.pallas import tpu as pltpu
from jax.experimental.layout import Layout, with_layout_constraint
from jax.sharding import PartitionSpec as P

GROUP_DIMENSION = 64
SHIFT_RANK = 32
ALL = ("seg", "span")

maximal_accuracy = lax.Precision.HIGHEST
ln_eps = 1e-05
gn_eps = 0.00064


def swap(block, bit):
    count = lax.axis_size("seg") * lax.axis_size("span")
    return lax.ppermute(block, ALL, [(i, i ^ bit) for i in range(count)])


def swap_core(block):
    return swap(block, 1)


def swap_low(block):
    return swap(block, 2)


def swap_high(block):
    return swap(block, 4)


def plane_groups():
    half = lax.axis_size("seg") // 2
    return [[2 * j + h for j in range(half)] for h in range(2)]


def in_order(own, other, second):
    return jnp.where(second, other, own), jnp.where(second, own, other)


def span_gather(block):
    place = lax.axis_index("span")
    low, core = place // 2, place % 2
    p0, p1 = in_order(block, swap_low(block), low == 1)
    q = swap_core(jnp.stack([p0, p1]))
    a0, a1 = in_order(p0, q[0], core == 1)
    b0, b1 = in_order(p1, q[1], core == 1)
    return jnp.concatenate([a0, a1, b0, b1], axis=0)


def span_reduce(part):
    place = lax.axis_index("span")
    low, core = place // 2, place % 2
    rows = part.shape[0] // 4
    b = part.reshape(2, 2, rows, part.shape[1])
    keep = jnp.where(core == 1, b[:, 1], b[:, 0])
    send = jnp.where(core == 1, b[:, 0], b[:, 1]).astype(jnp.bfloat16)
    got = swap_core(send)
    both = keep.astype(jnp.float32) + got.astype(jnp.float32)
    mine = jnp.where(low == 1, both[1], both[0])
    send = jnp.where(low == 1, both[0], both[1]).astype(jnp.bfloat16)
    return mine + swap_low(send).astype(jnp.float32)


def plane_gather(*blocks):
    high = lax.axis_index("seg") % 2
    pairs = [
        jnp.concatenate(in_order(block, swap_high(block), high == 1), axis=0) for block in blocks
    ]
    whole = lax.all_gather(
        jnp.concatenate(pairs, axis=1),
        "seg",
        axis=0,
        tiled=True,
        axis_index_groups=plane_groups(),
    )
    return with_layout_constraint(whole, Layout(major_to_minor=(0, 1)))


def plane_scatter(part):
    return lax.psum_scatter(
        part, "seg", scatter_dimension=0, tiled=True, axis_index_groups=plane_groups()
    )


def finish_scatter(pair):
    high = lax.axis_index("seg") % 2
    rows = pair.shape[0] // 2
    mine = jnp.where(high == 1, pair[rows:], pair[:rows])
    send = jnp.where(high == 1, pair[:rows], pair[rows:])
    return mine.astype(jnp.float32) + swap_high(send).astype(jnp.float32)


def split_columns(block):
    place = lax.axis_index("span")
    n = block.shape[1] // 4

    def columns(at):
        return lax.dynamic_slice_in_dim(block, at * n, n, 1)

    pieces = [columns(place)] + [swap(columns(place ^ bit), bit) for bit in (1, 2, 3)]
    result = jnp.zeros((4, block.shape[0], n), block.dtype)
    for bit, piece in enumerate(pieces):
        result = lax.dynamic_update_index_in_dim(result, piece, place ^ bit, 0)
    return result.reshape(4 * block.shape[0], n)


def join_columns(block):
    place = lax.axis_index("span")
    r, n = block.shape[0] // 4, block.shape[1]

    def rows(at):
        return lax.dynamic_slice_in_dim(block, at * r, r, 0)

    result = jnp.zeros((r, 4 * n), block.dtype)
    for bit in range(4):
        piece = rows(place ^ bit)
        if bit:
            piece = swap(piece, bit)
        result = lax.dynamic_update_slice_in_dim(result, piece, (place ^ bit) * n, 1)
    return result


def product_lower(left_arg, right_arg):
    return jnp.dot(left_arg, right_arg, preferred_element_type=jnp.float32)


def outer_sum(left_arg, right_arg):
    return jnp.einsum("td,te->de", left_arg, right_arg, preferred_element_type=jnp.float32)


def backward_product(gradient, weights):
    return jnp.einsum("te,de->td", gradient, weights, preferred_element_type=jnp.float32)


def norm_rows(values, gain_vec, offset):
    centre = values - jnp.mean(values, -1, keepdims=True)
    row_rstd = lax.rsqrt(jnp.mean(centre * centre, -1, keepdims=True) + ln_eps)
    unit_rows = centre * row_rstd
    return (unit_rows * gain_vec + offset, unit_rows, row_rstd)


def norm_back(gradient, unit_rows, row_rstd, gain_vec):
    scaled = gradient * gain_vec
    return row_rstd * (
        scaled
        - jnp.mean(scaled, -1, keepdims=True)
        - unit_rows * jnp.mean(scaled * unit_rows, -1, keepdims=True)
    )


def prior_rows(values):
    return jnp.concatenate([jnp.zeros_like(values[:1]), values[:-1]], axis=0)


def next_rows(values):
    return jnp.concatenate([values[1:], jnp.zeros_like(values[:1])], axis=0)


def reduce_small(part):
    place, high = lax.axis_index("span"), lax.axis_index("seg") % 2
    planes = lax.axis_size("seg") // 2
    width = part.shape[1]
    b = part.reshape(planes, 2, 2, 2, -1, width)
    for dim, bit, move in ((3, place % 2, swap_core), (2, place // 2, swap_low), (1, high, swap_high)):
        at0, at1 = (lax.index_in_dim(b, k, dim, keepdims=False) for k in (0, 1))
        mine, send = in_order(at0, at1, bit == 1)
        b = mine.astype(jnp.float32) + move(send.astype(jnp.bfloat16)).astype(jnp.float32)
    arrived = lax.all_to_all(
        b.astype(jnp.bfloat16), "seg", split_axis=0, concat_axis=0, tiled=True, axis_index_groups=plane_groups()
    )
    return arrived.astype(jnp.float32).sum(axis=0)


CHUNK = 64
PACK = 256


def mxu(a, b, contract):
    return lax.dot_general(
        a.astype(jnp.bfloat16),
        b.astype(jnp.bfloat16),
        (contract, ((), ())),
        preferred_element_type=jnp.float32,
    )


NN, NT, TN = ((1,), (0,)), ((1,), (1,)), ((0,), (0,))


def halves(values):
    high = values.astype(jnp.bfloat16)
    return high, (values - high.astype(jnp.float32)).astype(jnp.bfloat16)


def iota2(shape, dim):
    return lax.broadcasted_iota(jnp.int32, shape, dim)


def head_ones():
    shape = (PACK, PACK)
    same = iota2(shape, 0) // GROUP_DIMENSION == iota2(shape, 1) // GROUP_DIMENSION
    return jnp.where(same, 1.0, 0.0).astype(jnp.float32)


def spread(block, ones):
    return jnp.concatenate([block] * (PACK // CHUNK), axis=0) * ones


def fold(big, ones):
    kept = big * ones
    total = kept[:CHUNK]
    for h in range(1, PACK // CHUNK):
        total = total + kept[h * CHUNK : (h + 1) * CHUNK]
    return total


def head_sum(values, ones):
    high, rest = halves(values)
    return mxu(high, ones, NN) + mxu(rest, ones, NN)


def run_sum(which, values):
    high, rest = halves(values)
    return mxu(which, high, NN) + mxu(which, rest, NN)


def row_of(values, row):
    return values[row : row + 1]


def piece_factors(run, before):
    rows = iota2((CHUNK, PACK), 0)
    t, i = iota2((CHUNK, PACK), 0), iota2((CHUNK, PACK), 1) % CHUNK
    levels = []
    for half in (32, 16):
        upper = rows % (2 * half) >= half
        reference = jnp.broadcast_to(row_of(run, half - 1), run.shape)
        for start in range(2 * half, CHUNK, 2 * half):
            here = jnp.broadcast_to(row_of(run, start + half - 1), run.shape)
            reference = jnp.where(rows >= start, here, reference)
        scale = jnp.exp(jnp.where(upper, before - reference, reference - run))
        pairs = (t // (2 * half) == i // (2 * half)) & (t % (2 * half) >= half) & (i % (2 * half) < half)
        levels.append((jnp.where(upper, scale, 0.0), jnp.where(upper, 0.0, scale), pairs))
    reference = jnp.broadcast_to(row_of(run, 7), run.shape)
    for start in range(16, CHUNK, 16):
        here = jnp.broadcast_to(row_of(run, start + 7), run.shape)
        reference = jnp.where(rows >= start, here, reference)
    pairs = (t // 16 == i // 16) & (t > i)
    to_row = jnp.exp(jnp.minimum(before - reference, 80.0))
    to_prior = jnp.exp(jnp.minimum(reference - run, 80.0))
    levels.append((to_row, to_prior, pairs))
    return levels


def lower_ones():
    return jnp.where(iota2((CHUNK, CHUNK), 0) >= iota2((CHUNK, CHUNK), 1), 1.0, 0.0).astype(jnp.float32)


def decay_of(low_ref, up_ref, par_ref):
    log_decay = -jnp.exp(par_ref[0:1] + mxu(low_ref[...], up_ref[...], NT))
    run = run_sum(lower_ones(), log_decay)
    return log_decay, run, run - log_decay


def unit_heads(wkv, ones):
    centre = wkv - head_sum(wkv, ones) * (1.0 / GROUP_DIMENSION)
    rstd = lax.rsqrt(head_sum(centre * centre, ones) * (1.0 / GROUP_DIMENSION) + gn_eps)
    return centre * rstd, rstd


def lane_groups(refs, kinds):
    width = refs[0].shape[1]
    for g in range(width // PACK):
        lanes = pl.ds(g * PACK, PACK)
        part = {"c": lambda ref: ref.at[:, lanes], "r": lambda ref: ref.at[lanes], "s": lambda ref: ref.at[g]}
        yield [ref if kind == "w" else part[kind](ref) for ref, kind in zip(refs, kinds)]


def wkv_forward_kernel(*refs):
    for group in lane_groups(refs, "ccccwrcccccs"):
        forward_heads(*group)


def wkv_backward_kernel(*refs):
    for group in lane_groups(refs, "ccccwrccccccccccc" + "s"):
        backward_heads(*group)


def forward_heads(
    r_ref, k_ref, v_ref, gate_ref, low_ref, up_ref, par_ref, first_ref, mixed_ref, wkv_ref, held_ref, state
):
    ones = head_ones()

    @pl.when(pl.program_id(0) == 0)
    def _():
        state[...] = spread(first_ref[...], ones)

    r, k, v = r_ref[...], k_ref[...], v_ref[...]
    _, run, before = decay_of(low_ref, up_ref, par_ref)
    held_ref[...] = fold(state[...], ones)
    score = jnp.zeros((CHUNK, PACK), jnp.float32)
    for to_row, to_prior, pairs in piece_factors(run, before):
        score = jnp.where(pairs, mxu(r * to_row, spread(k * to_prior, ones), NT), score)
    out = mxu(score, spread(v, ones), NN) + mxu(r * jnp.exp(before), state[...], NT)
    out = out + head_sum(r * par_ref[1:2] * k, ones) * v
    wkv_ref[...] = out
    last = row_of(run, CHUNK - 1)
    state[...] = jnp.exp(last) * state[...] + mxu(v, k * jnp.exp(last - run), TN) * ones
    unit, _ = unit_heads(out, ones)
    gate = gate_ref[...]
    mixed_ref[...] = ((unit * par_ref[2:3] + par_ref[3:4]) * gate * jax.nn.sigmoid(gate)).astype(jnp.bfloat16)


def wkv_forward(r, k, v, gate, low, up, par, first):
    rows, columns = r.shape
    chunks = rows // CHUNK
    block = pl.BlockSpec((CHUNK, columns), lambda c: (c, 0))
    whole = lambda a: pl.BlockSpec(a.shape, lambda c: (0, 0))
    return pl.pallas_call(
        wkv_forward_kernel,
        grid=(chunks,),
        in_specs=[block] * 4
        + [
            pl.BlockSpec((CHUNK, low.shape[1]), lambda c: (c, 0)),
            whole(up),
            whole(par),
            whole(first),
        ],
        out_specs=[block, block, block],
        out_shape=[
            jax.ShapeDtypeStruct((rows, columns), jnp.bfloat16),
            jax.ShapeDtypeStruct((rows, columns), jnp.float32),
            jax.ShapeDtypeStruct((rows, columns), jnp.float32),
        ],
        scratch_shapes=[pltpu.VMEM((columns // PACK, PACK, PACK), jnp.float32)],
        compiler_params=pltpu.CompilerParams(
            dimension_semantics=("arbitrary",), vmem_limit_bytes=32 * 2**20
        ),
        cost_estimate=pl.CostEstimate(
            flops=2 * 9 * PACK * rows * columns, bytes_accessed=26 * rows * columns, transcendentals=8 * rows * columns
        ),
        name="wkv_forward",
    )(r, k, v, gate, low, up, par, first)


def backward_heads(
    r_ref, k_ref, v_ref, gate_ref, low_ref, up_ref, par_ref, wkv_ref, held_ref, gm_ref,
    gr_ref, gk_ref, gv_ref, gg_ref, gw_ref, sums_ref, first_ref, state,
):
    ones = head_ones()

    @pl.when(pl.program_id(0) == 0)
    def _():
        state[...] = jnp.zeros_like(state)
        sums_ref[...] = jnp.zeros_like(sums_ref)

    r, k, v, gate = r_ref[...], k_ref[...], v_ref[...], gate_ref[...]
    bonus, gain = par_ref[1:2], par_ref[2:3]

    def add_to(row, values):
        sums_ref[row : row + 1] = sums_ref[row : row + 1] + jnp.sum(values, axis=0, keepdims=True)

    unit, rstd = unit_heads(wkv_ref[...], ones)
    sig = jax.nn.sigmoid(gate)
    g_mixed = gm_ref[...].astype(jnp.float32)
    g_grouped = g_mixed * gate * sig
    grouped = unit * gain + par_ref[3:4]
    gg_ref[...] = (g_mixed * grouped * sig * (1.0 + gate * (1.0 - sig))).astype(jnp.bfloat16)
    add_to(2, g_grouped * unit)
    add_to(3, g_grouped)
    g_unit = g_grouped * gain
    scale = 1.0 / GROUP_DIMENSION
    g_out = rstd * (
        g_unit - head_sum(g_unit, ones) * scale - unit * (head_sum(g_unit * unit, ones) * scale)
    )

    log_decay, run, before = decay_of(low_ref, up_ref, par_ref)
    last = row_of(run, CHUNK - 1)
    start = spread(held_ref[...], ones)
    end_grad = state[...]
    v_wide = spread(v, ones)
    g_score = mxu(g_out, v_wide, NT)
    score = jnp.zeros((CHUNK, PACK), jnp.float32)
    from_start = jnp.exp(before)
    g_r = from_start * mxu(g_out, start, NN)
    to_end = jnp.exp(last - run)
    g_end = to_end * mxu(v, end_grad, NN)
    g_k = g_end
    for to_row, to_prior, pairs in piece_factors(run, before):
        r_level = (r * to_row).astype(jnp.bfloat16)
        k_level = spread(k * to_prior, ones).astype(jnp.bfloat16)
        score = jnp.where(pairs, mxu(r_level, k_level, NT), score)
        g_level = jnp.where(pairs, g_score, 0.0).astype(jnp.bfloat16)
        g_r = g_r + to_row * mxu(g_level, k_level, NN)
        g_k = g_k + to_prior * fold(mxu(g_level, r_level, TN), ones)
    g_v = fold(mxu(score, g_out, TN), ones) + mxu(k * to_end, end_grad, NT)
    g_before = r * g_r
    g_run = g_before - k * g_k
    g_last = jnp.sum(k * g_end, axis=0, keepdims=True) + jnp.exp(last) * jnp.sum(
        start * end_grad, axis=0, keepdims=True
    )
    upper = jnp.where(iota2((CHUNK, CHUNK), 0) <= iota2((CHUNK, CHUNK), 1), 1.0, 0.0).astype(jnp.float32)
    g_decay = run_sum(upper, g_run) - g_before + g_last
    g_expo = g_decay * log_decay
    gw_ref[...] = g_expo.astype(jnp.bfloat16)
    add_to(0, g_expo)
    g_diag = head_sum(g_out * v, ones)
    add_to(1, r * k * g_diag)
    gr_ref[...] = (g_r + bonus * k * g_diag).astype(jnp.bfloat16)
    gk_ref[...] = (g_k + bonus * r * g_diag).astype(jnp.bfloat16)
    gv_ref[...] = (g_v + head_sum(r * bonus * k, ones) * g_out).astype(jnp.bfloat16)
    state[...] = jnp.exp(last) * end_grad + mxu(g_out, r * from_start, TN) * ones

    @pl.when(pl.program_id(0) == pl.num_programs(0) - 1)
    def _():
        first_ref[...] = fold(state[...], ones)


def wkv_backward(r, k, v, gate, low, up, par, wkv, held, g_mixed):
    rows, columns = r.shape
    chunks = rows // CHUNK
    block = pl.BlockSpec((CHUNK, columns), lambda c: (chunks - 1 - c, 0))
    whole = lambda a: pl.BlockSpec(a.shape, lambda c: (0, 0))
    of_all = lambda n: pl.BlockSpec((n, columns), lambda c: (0, 0))
    low_type = jax.ShapeDtypeStruct((rows, columns), jnp.bfloat16)
    return pl.pallas_call(
        wkv_backward_kernel,
        grid=(chunks,),
        in_specs=[block] * 4
        + [
            pl.BlockSpec((CHUNK, low.shape[1]), lambda c: (chunks - 1 - c, 0)),
            whole(up),
            whole(par),
            block,
            block,
            block,
        ],
        out_specs=[block] * 5 + [of_all(8), of_all(GROUP_DIMENSION)],
        out_shape=[low_type] * 5
        + [
            jax.ShapeDtypeStruct((8, columns), jnp.float32),
            jax.ShapeDtypeStruct((GROUP_DIMENSION, columns), jnp.float32),
        ],
        scratch_shapes=[pltpu.VMEM((columns // PACK, PACK, PACK), jnp.float32)],
        compiler_params=pltpu.CompilerParams(
            dimension_semantics=("arbitrary",), vmem_limit_bytes=32 * 2**20
        ),
        cost_estimate=pl.CostEstimate(
            flops=2 * 24 * PACK * rows * columns, bytes_accessed=40 * rows * columns, transcendentals=12 * rows * columns
        ),
        name="wkv_backward",
    )(r, k, v, gate, low, up, par, wkv, held, g_mixed)


GRAD_COLUMNS = 256


def grad_kernel(left_ref, right_ref, *rest):
    out_ref, turned = rest[-2:]

    @pl.when(pl.program_id(0) == 0)
    def _():
        turned[...] = left_ref[...].T

    out_ref[...] = mxu(turned[...], right_ref[...], NN).astype(jnp.bfloat16)


def grad_into(left, right, total, at, into=None):
    rows, width = left.shape
    columns = right.shape[1]
    shift = at // GRAD_COLUMNS
    specs = [
        pl.BlockSpec((rows, width), lambda j: (0, 0)),
        pl.BlockSpec((rows, GRAD_COLUMNS), lambda j: (0, j)),
    ]
    operands = [left, right]
    alias = {}
    if into is not None:
        specs.append(pl.BlockSpec(memory_space=pltpu.HBM))
        operands.append(into)
        alias = {2: 0}
    return pl.pallas_call(
        grad_kernel,
        grid=(columns // GRAD_COLUMNS,),
        in_specs=specs,
        out_specs=pl.BlockSpec((width, GRAD_COLUMNS), lambda j: (0, j + shift)),
        out_shape=pltpu.HBM((width, total), jnp.bfloat16),
        scratch_shapes=[pltpu.VMEM((width, rows), jnp.bfloat16)],
        input_output_aliases=alias,
        compiler_params=pltpu.CompilerParams(
            dimension_semantics=("arbitrary",), vmem_limit_bytes=32 * 2**20
        ),
        cost_estimate=pl.CostEstimate(
            flops=2 * rows * width * columns,
            bytes_accessed=2 * (rows * (width + columns) + width * columns),
            transcendentals=0,
        ),
        name="weight_grad",
    )(*operands)


TILE = 256


def mixes_forward_kernel(
    unit_ref, w_ref, down_ref, up_ref, vec_ref,
    m0_ref, m1_ref, m2_ref, m3_ref, m4_ref, normed_ref, squash_ref, decay_ref, r_ref, k_ref, v_ref, g_ref,
    hidden, decay,
):
    phase, tile = pl.program_id(0), pl.program_id(1)
    rows, ranks = squash_ref.shape
    own = r_ref.shape[1]
    vec = vec_ref[...]
    normed = unit_ref[...] * vec[0:1] + vec[1:2]
    row = iota2(normed.shape, 0)
    shifted = jnp.where(row == 0, 0.0, pltpu.roll(normed, 1, 0)) - normed

    @pl.when((phase == 0) & (tile == 0))
    def _():
        hidden[...] = jnp.zeros_like(hidden)

    @pl.when(phase == 0)
    def _():
        hidden[...] = hidden[...] + mxu(normed + shifted * vec[2:3], down_ref[:, :ranks], NN)

    @pl.when((phase == 1) & (tile == 0))
    def _():
        squash_ref[...] = jnp.tanh(hidden[...])
        decay[...] = jnp.zeros_like(decay)
        for ref in (r_ref, k_ref, v_ref, g_ref):
            ref[...] = jnp.zeros_like(ref)

    @pl.when(phase == 1)
    def _():
        normed_ref[...] = normed
        group_col = iota2((rows, ranks), 1) // SHIFT_RANK
        squash_low = squash_ref[...].astype(jnp.bfloat16)
        up = up_ref[...]
        for g, mix_ref in enumerate((m0_ref, m1_ref, m2_ref, m3_ref, m4_ref)):
            squash_g = jnp.where(group_col == g, squash_low, 0)
            mix = (normed + shifted * (vec[3 + g : 4 + g] + mxu(squash_g, up, NT))).astype(jnp.bfloat16)
            mix_ref[...] = mix
            if g == 0:
                decay[...] = decay[...] + mxu(mix, down_ref[:, ranks:], NN)
            else:
                column = (None, 1, 2, 0, 3)[g] * own
                out = (None, k_ref, v_ref, r_ref, g_ref)[g]
                out[...] = out[...] + mxu(mix, w_ref[:, column : column + own], NN)

    @pl.when((phase == 1) & (tile == pl.num_programs(1) - 1))
    def _():
        decay_ref[...] = jnp.tanh(decay[...])


def mixes_forward(unit, proj_w, down, up_mods, vec, own):
    rows, width = unit.shape
    ranks = up_mods.shape[1]
    low = down.shape[1] - ranks
    tiles = width // TILE
    down_rows = lambda columns: pl.BlockSpec((TILE, columns), lambda p, n: (n, 0))
    across = lambda r: pl.BlockSpec((r, TILE), lambda p, n: (0, n))
    late = pl.BlockSpec((rows, TILE), lambda p, n: (0, n * p))
    whole = lambda columns: pl.BlockSpec((rows, columns), lambda p, n: (0, 0))
    kept = lambda columns, dtype: jax.ShapeDtypeStruct((rows, columns), dtype)
    return pl.pallas_call(
        mixes_forward_kernel,
        grid=(2, tiles),
        in_specs=[
            across(rows),
            pl.BlockSpec((TILE, 4 * own), lambda p, n: (n * p, 0)),
            down_rows(down.shape[1]),
            down_rows(ranks),
            across(vec.shape[0]),
        ],
        out_specs=[late] * 6 + [whole(ranks), whole(low)] + [whole(own)] * 4,
        out_shape=[kept(width, jnp.bfloat16)] * 5
        + [kept(width, jnp.float32), kept(ranks, jnp.float32), kept(low, jnp.float32)]
        + [kept(own, jnp.float32)] * 4,
        scratch_shapes=[pltpu.VMEM((rows, ranks), jnp.float32), pltpu.VMEM((rows, low), jnp.float32)],
        compiler_params=pltpu.CompilerParams(
            dimension_semantics=("arbitrary", "arbitrary"), vmem_limit_bytes=48 * 2**20
        ),
        cost_estimate=pl.CostEstimate(
            flops=2 * rows * width * (4 * own + 7 * ranks),
            bytes_accessed=2 * width * 4 * own + 22 * rows * width,
            transcendentals=0,
        ),
        name="mixes_forward",
    )(unit, proj_w, down, up_mods, vec)


def mixes_back_kernel(
    gk_ref, gv_ref, gr_ref, gg_ref, gd_ref, w_ref, down_ref, up_ref, vec_ref, squash_ref, normed_ref,
    out_ref, down_grad_ref, up_grad_ref, sums_ref,
    g_shift, g_norm, g_squash, g_hidden, g_up, g_sums,
):
    phase, tile = pl.program_id(0), pl.program_id(1)
    rows, ranks = squash_ref.shape
    own = gk_ref.shape[1]
    normed = normed_ref[...]
    row = iota2(normed.shape, 0)
    shifted = jnp.where(row == 0, 0.0, pltpu.roll(normed, 1, 0)) - normed
    squash = squash_ref[...]
    up = up_ref[...]
    vec = vec_ref[...]

    @pl.when((phase == 0) & (tile == 0))
    def _():
        g_squash[...] = jnp.zeros_like(g_squash)

    @pl.when(phase == 0)
    def _():
        group_col = iota2((rows, ranks), 1) // SHIFT_RANK
        group_wide = iota2((TILE, ranks), 1) // SHIFT_RANK
        squash_low = squash.astype(jnp.bfloat16)
        total_shift = jnp.zeros((rows, TILE), jnp.float32)
        total_norm = jnp.zeros((rows, TILE), jnp.float32)
        add_squash = jnp.zeros((rows, ranks), jnp.float32)
        add_up = jnp.zeros((TILE, ranks), jnp.float32)
        sums = []
        for g in range(5):
            squash_g = jnp.where(group_col == g, squash_low, 0)
            up_g = jnp.where(group_wide == g, up, 0)
            if g == 0:
                part = mxu(gd_ref[...], down_ref[:, ranks:], NT)
            else:
                column = (None, 1, 2, 0, 3)[g] * own
                grad = (None, gk_ref, gv_ref, gr_ref, gg_ref)[g]
                part = mxu(grad[...], w_ref[:, column : column + own], NT)
            coeff = vec[3 + g : 4 + g] + mxu(squash_g, up, NT)
            times = part * shifted
            times_low = times.astype(jnp.bfloat16)
            sums.append(jnp.sum(times, axis=0, keepdims=True))
            total_shift = total_shift + part * coeff
            total_norm = total_norm + part
            add_squash = add_squash + mxu(times_low, up_g, NN)
            add_up = add_up + mxu(times_low, squash_g, TN)
        g_shift[tile] = total_shift
        g_norm[tile] = total_norm
        g_squash[...] = g_squash[...] + add_squash
        g_up[tile] = add_up
        g_sums[tile] = jnp.concatenate(sums + [jnp.zeros((3, TILE), jnp.float32)], axis=0)

    @pl.when((phase == 1) & (tile == 0))
    def _():
        g_hidden[...] = (g_squash[...] * (1.0 - squash * squash)).astype(jnp.bfloat16)

    @pl.when(phase == 1)
    def _():
        blend = vec[2:3]
        mix_in = normed + shifted * blend
        part = mxu(g_hidden[...], down_ref[:, :ranks], NT)
        total_shift = g_shift[tile] + part * blend
        total = g_norm[tile] + part - total_shift
        total = total + jnp.where(row == rows - 1, 0.0, pltpu.roll(total_shift, rows - 1, 0))
        out_ref[...] = total.astype(jnp.bfloat16)
        unit = (normed - vec[1:2]) / vec[0:1]
        head = [
            jnp.sum(total * unit, axis=0, keepdims=True),
            jnp.sum(total, axis=0, keepdims=True),
            jnp.sum(part * shifted, axis=0, keepdims=True),
        ]
        sums_ref[...] = jnp.concatenate(head + [g_sums[tile][:5]], axis=0)
        down_grad_ref[...] = mxu(mix_in, g_hidden[...], TN)
        up_grad_ref[...] = g_up[tile]


def mixes_back(g_key, g_val, g_recept, g_gate, g_decay, proj_w, down, up_mods, vec, squash, normed):
    rows, width = normed.shape
    own, ranks = g_key.shape[1], squash.shape[1]
    tiles = width // TILE
    whole = lambda a: pl.BlockSpec(a.shape, lambda p, n: (0, 0))
    down_rows = lambda columns: pl.BlockSpec((TILE, columns), lambda p, n: (n, 0))
    first_only = pl.BlockSpec((TILE, 4 * own), lambda p, n: (n * (1 - p) + (tiles - 1) * p, 0))
    across = lambda r: pl.BlockSpec((r, TILE), lambda p, n: (0, n))
    late = lambda n_rows: pl.BlockSpec((n_rows, TILE), lambda p, n: (0, n * p))
    late_down = lambda columns: pl.BlockSpec((TILE, columns), lambda p, n: (n * p, 0))
    return pl.pallas_call(
        mixes_back_kernel,
        grid=(2, tiles),
        in_specs=[whole(g_key)] * 4
        + [
            whole(g_decay),
            first_only,
            down_rows(down.shape[1]),
            down_rows(ranks),
            across(vec.shape[0]),
            whole(squash),
            across(rows),
        ],
        out_specs=[late(rows), late_down(ranks), late_down(ranks), late(8)],
        out_shape=[
            jax.ShapeDtypeStruct((rows, width), jnp.bfloat16),
            jax.ShapeDtypeStruct((width, ranks), jnp.float32),
            jax.ShapeDtypeStruct((width, ranks), jnp.float32),
            jax.ShapeDtypeStruct((8, width), jnp.float32),
        ],
        scratch_shapes=[
            pltpu.VMEM((tiles, rows, TILE), jnp.float32),
            pltpu.VMEM((tiles, rows, TILE), jnp.float32),
            pltpu.VMEM((rows, ranks), jnp.float32),
            pltpu.VMEM((rows, ranks), jnp.bfloat16),
            pltpu.VMEM((tiles, TILE, ranks), jnp.float32),
            pltpu.VMEM((tiles, 8, TILE), jnp.float32),
        ],
        compiler_params=pltpu.CompilerParams(
            dimension_semantics=("arbitrary", "arbitrary"), vmem_limit_bytes=56 * 2**20
        ),
        cost_estimate=pl.CostEstimate(
            flops=2 * rows * width * (4 * own + 17 * ranks),
            bytes_accessed=2 * width * 4 * own + 10 * rows * width,
            transcendentals=0,
        ),
        name="mixes_back",
    )(g_key, g_val, g_recept, g_gate, g_decay, proj_w, down, up_mods, vec, squash, normed)


def shards(
    inputs,
    cotangent,
    states,
    vectors,
    time_mix_weight,
    output_weight,
    channel_receptance_weight,
    rank_down_weight,
    rank_up_weight,
    channel_key_weight,
    channel_value_weight,
):
    token_rows, width = inputs.shape
    ranks = 5 * SHIFT_RANK
    own_width = time_mix_weight.shape[2]
    hidden = channel_key_weight.shape[1]
    local_heads = own_width // GROUP_DIMENSION
    col_start = lax.axis_index("span") * own_width
    position = lax.axis_index("span") * token_rows

    x_seg = span_gather(inputs).astype(jnp.float32)
    small_rows = span_gather(
        jnp.concatenate([rank_down_weight, rank_up_weight.T, vectors.T], axis=1)
    )
    first = plane_gather(
        jnp.concatenate([time_mix_weight[g] for g in range(4)] + [output_weight.T], axis=1), small_rows
    )
    second = plane_gather(
        jnp.concatenate(
            [channel_key_weight, channel_value_weight.T, split_columns(channel_receptance_weight)], axis=1
        )
    )
    out_w = first[:, 4 * own_width : 5 * own_width]
    low_rank = first[:, 5 * own_width :]
    key_w, value_w, recept_w = second[:, :hidden], second[:, hidden : 2 * hidden], second[:, 2 * hidden :]
    rank_all = rank_down_weight.shape[1]
    down_weight = low_rank[:, :rank_all]
    up_mods, up_decay = low_rank[:, rank_all : rank_all + ranks], low_rank[:, rank_all + ranks : 2 * rank_all]
    vec = low_rank[:, 2 * rank_all :].T.astype(jnp.float32)

    def own_cols(line):
        return lax.dynamic_slice_in_dim(line, col_start, own_width, line.ndim - 1)

    def own_rows(values):
        return lax.dynamic_slice_in_dim(values, position, token_rows, 0)

    def place_rows(values):
        blank = jnp.zeros((width,) + values.shape[1:], jnp.float32)
        return lax.dynamic_update_slice_in_dim(blank, values, col_start, 0)

    x_in = inputs.astype(jnp.float32)
    _, unit_seg, _ = norm_rows(x_seg, 1.0, 0.0)
    *mixes, normed, squash, decay_tanh, recept, key_proj, val_proj, gate_pre = mixes_forward(
        unit_seg, first, down_weight, up_mods, vec, own_width
    )
    decay_low = decay_tanh.astype(jnp.bfloat16)
    up_decay_own = lax.dynamic_slice_in_dim(up_decay, col_start, own_width, 0)
    head_vec = jnp.concatenate([own_cols(vec[8:12]), jnp.zeros((4, own_width), jnp.float32)], axis=0)
    first_state = jnp.transpose(states[0], (2, 0, 1)).reshape(GROUP_DIMENSION, own_width)
    heads_in = (recept, key_proj, val_proj, gate_pre, decay_low, up_decay_own, head_vec)
    mixed, wkv, held = wkv_forward(*heads_in, first_state)
    resid = x_in + span_reduce(backward_product(mixed, out_w).astype(jnp.bfloat16))

    normed_two, unit_two, rstd_two = norm_rows(resid, vec[12], vec[13])
    n2 = span_gather(normed_two.astype(jnp.bfloat16)).astype(jnp.float32)
    shifted_two = prior_rows(n2) - n2
    key_in = (n2 + shifted_two * vec[14]).astype(jnp.bfloat16)
    rec_in = (n2 + shifted_two * vec[15]).astype(jnp.bfloat16)
    hidden_two = product_lower(key_in, key_w)
    active = jax.nn.relu(hidden_two)
    squared = (active * active).astype(jnp.bfloat16)
    rec_part = product_lower(rec_in, recept_w).astype(jnp.bfloat16)
    rec_pre = join_columns(rec_part)
    _, squared = lax.optimization_barrier((rec_part, squared))
    value_part, rec_pre = lax.optimization_barrier(
        (backward_product(squared, value_w).astype(jnp.bfloat16), rec_pre)
    )
    value_out = span_reduce(value_part)
    rec_gate = jax.nn.sigmoid(rec_pre.astype(jnp.float32))
    output = (resid + rec_gate * value_out).astype(jnp.bfloat16)

    grad_out = cotangent.astype(jnp.float32)
    g_value = (grad_out * rec_gate).astype(jnp.bfloat16)
    g_rec = (grad_out * value_out * rec_gate * (1.0 - rec_gate)).astype(jnp.bfloat16)
    g_value_all = span_gather(g_value)
    g_rec_own = split_columns(g_rec)
    cm_total = 2 * hidden
    cm_part = grad_into(g_value_all, squared, cm_total, hidden)
    g_value_all, cm_part = lax.optimization_barrier((g_value_all, cm_part))
    g_hid = (product_lower(g_value_all, value_w) * 2.0 * active).astype(jnp.bfloat16)
    cm_part = grad_into(key_in, g_hid, cm_total, 0, cm_part)
    cm_part, g_hid, g_rec_own = lax.optimization_barrier((cm_part, g_hid, g_rec_own))
    cm_pair = plane_scatter(cm_part)
    g_key_in = backward_product(g_hid, key_w)
    g_rec_in = backward_product(g_rec_own, recept_w)
    vec_fourteen = jnp.sum(g_key_in * shifted_two, axis=0)
    vec_fifteen = jnp.sum(g_rec_in * shifted_two, axis=0)
    g_shift_two = g_key_in * vec[14] + g_rec_in * vec[15]
    g_n2_part = g_key_in + g_rec_in - g_shift_two + next_rows(g_shift_two)
    g_n2 = span_reduce(g_n2_part.astype(jnp.bfloat16))
    vec_twelve = jnp.sum(g_n2 * unit_two, axis=0)
    vec_thirteen = jnp.sum(g_n2, axis=0)
    g_resid = grad_out + norm_back(g_n2, unit_two, rstd_two, vec[12])

    g_att = span_gather(g_resid.astype(jnp.bfloat16))
    g_mixed = product_lower(g_att, out_w)
    g_recept, g_key, g_val, g_gate, g_ww, head_sums, g_first = wkv_backward(
        *heads_in, wkv, held, g_mixed
    )
    state_grad = jnp.transpose(
        g_first.reshape(GROUP_DIMENSION, local_heads, GROUP_DIMENSION), (1, 2, 0)
    )[None]
    tm_total = 6 * own_width
    tm_part = grad_into(g_att, mixed, tm_total, 0)
    tm_part = grad_into(rec_in, g_rec_own, tm_total, 5 * own_width, tm_part)
    for at, mix, grad in ((1, 3, g_recept), (2, 1, g_key), (3, 2, g_val), (4, 4, g_gate)):
        tm_part = grad_into(mixes[mix], grad, tm_total, at * own_width, tm_part)
    g_key, g_ww, tm_part = lax.optimization_barrier((g_key, g_ww, tm_part))

    up_decay_grad = outer_sum(g_ww, decay_low)
    g_decay_hidden = (
        product_lower(g_ww, up_decay_own) * (1.0 - decay_tanh * decay_tanh)
    ).astype(jnp.bfloat16)
    down_decay_grad = outer_sum(mixes[0], g_decay_hidden)
    g_normed, down_mods_grad, up_mods_grad, width_sums = mixes_back(
        g_key, g_val, g_recept, g_gate, g_decay_hidden, first, down_weight, up_mods, vec, squash, normed
    )
    g_normed, cm_pair, tm_part = lax.optimization_barrier((g_normed, cm_pair, tm_part))
    tm_pair = plane_scatter(tm_part)
    cm_grad = finish_scatter(cm_pair)
    tm_grad = finish_scatter(tm_pair)
    g_n1 = span_reduce(g_normed)
    _, unit_own, rstd_own = norm_rows(x_in, vec[0], vec[1])
    x_grad = g_resid + norm_back(g_n1, unit_own, rstd_own, vec[0])
    vec_part = jnp.concatenate(
        [
            width_sums.T,
            place_rows(head_sums[:4].T),
            jnp.stack([vec_twelve, vec_thirteen, vec_fourteen, vec_fifteen]).T,
        ],
        axis=1,
    )
    small = reduce_small(
        jnp.concatenate(
            [down_mods_grad, down_decay_grad, up_mods_grad, place_rows(up_decay_grad), vec_part], axis=1
        )
    )
    down_grad, up_grad, vec_grad = (
        small[:, :rank_all],
        small[:, rank_all : 2 * rank_all].T,
        small[:, 2 * rank_all :].T,
    )
    rec_grad = join_columns(tm_grad[:, 5 * own_width :])
    value_grad = cm_grad[:, hidden:].T
    key_grad = cm_grad[:, :hidden]
    out_grad = tm_grad[:, :own_width].T
    proj_grad = jnp.moveaxis(tm_grad[:, own_width : 5 * own_width].reshape(-1, 4, own_width), 1, 0)
    return (
        output,
        x_grad,
        state_grad,
        vec_grad,
        proj_grad,
        out_grad,
        rec_grad,
        down_grad,
        up_grad,
        key_grad,
        value_grad,
    )


def solution(mesh):
    rows, columns = P(ALL, None), P(None, ALL)
    state = P("seg", "span", None, None)
    time_mix = P(None, "seg", "span")
    turned, straight = P("span", "seg"), P("seg", "span")
    return jax.shard_map(
        shards,
        mesh=mesh,
        in_specs=(
            rows, rows, state, columns, time_mix, turned, rows, rows, columns, straight, turned
        ),
        out_specs=(
            rows, rows, state, columns, time_mix, turned, rows, rows, columns, straight, turned
        ),
        check_vma=False,
    )
```

time: 855 us -> 584 us (0.68)
  matrix products: 214 us -> 42.1 us
  Pallas kernels: 0 us -> 131 us
  local copies, waits for them, and re-layouts: 167 us -> 42.7 us
  other arithmetic: 146 us -> 43.5 us
  blocking collectives: 80.7 us -> 0 us
  waiting for transfers between devices: 175 us -> 247 us
  starting transfers between devices: 45.5 us -> 57.4 us
    pallas_call x0 -> x12, Pallas kernels: none -> 131 us  [the longest x8 34.5 us: grad_into(): pl.pallas_call(grad_kernel, grid=(columns // GRAD_COLUMNS,), in_specs=spe...]
    all_gather x2 -> x0, blocking collectives: 80.7 us -> none  [gather_small(): return lax.all_gather(block, ALL, axis=0, tiled=True)]
    dot_general x15 -> x0, matrix products: 79 us -> none  [the longest x3 20 us: weighted_kv_local(): jnp.einsum('bihk,bihv->bhkv', key_end, content_tile, precision=maximal_ac...]
    all_gather x3 -> x2, waiting for transfers between devices: 0.02 us -> 64.8 us  [plane_gather(): lax.all_gather(jnp.concatenate(pairs, axis=1), 'seg', axis=0, tiled=True,...]
    unnamed x382 -> x149, local copies, waits for them, and re-layouts: 68 us -> 15.2 us
    dot_general x11 -> x4, matrix products: 64.6 us -> 20.5 us  [backward_product(): jnp.einsum('te,de->td', gradient, weights, preferred_element_type=jnp.flo...]
    reduce_sum x15 -> x0, other arithmetic: 39.3 us -> none  [the longest x1 13 us: shards(): vec_one = jnp.sum(g_normed, axis=0)]
    dot_general x11 -> x2, matrix products: 32.5 us -> 1.08 us  [outer_sum(): jnp.einsum('td,te->de', left_arg, right_arg, preferred_element_type=jnp.f...]
  transfers between devices with their start and end apart: 39 -> 43, of which waited for: 22 -> 30; matrix products, arithmetic and copies ran while one was open for 38% -> 17% of each run, Pallas kernels for 0% -> 20%
where the time goes in v2:
time: 584 us; the launch traced here: 579 us
  waiting for transfers between devices  247 us (42%)
  Pallas kernels  131 us (22%)
  starting transfers between devices  57.4 us (10%)
  other arithmetic  43.5 us (7%)
  local copies, waits for them, and re-layouts  42.7 us (7%)
  matrix products  42.1 us (7%)
  between operations  15.6 us (3%)
    ppermute x38, waiting for transfers between devices, swap(): return lax.ppermute(block, ALL, [(i, i ^ bit) for i in range(count)])  174 us
    all_gather x2, waiting for transfers between devices, plane_gather(): lax.all_gather(jnp.concatenate(pairs, axis=1), 'seg', axis=0, tiled=True,...  64.8 us
    ppermute x38, starting transfers between devices, swap(): return lax.ppermute(block, ALL, [(i, i ^ bit) for i in range(count)])  52.4 us
    pallas_call x8, Pallas kernels, grad_into(): pl.pallas_call(grad_kernel, grid=(columns // GRAD_COLUMNS,), in_specs=spe...  34.5 us
    pallas_call x1, Pallas kernels, mixes_back(): pl.pallas_call(mixes_back_kernel, grid=(2, tiles), in_specs=[whole(g_key)...  32.2 us
    pallas_call x1, Pallas kernels, mixes_forward(): pl.pallas_call(mixes_forward_kernel, grid=(2, tiles), in_specs=[across(ro...  24.7 us
    pallas_call x1, Pallas kernels, wkv_backward(): pl.pallas_call(wkv_backward_kernel, grid=(chunks,), in_specs=[block] * 4...  21.5 us
    dot_general x4, matrix products, backward_product(): jnp.einsum('te,de->td', gradient, weights, preferred_element_type=jnp.flo...  20.5 us
  transfers between devices with their start and end apart: 43, of which 30 were waited for; matrix products, arithmetic and copies ran while one was open for 17% of the time, Pallas kernels for 20%

profile of v2, /device:TPU:1, one launch (start us, length us, event | category | flops | bytes accessed | tf_op | source)
XLA Modules:
  0.0 579.1 jit_solution(6586373298801383610)
XLA Ops:
  20.2 9.2 %collective-permute-done.5 = bf16[64,464]{1,0:T(8,128)(2,1)S(1)} collective-permute-done((bf16[64,464]{1,0:T(8,128)(2,1)S(1)}, bf16[64,464]{1,0:T(8,128)(2,1)S(1)}, u32[]{:S(2)}, u32[]{:S(2)}) %collective-permute-start.5) | collective-permute-done | bytes 59424 | tf_op jit(solution)/shard_map/ppermute | solution.py:20
  37.9 11.8 %collective-permute-done.13 = bf16[64,4096]{1,0:T(8,128)(2,1)S(1)} collective-permute-done((bf16[64,4096]{1,0:T(8,128)(2,1)S(1)}, bf16[64,4096]{1,0:T(8,128)(2,1)S(1)}, u32[]{:S(2)}, u32[]{:S(2)}) %collective-permute-start.13) | collective-permute-done | bytes 524320 | tf_op jit(solution)/shard_map/ppermute | solution.py:20
  52.5 10.8 %collective-permute-done = bf16[128,2048]{1,0:T(8,128)(2,1)S(1)} collective-permute-done((bf16[128,2048]{1,0:T(8,128)(2,1)S(1)}, bf16[128,2048]{1,0:T(8,128)(2,1)S(1)}, u32[]{:S(2)}, u32[]{:S(2)}) %collective-permute-start) | collective-permute-done | bytes 524320 | tf_op jit(solution)/shard_map/ppermute | solution.py:20
  71.7 4.6 fusion.8.unit_ref
  76.3 46.7 %all-gather.3.cloned.1.call-done.w_ref = bf16[2048,3024]{1,0:T(8,128)(2,1)} async-done(((bf16[128,3024]{1,0:T(8,128)(2,1)}), bf16[2048,3024]{1,0:T(8,128)(2,1)}) %all-gather.3.cloned.1.call-update) | async-done | bytes 12386320 | tf_op jit(solution)/shard_map/all_gather | solution.py:73
  129.0 24.7 %mixes_forward.1 = (bf16[512,2048]{1,0:T(8,128)(2,1)}, bf16[512,2048]{1,0:T(8,128)(2,1)}, bf16[512,2048]{1,0:T(8,128)(2,1)}, bf16[512,2048]{1,0:T(8,128)(2,1)}, ...) custom-call(f32[512,2048]{1,0:T(8,128)} %fusion.8.unit_ref, ...), custom_call_target="tpu_custom_call" | custom-call | flops 6643777536 | bytes 31457280 | tf_op jit(solution)/shard_map/mixes_forward/pallas_call | solution.py:569
  153.9 17.9 %wkv_forward.1 = (bf16[512,512]{1,0:T(8,128)(2,1)S(1)}, f32[512,512]{1,0:T(8,128)S(1)}, f32[512,512]{1,0:T(8,128)S(1)}) custom-call(f32[512,512]{1,0:T(8,128)S(1)} %get-tuple-element.51.refs_0_, f32[512,512]{1,0:T(8,128)S(1)} %get-tuple-element.52.refs_1_, f32[512,512]{1,0:T(8,128)S(1)} %get-tuple-element.53.refs_2_, ...), custom_call_target="tpu_custom_call" | custom-call | flops 1207959552 | bytes 6815744 | tf_op jit(solution)/shard_map/wkv_forward/pallas_call | solution.py:323
  171.8 3.6 convolution_convert_fusion
  181.3 11.4 %collective-permute-done.7 = bf16[128,2048]{1,0:T(8,128)(2,1)S(1)} collective-permute-done((bf16[128,2048]{1,0:T(8,128)(2,1)S(1)}, bf16[128,2048]{1,0:T(8,128)(2,1)S(1)}, u32[]{:S(2)}, u32[]{:S(2)}) %collective-permute-start.7) | collective-permute-done | bytes 524320 | tf_op jit(solution)/shard_map/ppermute | solution.py:20
  195.4 11.2 %collective-permute-done.8 = bf16[128,2048]{1,0:T(8,128)(2,1)S(1)} collective-permute-done((bf16[128,2048]{1,0:T(8,128)(2,1)S(1)}, bf16[128,2048]{1,0:T(8,128)(2,1)S(1)}, u32[]{:S(2)}, u32[]{:S(2)}) %collective-permute-start.8) | collective-permute-done | bytes 524320 | tf_op jit(solution)/shard_map/ppermute | solution.py:20
  218.3 18.1 %all-gather.5.cloned.1.call-done = bf16[2048,4096]{1,0:T(8,128)(2,1)} async-done(((bf16[128,4096]{1,0:T(8,128)(2,1)}), bf16[2048,4096]{1,0:T(8,128)(2,1)}) %all-gather.5.cloned.1.call-update) | async-done | bytes 16777232 | tf_op jit(solution)/shard_map/all_gather | solution.py:73
  236.4 3.5 fusion.25
  242.5 9.0 %multiply_convert_fusion.1 = (bf16[512,1792]{1,0:T(8,128)(2,1)S(1)}, f32[512,1792]{1,0:T(8,128)}) fusion(bf16[512,2048]{1,0:T(8,128)(2,1)S(1)} %get-tuple-element.139.left_ref, bf16[2048,4096]{1,0:T(8,128)(2,1)} %all-gather.5.cloned.1.call-done), kind=kOutput, calls=%fused_computation.21 | convolution fusion | flops 3760848896 | bytes 14942208 | tf_op jit(solution)/shard_map/dot_general | solution.py:128
  251.5 4.3 fusion.13
  260.7 12.1 %collective-permute-done.18 = bf16[128,2048]{1,0:T(8,128)(2,1)S(1)} collective-permute-done((bf16[128,2048]{1,0:T(8,128)(2,1)S(1)}, bf16[128,2048]{1,0:T(8,128)(2,1)S(1)}, u32[]{:S(2)}, u32[]{:S(2)}) %collective-permute-start.18) | collective-permute-done | bytes 524320 | tf_op jit(solution)/shard_map/ppermute | solution.py:20
  275.6 11.2 %collective-permute-done.19 = bf16[128,2048]{1,0:T(8,128)(2,1)S(1)} collective-permute-done((bf16[128,2048]{1,0:T(8,128)(2,1)S(1)}, bf16[128,2048]{1,0:T(8,128)(2,1)S(1)}, u32[]{:S(2)}, u32[]{:S(2)}) %collective-permute-start.19) | collective-permute-done | bytes 524320 | tf_op jit(solution)/shard_map/ppermute | solution.py:20
  297.7 7.7 %weight_grad.8.rest_0_ = bf16[2048,3584]{1,0:T(8,128)(2,1)} custom-call(bf16[512,2048]{1,0:T(8,128)(2,1)S(1)} %pad_maximum_fusion.2.left_ref, bf16[512,1792]{1,0:T(8,128)(2,1)S(1)} %get-tuple-element.57.right_ref), custom_call_target="tpu_custom_call" | custom-call | flops 3758096384 | bytes 11272192 | tf_op jit(solution)/shard_map/weight_grad/pallas_call | solution.py:486
  305.4 5.8 %multiply_convert_fusion.right_ref = bf16[512,1792]{1,0:T(8,128)(2,1)S(1)} fusion(f32[512,1792]{1,0:T(8,128)} %get-tuple-element.217, bf16[512,2048]{1,0:T(8,128)(2,1)S(1)} %pad_maximum_fusion.2.left_ref, bf16[2048,4096]{1,0:T(8,128)(2,1)S(1)} %bitcast.353), kind=kOutput, calls=%fused_computation.20 | convolution fusion | flops 3761766400 | bytes 14942208 | tf_op jit(solution)/shard_map/dot_general | solution.py:128
  311.2 7.6 %weight_grad.9 = bf16[2048,3584]{1,0:T(8,128)(2,1)} custom-call(bf16[512,2048]{1,0:T(8,128)(2,1)S(1)} %get-tuple-element.139.left_ref, bf16[512,1792]{1,0:T(8,128)(2,1)S(1)} %multiply_convert_fusion.right_ref, bf16[2048,3584]{1,0:T(8,128)(2,1)} %weight_grad.8.rest_0_), custom_call_target="tpu_custom_call", output_to_operand_aliasing={{}: (2, {})} | custom-call | flops 3758096384 | bytes 11272192 | tf_op jit(solution)/shard_map/weight_grad/pallas_call | solution.py:486
  324.0 9.5 %multiply_reduce_fusion.1 = (f32[2048]{0:T(1024)}, f32[2048]{0:T(1024)}, f32[512,2048]{1,0:T(8,128)}, f32[512,2048]{1,0:T(8,128)}) fusion(f32[511,2048]{1,0:T(8,128)S(1)} %bitcast.326, bf16[128,2048]{1,0:T(8,128)(2,1)S(1)} %copy-done.42, bf16[128,2048]{1,0:T(8,128)(2,1)S(1)} %copy-done.44, bf16[128,2048]{1,0:T(8,128)(2,1)S(1)} %copy-done.40, ...), kind=kOutput, calls=%fused_computation.14 | convolution fusion | flops 3774869504 | bytes 28073984 | tf_op jit(solution)/shard_map/te,de->td/dot_general | solution.py:136
  343.6 12.3 %collective-permute-done.25 = bf16[128,2048]{1,0:T(8,128)(2,1)S(1)} collective-permute-done((bf16[128,2048]{1,0:T(8,128)(2,1)S(1)}, bf16[128,2048]{1,0:T(8,128)(2,1)S(1)}, u32[]{:S(2)}, u32[]{:S(2)}) %collective-permute-start.25) | collective-permute-done | bytes 524320 | tf_op jit(solution)/shard_map/ppermute | solution.py:20
  359.5 11.5 %collective-permute-done.26 = bf16[128,2048]{1,0:T(8,128)(2,1)S(1)} collective-permute-done((bf16[128,2048]{1,0:T(8,128)(2,1)S(1)}, bf16[128,2048]{1,0:T(8,128)(2,1)S(1)}, u32[]{:S(2)}, u32[]{:S(2)}) %collective-permute-start.26) | collective-permute-done | bytes 524320 | tf_op jit(solution)/shard_map/ppermute | solution.py:20
  386.0 21.5 %wkv_backward.1 = (bf16[512,512]{1,0:T(8,128)(2,1)S(1)}, bf16[512,512]{1,0:T(8,128)(2,1)S(1)}, bf16[512,512]{1,0:T(8,128)(2,1)S(1)}, bf16[512,512]{1,0:T(8,128)(...) custom-call(f32[512,512]{1,0:T(8,128)S(1)} %copy-done.11, ...), custom_call_target="tpu_custom_call" | custom-call | flops 3221225472 | bytes 10485760 | tf_op jit(solution)/shard_map/wkv_backward/pallas_call | solution.py:430
  421.4 32.2 %mixes_back.1 = (bf16[512,2048]{1,0:T(8,128)(2,1)}, f32[2048,160]{1,0:T(8,128)}, f32[2048,160]{1,0:T(8,128)}, f32[8,2048]{1,0:T(8,128)}) custom-call(bf16[512,512]{1,0:T(8,128)(2,1)} %copy-done.19, bf16[512,512]{1,0:T(8,128)(2,1)} %copy-done.20, bf16[512,512]{1,0:T(8,128)(2,1)} %copy-done.18, bf16[512,512]{1,0:T(8,128)(2,1)} %copy-done.21, ...), custom_call_target="tpu_custom_call" | custom-call | flops 9999220736 | bytes 18874368 | tf_op jit(solution)/shard_map/mixes_back/pallas_call | solution.py:682
  461.1 8.2 %concatenate.63 = f32[2048,464]{1,0:T(8,128)} concatenate(f32[2048,160]{1,0:T(8,128)} %get-tuple-element.84, f32[2048,64]{1,0:T(8,128)S(1)} %fusion.62, f32[2048,160]{1,0:T(8,128)} %get-tuple-element.86, f32[2048,64]{1,0:T(8,128)} %copy-done.47, f32[2048,8]{1,0:T(8,128)} %copy.107, f32[2048,4]{1,0:T(8,128)} %bitcast_dynamic-update-slice_fusion, f32[2048,4]{1,0:T(8,128)} %bitcast.341), dimensions={1} | concatenate | bytes 7602176 | tf_op jit(solution)/shard_map/concatenate | solution.py:866
  479.2 11.8 %collective-permute-done.31 = bf16[16,2,16,464]{3,2,1,0:T(8,128)(2,1)S(1)} collective-permute-done((bf16[16,2,16,464]{3,2,1,0:T(8,128)(2,1)S(1)}, bf16[16,2,16,464]{3,2,1,0:T(8,128)(2,1)S(1)}, u32[]{:S(2)}, u32[]{:S(2)}) %collective-permute-start.31) | collective-permute-done | bytes 475168 | tf_op jit(solution)/shard_map/ppermute | solution.py:20
  497.2 5.6 collective-permute-done.32
  505.0 4.9 all-to-all-start
  510.7 8.5 %all-to-all-done = bf16[16,16,464]{2,1,0:T(8,128)(2,1)S(1)} async-done(((bf16[16,16,464]{2,1,0:T(8,128)(2,1)}), bf16[16,16,464]{2,1,0:T(8,128)(2,1)S(1)}, u32[]{:S(2)}, u32[]{:S(2)}) %all-to-all-start) | async-done | bytes 237600 | tf_op jit(solution)/shard_map/all_to_all | solution.py:172
  527.8 9.8 %collective-permute-done.37 = bf16[64,3584]{1,0:T(8,128)(2,1)S(1)} collective-permute-done((bf16[64,3584]{1,0:T(8,128)(2,1)S(1)}, bf16[64,3584]{1,0:T(8,128)(2,1)S(1)}, u32[]{:S(2)}, u32[]{:S(2)}) %collective-permute-start.37) | collective-permute-done | bytes 458784 | tf_op jit(solution)/shard_map/ppermute | solution.py:20
  538.8 10.3 %collective-permute-done.29 = bf16[128,2048]{1,0:T(8,128)(2,1)S(1)} collective-permute-done((bf16[128,2048]{1,0:T(8,128)(2,1)S(1)}, bf16[128,2048]{1,0:T(8,128)(2,1)S(1)}, u32[]{:S(2)}, u32[]{:S(2)}) %collective-permute-start.29) | collective-permute-done | bytes 524320 | tf_op jit(solution)/shard_map/ppermute | solution.py:20
  553.0 9.1 %collective-permute-done.33 = bf16[64,3072]{1,0:T(8,128)(2,1)S(1)} collective-permute-done((bf16[64,3072]{1,0:T(8,128)(2,1)S(1)}, bf16[64,3072]{1,0:T(8,128)(2,1)S(1)}, u32[]{:S(2)}, u32[]{:S(2)}) %collective-permute-start.33) | collective-permute-done | bytes 393248 | tf_op jit(solution)/shard_map/ppermute | solution.py:20
  (357 shorter events, 177.2 us)
Async XLA Ops:
  7.2 115.8 %all-gather.3.cloned.1.call-start = ((), (), s32[]{:S(2)}) async-start(), calls=%async_computation.3 | async-start | bytes 13369344 | tf_op jit(solution)/shard_map/all_gather | solution.py:73
  8.9 5.5 collective-permute-start.3
  15.2 4.5 collective-permute-start.4
  17.1 12.3 %collective-permute-start.2 = (bf16[64,2560]{1,0:T(8,128)(2,1)S(1)}, bf16[64,2560]{1,0:T(8,128)(2,1)S(1)}, u32[]{:S(2)}, u32[]{:S(2)}) collective-permute-start(bf16[64,2560]{1,0:T(8,128)(2,1)S(1)} %bitcast_dynamic-update-slice_fusion.5), channel_id=1, source_target_pairs={{0,4},{1,5},{2,6},{3,7},{4,0},{5,1},{6,2},{7,3},{8,12},{9,13},{10,... | collective-permute-start | bytes 983048 | tf_op jit(solution)/shard_map/ppermute | solution.py:20
  19.8 9.6 %collective-permute-start.5 = (bf16[64,464]{1,0:T(8,128)(2,1)S(1)}, bf16[64,464]{1,0:T(8,128)(2,1)S(1)}, u32[]{:S(2)}, u32[]{:S(2)}) collective-permute-start(bf16[64,464]{1,0:T(8,128)(2,1)S(1)} %pad_maximum_fusion.10), channel_id=1, source_target_pairs={{0,4},{1,5},{2,6},{3,7},{4,0},{5,1},{6,2},{7,3},{8,12},{9,13},{10,... | collective-permute-start | bytes 178184 | tf_op jit(solution)/shard_map/ppermute | solution.py:20
  30.5 205.9 %all-gather.5.cloned.1.call-start = ((), (), s32[]{:S(2)}) async-start(), calls=%async_computation.4 | async-start | bytes 17825792 | tf_op jit(solution)/shard_map/all_gather | solution.py:73
  35.0 14.7 %collective-permute-start.13 = (bf16[64,4096]{1,0:T(8,128)(2,1)S(1)}, bf16[64,4096]{1,0:T(8,128)(2,1)S(1)}, u32[]{:S(2)}, u32[]{:S(2)}) collective-permute-start(bf16[64,4096]{1,0:T(8,128)(2,1)S(1)} %pad_maximum_fusion.9), channel_id=1, source_target_pairs={{0,4},{1,5},{2,6},{3,7},{4,0},{5,1},{6,2},{7,3},{8,12},{9,13},{10,... | collective-permute-start | bytes 1572872 | tf_op jit(solution)/shard_map/ppermute | solution.py:20
  50.9 402.7 %reduce-scatter.3.cloned.1.call-start = ((), (), s32[]{:S(2)}) async-start(), calls=%async_computation.5 | async-start | bytes 15597568 | tf_op jit(solution)/shard_map/reduce_scatter | solution.py:84
  51.0 12.2 %collective-permute-start = (bf16[128,2048]{1,0:T(8,128)(2,1)S(1)}, bf16[128,2048]{1,0:T(8,128)(2,1)S(1)}, u32[]{:S(2)}, u32[]{:S(2)}) collective-permute-start(bf16[128,2048]{1,0:T(8,128)(2,1)S(1)} %copy-done.33), channel_id=1, source_target_pairs={{0,2},{1,3},{2,0},{3,1},{4,6},{5,7},{6,4},{7,5},{8,10},{9,11},{10,... | collective-permute-start | bytes 1572872 | tf_op jit(solution)/shard_map/ppermute | solution.py:20
  64.4 4.9 collective-permute-start.1
  179.4 13.3 %collective-permute-start.7 = (bf16[128,2048]{1,0:T(8,128)(2,1)S(1)}, bf16[128,2048]{1,0:T(8,128)(2,1)S(1)}, u32[]{:S(2)}, u32[]{:S(2)}) collective-permute-start(bf16[128,2048]{1,0:T(8,128)(2,1)S(1)} %fusion.46), channel_id=1, source_target_pairs={{0,2},{1,3},{2,0},{3,1},{4,6},{5,7},{6,4},{7,5},{8,10},{9,11},{10,... | collective-permute-start | bytes 1572872 | tf_op jit(solution)/shard_map/ppermute | solution.py:20
  194.2 12.5 %collective-permute-start.8 = (bf16[128,2048]{1,0:T(8,128)(2,1)S(1)}, bf16[128,2048]{1,0:T(8,128)(2,1)S(1)}, u32[]{:S(2)}, u32[]{:S(2)}) collective-permute-start(bf16[128,2048]{1,0:T(8,128)(2,1)S(1)} %add_convert_fusion.4), channel_id=1, source_target_pairs={{0,2},{1,3},{2,0},{3,1},{4,6},{5,7},{6,4},{7,5},{8,10},{9,11},{10,... | collective-permute-start | bytes 1572872 | tf_op jit(solution)/shard_map/ppermute | solution.py:20
  208.2 4.8 collective-permute-start.9
  240.0 15.8 %collective-permute-start.14 = (bf16[128,512]{1,0:T(8,128)(2,1)S(1)}, bf16[128,512]{1,0:T(8,128)(2,1)S(1)}, u32[]{:S(2)}, u32[]{:S(2)}) collective-permute-start(bf16[128,512]{1,0:T(8,128)(2,1)S(1)} %get-tuple-element.190), channel_id=1, source_target_pairs={{0,1},{1,0},{2,3},{3,2},{4,5},{5,4},{6,7},{7,6},{8,9},{9,8},{10,11... | collective-permute-start | bytes 393224 | tf_op jit(solution)/shard_map/ppermute | solution.py:20
  240.8 15.1 %collective-permute-start.15 = (bf16[128,512]{1,0:T(8,128)(2,1)S(1)}, bf16[128,512]{1,0:T(8,128)(2,1)S(1)}, u32[]{:S(2)}, u32[]{:S(2)}) collective-permute-start(bf16[128,512]{1,0:T(8,128)(2,1)S(1)} %get-tuple-element.189), channel_id=1, source_target_pairs={{0,2},{1,3},{2,0},{3,1},{4,6},{5,7},{6,4},{7,5},{8,10},{9,11},{10,... | collective-permute-start | bytes 393224 | tf_op jit(solution)/shard_map/ppermute | solution.py:20
  242.0 13.9 %collective-permute-start.16 = (bf16[128,512]{1,0:T(8,128)(2,1)S(1)}, bf16[128,512]{1,0:T(8,128)(2,1)S(1)}, u32[]{:S(2)}, u32[]{:S(2)}) collective-permute-start(bf16[128,512]{1,0:T(8,128)(2,1)S(1)} %get-tuple-element.188), channel_id=1, source_target_pairs={{0,3},{1,2},{2,1},{3,0},{4,7},{5,6},{6,5},{7,4},{8,11},{9,10},{10,... | collective-permute-start | bytes 393224 | tf_op jit(solution)/shard_map/ppermute | solution.py:20
  259.4 13.4 %collective-permute-start.18 = (bf16[128,2048]{1,0:T(8,128)(2,1)S(1)}, bf16[128,2048]{1,0:T(8,128)(2,1)S(1)}, u32[]{:S(2)}, u32[]{:S(2)}) collective-permute-start(bf16[128,2048]{1,0:T(8,128)(2,1)S(1)} %fusion.47), channel_id=1, source_target_pairs={{0,2},{1,3},{2,0},{3,1},{4,6},{5,7},{6,4},{7,5},{8,10},{9,11},{10,... | collective-permute-start | bytes 1572872 | tf_op jit(solution)/shard_map/ppermute | solution.py:20
  274.4 12.5 %collective-permute-start.19 = (bf16[128,2048]{1,0:T(8,128)(2,1)S(1)}, bf16[128,2048]{1,0:T(8,128)(2,1)S(1)}, u32[]{:S(2)}, u32[]{:S(2)}) collective-permute-start(bf16[128,2048]{1,0:T(8,128)(2,1)S(1)} %get-tuple-element.163), channel_id=1, source_target_pairs={{0,2},{1,3},{2,0},{3,1},{4,6},{5,7},{6,4},{7,5},{8,10},{9,11},{10,... | collective-permute-start | bytes 1572872 | tf_op jit(solution)/shard_map/ppermute | solution.py:20
  287.0 10.2 %collective-permute-start.20 = (bf16[2,128,2048]{2,1,0:T(8,128)(2,1)S(1)}, bf16[2,128,2048]{2,1,0:T(8,128)(2,1)S(1)}, u32[]{:S(2)}, u32[]{:S(2)}) collective-permute-start(bf16[2,128,2048]{2,1,0:T(8,128)(2,1)S(1)} %pad_maximum_fusion.7), channel_id=1, source_target_pairs={{0,1},{1,0},{2,3},{3,2},{4,5},{5,4},{6,7},{7,6},{8,9},{9,8},{10,11... | collective-permute-start | bytes 3145736 | tf_op jit(solution)/shard_map/ppermute | solution.py:20
  289.1 4.7 collective-permute-start.22
  290.4 6.8 %collective-permute-start.23 = (bf16[128,512]{1,0:T(8,128)(2,1)S(1)}, bf16[128,512]{1,0:T(8,128)(2,1)S(1)}, u32[]{:S(2)}, u32[]{:S(2)}) collective-permute-start(bf16[128,512]{1,0:T(8,128)(2,1)S(1)} %get-tuple-element.185), channel_id=1, source_target_pairs={{0,3},{1,2},{2,1},{3,0},{4,7},{5,6},{6,5},{7,4},{8,11},{9,10},{10,... | collective-permute-start | bytes 393224 | tf_op jit(solution)/shard_map/ppermute | solution.py:20
  320.1 229.4 %reduce-scatter.5.cloned.1.call-start = ((), (), s32[]{:S(2)}) async-start(), calls=%async_computation.6 | async-start | bytes 13369344 | tf_op jit(solution)/shard_map/reduce_scatter | solution.py:84
  342.3 13.6 %collective-permute-start.25 = (bf16[128,2048]{1,0:T(8,128)(2,1)S(1)}, bf16[128,2048]{1,0:T(8,128)(2,1)S(1)}, u32[]{:S(2)}, u32[]{:S(2)}) collective-permute-start(bf16[128,2048]{1,0:T(8,128)(2,1)S(1)} %fusion.48), channel_id=1, source_target_pairs={{0,2},{1,3},{2,0},{3,1},{4,6},{5,7},{6,4},{7,5},{8,10},{9,11},{10,... | collective-permute-start | bytes 1572872 | tf_op jit(solution)/shard_map/ppermute | solution.py:20
  358.1 12.9 %collective-permute-start.26 = (bf16[128,2048]{1,0:T(8,128)(2,1)S(1)}, bf16[128,2048]{1,0:T(8,128)(2,1)S(1)}, u32[]{:S(2)}, u32[]{:S(2)}) collective-permute-start(bf16[128,2048]{1,0:T(8,128)(2,1)S(1)} %get-tuple-element.133), channel_id=1, source_target_pairs={{0,2},{1,3},{2,0},{3,1},{4,6},{5,7},{6,4},{7,5},{8,10},{9,11},{10,... | collective-permute-start | bytes 1572872 | tf_op jit(solution)/shard_map/ppermute | solution.py:20
  477.6 13.3 %collective-permute-start.31 = (bf16[16,2,16,464]{3,2,1,0:T(8,128)(2,1)S(1)}, bf16[16,2,16,464]{3,2,1,0:T(8,128)(2,1)S(1)}, u32[]{:S(2)}, u32[]{:S(2)}) collective-permute-start(bf16[16,2,16,464]{3,2,1,0:T(8,128)(2,1)S(1)} %fusion.50), channel_id=1, source_target_pairs={{0,2},{1,3},{2,0},{3,1},{4,6},{5,7},{6,4},{7,5},{8,10},{9,11},{10,... | collective-permute-start | bytes 1425416 | tf_op jit(solution)/shard_map/ppermute | solution.py:20
  494.4 8.5 %collective-permute-start.32 = (bf16[16,16,464]{2,1,0:T(8,128)(2,1)}, bf16[16,16,464]{2,1,0:T(8,128)(2,1)S(1)}, u32[]{:S(2)}, u32[]{:S(2)}) collective-permute-start(bf16[16,16,464]{2,1,0:T(8,128)(2,1)} %fusion.54), channel_id=1, source_target_pairs={{0,4},{1,5},{2,6},{3,7},{4,0},{5,1},{6,2},{7,3},{8,12},{9,13},{10,... | collective-permute-start | bytes 712712 | tf_op jit(solution)/shard_map/ppermute | solution.py:20
  505.0 14.2 %all-to-all-start = ((bf16[16,16,464]{2,1,0:T(8,128)(2,1)}), bf16[16,16,464]{2,1,0:T(8,128)(2,1)S(1)}, u32[]{:S(2)}, u32[]{:S(2)}) async-start(bf16[16,16,464]{2,1,0:T(8,128)(2,1)} %fusion.53), calls=%async_computation.1 | async-start | bytes 524288 | tf_op jit(solution)/shard_map/all_to_all | solution.py:172
  520.1 6.0 %collective-permute-start.28 = (bf16[2,128,2048]{2,1,0:T(8,128)(2,1)S(1)}, bf16[2,128,2048]{2,1,0:T(8,128)(2,1)S(1)}, u32[]{:S(2)}, u32[]{:S(2)}) collective-permute-start(bf16[2,128,2048]{2,1,0:T(8,128)(2,1)S(1)} %select_bitcast_fusion), channel_id=1, source_target_pairs={{0,1},{1,0},{2,3},{3,2},{4,5},{5,4},{6,7},{7,6},{8,9},{9,8},{10,11... | collective-permute-start | bytes 3145736 | tf_op jit(solution)/shard_map/ppermute | solution.py:20
  523.9 13.7 %collective-permute-start.37 = (bf16[64,3584]{1,0:T(8,128)(2,1)S(1)}, bf16[64,3584]{1,0:T(8,128)(2,1)S(1)}, u32[]{:S(2)}, u32[]{:S(2)}) collective-permute-start(bf16[64,3584]{1,0:T(8,128)(2,1)S(1)} %broadcast_select_fusion.26), channel_id=1, source_target_pairs={{0,4},{1,5},{2,6},{3,7},{4,0},{5,1},{6,2},{7,3},{8,12},{9,13},{10,... | collective-permute-start | bytes 1376264 | tf_op jit(solution)/shard_map/ppermute | solution.py:20
  526.7 22.4 %collective-permute-start.29 = (bf16[128,2048]{1,0:T(8,128)(2,1)S(1)}, bf16[128,2048]{1,0:T(8,128)(2,1)S(1)}, u32[]{:S(2)}, u32[]{:S(2)}) collective-permute-start(bf16[128,2048]{1,0:T(8,128)(2,1)S(1)} %fusion.49), channel_id=1, source_target_pairs={{0,2},{1,3},{2,0},{3,1},{4,6},{5,7},{6,4},{7,5},{8,10},{9,11},{10,... | collective-permute-start | bytes 1572872 | tf_op jit(solution)/shard_map/ppermute | solution.py:20
  550.7 11.4 %collective-permute-start.33 = (bf16[64,3072]{1,0:T(8,128)(2,1)S(1)}, bf16[64,3072]{1,0:T(8,128)(2,1)S(1)}, u32[]{:S(2)}, u32[]{:S(2)}) collective-permute-start(bf16[64,3072]{1,0:T(8,128)(2,1)S(1)} %broadcast_select_fusion.27), channel_id=1, source_target_pairs={{0,4},{1,5},{2,6},{3,7},{4,0},{5,1},{6,2},{7,3},{8,12},{9,13},{10,... | collective-permute-start | bytes 1179656 | tf_op jit(solution)/shard_map/ppermute | solution.py:20
  564.1 5.8 collective-permute-start.34
  (83 other events, 879.7 us)
Sparse Core Ops, SparseCore 0:
  30.6 92.3 all-gather.2
  125.1 111.1 all-gather.4
  320.2 100.2 reduce-scatter.2
  453.8 95.1 reduce-scatter.4

commit v3 on v2

--- a/solution.py
+++ b/solution.py
@@ -65,13 +65,17 @@
     return mine + swap_low(send).astype(jnp.float32)
 
 
-def plane_gather(*blocks):
+def both_planes(laid, *blocks):
     high = lax.axis_index("seg") % 2
-    pairs = [
-        jnp.concatenate(in_order(block, swap_high(block), high == 1), axis=0) for block in blocks
-    ]
+    own, other = (
+        jnp.concatenate(laid(*got), axis=1) for got in (blocks, [swap_high(block) for block in blocks])
+    )
+    return jnp.concatenate(in_order(own, other, high == 1), axis=0)
+
+
+def plane_gather(pair):
     whole = lax.all_gather(
-        jnp.concatenate(pairs, axis=1),
+        pair,
         "seg",
         axis=0,
         tiled=True,
@@ -86,12 +90,28 @@
     )
 
 
-def finish_scatter(pair):
+def plane_halves(pair):
     high = lax.axis_index("seg") % 2
     rows = pair.shape[0] // 2
-    mine = jnp.where(high == 1, pair[rows:], pair[:rows])
-    send = jnp.where(high == 1, pair[:rows], pair[rows:])
+    return in_order(pair[:rows], pair[rows:], high == 1)
+
+
+def finish_scatter(mine, send):
     return mine.astype(jnp.float32) + swap_high(send).astype(jnp.float32)
+
+
+def gather_and_split(small, wide):
+    place = lax.axis_index("span")
+    n = wide.shape[1] // 4
+    messages = [
+        jnp.concatenate([lax.dynamic_slice_in_dim(wide, (place ^ bit) * n, n, 1), small], axis=1)
+        for bit in range(4)
+    ]
+    pieces = [m if bit == 0 else swap(m, bit) for bit, m in enumerate(messages)]
+    result = jnp.zeros((4, *messages[0].shape), small.dtype)
+    for bit, piece in enumerate(pieces):
+        result = lax.dynamic_update_index_in_dim(result, piece, place ^ bit, 0)
+    return pieces[1], result.reshape(4 * small.shape[0], -1)
 
 
 def split_columns(block):
@@ -160,19 +180,29 @@
     return jnp.concatenate([values[1:], jnp.zeros_like(values[:1])], axis=0)
 
 
-def reduce_small(part):
+def reduce_small(part, pair):
     place, high = lax.axis_index("span"), lax.axis_index("seg") % 2
     planes = lax.axis_size("seg") // 2
     width = part.shape[1]
     b = part.reshape(planes, 2, 2, 2, -1, width)
-    for dim, bit, move in ((3, place % 2, swap_core), (2, place // 2, swap_low), (1, high, swap_high)):
+
+    def summed(b, dim, bit, move):
         at0, at1 = (lax.index_in_dim(b, k, dim, keepdims=False) for k in (0, 1))
         mine, send = in_order(at0, at1, bit == 1)
-        b = mine.astype(jnp.float32) + move(send.astype(jnp.bfloat16)).astype(jnp.float32)
+        return mine.astype(jnp.float32) + move(send.astype(jnp.bfloat16)).astype(jnp.float32)
+
+    b = summed(summed(b, 3, place % 2, swap_core), 2, place // 2, swap_low)
+    b, pair = lax.optimization_barrier((b, pair))
+    finished = finish_scatter(*plane_halves(pair))
     arrived = lax.all_to_all(
-        b.astype(jnp.bfloat16), "seg", split_axis=0, concat_axis=0, tiled=True, axis_index_groups=plane_groups()
-    )
-    return arrived.astype(jnp.float32).sum(axis=0)
+        summed(b, 1, high, swap_high).astype(jnp.bfloat16),
+        "seg",
+        split_axis=0,
+        concat_axis=0,
+        tiled=True,
+        axis_index_groups=plane_groups(),
+    )
+    return arrived.astype(jnp.float32).sum(axis=0), finished
 
 
 CHUNK = 64
@@ -456,26 +486,24 @@
     )(r, k, v, gate, low, up, par, wkv, held, g_mixed)
 
 
-GRAD_COLUMNS = 256
+GRAD_ROWS, GRAD_COLUMNS = 512, 256
 
 
 def grad_kernel(left_ref, right_ref, *rest):
-    out_ref, turned = rest[-2:]
-
-    @pl.when(pl.program_id(0) == 0)
-    def _():
-        turned[...] = left_ref[...].T
-
-    out_ref[...] = mxu(turned[...], right_ref[...], NN).astype(jnp.bfloat16)
+    out_ref = rest[-1]
+    turned = left_ref[...].T
+    for at in range(0, out_ref.shape[1], GRAD_COLUMNS):
+        columns = slice(at, at + GRAD_COLUMNS)
+        out_ref[:, columns] = mxu(turned, right_ref[:, columns], NN).astype(jnp.bfloat16)
 
 
 def grad_into(left, right, total, at, into=None):
     rows, width = left.shape
     columns = right.shape[1]
-    shift = at // GRAD_COLUMNS
+    shift = at // columns
     specs = [
-        pl.BlockSpec((rows, width), lambda j: (0, 0)),
-        pl.BlockSpec((rows, GRAD_COLUMNS), lambda j: (0, j)),
+        pl.BlockSpec((rows, GRAD_ROWS), lambda i: (0, i)),
+        pl.BlockSpec((rows, columns), lambda i: (0, 0)),
     ]
     operands = [left, right]
     alias = {}
@@ -485,11 +513,10 @@
         alias = {2: 0}
     return pl.pallas_call(
         grad_kernel,
-        grid=(columns // GRAD_COLUMNS,),
+        grid=(width // GRAD_ROWS,),
         in_specs=specs,
-        out_specs=pl.BlockSpec((width, GRAD_COLUMNS), lambda j: (0, j + shift)),
+        out_specs=pl.BlockSpec((GRAD_ROWS, columns), lambda i: (i, shift)),
         out_shape=pltpu.HBM((width, total), jnp.bfloat16),
-        scratch_shapes=[pltpu.VMEM((width, rows), jnp.bfloat16)],
         input_output_aliases=alias,
         compiler_params=pltpu.CompilerParams(
             dimension_semantics=("arbitrary",), vmem_limit_bytes=32 * 2**20
@@ -503,21 +530,31 @@
     )(*operands)
 
 
-TILE = 256
+LOW = 256
+SHIFT_LANES = 5 * SHIFT_RANK
+LANES = SHIFT_LANES + 64
+
+TILE = 512
+
+
+def lane_group(shape):
+    return iota2(shape, 1) // SHIFT_RANK
 
 
 def mixes_forward_kernel(
     unit_ref, w_ref, down_ref, up_ref, vec_ref,
-    m0_ref, m1_ref, m2_ref, m3_ref, m4_ref, normed_ref, squash_ref, decay_ref, r_ref, k_ref, v_ref, g_ref,
-    hidden, decay,
+    m0_ref, m1_ref, m2_ref, m3_ref, m4_ref, normed_ref, squash_ref, r_ref, k_ref, v_ref, g_ref,
+    hidden, grouped,
 ):
     phase, tile = pl.program_id(0), pl.program_id(1)
-    rows, ranks = squash_ref.shape
+    rows = unit_ref.shape[0]
     own = r_ref.shape[1]
     vec = vec_ref[...]
     normed = unit_ref[...] * vec[0:1] + vec[1:2]
     row = iota2(normed.shape, 0)
     shifted = jnp.where(row == 0, 0.0, pltpu.roll(normed, 1, 0)) - normed
+    down = down_ref[...]
+    of_shift = iota2(down.shape, 1) < SHIFT_LANES
 
     @pl.when((phase == 0) & (tile == 0))
     def _():
@@ -525,27 +562,28 @@
 
     @pl.when(phase == 0)
     def _():
-        hidden[...] = hidden[...] + mxu(normed + shifted * vec[2:3], down_ref[:, :ranks], NN)
+        hidden[...] = hidden[...] + mxu(normed + shifted * vec[2:3], jnp.where(of_shift, down, 0), NN)
 
     @pl.when((phase == 1) & (tile == 0))
     def _():
-        squash_ref[...] = jnp.tanh(hidden[...])
-        decay[...] = jnp.zeros_like(decay)
+        squash = jnp.tanh(hidden[...])
+        squash_ref[...] = squash
+        group = lane_group(squash.shape)
+        for g in range(5):
+            grouped[g] = jnp.where(group == g, squash, 0.0).astype(jnp.bfloat16)
+        hidden[...] = jnp.zeros_like(hidden)
         for ref in (r_ref, k_ref, v_ref, g_ref):
             ref[...] = jnp.zeros_like(ref)
 
     @pl.when(phase == 1)
     def _():
         normed_ref[...] = normed
-        group_col = iota2((rows, ranks), 1) // SHIFT_RANK
-        squash_low = squash_ref[...].astype(jnp.bfloat16)
         up = up_ref[...]
         for g, mix_ref in enumerate((m0_ref, m1_ref, m2_ref, m3_ref, m4_ref)):
-            squash_g = jnp.where(group_col == g, squash_low, 0)
-            mix = (normed + shifted * (vec[3 + g : 4 + g] + mxu(squash_g, up, NT))).astype(jnp.bfloat16)
+            mix = (normed + shifted * (vec[3 + g : 4 + g] + mxu(grouped[g], up, NT))).astype(jnp.bfloat16)
             mix_ref[...] = mix
             if g == 0:
-                decay[...] = decay[...] + mxu(mix, down_ref[:, ranks:], NN)
+                hidden[...] = hidden[...] + mxu(mix, jnp.where(of_shift, 0, down), NN)
             else:
                 column = (None, 1, 2, 0, 3)[g] * own
                 out = (None, k_ref, v_ref, r_ref, g_ref)[g]
@@ -553,15 +591,13 @@
 
     @pl.when((phase == 1) & (tile == pl.num_programs(1) - 1))
     def _():
-        decay_ref[...] = jnp.tanh(decay[...])
-
-
-def mixes_forward(unit, proj_w, down, up_mods, vec, own):
+        squash_ref[...] = squash_ref[...] + jnp.tanh(hidden[...])
+
+
+def mixes_forward(unit, first, low_at, vec, own):
     rows, width = unit.shape
-    ranks = up_mods.shape[1]
-    low = down.shape[1] - ranks
     tiles = width // TILE
-    down_rows = lambda columns: pl.BlockSpec((TILE, columns), lambda p, n: (n, 0))
+    block = low_at // LOW
     across = lambda r: pl.BlockSpec((r, TILE), lambda p, n: (0, n))
     late = pl.BlockSpec((rows, TILE), lambda p, n: (0, n * p))
     whole = lambda columns: pl.BlockSpec((rows, columns), lambda p, n: (0, 0))
@@ -572,77 +608,76 @@
         in_specs=[
             across(rows),
             pl.BlockSpec((TILE, 4 * own), lambda p, n: (n * p, 0)),
-            down_rows(down.shape[1]),
-            down_rows(ranks),
+            pl.BlockSpec((TILE, LOW), lambda p, n: (n, block)),
+            pl.BlockSpec((TILE, LOW), lambda p, n: (n, block + 1)),
             across(vec.shape[0]),
         ],
-        out_specs=[late] * 6 + [whole(ranks), whole(low)] + [whole(own)] * 4,
+        out_specs=[late] * 6 + [whole(LOW)] + [whole(own)] * 4,
         out_shape=[kept(width, jnp.bfloat16)] * 5
-        + [kept(width, jnp.float32), kept(ranks, jnp.float32), kept(low, jnp.float32)]
+        + [kept(width, jnp.float32), kept(LOW, jnp.float32)]
         + [kept(own, jnp.float32)] * 4,
-        scratch_shapes=[pltpu.VMEM((rows, ranks), jnp.float32), pltpu.VMEM((rows, low), jnp.float32)],
+        scratch_shapes=[pltpu.VMEM((rows, LOW), jnp.float32), pltpu.VMEM((5, rows, LOW), jnp.bfloat16)],
         compiler_params=pltpu.CompilerParams(
             dimension_semantics=("arbitrary", "arbitrary"), vmem_limit_bytes=48 * 2**20
         ),
         cost_estimate=pl.CostEstimate(
-            flops=2 * rows * width * (4 * own + 7 * ranks),
+            flops=2 * rows * width * (4 * own + 7 * LOW),
             bytes_accessed=2 * width * 4 * own + 22 * rows * width,
             transcendentals=0,
         ),
         name="mixes_forward",
-    )(unit, proj_w, down, up_mods, vec)
+    )(unit, first, first, first, vec)
 
 
 def mixes_back_kernel(
     gk_ref, gv_ref, gr_ref, gg_ref, gd_ref, w_ref, down_ref, up_ref, vec_ref, squash_ref, normed_ref,
-    out_ref, down_grad_ref, up_grad_ref, sums_ref,
-    g_shift, g_norm, g_squash, g_hidden, g_up, g_sums,
+    mix_ref, sums_ref, out_ref, small_ref,
+    g_shift, g_norm, g_squash, g_hidden, g_up, g_sums, grouped, turned,
 ):
     phase, tile = pl.program_id(0), pl.program_id(1)
-    rows, ranks = squash_ref.shape
+    rows = squash_ref.shape[0]
     own = gk_ref.shape[1]
     normed = normed_ref[...]
     row = iota2(normed.shape, 0)
     shifted = jnp.where(row == 0, 0.0, pltpu.roll(normed, 1, 0)) - normed
     squash = squash_ref[...]
-    up = up_ref[...]
     vec = vec_ref[...]
 
     @pl.when((phase == 0) & (tile == 0))
     def _():
         g_squash[...] = jnp.zeros_like(g_squash)
+        group = lane_group(squash.shape)
+        for g in range(5):
+            grouped[g] = jnp.where(group == g, squash, 0.0).astype(jnp.bfloat16)
+        turned[...] = squash.astype(jnp.bfloat16).T
 
     @pl.when(phase == 0)
     def _():
-        group_col = iota2((rows, ranks), 1) // SHIFT_RANK
-        group_wide = iota2((TILE, ranks), 1) // SHIFT_RANK
-        squash_low = squash.astype(jnp.bfloat16)
+        up = up_ref[...]
+        group_wide = lane_group(up.shape)
         total_shift = jnp.zeros((rows, TILE), jnp.float32)
         total_norm = jnp.zeros((rows, TILE), jnp.float32)
-        add_squash = jnp.zeros((rows, ranks), jnp.float32)
-        add_up = jnp.zeros((TILE, ranks), jnp.float32)
+        add_squash = jnp.zeros((rows, LOW), jnp.float32)
         sums = []
         for g in range(5):
-            squash_g = jnp.where(group_col == g, squash_low, 0)
-            up_g = jnp.where(group_wide == g, up, 0)
             if g == 0:
-                part = mxu(gd_ref[...], down_ref[:, ranks:], NT)
+                part = mxu(gd_ref[...], down_ref[...], NT)
             else:
                 column = (None, 1, 2, 0, 3)[g] * own
                 grad = (None, gk_ref, gv_ref, gr_ref, gg_ref)[g]
                 part = mxu(grad[...], w_ref[:, column : column + own], NT)
-            coeff = vec[3 + g : 4 + g] + mxu(squash_g, up, NT)
+            coeff = vec[3 + g : 4 + g] + mxu(grouped[g], up, NT)
             times = part * shifted
             times_low = times.astype(jnp.bfloat16)
             sums.append(jnp.sum(times, axis=0, keepdims=True))
             total_shift = total_shift + part * coeff
             total_norm = total_norm + part
-            add_squash = add_squash + mxu(times_low, up_g, NN)
-            add_up = add_up + mxu(times_low, squash_g, TN)
+            add_squash = add_squash + mxu(times_low, jnp.where(group_wide == g, up, 0), NN)
+            lanes = slice(g * SHIFT_RANK, (g + 1) * SHIFT_RANK)
+            g_up[tile, lanes] = mxu(turned[lanes], times_low, NN)
         g_shift[tile] = total_shift
         g_norm[tile] = total_norm
         g_squash[...] = g_squash[...] + add_squash
-        g_up[tile] = add_up
         g_sums[tile] = jnp.concatenate(sums + [jnp.zeros((3, TILE), jnp.float32)], axis=0)
 
     @pl.when((phase == 1) & (tile == 0))
@@ -652,8 +687,7 @@
     @pl.when(phase == 1)
     def _():
         blend = vec[2:3]
-        mix_in = normed + shifted * blend
-        part = mxu(g_hidden[...], down_ref[:, :ranks], NT)
+        part = mxu(g_hidden[...], down_ref[...], NT)
         total_shift = g_shift[tile] + part * blend
         total = g_norm[tile] + part - total_shift
         total = total + jnp.where(row == rows - 1, 0.0, pltpu.roll(total_shift, rows - 1, 0))
@@ -664,59 +698,65 @@
             jnp.sum(total, axis=0, keepdims=True),
             jnp.sum(part * shifted, axis=0, keepdims=True),
         ]
-        sums_ref[...] = jnp.concatenate(head + [g_sums[tile][:5]], axis=0)
-        down_grad_ref[...] = mxu(mix_in, g_hidden[...], TN)
-        up_grad_ref[...] = g_up[tile]
-
-
-def mixes_back(g_key, g_val, g_recept, g_gate, g_decay, proj_w, down, up_mods, vec, squash, normed):
+        sums = jnp.concatenate(head + [g_sums[tile][:5], sums_ref[...]], axis=0)
+        shape = (sums.shape[0], LOW)
+        behind = jnp.where(iota2(shape, 1) == LANES + iota2(shape, 0), 1.0, 0.0)
+        small_ref[:, :LOW] = (
+            mxu(normed + shifted * blend, g_hidden[...], TN) + mxu(mix_ref[...], gd_ref[...], TN)
+        ).astype(jnp.bfloat16)
+        small_ref[:, LOW:] = mxu(sums, behind, TN).astype(jnp.bfloat16)
+        small_ref[:, LOW : LOW + SHIFT_LANES] = g_up[tile].T.astype(jnp.bfloat16)
+
+
+def mixes_back(g_key, g_val, g_recept, g_gate, g_decay, first, low_at, vec, squash, normed, mix, sums):
     rows, width = normed.shape
-    own, ranks = g_key.shape[1], squash.shape[1]
+    own = g_key.shape[1]
     tiles = width // TILE
+    block = low_at // LOW
     whole = lambda a: pl.BlockSpec(a.shape, lambda p, n: (0, 0))
-    down_rows = lambda columns: pl.BlockSpec((TILE, columns), lambda p, n: (n, 0))
-    first_only = pl.BlockSpec((TILE, 4 * own), lambda p, n: (n * (1 - p) + (tiles - 1) * p, 0))
     across = lambda r: pl.BlockSpec((r, TILE), lambda p, n: (0, n))
-    late = lambda n_rows: pl.BlockSpec((n_rows, TILE), lambda p, n: (0, n * p))
-    late_down = lambda columns: pl.BlockSpec((TILE, columns), lambda p, n: (n * p, 0))
+    late = lambda r: pl.BlockSpec((r, TILE), lambda p, n: (0, n * p))
+    early = lambda p, n: n * (1 - p) + (tiles - 1) * p
     return pl.pallas_call(
         mixes_back_kernel,
         grid=(2, tiles),
         in_specs=[whole(g_key)] * 4
         + [
             whole(g_decay),
-            first_only,
-            down_rows(down.shape[1]),
-            down_rows(ranks),
+            pl.BlockSpec((TILE, 4 * own), lambda p, n: (early(p, n), 0)),
+            pl.BlockSpec((TILE, LOW), lambda p, n: (n, block)),
+            pl.BlockSpec((TILE, LOW), lambda p, n: (early(p, n), block + 1)),
             across(vec.shape[0]),
             whole(squash),
             across(rows),
+            late(rows),
+            late(sums.shape[0]),
         ],
-        out_specs=[late(rows), late_down(ranks), late_down(ranks), late(8)],
+        out_specs=[late(rows), pl.BlockSpec((TILE, 2 * LOW), lambda p, n: (n * p, 0))],
         out_shape=[
             jax.ShapeDtypeStruct((rows, width), jnp.bfloat16),
-            jax.ShapeDtypeStruct((width, ranks), jnp.float32),
-            jax.ShapeDtypeStruct((width, ranks), jnp.float32),
-            jax.ShapeDtypeStruct((8, width), jnp.float32),
+            jax.ShapeDtypeStruct((width, 2 * LOW), jnp.bfloat16),
         ],
         scratch_shapes=[
             pltpu.VMEM((tiles, rows, TILE), jnp.float32),
             pltpu.VMEM((tiles, rows, TILE), jnp.float32),
-            pltpu.VMEM((rows, ranks), jnp.float32),
-            pltpu.VMEM((rows, ranks), jnp.bfloat16),
-            pltpu.VMEM((tiles, TILE, ranks), jnp.float32),
+            pltpu.VMEM((rows, LOW), jnp.float32),
+            pltpu.VMEM((rows, LOW), jnp.bfloat16),
+            pltpu.VMEM((tiles, SHIFT_LANES, TILE), jnp.float32),
             pltpu.VMEM((tiles, 8, TILE), jnp.float32),
+            pltpu.VMEM((5, rows, LOW), jnp.bfloat16),
+            pltpu.VMEM((LOW, rows), jnp.bfloat16),
         ],
         compiler_params=pltpu.CompilerParams(
             dimension_semantics=("arbitrary", "arbitrary"), vmem_limit_bytes=56 * 2**20
         ),
         cost_estimate=pl.CostEstimate(
-            flops=2 * rows * width * (4 * own + 17 * ranks),
+            flops=2 * rows * width * (4 * own + 17 * LOW),
             bytes_accessed=2 * width * 4 * own + 10 * rows * width,
             transcendentals=0,
         ),
         name="mixes_back",
-    )(g_key, g_val, g_recept, g_gate, g_decay, proj_w, down, up_mods, vec, squash, normed)
+    )(g_key, g_val, g_recept, g_gate, g_decay, first, first, first, vec, squash, normed, mix, sums)
 
 
 def shards(
@@ -733,7 +773,6 @@
     channel_value_weight,
 ):
     token_rows, width = inputs.shape
-    ranks = 5 * SHIFT_RANK
     own_width = time_mix_weight.shape[2]
     hidden = channel_key_weight.shape[1]
     local_heads = own_width // GROUP_DIMENSION
@@ -741,24 +780,25 @@
     position = lax.axis_index("span") * token_rows
 
     x_seg = span_gather(inputs).astype(jnp.float32)
-    small_rows = span_gather(
-        jnp.concatenate([rank_down_weight, rank_up_weight.T, vectors.T], axis=1)
-    )
-    first = plane_gather(
-        jnp.concatenate([time_mix_weight[g] for g in range(4)] + [output_weight.T], axis=1), small_rows
-    )
+    def blank(count):
+        return jnp.zeros((token_rows // 8, count), jnp.bfloat16)
+
+    small_rows = jnp.concatenate(
+        [rank_down_weight, blank(LOW - LANES), rank_up_weight.T, vectors.T, blank(LOW - LANES - 16)], axis=1
+    )
+    early, span_rows = gather_and_split(small_rows, channel_receptance_weight)
+    _, time_mix_weight, output_weight = lax.optimization_barrier((early, time_mix_weight, output_weight))
+    weights = both_planes(
+        lambda proj, out: [proj[g] for g in range(4)] + [out.T], time_mix_weight, output_weight
+    )
+    first = plane_gather(jnp.concatenate([weights, both_planes(lambda rows: [rows], span_rows)], axis=1))
     second = plane_gather(
-        jnp.concatenate(
-            [channel_key_weight, channel_value_weight.T, split_columns(channel_receptance_weight)], axis=1
-        )
-    )
-    out_w = first[:, 4 * own_width : 5 * own_width]
-    low_rank = first[:, 5 * own_width :]
-    key_w, value_w, recept_w = second[:, :hidden], second[:, hidden : 2 * hidden], second[:, 2 * hidden :]
-    rank_all = rank_down_weight.shape[1]
-    down_weight = low_rank[:, :rank_all]
-    up_mods, up_decay = low_rank[:, rank_all : rank_all + ranks], low_rank[:, rank_all + ranks : 2 * rank_all]
-    vec = low_rank[:, 2 * rank_all :].T.astype(jnp.float32)
+        both_planes(lambda key, value: [key, value.T], channel_key_weight, channel_value_weight)
+    )
+    low_at = 6 * own_width
+    out_w, recept_w = first[:, 4 * own_width : 5 * own_width], first[:, 5 * own_width : low_at]
+    up_at = low_at + LOW
+    vec = first[:, up_at + LANES : up_at + LANES + 16].T.astype(jnp.float32)
 
     def own_cols(line):
         return lax.dynamic_slice_in_dim(line, col_start, own_width, line.ndim - 1)
@@ -766,20 +806,18 @@
     def own_rows(values):
         return lax.dynamic_slice_in_dim(values, position, token_rows, 0)
 
-    def place_rows(values):
-        blank = jnp.zeros((width,) + values.shape[1:], jnp.float32)
-        return lax.dynamic_update_slice_in_dim(blank, values, col_start, 0)
-
     x_in = inputs.astype(jnp.float32)
     _, unit_seg, _ = norm_rows(x_seg, 1.0, 0.0)
-    *mixes, normed, squash, decay_tanh, recept, key_proj, val_proj, gate_pre = mixes_forward(
-        unit_seg, first, down_weight, up_mods, vec, own_width
-    )
-    decay_low = decay_tanh.astype(jnp.bfloat16)
-    up_decay_own = lax.dynamic_slice_in_dim(up_decay, col_start, own_width, 0)
+    *mixes, normed, squash, recept, key_proj, val_proj, gate_pre = mixes_forward(
+        unit_seg, first, low_at, vec, own_width
+    )
+    lane = lax.broadcasted_iota(jnp.int32, squash.shape, 1)
+    of_decay = (lane >= SHIFT_LANES) & (lane < LANES)
+    decay_low = jnp.where(of_decay, squash, 0.0).astype(jnp.bfloat16)
+    up_own = lax.dynamic_slice(first, (col_start, up_at), (own_width, LOW))
     head_vec = jnp.concatenate([own_cols(vec[8:12]), jnp.zeros((4, own_width), jnp.float32)], axis=0)
     first_state = jnp.transpose(states[0], (2, 0, 1)).reshape(GROUP_DIMENSION, own_width)
-    heads_in = (recept, key_proj, val_proj, gate_pre, decay_low, up_decay_own, head_vec)
+    heads_in = (recept, key_proj, val_proj, gate_pre, decay_low, up_own, head_vec)
     mixed, wkv, held = wkv_forward(*heads_in, first_state)
     resid = x_in + span_reduce(backward_product(mixed, out_w).astype(jnp.bfloat16))
 
@@ -788,16 +826,21 @@
     shifted_two = prior_rows(n2) - n2
     key_in = (n2 + shifted_two * vec[14]).astype(jnp.bfloat16)
     rec_in = (n2 + shifted_two * vec[15]).astype(jnp.bfloat16)
+    rec_part = product_lower(rec_in, recept_w).astype(jnp.bfloat16)
+    rec_pre, second = lax.optimization_barrier((join_columns(rec_part), second))
+    key_w, value_w = second[:, :hidden], second[:, hidden:]
     hidden_two = product_lower(key_in, key_w)
     active = jax.nn.relu(hidden_two)
     squared = (active * active).astype(jnp.bfloat16)
-    rec_part = product_lower(rec_in, recept_w).astype(jnp.bfloat16)
-    rec_pre = join_columns(rec_part)
-    _, squared = lax.optimization_barrier((rec_part, squared))
-    value_part, rec_pre = lax.optimization_barrier(
-        (backward_product(squared, value_w).astype(jnp.bfloat16), rec_pre)
-    )
-    value_out = span_reduce(value_part)
+    active = active.astype(jnp.bfloat16)
+    half = width // 2
+    value_out = jnp.concatenate(
+        [
+            span_reduce(backward_product(squared, value_w[at : at + half]).astype(jnp.bfloat16))
+            for at in (0, half)
+        ],
+        axis=1,
+    )
     rec_gate = jax.nn.sigmoid(rec_pre.astype(jnp.float32))
     output = (resid + rec_gate * value_out).astype(jnp.bfloat16)
 
@@ -805,12 +848,14 @@
     g_value = (grad_out * rec_gate).astype(jnp.bfloat16)
     g_rec = (grad_out * value_out * rec_gate * (1.0 - rec_gate)).astype(jnp.bfloat16)
     g_value_all = span_gather(g_value)
+    g_value_all, g_rec = lax.optimization_barrier((g_value_all, g_rec))
     g_rec_own = split_columns(g_rec)
-    cm_total = 2 * hidden
+    cm_total = 2 * hidden + own_width
     cm_part = grad_into(g_value_all, squared, cm_total, hidden)
     g_value_all, cm_part = lax.optimization_barrier((g_value_all, cm_part))
-    g_hid = (product_lower(g_value_all, value_w) * 2.0 * active).astype(jnp.bfloat16)
+    g_hid = (product_lower(g_value_all, value_w) * 2.0 * active.astype(jnp.float32)).astype(jnp.bfloat16)
     cm_part = grad_into(key_in, g_hid, cm_total, 0, cm_part)
+    cm_part = grad_into(rec_in, g_rec_own, cm_total, 2 * hidden, cm_part)
     cm_part, g_hid, g_rec_own = lax.optimization_barrier((cm_part, g_hid, g_rec_own))
     cm_pair = plane_scatter(cm_part)
     g_key_in = backward_product(g_hid, key_w)
@@ -832,51 +877,45 @@
     state_grad = jnp.transpose(
         g_first.reshape(GROUP_DIMENSION, local_heads, GROUP_DIMENSION), (1, 2, 0)
     )[None]
-    tm_total = 6 * own_width
+    tm_total = 5 * own_width
     tm_part = grad_into(g_att, mixed, tm_total, 0)
-    tm_part = grad_into(rec_in, g_rec_own, tm_total, 5 * own_width, tm_part)
     for at, mix, grad in ((1, 3, g_recept), (2, 1, g_key), (3, 2, g_val), (4, 4, g_gate)):
         tm_part = grad_into(mixes[mix], grad, tm_total, at * own_width, tm_part)
-    g_key, g_ww, tm_part = lax.optimization_barrier((g_key, g_ww, tm_part))
-
+    tm_part, cm_pair = lax.optimization_barrier((tm_part, cm_pair))
+    tm_pair = plane_scatter(tm_part)
+    g_key, g_ww, cm_pair = lax.optimization_barrier((g_key, g_ww, cm_pair))
+
+    g_decay_hidden = jnp.where(
+        of_decay, product_lower(g_ww, up_own) * (1.0 - squash * squash), 0.0
+    ).astype(jnp.bfloat16)
     up_decay_grad = outer_sum(g_ww, decay_low)
-    g_decay_hidden = (
-        product_lower(g_ww, up_decay_own) * (1.0 - decay_tanh * decay_tanh)
-    ).astype(jnp.bfloat16)
-    down_decay_grad = outer_sum(mixes[0], g_decay_hidden)
-    g_normed, down_mods_grad, up_mods_grad, width_sums = mixes_back(
-        g_key, g_val, g_recept, g_gate, g_decay_hidden, first, down_weight, up_mods, vec, squash, normed
-    )
-    g_normed, cm_pair, tm_part = lax.optimization_barrier((g_normed, cm_pair, tm_part))
-    tm_pair = plane_scatter(tm_part)
-    cm_grad = finish_scatter(cm_pair)
-    tm_grad = finish_scatter(tm_pair)
+    other_sums = jnp.concatenate(
+        [
+            lax.dynamic_update_slice_in_dim(jnp.zeros((4, width), jnp.float32), head_sums[:4], col_start, 1),
+            jnp.stack([vec_twelve, vec_thirteen, vec_fourteen, vec_fifteen]),
+        ],
+        axis=0,
+    )
+    g_normed, small_part = mixes_back(
+        g_key, g_val, g_recept, g_gate, g_decay_hidden, first, low_at, vec, squash, normed, mixes[0], other_sums
+    )
+    own_part = lax.dynamic_slice(small_part, (col_start, LOW), (own_width, LOW))
+    small_part = lax.dynamic_update_slice(
+        small_part, (own_part.astype(jnp.float32) + up_decay_grad).astype(jnp.bfloat16), (col_start, LOW)
+    )
+    small, cm_grad = reduce_small(small_part, cm_pair)
+    tm_grad = finish_scatter(*plane_halves(tm_pair))
     g_n1 = span_reduce(g_normed)
     _, unit_own, rstd_own = norm_rows(x_in, vec[0], vec[1])
     x_grad = g_resid + norm_back(g_n1, unit_own, rstd_own, vec[0])
-    vec_part = jnp.concatenate(
-        [
-            width_sums.T,
-            place_rows(head_sums[:4].T),
-            jnp.stack([vec_twelve, vec_thirteen, vec_fourteen, vec_fifteen]).T,
-        ],
-        axis=1,
-    )
-    small = reduce_small(
-        jnp.concatenate(
-            [down_mods_grad, down_decay_grad, up_mods_grad, place_rows(up_decay_grad), vec_part], axis=1
-        )
-    )
-    down_grad, up_grad, vec_grad = (
-        small[:, :rank_all],
-        small[:, rank_all : 2 * rank_all].T,
-        small[:, 2 * rank_all :].T,
-    )
-    rec_grad = join_columns(tm_grad[:, 5 * own_width :])
-    value_grad = cm_grad[:, hidden:].T
+    down_grad = small[:, :LANES]
+    up_grad = small[:, LOW : LOW + LANES].T
+    vec_grad = small[:, LOW + LANES : LOW + LANES + 16].T
+    rec_grad = join_columns(cm_grad[:, 2 * hidden :])
+    value_grad = cm_grad[:, hidden : 2 * hidden].T
     key_grad = cm_grad[:, :hidden]
     out_grad = tm_grad[:, :own_width].T
-    proj_grad = jnp.moveaxis(tm_grad[:, own_width : 5 * own_width].reshape(-1, 4, own_width), 1, 0)
+    proj_grad = jnp.moveaxis(tm_grad[:, own_width:].reshape(-1, 4, own_width), 1, 0)
     return (
         output,
         x_grad,

time: 584 us -> 536 us (0.918)
  local copies, waits for them, and re-layouts: 42.7 us -> 19.9 us
  Pallas kernels: 131 us -> 118 us
  waiting for transfers between devices: 247 us -> 236 us
    ppermute x38 -> x40, waiting for transfers between devices: 174 us -> 143 us  [swap(): return lax.ppermute(block, ALL, [(i, i ^ bit) for i in range(count)])]
    reduce_scatter x2, waiting for transfers between devices: 0.03 us -> 17.2 us  [plane_scatter(): lax.psum_scatter(part, 'seg', scatter_dimension=0, tiled=True, axis_index...]
    unnamed x149 -> x133, local copies, waits for them, and re-layouts: 15.2 us -> 7.49 us
    pallas_call x1, Pallas kernels: 32.2 us -> 25.6 us  [mixes_back(): pl.pallas_call(mixes_back_kernel, grid=(2, tiles), in_specs=[whole(g_key)...]
    dot_general x4 -> x5, matrix products: 20.5 us -> 18.3 us  [backward_product(): jnp.einsum('te,de->td', gradient, weights, preferred_element_type=jnp.flo...]
    ppermute x38 -> x40, starting transfers between devices: 52.4 us -> 53.2 us  [swap(): return lax.ppermute(block, ALL, [(i, i ^ bit) for i in range(count)])]
  transfers between devices with their start and end apart: 43 -> 45, of which waited for: 30 -> 30; matrix products, arithmetic and copies ran while one was open for 17% -> 16% of each run, Pallas kernels for 20% -> 22%
where the time goes in v3:
time: 536 us; the launch traced here: 531 us
  waiting for transfers between devices  236 us (44%)
  Pallas kernels  118 us (22%)
  starting transfers between devices  58.4 us (11%)
  other arithmetic  44.1 us (8%)
  matrix products  39.1 us (7%)
  local copies, waits for them, and re-layouts  19.9 us (4%)
  between operations  15.7 us (3%)
    ppermute x40, waiting for transfers between devices, swap(): return lax.ppermute(block, ALL, [(i, i ^ bit) for i in range(count)])  143 us
    all_gather x2, waiting for transfers between devices, plane_gather(): lax.all_gather(pair, 'seg', axis=0, tiled=True, axis_index_groups=plane_g...  68.7 us
    ppermute x40, starting transfers between devices, swap(): return lax.ppermute(block, ALL, [(i, i ^ bit) for i in range(count)])  53.2 us
    pallas_call x8, Pallas kernels, grad_into(): pl.pallas_call(grad_kernel, grid=(width // GRAD_ROWS,), in_specs=specs, o...  32.2 us
    pallas_call x1, Pallas kernels, mixes_back(): pl.pallas_call(mixes_back_kernel, grid=(2, tiles), in_specs=[whole(g_key)...  25.6 us
    pallas_call x1, Pallas kernels, wkv_backward(): pl.pallas_call(wkv_backward_kernel, grid=(chunks,), in_specs=[block] * 4...  21.5 us
    pallas_call x1, Pallas kernels, mixes_forward(): pl.pallas_call(mixes_forward_kernel, grid=(2, tiles), in_specs=[across(ro...  20.4 us
    dot_general x5, matrix products, product_lower(): return jnp.dot(left_arg, right_arg, preferred_element_type=jnp.float32)  18.6 us
  transfers between devices with their start and end apart: 45, of which 30 were waited for; matrix products, arithmetic and copies ran while one was open for 16% of the time, Pallas kernels for 22%

profile of v3, /device:TPU:1, one launch (start us, length us, event | category | flops | bytes accessed | tf_op | source)
XLA Modules:
  0.0 531.3 jit_solution(9082844678310038710)
XLA Ops:
  33.5 4.6 collective-permute-done.16
  38.0 4.9 collective-permute-done.15
  45.5 10.4 %collective-permute-done = bf16[128,2048]{1,0:T(8,128)(2,1)S(1)} collective-permute-done((bf16[128,2048]{1,0:T(8,128)(2,1)S(1)}, bf16[128,2048]{1,0:T(8,128)(2,1)S(1)}, u32[]{:S(2)}, u32[]{:S(2)}) %collective-permute-start) | collective-permute-done | bytes 524320 | tf_op jit(solution)/shard_map/ppermute | solution.py:20
  64.9 4.6 fusion.6.unit_ref
  69.5 64.4 %all-gather.3.cloned.1.call-done.w_ref.down_ref.up_ref = bf16[2048,3584]{1,0:T(8,128)(2,1)} async-done(((bf16[128,3584]{1,0:T(8,128)(2,1)}), bf16[2048,3584]{1,0:T(8,128)(2,1)}) %all-gather.3.cloned.1.call-update) | async-done | bytes 14680080 | tf_op jit(solution)/shard_map/all_gather | solution.py:77
  135.4 20.4 %mixes_forward.1 = (bf16[512,2048]{1,0:T(8,128)(2,1)}, bf16[512,2048]{1,0:T(8,128)(2,1)}, bf16[512,2048]{1,0:T(8,128)(2,1)}, bf16[512,2048]{1,0:T(8,128)(2,1)}, ...) custom-call(f32[512,2048]{1,0:T(8,128)} %fusion.6.unit_ref, ...), custom_call_target="tpu_custom_call" | custom-call | flops 8053063680 | bytes 31457280 | tf_op jit(solution)/shard_map/mixes_forward/pallas_call | solution.py:605
  157.0 18.1 %wkv_forward.1 = (bf16[512,512]{1,0:T(8,128)(2,1)S(1)}, f32[512,512]{1,0:T(8,128)S(1)}, f32[512,512]{1,0:T(8,128)S(1)}) custom-call(f32[512,512]{1,0:T(8,128)S(1)} %get-tuple-element.54.refs_0_, f32[512,512]{1,0:T(8,128)S(1)} %get-tuple-element.55.refs_1_, f32[512,512]{1,0:T(8,128)S(1)} %get-tuple-element.56.refs_2_, ...), custom_call_target="tpu_custom_call" | custom-call | flops 1207959552 | bytes 6815744 | tf_op jit(solution)/shard_map/wkv_forward/pallas_call | solution.py:353
  175.1 3.8 convolution_convert_fusion
  185.0 11.5 %collective-permute-done.9 = bf16[128,2048]{1,0:T(8,128)(2,1)S(1)} collective-permute-done((bf16[128,2048]{1,0:T(8,128)(2,1)S(1)}, bf16[128,2048]{1,0:T(8,128)(2,1)S(1)}, u32[]{:S(2)}, u32[]{:S(2)}) %collective-permute-start.9) | collective-permute-done | bytes 524320 | tf_op jit(solution)/shard_map/ppermute | solution.py:20
  199.6 11.3 %collective-permute-done.10 = bf16[128,2048]{1,0:T(8,128)(2,1)S(1)} collective-permute-done((bf16[128,2048]{1,0:T(8,128)(2,1)S(1)}, bf16[128,2048]{1,0:T(8,128)(2,1)S(1)}, u32[]{:S(2)}, u32[]{:S(2)}) %collective-permute-start.10) | collective-permute-done | bytes 524320 | tf_op jit(solution)/shard_map/ppermute | solution.py:20
  232.1 4.3 all-gather.5.cloned.1.call-done
  236.5 7.8 %multiply_convert_fusion.1 = (bf16[512,1792]{1,0:T(8,128)(2,1)S(1)}, bf16[512,1792]{1,0:T(8,128)(2,1)S(1)}) fusion(bf16[512,2048]{1,0:T(8,128)(2,1)} %get-tuple-element.131.left_ref, bf16[2048,3584]{1,0:T(8,128)(2,1)} %all-gather.5.cloned.1.call-done), kind=kOutput, calls=%fused_computation.23 | convolution fusion | flops 3761766400 | bytes 13107200 | tf_op jit(solution)/shard_map/dot_general | solution.py:148
  253.1 4.3 collective-permute-done.20
  257.5 5.5 %collective-permute-done.18 = bf16[128,1024]{1,0:T(8,128)(2,1)S(1)} collective-permute-done((bf16[128,1024]{1,0:T(8,128)(2,1)S(1)}, bf16[128,1024]{1,0:T(8,128)(2,1)S(1)}, u32[]{:S(2)}, u32[]{:S(2)}) %collective-permute-start.18) | collective-permute-done | bytes 262176 | tf_op jit(solution)/shard_map/ppermute | solution.py:20
  265.8 10.9 %collective-permute-done.21 = bf16[128,2048]{1,0:T(8,128)(2,1)S(1)} collective-permute-done((bf16[128,2048]{1,0:T(8,128)(2,1)S(1)}, bf16[128,2048]{1,0:T(8,128)(2,1)S(1)}, u32[]{:S(2)}, u32[]{:S(2)}) %collective-permute-start.21) | collective-permute-done | bytes 524320 | tf_op jit(solution)/shard_map/ppermute | solution.py:20
  284.3 6.3 %weight_grad.8.rest_0_ = bf16[2048,4096]{1,0:T(8,128)(2,1)} custom-call(bf16[512,2048]{1,0:T(8,128)(2,1)S(1)} %pad_maximum_fusion.2.left_ref, bf16[512,1792]{1,0:T(8,128)(2,1)S(1)} %get-tuple-element.198.right_ref), custom_call_target="tpu_custom_call" | custom-call | flops 3758096384 | bytes 11272192 | tf_op jit(solution)/shard_map/weight_grad/pallas_call | solution.py:514
  290.5 4.0 multiply_convert_fusion.right_ref
  294.5 6.2 %weight_grad.9.rest_0_ = bf16[2048,4096]{1,0:T(8,128)(2,1)} custom-call(bf16[512,2048]{1,0:T(8,128)(2,1)S(1)} %copy-done, bf16[512,1792]{1,0:T(8,128)(2,1)S(1)} %multiply_convert_fusion.right_ref, bf16[2048,4096]{1,0:T(8,128)(2,1)} %weight_grad.8.rest_0_), custom_call_target="tpu_custom_call", output_to_operand_aliasing={{}: (2, {})} | custom-call | flops 3758096384 | bytes 11272192 | tf_op jit(solution)/shard_map/weight_grad/pallas_call | solution.py:514
  305.8 6.4 %fusion.2 = f32[512,2048]{1,0:T(8,128)S(1)} fusion(bf16[512,1792]{1,0:T(8,128)(2,1)S(1)} %copy-done.12, bf16[2048,3584]{1,0:T(8,128)(2,1)} %all-gather.5.cloned.1.call-done), kind=kOutput, calls=%fused_computation.2 | convolution fusion | flops 3758096384 | bytes 13369344 | tf_op jit(solution)/shard_map/te,de->td/dot_general | solution.py:156
  312.3 3.9 multiply_reduce_fusion
  323.2 12.3 %collective-permute-done.27 = bf16[128,2048]{1,0:T(8,128)(2,1)S(1)} collective-permute-done((bf16[128,2048]{1,0:T(8,128)(2,1)S(1)}, bf16[128,2048]{1,0:T(8,128)(2,1)S(1)}, u32[]{:S(2)}, u32[]{:S(2)}) %collective-permute-start.27) | collective-permute-done | bytes 524320 | tf_op jit(solution)/shard_map/ppermute | solution.py:20
  338.8 11.5 %collective-permute-done.28 = bf16[128,2048]{1,0:T(8,128)(2,1)S(1)} collective-permute-done((bf16[128,2048]{1,0:T(8,128)(2,1)S(1)}, bf16[128,2048]{1,0:T(8,128)(2,1)S(1)}, u32[]{:S(2)}, u32[]{:S(2)}) %collective-permute-start.28) | collective-permute-done | bytes 524320 | tf_op jit(solution)/shard_map/ppermute | solution.py:20
  361.8 21.5 %wkv_backward.1 = (bf16[512,512]{1,0:T(8,128)(2,1)S(1)}, bf16[512,512]{1,0:T(8,128)(2,1)S(1)}, bf16[512,512]{1,0:T(8,128)(2,1)S(1)}, bf16[512,512]{1,0:T(8,128)(...) custom-call(f32[512,512]{1,0:T(8,128)S(1)} %copy-done.15, ...), custom_call_target="tpu_custom_call" | custom-call | flops 3221225472 | bytes 10485760 | tf_op jit(solution)/shard_map/wkv_backward/pallas_call | solution.py:460
  396.7 17.2 %reduce-scatter.3.cloned.1.call-done = bf16[128,4096]{1,0:T(8,128)(2,1)} async-done(((bf16[2048,4096]{1,0:T(8,128)(2,1)}), bf16[128,4096]{1,0:T(8,128)(2,1)}) %reduce-scatter.3.cloned.1.call-update) | async-done | bytes 1048592 | tf_op jit(solution)/shard_map/reduce_scatter | solution.py:88
  415.6 25.6 %mixes_back.1 = (bf16[512,2048]{1,0:T(8,128)(2,1)}, bf16[2048,512]{1,0:T(8,128)(2,1)}) custom-call(bf16[512,512]{1,0:T(8,128)(2,1)} %copy-done.4, bf16[512,512]{1,0:T(8,128)(2,1)} %copy-done.5, bf16[512,512]{1,0:T(8,128)(2,1)} %copy-done.3, bf16[512,512]{1,0:T(8,128)(2,1)} %copy-done.6, bf16[512,256]{1,0:T(8,128)(2,1)} %fusion.34.gd_ref, ...), custom_call_target="tpu_custom_call" | custom-call | flops 13421772800 | bytes 18874368 | tf_op jit(solution)/shard_map/mixes_back/pallas_call | solution.py:720
  456.0 9.8 %collective-permute-done.33 = bf16[16,2,16,512]{3,2,1,0:T(8,128)(2,1)S(1)} collective-permute-done((bf16[16,2,16,512]{3,2,1,0:T(8,128)(2,1)S(1)}, bf16[16,2,16,512]{3,2,1,0:T(8,128)(2,1)S(1)}, u32[]{:S(2)}, u32[]{:S(2)}) %collective-permute-start.33) | collective-permute-done | bytes 524320 | tf_op jit(solution)/shard_map/ppermute | solution.py:20
  469.0 8.0 %collective-permute-done.31 = bf16[128,2048]{1,0:T(8,128)(2,1)S(1)} collective-permute-done((bf16[128,2048]{1,0:T(8,128)(2,1)S(1)}, bf16[128,2048]{1,0:T(8,128)(2,1)S(1)}, u32[]{:S(2)}, u32[]{:S(2)}) %collective-permute-start.31) | collective-permute-done | bytes 524320 | tf_op jit(solution)/shard_map/ppermute | solution.py:20
  481.2 3.4 collective-permute-done.34
  485.5 5.1 all-to-all-start
  493.2 7.8 %all-to-all-done = bf16[16,16,512]{2,1,0:T(8,128)(2,1)S(1)} async-done(((bf16[16,16,512]{2,1,0:T(8,128)(2,1)}), bf16[16,16,512]{2,1,0:T(8,128)(2,1)S(1)}, u32[]{:S(2)}, u32[]{:S(2)}) %all-to-all-start) | async-done | bytes 262176 | tf_op jit(solution)/shard_map/all_to_all | solution.py:197
  503.8 3.5 collective-permute-start.37
  512.0 9.6 %collective-permute-done.35 = bf16[64,2560]{1,0:T(8,128)(2,1)S(1)} collective-permute-done((bf16[64,2560]{1,0:T(8,128)(2,1)S(1)}, bf16[64,2560]{1,0:T(8,128)(2,1)S(1)}, u32[]{:S(2)}, u32[]{:S(2)}) %collective-permute-start.35) | collective-permute-done | bytes 327712 | tf_op jit(solution)/shard_map/ppermute | solution.py:20
  (341 shorter events, 166.9 us)
Async XLA Ops:
  7.2 126.7 %all-gather.3.cloned.1.call-start = ((), (), s32[]{:S(2)}) async-start(), calls=%async_computation.3 | async-start | bytes 15597568 | tf_op jit(solution)/shard_map/all_gather | solution.py:77
  9.7 5.7 %collective-permute-start.2 = (bf16[16,1024]{1,0:T(8,128)(2,1)S(1)}, bf16[16,1024]{1,0:T(8,128)(2,1)S(1)}, u32[]{:S(2)}, u32[]{:S(2)}) collective-permute-start(bf16[16,1024]{1,0:T(8,128)(2,1)S(1)} %concatenate.69), channel_id=1, source_target_pairs={{0,1},{1,0},{2,3},{3,2},{4,5},{5,4},{6,7},{7,6},{8,9},{9,8},{10,11... | collective-permute-start | bytes 98312 | tf_op jit(solution)/shard_map/ppermute | solution.py:20
  12.0 7.4 %collective-permute-start.5 = (bf16[16,1024]{1,0:T(8,128)(2,1)S(1)}, bf16[16,1024]{1,0:T(8,128)(2,1)S(1)}, u32[]{:S(2)}, u32[]{:S(2)}) collective-permute-start(bf16[16,1024]{1,0:T(8,128)(2,1)S(1)} %concatenate.74), channel_id=1, source_target_pairs={{0,2},{1,3},{2,0},{3,1},{4,6},{5,7},{6,4},{7,5},{8,10},{9,11},{10,... | collective-permute-start | bytes 98312 | tf_op jit(solution)/shard_map/ppermute | solution.py:20
  15.4 12.4 %collective-permute-start.3 = (bf16[4,64,512]{2,1,0:T(8,128)(2,1)}, bf16[4,64,512]{2,1,0:T(8,128)(2,1)S(1)}, u32[]{:S(2)}, u32[]{:S(2)}) collective-permute-start(bf16[4,64,512]{2,1,0:T(8,128)(2,1)} %param.15), channel_id=1, source_target_pairs={{0,4},{1,5},{2,6},{3,7},{4,0},{5,1},{6,2},{7,3},{8,12},{9,13},{10,... | collective-permute-start | bytes 786440 | tf_op jit(solution)/shard_map/ppermute | solution.py:20
  19.4 8.4 %collective-permute-start.7 = (bf16[64,1024]{1,0:T(8,128)(2,1)S(1)}, bf16[64,1024]{1,0:T(8,128)(2,1)S(1)}, u32[]{:S(2)}, u32[]{:S(2)}) collective-permute-start(bf16[64,1024]{1,0:T(8,128)(2,1)S(1)} %bitcast.361), channel_id=1, source_target_pairs={{0,4},{1,5},{2,6},{3,7},{4,0},{5,1},{6,2},{7,3},{8,12},{9,13},{10,... | collective-permute-start | bytes 393224 | tf_op jit(solution)/shard_map/ppermute | solution.py:20
  20.2 9.0 %collective-permute-start.4 = (bf16[512,64]{0,1:T(8,128)(2,1)}, bf16[512,64]{0,1:T(8,128)(2,1)S(1)}, u32[]{:S(2)}, u32[]{:S(2)}) collective-permute-start(bf16[512,64]{0,1:T(8,128)(2,1)} %param.16), channel_id=1, source_target_pairs={{0,4},{1,5},{2,6},{3,7},{4,0},{5,1},{6,2},{7,3},{8,12},{9,13},{10,... | collective-permute-start | bytes 196616 | tf_op jit(solution)/shard_map/ppermute | solution.py:20
  30.3 206.2 %all-gather.5.cloned.1.call-start = ((), (), s32[]{:S(2)}) async-start(), calls=%async_computation.4 | async-start | bytes 15597568 | tf_op jit(solution)/shard_map/all_gather | solution.py:77
  30.3 7.7 %collective-permute-start.16 = (bf16[1792,64]{0,1:T(8,128)(2,1)S(1)}, bf16[1792,64]{0,1:T(8,128)(2,1)S(1)}, u32[]{:S(2)}, u32[]{:S(2)}) collective-permute-start(bf16[1792,64]{0,1:T(8,128)(2,1)S(1)} %copy-done.51), channel_id=1, source_target_pairs={{0,4},{1,5},{2,6},{3,7},{4,0},{5,1},{6,2},{7,3},{8,12},{9,13},{10,... | collective-permute-start | bytes 688136 | tf_op jit(solution)/shard_map/ppermute | solution.py:20
  33.3 9.6 %collective-permute-start.15 = (bf16[64,1792]{1,0:T(8,128)(2,1)S(1)}, bf16[64,1792]{1,0:T(8,128)(2,1)S(1)}, u32[]{:S(2)}, u32[]{:S(2)}) collective-permute-start(bf16[64,1792]{1,0:T(8,128)(2,1)S(1)} %copy-done.52), channel_id=1, source_target_pairs={{0,4},{1,5},{2,6},{3,7},{4,0},{5,1},{6,2},{7,3},{8,12},{9,13},{10,... | collective-permute-start | bytes 688136 | tf_op jit(solution)/shard_map/ppermute | solution.py:20
  44.1 369.7 %reduce-scatter.3.cloned.1.call-start = ((), (), s32[]{:S(2)}) async-start(), calls=%async_computation.5 | async-start | bytes 17825792 | tf_op jit(solution)/shard_map/reduce_scatter | solution.py:88
  44.2 11.7 %collective-permute-start = (bf16[128,2048]{1,0:T(8,128)(2,1)S(1)}, bf16[128,2048]{1,0:T(8,128)(2,1)S(1)}, u32[]{:S(2)}, u32[]{:S(2)}) collective-permute-start(bf16[128,2048]{1,0:T(8,128)(2,1)S(1)} %copy-done.35), channel_id=1, source_target_pairs={{0,2},{1,3},{2,0},{3,1},{4,6},{5,7},{6,4},{7,5},{8,10},{9,11},{10,... | collective-permute-start | bytes 1572872 | tf_op jit(solution)/shard_map/ppermute | solution.py:20
  57.0 5.4 %collective-permute-start.1 = (bf16[2,128,2048]{2,1,0:T(8,128)(2,1)}, bf16[2,128,2048]{2,1,0:T(8,128)(2,1)S(1)}, u32[]{:S(2)}, u32[]{:S(2)}) collective-permute-start(bf16[2,128,2048]{2,1,0:T(8,128)(2,1)} %pad_maximum_fusion.4), channel_id=1, source_target_pairs={{0,1},{1,0},{2,3},{3,2},{4,5},{5,4},{6,7},{7,6},{8,9},{9,8},{10,11... | collective-permute-start | bytes 3145736 | tf_op jit(solution)/shard_map/ppermute | solution.py:20
  183.1 13.3 %collective-permute-start.9 = (bf16[128,2048]{1,0:T(8,128)(2,1)S(1)}, bf16[128,2048]{1,0:T(8,128)(2,1)S(1)}, u32[]{:S(2)}, u32[]{:S(2)}) collective-permute-start(bf16[128,2048]{1,0:T(8,128)(2,1)S(1)} %fusion.53), channel_id=1, source_target_pairs={{0,2},{1,3},{2,0},{3,1},{4,6},{5,7},{6,4},{7,5},{8,10},{9,11},{10,... | collective-permute-start | bytes 1572872 | tf_op jit(solution)/shard_map/ppermute | solution.py:20
  197.9 12.9 %collective-permute-start.10 = (bf16[128,2048]{1,0:T(8,128)(2,1)S(1)}, bf16[128,2048]{1,0:T(8,128)(2,1)S(1)}, u32[]{:S(2)}, u32[]{:S(2)}) collective-permute-start(bf16[128,2048]{1,0:T(8,128)(2,1)S(1)} %add_convert_fusion.4), channel_id=1, source_target_pairs={{0,2},{1,3},{2,0},{3,1},{4,6},{5,7},{6,4},{7,5},{8,10},{9,11},{10,... | collective-permute-start | bytes 1572872 | tf_op jit(solution)/shard_map/ppermute | solution.py:20
  224.8 7.3 %collective-permute-start.14 = (bf16[128,512]{1,0:T(8,128)(2,1)S(1)}, bf16[128,512]{1,0:T(8,128)(2,1)S(1)}, u32[]{:S(2)}, u32[]{:S(2)}) collective-permute-start(bf16[128,512]{1,0:T(8,128)(2,1)S(1)} %get-tuple-element.177), channel_id=1, source_target_pairs={{0,3},{1,2},{2,1},{3,0},{4,7},{5,6},{6,5},{7,4},{8,11},{9,10},{10,... | collective-permute-start | bytes 393224 | tf_op jit(solution)/shard_map/ppermute | solution.py:20
  249.9 7.5 %collective-permute-start.20 = (bf16[128,1024]{1,0:T(8,128)(2,1)S(1)}, bf16[128,1024]{1,0:T(8,128)(2,1)S(1)}, u32[]{:S(2)}, u32[]{:S(2)}) collective-permute-start(bf16[128,1024]{1,0:T(8,128)(2,1)S(1)} %fusion.60), channel_id=1, source_target_pairs={{0,2},{1,3},{2,0},{3,1},{4,6},{5,7},{6,4},{7,5},{8,10},{9,11},{10,... | collective-permute-start | bytes 786440 | tf_op jit(solution)/shard_map/ppermute | solution.py:20
  251.8 11.2 %collective-permute-start.18 = (bf16[128,1024]{1,0:T(8,128)(2,1)S(1)}, bf16[128,1024]{1,0:T(8,128)(2,1)S(1)}, u32[]{:S(2)}, u32[]{:S(2)}) collective-permute-start(bf16[128,1024]{1,0:T(8,128)(2,1)S(1)} %fusion.59), channel_id=1, source_target_pairs={{0,2},{1,3},{2,0},{3,1},{4,6},{5,7},{6,4},{7,5},{8,10},{9,11},{10,... | collective-permute-start | bytes 786440 | tf_op jit(solution)/shard_map/ppermute | solution.py:20
  264.5 12.2 %collective-permute-start.21 = (bf16[128,2048]{1,0:T(8,128)(2,1)S(1)}, bf16[128,2048]{1,0:T(8,128)(2,1)S(1)}, u32[]{:S(2)}, u32[]{:S(2)}) collective-permute-start(bf16[128,2048]{1,0:T(8,128)(2,1)S(1)} %get-tuple-element.156), channel_id=1, source_target_pairs={{0,2},{1,3},{2,0},{3,1},{4,6},{5,7},{6,4},{7,5},{8,10},{9,11},{10,... | collective-permute-start | bytes 1572872 | tf_op jit(solution)/shard_map/ppermute | solution.py:20
  282.0 18.8 %collective-permute-start.23 = (bf16[128,512]{1,0:T(8,128)(2,1)S(1)}, bf16[128,512]{1,0:T(8,128)(2,1)S(1)}, u32[]{:S(2)}, u32[]{:S(2)}) collective-permute-start(bf16[128,512]{1,0:T(8,128)(2,1)S(1)} %get-tuple-element.176), channel_id=1, source_target_pairs={{0,1},{1,0},{2,3},{3,2},{4,5},{5,4},{6,7},{7,6},{8,9},{9,8},{10,11... | collective-permute-start | bytes 393224 | tf_op jit(solution)/shard_map/ppermute | solution.py:20
  282.5 18.3 %collective-permute-start.24 = (bf16[128,512]{1,0:T(8,128)(2,1)S(1)}, bf16[128,512]{1,0:T(8,128)(2,1)S(1)}, u32[]{:S(2)}, u32[]{:S(2)}) collective-permute-start(bf16[128,512]{1,0:T(8,128)(2,1)S(1)} %get-tuple-element.175), channel_id=1, source_target_pairs={{0,2},{1,3},{2,0},{3,1},{4,6},{5,7},{6,4},{7,5},{8,10},{9,11},{10,... | collective-permute-start | bytes 393224 | tf_op jit(solution)/shard_map/ppermute | solution.py:20
  283.7 17.1 %collective-permute-start.25 = (bf16[128,512]{1,0:T(8,128)(2,1)S(1)}, bf16[128,512]{1,0:T(8,128)(2,1)S(1)}, u32[]{:S(2)}, u32[]{:S(2)}) collective-permute-start(bf16[128,512]{1,0:T(8,128)(2,1)S(1)} %get-tuple-element.174), channel_id=1, source_target_pairs={{0,3},{1,2},{2,1},{3,0},{4,7},{5,6},{6,5},{7,4},{8,11},{9,10},{10,... | collective-permute-start | bytes 393224 | tf_op jit(solution)/shard_map/ppermute | solution.py:20
  304.3 205.7 %reduce-scatter.5.cloned.1.call-start = ((), (), s32[]{:S(2)}) async-start(), calls=%async_computation.6 | async-start | bytes 11141120 | tf_op jit(solution)/shard_map/reduce_scatter | solution.py:88
  321.9 13.6 %collective-permute-start.27 = (bf16[128,2048]{1,0:T(8,128)(2,1)S(1)}, bf16[128,2048]{1,0:T(8,128)(2,1)S(1)}, u32[]{:S(2)}, u32[]{:S(2)}) collective-permute-start(bf16[128,2048]{1,0:T(8,128)(2,1)S(1)} %fusion.54), channel_id=1, source_target_pairs={{0,2},{1,3},{2,0},{3,1},{4,6},{5,7},{6,4},{7,5},{8,10},{9,11},{10,... | collective-permute-start | bytes 1572872 | tf_op jit(solution)/shard_map/ppermute | solution.py:20
  337.6 12.7 %collective-permute-start.28 = (bf16[128,2048]{1,0:T(8,128)(2,1)S(1)}, bf16[128,2048]{1,0:T(8,128)(2,1)S(1)}, u32[]{:S(2)}, u32[]{:S(2)}) collective-permute-start(bf16[128,2048]{1,0:T(8,128)(2,1)S(1)} %get-tuple-element.124), channel_id=1, source_target_pairs={{0,2},{1,3},{2,0},{3,1},{4,6},{5,7},{6,4},{7,5},{8,10},{9,11},{10,... | collective-permute-start | bytes 1572872 | tf_op jit(solution)/shard_map/ppermute | solution.py:20
  448.2 5.6 %collective-permute-start.30 = (bf16[2,128,2048]{2,1,0:T(8,128)(2,1)}, bf16[2,128,2048]{2,1,0:T(8,128)(2,1)}, u32[]{:S(2)}, u32[]{:S(2)}) collective-permute-start(bf16[2,128,2048]{2,1,0:T(8,128)(2,1)} %select_bitcast_fusion), channel_id=1, source_target_pairs={{0,1},{1,0},{2,3},{3,2},{4,5},{5,4},{6,7},{7,6},{8,9},{9,8},{10,11... | collective-permute-start | bytes 3145736 | tf_op jit(solution)/shard_map/ppermute | solution.py:20
  452.4 13.4 %collective-permute-start.33 = (bf16[16,2,16,512]{3,2,1,0:T(8,128)(2,1)S(1)}, bf16[16,2,16,512]{3,2,1,0:T(8,128)(2,1)S(1)}, u32[]{:S(2)}, u32[]{:S(2)}) collective-permute-start(bf16[16,2,16,512]{3,2,1,0:T(8,128)(2,1)S(1)} %fusion.56), channel_id=1, source_target_pairs={{0,2},{1,3},{2,0},{3,1},{4,6},{5,7},{6,4},{7,5},{8,10},{9,11},{10,... | collective-permute-start | bytes 1572872 | tf_op jit(solution)/shard_map/ppermute | solution.py:20
  455.7 21.4 %collective-permute-start.31 = (bf16[128,2048]{1,0:T(8,128)(2,1)S(1)}, bf16[128,2048]{1,0:T(8,128)(2,1)S(1)}, u32[]{:S(2)}, u32[]{:S(2)}) collective-permute-start(bf16[128,2048]{1,0:T(8,128)(2,1)S(1)} %fusion.55), channel_id=1, source_target_pairs={{0,2},{1,3},{2,0},{3,1},{4,6},{5,7},{6,4},{7,5},{8,10},{9,11},{10,... | collective-permute-start | bytes 1572872 | tf_op jit(solution)/shard_map/ppermute | solution.py:20
  466.2 18.4 %collective-permute-start.34 = (bf16[16,16,512]{2,1,0:T(8,128)(2,1)S(1)}, bf16[16,16,512]{2,1,0:T(8,128)(2,1)S(1)}, u32[]{:S(2)}, u32[]{:S(2)}) collective-permute-start(bf16[16,16,512]{2,1,0:T(8,128)(2,1)S(1)} %fusion.61), channel_id=1, source_target_pairs={{0,4},{1,5},{2,6},{3,7},{4,0},{5,1},{6,2},{7,3},{8,12},{9,13},{10,... | collective-permute-start | bytes 786440 | tf_op jit(solution)/shard_map/ppermute | solution.py:20
  478.5 24.0 %collective-permute-start.36 = (bf16[64,4096]{1,0:T(8,128)(2,1)S(1)}, bf16[64,4096]{1,0:T(8,128)(2,1)}, u32[]{:S(2)}, u32[]{:S(2)}) collective-permute-start(bf16[64,4096]{1,0:T(8,128)(2,1)S(1)} %broadcast_select_fusion), channel_id=1, source_target_pairs={{0,4},{1,5},{2,6},{3,7},{4,0},{5,1},{6,2},{7,3},{8,12},{9,13},{10,... | collective-permute-start | bytes 1572872 | tf_op jit(solution)/shard_map/ppermute | solution.py:20
  485.5 15.6 %all-to-all-start = ((bf16[16,16,512]{2,1,0:T(8,128)(2,1)}), bf16[16,16,512]{2,1,0:T(8,128)(2,1)S(1)}, u32[]{:S(2)}, u32[]{:S(2)}) async-start(bf16[16,16,512]{2,1,0:T(8,128)(2,1)} %fusion.58), calls=%async_computation.1 | async-start | bytes 524288 | tf_op jit(solution)/shard_map/all_to_all | solution.py:197
  503.8 8.2 %collective-permute-start.37 = (f32[16,512]{1,0:T(8,128)S(1)}, f32[16,512]{1,0:T(8,128)S(1)}, u32[]{:S(2)}, u32[]{:S(2)}) collective-permute-start(f32[16,512]{1,0:T(8,128)S(1)} %get-tuple-element.185), channel_id=1, source_target_pairs={{0,1},{1,0},{2,3},{3,2},{4,5},{5,4},{6,7},{7,6},{8,9},{9,8},{10,11... | collective-permute-start | bytes 98312 | tf_op jit(solution)/shard_map/ppermute | solution.py:20
  511.1 10.5 %collective-permute-start.35 = (bf16[64,2560]{1,0:T(8,128)(2,1)S(1)}, bf16[64,2560]{1,0:T(8,128)(2,1)S(1)}, u32[]{:S(2)}, u32[]{:S(2)}) collective-permute-start(bf16[64,2560]{1,0:T(8,128)(2,1)S(1)} %broadcast_select_fusion.27), channel_id=1, source_target_pairs={{0,4},{1,5},{2,6},{3,7},{4,0},{5,1},{6,2},{7,3},{8,12},{9,13},{10,... | collective-permute-start | bytes 983048 | tf_op jit(solution)/shard_map/ppermute | solution.py:20
  (74 other events, 831.9 us)
Sparse Core Ops, SparseCore 0:
  30.4 103.4 all-gather.2
  136.0 100.3 all-gather.4
  304.4 109.3 reduce-scatter.2
  417.1 92.2 reduce-scatter.4

commit v4 on v3

--- a/solution.py
+++ b/solution.py
@@ -41,28 +41,53 @@
     return jnp.where(second, other, own), jnp.where(second, own, other)
 
 
-def span_gather(block):
+def span_gather(block, axis=0):
     place = lax.axis_index("span")
     low, core = place // 2, place % 2
     p0, p1 = in_order(block, swap_low(block), low == 1)
     q = swap_core(jnp.stack([p0, p1]))
     a0, a1 = in_order(p0, q[0], core == 1)
     b0, b1 = in_order(p1, q[1], core == 1)
-    return jnp.concatenate([a0, a1, b0, b1], axis=0)
+    return jnp.concatenate([a0, a1, b0, b1], axis=axis)
+
+
+def core_reduce(part):
+    core = lax.axis_index("span") % 2
+    half = part.shape[1] // 2
+    keep, send = in_order(part[:, :half], part[:, half:], core == 1)
+    return keep.astype(jnp.float32) + swap_core(send.astype(jnp.bfloat16)).astype(jnp.float32)
+
+
+def over_cores(part):
+    core = lax.axis_index("span") % 2
+    b = part.reshape(2, 2, part.shape[0] // 4, part.shape[1])
+    keep, send = in_order(b[:, 0], b[:, 1], core == 1)
+    return keep.astype(jnp.float32) + swap_core(send.astype(jnp.bfloat16)).astype(jnp.float32)
+
+
+def over_low(both):
+    low = lax.axis_index("span") // 2
+    mine, send = in_order(both[0], both[1], low == 1)
+    return mine + swap_low(send.astype(jnp.bfloat16)).astype(jnp.float32)
 
 
 def span_reduce(part):
-    place = lax.axis_index("span")
-    low, core = place // 2, place % 2
-    rows = part.shape[0] // 4
-    b = part.reshape(2, 2, rows, part.shape[1])
-    keep = jnp.where(core == 1, b[:, 1], b[:, 0])
-    send = jnp.where(core == 1, b[:, 0], b[:, 1]).astype(jnp.bfloat16)
-    got = swap_core(send)
-    both = keep.astype(jnp.float32) + got.astype(jnp.float32)
-    mine = jnp.where(low == 1, both[1], both[0])
-    send = jnp.where(low == 1, both[0], both[1]).astype(jnp.bfloat16)
-    return mine + swap_low(send).astype(jnp.float32)
+    return over_low(over_cores(part))
+
+
+def fill_pair(rows):
+    half = rows.shape[2] // 2
+    return jnp.concatenate([rows[:, :, :half], rows[:, :, half:]], axis=1)
+
+
+def from_pair(pairs):
+    half = pairs.shape[1] // 2
+    return jnp.concatenate([pairs[:, :half], pairs[:, half:]], axis=2)
+
+
+def other_plane(rows, got):
+    high = lax.axis_index("seg") % 2
+    return jnp.stack(in_order(rows, got, high == 1), axis=1).reshape(-1, rows.shape[2])
 
 
 def both_planes(laid, *blocks):
@@ -180,7 +205,7 @@
     return jnp.concatenate([values[1:], jnp.zeros_like(values[:1])], axis=0)
 
 
-def reduce_small(part, pair):
+def reduce_small(part, both, pair):
     place, high = lax.axis_index("span"), lax.axis_index("seg") % 2
     planes = lax.axis_size("seg") // 2
     width = part.shape[1]
@@ -192,18 +217,18 @@
         return mine.astype(jnp.float32) + move(send.astype(jnp.bfloat16)).astype(jnp.float32)
 
     b = summed(summed(b, 3, place % 2, swap_core), 2, place // 2, swap_low)
+    b, both = lax.optimization_barrier((b, both))
+    rows = over_low(both)
+    b = summed(b, 1, high, swap_high).astype(jnp.bfloat16)
     b, pair = lax.optimization_barrier((b, pair))
     finished = finish_scatter(*plane_halves(pair))
     arrived = lax.all_to_all(
-        summed(b, 1, high, swap_high).astype(jnp.bfloat16),
-        "seg",
-        split_axis=0,
-        concat_axis=0,
-        tiled=True,
-        axis_index_groups=plane_groups(),
-    )
-    return arrived.astype(jnp.float32).sum(axis=0), finished
-
+        b, "seg", split_axis=0, concat_axis=0, tiled=True, axis_index_groups=plane_groups()
+    )
+    return arrived.astype(jnp.float32).sum(axis=0), rows, finished
+
+
+SOON = pl.CostEstimate(flops=2**20, bytes_accessed=2**16, transcendentals=0)
 
 CHUNK = 64
 PACK = 256
@@ -370,9 +395,7 @@
         compiler_params=pltpu.CompilerParams(
             dimension_semantics=("arbitrary",), vmem_limit_bytes=32 * 2**20
         ),
-        cost_estimate=pl.CostEstimate(
-            flops=2 * 9 * PACK * rows * columns, bytes_accessed=26 * rows * columns, transcendentals=8 * rows * columns
-        ),
+        cost_estimate=SOON,
         name="wkv_forward",
     )(r, k, v, gate, low, up, par, first)
 
@@ -479,9 +502,7 @@
         compiler_params=pltpu.CompilerParams(
             dimension_semantics=("arbitrary",), vmem_limit_bytes=32 * 2**20
         ),
-        cost_estimate=pl.CostEstimate(
-            flops=2 * 24 * PACK * rows * columns, bytes_accessed=40 * rows * columns, transcendentals=12 * rows * columns
-        ),
+        cost_estimate=SOON,
         name="wkv_backward",
     )(r, k, v, gate, low, up, par, wkv, held, g_mixed)
 
@@ -521,13 +542,32 @@
         compiler_params=pltpu.CompilerParams(
             dimension_semantics=("arbitrary",), vmem_limit_bytes=32 * 2**20
         ),
-        cost_estimate=pl.CostEstimate(
-            flops=2 * rows * width * columns,
-            bytes_accessed=2 * (rows * (width + columns) + width * columns),
-            transcendentals=0,
-        ),
+        cost_estimate=SOON,
         name="weight_grad",
     )(*operands)
+
+
+def copy_kernel(block_ref, into_ref, out_ref):
+    out_ref[...] = block_ref[...]
+
+
+def copy_into(block, at, into):
+    rows, columns = block.shape
+    shift = at // columns
+    return pl.pallas_call(
+        copy_kernel,
+        grid=(rows // GRAD_ROWS,),
+        in_specs=[
+            pl.BlockSpec((GRAD_ROWS, columns), lambda i: (i, 0)),
+            pl.BlockSpec(memory_space=pltpu.HBM),
+        ],
+        out_specs=pl.BlockSpec((GRAD_ROWS, columns), lambda i: (i, shift)),
+        out_shape=pltpu.HBM(into.shape, into.dtype),
+        input_output_aliases={1: 0},
+        compiler_params=pltpu.CompilerParams(dimension_semantics=("arbitrary",)),
+        cost_estimate=SOON,
+        name="copy_into",
+    )(block, into)
 
 
 LOW = 256
@@ -535,6 +575,25 @@
 LANES = SHIFT_LANES + 64
 
 TILE = 512
+
+
+def vectors_kernel(up_ref, out_ref):
+    turned = up_ref[...].astype(jnp.float32).T
+    out_ref[...] = turned[LANES : LANES + 16]
+
+
+def turn_vectors(first, up_at):
+    width = first.shape[0]
+    return pl.pallas_call(
+        vectors_kernel,
+        grid=(width // TILE,),
+        in_specs=[pl.BlockSpec((TILE, LOW), lambda n: (n, up_at // LOW))],
+        out_specs=pl.BlockSpec((16, TILE), lambda n: (0, n)),
+        out_shape=jax.ShapeDtypeStruct((16, width), jnp.float32),
+        compiler_params=pltpu.CompilerParams(dimension_semantics=("arbitrary",)),
+        cost_estimate=SOON,
+        name="turn_vectors",
+    )(first)
 
 
 def lane_group(shape):
@@ -618,13 +677,9 @@
         + [kept(own, jnp.float32)] * 4,
         scratch_shapes=[pltpu.VMEM((rows, LOW), jnp.float32), pltpu.VMEM((5, rows, LOW), jnp.bfloat16)],
         compiler_params=pltpu.CompilerParams(
-            dimension_semantics=("arbitrary", "arbitrary"), vmem_limit_bytes=48 * 2**20
+            dimension_semantics=("arbitrary", "arbitrary"), vmem_limit_bytes=54 * 2**20
         ),
-        cost_estimate=pl.CostEstimate(
-            flops=2 * rows * width * (4 * own + 7 * LOW),
-            bytes_accessed=2 * width * 4 * own + 22 * rows * width,
-            transcendentals=0,
-        ),
+        cost_estimate=SOON,
         name="mixes_forward",
     )(unit, first, first, first, vec)
 
@@ -750,11 +805,7 @@
         compiler_params=pltpu.CompilerParams(
             dimension_semantics=("arbitrary", "arbitrary"), vmem_limit_bytes=56 * 2**20
         ),
-        cost_estimate=pl.CostEstimate(
-            flops=2 * rows * width * (4 * own + 17 * LOW),
-            bytes_accessed=2 * width * 4 * own + 10 * rows * width,
-            transcendentals=0,
-        ),
+        cost_estimate=SOON,
         name="mixes_back",
     )(g_key, g_val, g_recept, g_gate, g_decay, first, first, first, vec, squash, normed, mix, sums)
 
@@ -773,6 +824,7 @@
     channel_value_weight,
 ):
     token_rows, width = inputs.shape
+    seg_count = lax.axis_size("seg")
     own_width = time_mix_weight.shape[2]
     hidden = channel_key_weight.shape[1]
     local_heads = own_width // GROUP_DIMENSION
@@ -780,6 +832,7 @@
     position = lax.axis_index("span") * token_rows
 
     x_seg = span_gather(inputs).astype(jnp.float32)
+    grad_columns = split_columns(cotangent).astype(jnp.float32)
     def blank(count):
         return jnp.zeros((token_rows // 8, count), jnp.bfloat16)
 
@@ -787,16 +840,25 @@
         [rank_down_weight, blank(LOW - LANES), rank_up_weight.T, vectors.T, blank(LOW - LANES - 16)], axis=1
     )
     early, span_rows = gather_and_split(small_rows, channel_receptance_weight)
-    _, time_mix_weight, output_weight = lax.optimization_barrier((early, time_mix_weight, output_weight))
-    weights = both_planes(
-        lambda proj, out: [proj[g] for g in range(4)] + [out.T], time_mix_weight, output_weight
-    )
-    first = plane_gather(jnp.concatenate([weights, both_planes(lambda rows: [rows], span_rows)], axis=1))
-    second = plane_gather(
-        both_planes(lambda key, value: [key, value.T], channel_key_weight, channel_value_weight)
-    )
-    low_at = 6 * own_width
-    out_w, recept_w = first[:, 4 * own_width : 5 * own_width], first[:, 5 * own_width : low_at]
+    _, time_mix_weight = lax.optimization_barrier((early, time_mix_weight))
+    weights = both_planes(lambda proj: [proj[g] for g in range(4)], time_mix_weight)
+    small_pair = both_planes(lambda rows: [rows], span_rows[:, own_width:])
+    late_pairs = [fill_pair(rows[None])[0] for rows in (output_weight.T, span_rows[:, :own_width])]
+    first = plane_gather(jnp.concatenate([weights, small_pair] + late_pairs, axis=1))
+    _, unit_seg, _ = norm_rows(x_seg, 1.0, 0.0)
+    second_pair = both_planes(lambda key, value: [key, value.T], channel_key_weight, channel_value_weight)
+    second_pair, unit_seg, grad_columns = lax.optimization_barrier((second_pair, unit_seg, grad_columns))
+    second = plane_gather(second_pair)
+    low_at = 4 * own_width
+    late_at = low_at + 2 * LOW
+
+    def late_rows(at):
+        pairs = first[:, at : at + own_width // 2].reshape(-1, 2 * (width // seg_count), own_width // 2)
+        return from_pair(pairs)
+
+    out_half, recept_half = late_rows(late_at), late_rows(late_at + own_width // 2)
+    late_got = swap_high(jnp.concatenate([out_half, recept_half], axis=2))
+    out_got, recept_got = late_got[:, :, :own_width], late_got[:, :, own_width:]
     up_at = low_at + LOW
     vec = first[:, up_at + LANES : up_at + LANES + 16].T.astype(jnp.float32)
 
@@ -807,7 +869,6 @@
         return lax.dynamic_slice_in_dim(values, position, token_rows, 0)
 
     x_in = inputs.astype(jnp.float32)
-    _, unit_seg, _ = norm_rows(x_seg, 1.0, 0.0)
     *mixes, normed, squash, recept, key_proj, val_proj, gate_pre = mixes_forward(
         unit_seg, first, low_at, vec, own_width
     )
@@ -817,8 +878,10 @@
     up_own = lax.dynamic_slice(first, (col_start, up_at), (own_width, LOW))
     head_vec = jnp.concatenate([own_cols(vec[8:12]), jnp.zeros((4, own_width), jnp.float32)], axis=0)
     first_state = jnp.transpose(states[0], (2, 0, 1)).reshape(GROUP_DIMENSION, own_width)
+    out_w = other_plane(out_half, out_got)
     heads_in = (recept, key_proj, val_proj, gate_pre, decay_low, up_own, head_vec)
     mixed, wkv, held = wkv_forward(*heads_in, first_state)
+    recept_w = other_plane(recept_half, recept_got)
     resid = x_in + span_reduce(backward_product(mixed, out_w).astype(jnp.bfloat16))
 
     normed_two, unit_two, rstd_two = norm_rows(resid, vec[12], vec[13])
@@ -826,50 +889,55 @@
     shifted_two = prior_rows(n2) - n2
     key_in = (n2 + shifted_two * vec[14]).astype(jnp.bfloat16)
     rec_in = (n2 + shifted_two * vec[15]).astype(jnp.bfloat16)
-    rec_part = product_lower(rec_in, recept_w).astype(jnp.bfloat16)
-    rec_pre, second = lax.optimization_barrier((join_columns(rec_part), second))
+    rec_gate = jax.nn.sigmoid(product_lower(rec_in, recept_w))
+    g_value = (grad_columns * rec_gate).astype(jnp.bfloat16)
+    g_value, second = lax.optimization_barrier((g_value, second))
+    g_value_all = span_gather(g_value, 1)
     key_w, value_w = second[:, :hidden], second[:, hidden:]
     hidden_two = product_lower(key_in, key_w)
     active = jax.nn.relu(hidden_two)
     squared = (active * active).astype(jnp.bfloat16)
     active = active.astype(jnp.bfloat16)
-    half = width // 2
-    value_out = jnp.concatenate(
-        [
-            span_reduce(backward_product(squared, value_w[at : at + half]).astype(jnp.bfloat16))
-            for at in (0, half)
-        ],
-        axis=1,
-    )
-    rec_gate = jax.nn.sigmoid(rec_pre.astype(jnp.float32))
-    output = (resid + rec_gate * value_out).astype(jnp.bfloat16)
-
-    grad_out = cotangent.astype(jnp.float32)
-    g_value = (grad_out * rec_gate).astype(jnp.bfloat16)
-    g_rec = (grad_out * value_out * rec_gate * (1.0 - rec_gate)).astype(jnp.bfloat16)
-    g_value_all = span_gather(g_value)
-    g_value_all, g_rec = lax.optimization_barrier((g_value_all, g_rec))
-    g_rec_own = split_columns(g_rec)
-    cm_total = 2 * hidden + own_width
+
+    low = lax.axis_index("span") // 2
+
+    def value_columns(which):
+        weights = lax.dynamic_slice(second, (which * (width // 2), hidden), (width // 2, hidden))
+        return core_reduce(backward_product(squared, weights).astype(jnp.bfloat16))
+
+    far, near = value_columns(1 - low), value_columns(low)
+    far, g_value_all = lax.optimization_barrier((far.astype(jnp.bfloat16), g_value_all))
+    far = swap_low(far)
+    cm_total = 2 * hidden
+    g_hid = (product_lower(g_value_all, value_w) * 2.0 * active.astype(jnp.float32)).astype(jnp.bfloat16)
+    g_value_all, g_hid = lax.optimization_barrier((g_value_all, g_hid))
     cm_part = grad_into(g_value_all, squared, cm_total, hidden)
-    g_value_all, cm_part = lax.optimization_barrier((g_value_all, cm_part))
-    g_hid = (product_lower(g_value_all, value_w) * 2.0 * active.astype(jnp.float32)).astype(jnp.bfloat16)
+    far, near, cm_part = lax.optimization_barrier((far, near, cm_part))
     cm_part = grad_into(key_in, g_hid, cm_total, 0, cm_part)
-    cm_part = grad_into(rec_in, g_rec_own, cm_total, 2 * hidden, cm_part)
-    cm_part, g_hid, g_rec_own = lax.optimization_barrier((cm_part, g_hid, g_rec_own))
+    cm_part, g_hid = lax.optimization_barrier((cm_part, g_hid))
     cm_pair = plane_scatter(cm_part)
+    value_out = near + far.astype(jnp.float32)
+    gated = (rec_gate * value_out).astype(jnp.bfloat16)
+    g_rec = (grad_columns * value_out * rec_gate * (1.0 - rec_gate)).astype(jnp.bfloat16)
     g_key_in = backward_product(g_hid, key_w)
-    g_rec_in = backward_product(g_rec_own, recept_w)
+    g_rec_in = backward_product(g_rec, recept_w)
     vec_fourteen = jnp.sum(g_key_in * shifted_two, axis=0)
     vec_fifteen = jnp.sum(g_rec_in * shifted_two, axis=0)
     g_shift_two = g_key_in * vec[14] + g_rec_in * vec[15]
     g_n2_part = g_key_in + g_rec_in - g_shift_two + next_rows(g_shift_two)
     g_n2 = span_reduce(g_n2_part.astype(jnp.bfloat16))
+    rec_part = grad_into(rec_in, g_rec, own_width, 0)
+    g_n2, rec_part = lax.optimization_barrier((g_n2, rec_part))
     vec_twelve = jnp.sum(g_n2 * unit_two, axis=0)
     vec_thirteen = jnp.sum(g_n2, axis=0)
-    g_resid = grad_out + norm_back(g_n2, unit_two, rstd_two, vec[12])
+    g_resid = cotangent.astype(jnp.float32) + norm_back(g_n2, unit_two, rstd_two, vec[12])
 
     g_att = span_gather(g_resid.astype(jnp.bfloat16))
+    rec_part = rec_part.reshape(seg_count // 2, 2, width // seg_count, own_width)
+    rec_mine, rec_send = in_order(rec_part[:, 0], rec_part[:, 1], lax.axis_index("seg") % 2 == 1)
+    g_att, gated, rec_send = lax.optimization_barrier((g_att, gated, rec_send))
+    rec_got = swap_high(rec_send)
+    gated_rows = join_columns(gated)
     g_mixed = product_lower(g_att, out_w)
     g_recept, g_key, g_val, g_gate, g_ww, head_sums, g_first = wkv_backward(
         *heads_in, wkv, held, g_mixed
@@ -877,11 +945,17 @@
     state_grad = jnp.transpose(
         g_first.reshape(GROUP_DIMENSION, local_heads, GROUP_DIMENSION), (1, 2, 0)
     )[None]
-    tm_total = 5 * own_width
+    tm_total = 5 * own_width + own_width // 2
     tm_part = grad_into(g_att, mixed, tm_total, 0)
+    rec_got, g_recept = lax.optimization_barrier((rec_got, g_recept))
+    rec_sum = (rec_mine.astype(jnp.float32) + rec_got.astype(jnp.float32)).astype(jnp.bfloat16)
+    tm_part = lax.dynamic_update_slice(
+        tm_part, fill_pair(rec_sum).reshape(width, own_width // 2), (0, 5 * own_width)
+    )
     for at, mix, grad in ((1, 3, g_recept), (2, 1, g_key), (3, 2, g_val), (4, 4, g_gate)):
         tm_part = grad_into(mixes[mix], grad, tm_total, at * own_width, tm_part)
-    tm_part, cm_pair = lax.optimization_barrier((tm_part, cm_pair))
+    tm_part, cm_pair, gated_rows = lax.optimization_barrier((tm_part, cm_pair, gated_rows))
+    output = (resid + gated_rows.astype(jnp.float32)).astype(jnp.bfloat16)
     tm_pair = plane_scatter(tm_part)
     g_key, g_ww, cm_pair = lax.optimization_barrier((g_key, g_ww, cm_pair))
 
@@ -903,19 +977,19 @@
     small_part = lax.dynamic_update_slice(
         small_part, (own_part.astype(jnp.float32) + up_decay_grad).astype(jnp.bfloat16), (col_start, LOW)
     )
-    small, cm_grad = reduce_small(small_part, cm_pair)
-    tm_grad = finish_scatter(*plane_halves(tm_pair))
-    g_n1 = span_reduce(g_normed)
+    small, g_n1, cm_grad = reduce_small(small_part, over_cores(g_normed), cm_pair)
+    rec_own = from_pair(tm_pair[None, :, 5 * own_width :])[0]
+    tm_grad = finish_scatter(*plane_halves(tm_pair[:, : 5 * own_width]))
     _, unit_own, rstd_own = norm_rows(x_in, vec[0], vec[1])
     x_grad = g_resid + norm_back(g_n1, unit_own, rstd_own, vec[0])
     down_grad = small[:, :LANES]
     up_grad = small[:, LOW : LOW + LANES].T
     vec_grad = small[:, LOW + LANES : LOW + LANES + 16].T
-    rec_grad = join_columns(cm_grad[:, 2 * hidden :])
-    value_grad = cm_grad[:, hidden : 2 * hidden].T
+    rec_grad = join_columns(rec_own).astype(jnp.float32)
+    value_grad = cm_grad[:, hidden:].T
     key_grad = cm_grad[:, :hidden]
     out_grad = tm_grad[:, :own_width].T
-    proj_grad = jnp.moveaxis(tm_grad[:, own_width:].reshape(-1, 4, own_width), 1, 0)
+    proj_grad = jnp.moveaxis(tm_grad[:, own_width : 5 * own_width].reshape(-1, 4, own_width), 1, 0)
     return (
         output,
         x_grad,

time: 536 us -> 496 us (0.925)
  waiting for transfers between devices: 236 us -> 174 us
  local copies, waits for them, and re-layouts: 19.9 us -> 35.1 us
  other arithmetic: 44.1 us -> 58.9 us
  starting transfers between devices: 58.4 us -> 49.9 us
    ppermute x40, waiting for transfers between devices: 143 us -> 110 us  [swap(): return lax.ppermute(block, ALL, [(i, i ^ bit) for i in range(count)])]
    all_gather x2, waiting for transfers between devices: 68.7 us -> 52.6 us  [plane_gather(): lax.all_gather(pair, 'seg', axis=0, tiled=True, axis_index_groups=plane_g...]
    reduce_scatter x2, waiting for transfers between devices: 17.2 us -> 6.91 us  [plane_scatter(): lax.psum_scatter(part, 'seg', scatter_dimension=0, tiled=True, axis_index...]
    ppermute x40, starting transfers between devices: 53.2 us -> 43.9 us  [swap(): return lax.ppermute(block, ALL, [(i, i ^ bit) for i in range(count)])]
    unnamed x133 -> x153, local copies, waits for them, and re-layouts: 7.49 us -> 14.5 us
    another operation x0 -> x3, other arithmetic: none -> 6.18 us  [other_plane(): jnp.stack(in_order(rows, got, high == 1), axis=1).reshape(-1, rows.shape[2])]
    convert_element_type x8 -> x11, other arithmetic: 5.43 us -> 11.5 us  [the longest x1 2.73 us: shards(): gated = (rec_gate * value_out).astype(jnp.bfloat16)]
  transfers between devices with their start and end apart: 45 -> 45, of which waited for: 30 -> 24; matrix products, arithmetic and copies ran while one was open for 16% -> 22% of each run, Pallas kernels for 22% -> 23%
where the time goes in v4:
time: 496 us; the launch traced here: 488 us
  waiting for transfers between devices  174 us (35%)
  Pallas kernels  119 us (24%)
  other arithmetic  58.9 us (12%)
  starting transfers between devices  49.9 us (10%)
  local copies, waits for them, and re-layouts  35.1 us (7%)
  matrix products  34.5 us (7%)
  between operations  15.7 us (3%)
    ppermute x40, waiting for transfers between devices, swap(): return lax.ppermute(block, ALL, [(i, i ^ bit) for i in range(count)])  110 us
    all_gather x2, waiting for transfers between devices, plane_gather(): lax.all_gather(pair, 'seg', axis=0, tiled=True, axis_index_groups=plane_g...  52.6 us
    ppermute x40, starting transfers between devices, swap(): return lax.ppermute(block, ALL, [(i, i ^ bit) for i in range(count)])  43.9 us
    pallas_call x8, Pallas kernels, grad_into(): pl.pallas_call(grad_kernel, grid=(width // GRAD_ROWS,), in_specs=specs, o...  32.1 us
    pallas_call x1, Pallas kernels, mixes_back(): pl.pallas_call(mixes_back_kernel, grid=(2, tiles), in_specs=[whole(g_key)...  25.8 us
    pallas_call x1, Pallas kernels, mixes_forward(): pl.pallas_call(mixes_forward_kernel, grid=(2, tiles), in_specs=[across(ro...  21.8 us
    pallas_call x1, Pallas kernels, wkv_backward(): pl.pallas_call(wkv_backward_kernel, grid=(chunks,), in_specs=[block] * 4...  21.6 us
    pallas_call x1, Pallas kernels, wkv_forward(): pl.pallas_call(wkv_forward_kernel, grid=(chunks,), in_specs=[block] * 4 +...  18.1 us
  transfers between devices with their start and end apart: 45, of which 24 were waited for; matrix products, arithmetic and copies ran while one was open for 22% of the time, Pallas kernels for 23%

profile of v4, /device:TPU:1, one launch (start us, length us, event | category | flops | bytes accessed | tf_op | source)
XLA Modules:
  0.0 488.0 jit_solution(12371603537545183123)
XLA Ops:
  22.2 6.9 %collective-permute-done.8 = bf16[4,64,512]{2,1,0:T(8,128)(2,1)S(1)} collective-permute-done((bf16[4,64,512]{2,1,0:T(8,128)(2,1)}, bf16[4,64,512]{2,1,0:T(8,128)(2,1)S(1)}, u32[]{:S(2)}, u32[]{:S(2)}) %collective-permute-start.8) | collective-permute-done | bytes 262176 | tf_op jit(solution)/shard_map/ppermute | solution.py:20
  37.0 11.4 %collective-permute-done.5 = bf16[128,512]{1,0:T(8,128)(2,1)S(1)} collective-permute-done((bf16[128,512]{1,0:T(8,128)(2,1)S(1)}, bf16[128,512]{1,0:T(8,128)(2,1)S(1)}, u32[]{:S(2)}, u32[]{:S(2)}) %collective-permute-start.5) | collective-permute-done | bytes 131104 | tf_op jit(solution)/shard_map/ppermute | solution.py:20
  48.3 3.7 collective-permute-done.6
  56.2 4.9 %collective-permute-done = bf16[64,1792]{1,0:T(8,128)(2,1)S(1)} collective-permute-done((bf16[64,1792]{1,0:T(8,128)(2,1)S(1)}, bf16[64,1792]{1,0:T(8,128)(2,1)S(1)}, u32[]{:S(2)}, u32[]{:S(2)}) %collective-permute-start) | collective-permute-done | bytes 229408 | tf_op jit(solution)/shard_map/ppermute | solution.py:20
  64.7 4.6 fusion.6.unit_ref
  69.4 52.6 %all-gather.3.cloned.1.call-done.w_ref.down_ref.up_ref = bf16[2048,3072]{1,0:T(8,128)(2,1)} async-done(((bf16[128,3072]{1,0:T(8,128)(2,1)}), bf16[2048,3072]{1,0:T(8,128)(2,1)}) %all-gather.3.cloned.1.call-update) | async-done | bytes 12582928 | tf_op jit(solution)/shard_map/all_gather | solution.py:102
  130.6 21.8 %mixes_forward.1 = (bf16[512,2048]{1,0:T(8,128)(2,1)}, bf16[512,2048]{1,0:T(8,128)(2,1)}, bf16[512,2048]{1,0:T(8,128)(2,1)}, bf16[512,2048]{1,0:T(8,128)(2,1)}, ...) custom-call(f32[512,2048]{1,0:T(8,128)} %fusion.6.unit_ref, ...), custom_call_target="tpu_custom_call" | custom-call | flops 1048576 | bytes 65536 | tf_op jit(solution)/shard_map/mixes_forward/pallas_call | solution.py:664
  158.5 18.1 %wkv_forward.1 = (bf16[512,512]{1,0:T(8,128)(2,1)S(1)}, f32[512,512]{1,0:T(8,128)S(1)}, f32[512,512]{1,0:T(8,128)S(1)}) custom-call(f32[512,512]{1,0:T(8,128)S(1)} %copy-done.2, f32[512,512]{1,0:T(8,128)S(1)} %copy-done.4, f32[512,512]{1,0:T(8,128)S(1)} %copy-done.6, f32[512,512]{1,0:T(8,128)S(1)} %copy-done.8, ...), custom_call_target="tpu_custom_call" | custom-call | flops 1048576 | bytes 65536 | tf_op jit(solution)/shard_map/wkv_forward/pallas_call | solution.py:378
  176.7 4.6 select_bitcast_fusion.4
  189.1 11.0 %collective-permute-done.14 = bf16[128,2048]{1,0:T(8,128)(2,1)S(1)} collective-permute-done((bf16[128,2048]{1,0:T(8,128)(2,1)S(1)}, bf16[128,2048]{1,0:T(8,128)(2,1)S(1)}, u32[]{:S(2)}, u32[]{:S(2)}) %collective-permute-start.14) | collective-permute-done | bytes 524320 | tf_op jit(solution)/shard_map/ppermute | solution.py:20
  202.3 11.8 %collective-permute-done.15 = bf16[128,2048]{1,0:T(8,128)(2,1)S(1)} collective-permute-done((bf16[128,2048]{1,0:T(8,128)(2,1)S(1)}, bf16[128,2048]{1,0:T(8,128)(2,1)S(1)}, u32[]{:S(2)}, u32[]{:S(2)}) %collective-permute-start.15) | collective-permute-done | bytes 524320 | tf_op jit(solution)/shard_map/ppermute | solution.py:20
  229.8 7.2 %multiply_convert_fusion.1 = (bf16[512,1792]{1,0:T(8,128)(2,1)S(1)}, bf16[512,1792]{1,0:T(8,128)(2,1)S(1)}) fusion(bf16[512,2048]{1,0:T(8,128)(2,1)S(1)} %get-tuple-element.159.left_ref, bf16[2048,3584]{1,0:T(8,128)(2,1)} %all-gather.5.cloned.1.call-done), kind=kOutput, calls=%fused_computation.23 | convolution fusion | flops 3761766400 | bytes 13107200 | tf_op jit(solution)/shard_map/dot_general | solution.py:173
  249.6 4.0 multiply_convert_fusion.right_ref
  253.6 6.3 %weight_grad.8.rest_0_ = bf16[2048,3584]{1,0:T(8,128)(2,1)} custom-call(bf16[512,2048]{1,0:T(8,128)(2,1)S(1)} %pad_maximum_fusion.5.left_ref, bf16[512,1792]{1,0:T(8,128)(2,1)S(1)} %get-tuple-element.254.right_ref), custom_call_target="tpu_custom_call" | custom-call | flops 1048576 | bytes 65536 | tf_op jit(solution)/shard_map/weight_grad/pallas_call | solution.py:535
  262.9 6.2 %weight_grad.9 = bf16[2048,3584]{1,0:T(8,128)(2,1)} custom-call(bf16[512,2048]{1,0:T(8,128)(2,1)S(1)} %get-tuple-element.159.left_ref, bf16[512,1792]{1,0:T(8,128)(2,1)S(1)} %multiply_convert_fusion.right_ref, bf16[2048,3584]{1,0:T(8,128)(2,1)} %weight_grad.8.rest_0_), custom_call_target="tpu_custom_call", output_to_operand_aliasing={{}: (2, {})} | custom-call | flops 1048576 | bytes 65536 | tf_op jit(solution)/shard_map/weight_grad/pallas_call | solution.py:535
  273.5 6.4 %fusion.2 = f32[512,2048]{1,0:T(8,128)S(1)} fusion(bf16[512,1792]{1,0:T(8,128)(2,1)S(1)} %copy-done.19, bf16[2048,3584]{1,0:T(8,128)(2,1)} %all-gather.5.cloned.1.call-done), kind=kOutput, calls=%fused_computation.2 | convolution fusion | flops 3758096384 | bytes 13369344 | tf_op jit(solution)/shard_map/te,de->td/dot_general | solution.py:181
  290.5 3.2 weight_grad.10
  293.6 9.1 %collective-permute-done.23 = bf16[128,2048]{1,0:T(8,128)(2,1)S(1)} collective-permute-done((bf16[128,2048]{1,0:T(8,128)(2,1)S(1)}, bf16[128,2048]{1,0:T(8,128)(2,1)S(1)}, u32[]{:S(2)}, u32[]{:S(2)}) %collective-permute-start.23) | collective-permute-done | bytes 524320 | tf_op jit(solution)/shard_map/ppermute | solution.py:20
  305.5 11.8 %collective-permute-done.24 = bf16[128,2048]{1,0:T(8,128)(2,1)S(1)} collective-permute-done((bf16[128,2048]{1,0:T(8,128)(2,1)S(1)}, bf16[128,2048]{1,0:T(8,128)(2,1)S(1)}, u32[]{:S(2)}, u32[]{:S(2)}) %collective-permute-start.24) | collective-permute-done | bytes 524320 | tf_op jit(solution)/shard_map/ppermute | solution.py:20
  330.4 3.3 weight_grad.11
  333.7 21.6 %wkv_backward.1 = (bf16[512,512]{1,0:T(8,128)(2,1)S(1)}, bf16[512,512]{1,0:T(8,128)(2,1)S(1)}, bf16[512,512]{1,0:T(8,128)(2,1)S(1)}, bf16[512,512]{1,0:T(8,128)(...) custom-call(f32[512,512]{1,0:T(8,128)S(1)} %copy-done.3, ...), custom_call_target="tpu_custom_call" | custom-call | flops 1048576 | bytes 65536 | tf_op jit(solution)/shard_map/wkv_backward/pallas_call | solution.py:483
  360.1 3.3 weight_grad.12.rest_0_
  363.4 3.3 weight_grad.13.rest_0_
  366.7 3.4 weight_grad.14.rest_0_
  370.0 3.3 weight_grad.15
  375.3 25.8 %mixes_back.1 = (bf16[512,2048]{1,0:T(8,128)(2,1)}, bf16[2048,512]{1,0:T(8,128)(2,1)}) custom-call(bf16[512,512]{1,0:T(8,128)(2,1)} %copy-done.11, bf16[512,512]{1,0:T(8,128)(2,1)} %copy-done.12, bf16[512,512]{1,0:T(8,128)(2,1)} %copy-done.10, bf16[512,512]{1,0:T(8,128)(2,1)} %copy-done.13, bf16[512,256]{1,0:T(8,128)(2,1)} %fusion.28.gd_ref, ...), custom_call_target="tpu_custom_call" | custom-call | flops 1048576 | bytes 65536 | tf_op jit(solution)/shard_map/mixes_back/pallas_call | solution.py:775
  413.2 12.0 %collective-permute-done.31 = bf16[16,2,16,512]{3,2,1,0:T(8,128)(2,1)S(1)} collective-permute-done((bf16[16,2,16,512]{3,2,1,0:T(8,128)(2,1)S(1)}, bf16[16,2,16,512]{3,2,1,0:T(8,128)(2,1)S(1)}, u32[]{:S(2)}, u32[]{:S(2)}) %collective-permute-start.31) | collective-permute-done | bytes 524320 | tf_op jit(solution)/shard_map/ppermute | solution.py:20
  429.4 4.2 collective-permute-done.34
  434.5 5.9 %all-to-all-start = ((bf16[16,16,512]{2,1,0:T(8,128)(2,1)}), bf16[16,16,512]{2,1,0:T(8,128)(2,1)}, u32[]{:S(2)}, u32[]{:S(2)}) async-start(bf16[16,16,512]{2,1,0:T(8,128)(2,1)} %fusion.48), calls=%async_computation.1 | async-start | bytes 524288 | tf_op jit(solution)/shard_map/all_to_all | solution.py:225
  443.6 4.4 all-to-all-done
  457.0 6.9 %reduce-scatter.5.cloned.1.call-done = bf16[128,2816]{1,0:T(8,128)(2,1)} async-done(((bf16[2048,2816]{1,0:T(8,128)(2,1)}), bf16[128,2816]{1,0:T(8,128)(2,1)}) %reduce-scatter.5.cloned.1.call-update) | async-done | bytes 720912 | tf_op jit(solution)/shard_map/reduce_scatter | solution.py:113
  471.8 7.6 %collective-permute-done.35 = bf16[64,2560]{1,0:T(8,128)(2,1)S(1)} collective-permute-done((bf16[64,2560]{1,0:T(8,128)(2,1)S(1)}, bf16[64,2560]{1,0:T(8,128)(2,1)S(1)}, u32[]{:S(2)}, u32[]{:S(2)}) %collective-permute-start.35) | collective-permute-done | bytes 327712 | tf_op jit(solution)/shard_map/ppermute | solution.py:20
  (380 shorter events, 161.8 us)
Async XLA Ops:
  7.2 114.9 %all-gather.3.cloned.1.call-start = ((), (), s32[]{:S(2)}) async-start(), calls=%async_computation.3 | async-start | bytes 13369344 | tf_op jit(solution)/shard_map/all_gather | solution.py:102
  9.6 6.4 %collective-permute-start.7 = (bf16[16,1024]{1,0:T(8,128)(2,1)S(1)}, bf16[16,1024]{1,0:T(8,128)(2,1)S(1)}, u32[]{:S(2)}, u32[]{:S(2)}) collective-permute-start(bf16[16,1024]{1,0:T(8,128)(2,1)S(1)} %concatenate.91), channel_id=1, source_target_pairs={{0,1},{1,0},{2,3},{3,2},{4,5},{5,4},{6,7},{7,6},{8,9},{9,8},{10,11... | collective-permute-start | bytes 98312 | tf_op jit(solution)/shard_map/ppermute | solution.py:20
  20.2 9.0 %collective-permute-start.8 = (bf16[4,64,512]{2,1,0:T(8,128)(2,1)}, bf16[4,64,512]{2,1,0:T(8,128)(2,1)S(1)}, u32[]{:S(2)}, u32[]{:S(2)}) collective-permute-start(bf16[4,64,512]{2,1,0:T(8,128)(2,1)} %param.15), channel_id=1, source_target_pairs={{0,4},{1,5},{2,6},{3,7},{4,0},{5,1},{6,2},{7,3},{8,12},{9,13},{10,... | collective-permute-start | bytes 786440 | tf_op jit(solution)/shard_map/ppermute | solution.py:20
  30.3 198.9 %all-gather.5.cloned.1.call-start = ((), (), s32[]{:S(2)}) async-start(), calls=%async_computation.4 | async-start | bytes 15597568 | tf_op jit(solution)/shard_map/all_gather | solution.py:102
  30.4 5.3 %collective-permute-start.4 = (bf16[128,512]{1,0:T(8,128)(2,1)S(1)}, bf16[128,512]{1,0:T(8,128)(2,1)S(1)}, u32[]{:S(2)}, u32[]{:S(2)}) collective-permute-start(bf16[128,512]{1,0:T(8,128)(2,1)S(1)} %get-tuple-element.220), channel_id=1, source_target_pairs={{0,1},{1,0},{2,3},{3,2},{4,5},{5,4},{6,7},{7,6},{8,9},{9,8},{10,11... | collective-permute-start | bytes 393224 | tf_op jit(solution)/shard_map/ppermute | solution.py:20
  31.9 20.2 %collective-permute-start.2 = (bf16[128,2048]{1,0:T(8,128)(2,1)S(1)}, bf16[128,2048]{1,0:T(8,128)(2,1)S(1)}, u32[]{:S(2)}, u32[]{:S(2)}) collective-permute-start(bf16[128,2048]{1,0:T(8,128)(2,1)S(1)} %copy-done.31), channel_id=1, source_target_pairs={{0,2},{1,3},{2,0},{3,1},{4,6},{5,7},{6,4},{7,5},{8,10},{9,11},{10,... | collective-permute-start | bytes 1572872 | tf_op jit(solution)/shard_map/ppermute | solution.py:20
  31.9 16.4 %collective-permute-start.5 = (bf16[128,512]{1,0:T(8,128)(2,1)S(1)}, bf16[128,512]{1,0:T(8,128)(2,1)S(1)}, u32[]{:S(2)}, u32[]{:S(2)}) collective-permute-start(bf16[128,512]{1,0:T(8,128)(2,1)S(1)} %get-tuple-element.219), channel_id=1, source_target_pairs={{0,2},{1,3},{2,0},{3,1},{4,6},{5,7},{6,4},{7,5},{8,10},{9,11},{10,... | collective-permute-start | bytes 393224 | tf_op jit(solution)/shard_map/ppermute | solution.py:20
  33.4 18.7 %collective-permute-start.6 = (bf16[128,512]{1,0:T(8,128)(2,1)S(1)}, bf16[128,512]{1,0:T(8,128)(2,1)S(1)}, u32[]{:S(2)}, u32[]{:S(2)}) collective-permute-start(bf16[128,512]{1,0:T(8,128)(2,1)S(1)} %get-tuple-element.218), channel_id=1, source_target_pairs={{0,3},{1,2},{2,1},{3,0},{4,7},{5,6},{6,5},{7,4},{8,11},{9,10},{10,... | collective-permute-start | bytes 393224 | tf_op jit(solution)/shard_map/ppermute | solution.py:20
  33.8 22.4 %collective-permute-start.1 = (bf16[1792,64]{0,1:T(8,128)(2,1)S(1)}, bf16[1792,64]{0,1:T(8,128)(2,1)S(1)}, u32[]{:S(2)}, u32[]{:S(2)}) collective-permute-start(bf16[1792,64]{0,1:T(8,128)(2,1)S(1)} %copy-done.64), channel_id=1, source_target_pairs={{0,4},{1,5},{2,6},{3,7},{4,0},{5,1},{6,2},{7,3},{8,12},{9,13},{10,... | collective-permute-start | bytes 688136 | tf_op jit(solution)/shard_map/ppermute | solution.py:20
  35.7 25.4 %collective-permute-start = (bf16[64,1792]{1,0:T(8,128)(2,1)S(1)}, bf16[64,1792]{1,0:T(8,128)(2,1)S(1)}, u32[]{:S(2)}, u32[]{:S(2)}) collective-permute-start(bf16[64,1792]{1,0:T(8,128)(2,1)S(1)} %copy-done.65), channel_id=1, source_target_pairs={{0,4},{1,5},{2,6},{3,7},{4,0},{5,1},{6,2},{7,3},{8,12},{9,13},{10,... | collective-permute-start | bytes 688136 | tf_op jit(solution)/shard_map/ppermute | solution.py:20
  53.3 9.0 %collective-permute-start.3 = (bf16[2,128,2048]{2,1,0:T(8,128)(2,1)}, bf16[2,128,2048]{2,1,0:T(8,128)(2,1)S(1)}, u32[]{:S(2)}, u32[]{:S(2)}) collective-permute-start(bf16[2,128,2048]{2,1,0:T(8,128)(2,1)} %pad_maximum_fusion.7), channel_id=1, source_target_pairs={{0,1},{1,0},{2,3},{3,2},{4,5},{5,4},{6,7},{7,6},{8,9},{9,8},{10,11... | collective-permute-start | bytes 3145736 | tf_op jit(solution)/shard_map/ppermute | solution.py:20
  69.3 304.0 %reduce-scatter.3.cloned.1.call-start = ((), (), s32[]{:S(2)}) async-start(), calls=%async_computation.5 | async-start | bytes 15597568 | tf_op jit(solution)/shard_map/reduce_scatter | solution.py:113
  125.5 51.2 %collective-permute-start.12 = (bf16[16,64,1024]{2,1,0:T(8,128)(2,1)}, bf16[16,64,1024]{2,1,0:T(8,128)(2,1)}, u32[]{:S(2)}, u32[]{:S(2)}) collective-permute-start(bf16[16,64,1024]{2,1,0:T(8,128)(2,1)} %pad_maximum_fusion.1), channel_id=1, source_target_pairs={{0,4},{1,5},{2,6},{3,7},{4,0},{5,1},{6,2},{7,3},{8,12},{9,13},{10,... | collective-permute-start | bytes 6291464 | tf_op jit(solution)/shard_map/ppermute | solution.py:20
  186.8 13.3 %collective-permute-start.14 = (bf16[128,2048]{1,0:T(8,128)(2,1)S(1)}, bf16[128,2048]{1,0:T(8,128)(2,1)S(1)}, u32[]{:S(2)}, u32[]{:S(2)}) collective-permute-start(bf16[128,2048]{1,0:T(8,128)(2,1)S(1)} %fusion.43), channel_id=1, source_target_pairs={{0,2},{1,3},{2,0},{3,1},{4,6},{5,7},{6,4},{7,5},{8,10},{9,11},{10,... | collective-permute-start | bytes 1572872 | tf_op jit(solution)/shard_map/ppermute | solution.py:20
  201.7 12.5 %collective-permute-start.15 = (bf16[128,2048]{1,0:T(8,128)(2,1)S(1)}, bf16[128,2048]{1,0:T(8,128)(2,1)S(1)}, u32[]{:S(2)}, u32[]{:S(2)}) collective-permute-start(bf16[128,2048]{1,0:T(8,128)(2,1)S(1)} %add_convert_fusion.5), channel_id=1, source_target_pairs={{0,2},{1,3},{2,0},{3,1},{4,6},{5,7},{6,4},{7,5},{8,10},{9,11},{10,... | collective-permute-start | bytes 1572872 | tf_op jit(solution)/shard_map/ppermute | solution.py:20
  229.2 13.3 %collective-permute-start.18 = (bf16[512,512]{1,0:T(8,128)(2,1)}, bf16[512,512]{1,0:T(8,128)(2,1)S(1)}, u32[]{:S(2)}, u32[]{:S(2)}) collective-permute-start(bf16[512,512]{1,0:T(8,128)(2,1)} %get-tuple-element.80), channel_id=1, source_target_pairs={{0,2},{1,3},{2,0},{3,1},{4,6},{5,7},{6,4},{7,5},{8,10},{9,11},{10,... | collective-permute-start | bytes 1572872 | tf_op jit(solution)/shard_map/ppermute | solution.py:20
  242.7 5.5 %collective-permute-start.19 = (bf16[2,512,512]{2,1,0:T(8,128)(2,1)S(1)}, bf16[2,512,512]{2,1,0:T(8,128)(2,1)S(1)}, u32[]{:S(2)}, u32[]{:S(2)}) collective-permute-start(bf16[2,512,512]{2,1,0:T(8,128)(2,1)S(1)} %pad_maximum_fusion.11), channel_id=1, source_target_pairs={{0,1},{1,0},{2,3},{3,2},{4,5},{5,4},{6,7},{7,6},{8,9},{9,8},{10,11... | collective-permute-start | bytes 3145736 | tf_op jit(solution)/shard_map/ppermute | solution.py:20
  248.7 13.4 %collective-permute-start.20 = (bf16[512,512]{1,0:T(8,128)(2,1)S(1)}, bf16[512,512]{1,0:T(8,128)(2,1)S(1)}, u32[]{:S(2)}, u32[]{:S(2)}) collective-permute-start(bf16[512,512]{1,0:T(8,128)(2,1)S(1)} %add_convert_fusion.4), channel_id=1, source_target_pairs={{0,2},{1,3},{2,0},{3,1},{4,6},{5,7},{6,4},{7,5},{8,10},{9,11},{10,... | collective-permute-start | bytes 1572872 | tf_op jit(solution)/shard_map/ppermute | solution.py:20
  269.2 194.7 %reduce-scatter.5.cloned.1.call-start = ((), (), s32[]{:S(2)}) async-start(), calls=%async_computation.6 | async-start | bytes 12255232 | tf_op jit(solution)/shard_map/reduce_scatter | solution.py:113
  289.4 13.3 %collective-permute-start.23 = (bf16[128,2048]{1,0:T(8,128)(2,1)S(1)}, bf16[128,2048]{1,0:T(8,128)(2,1)S(1)}, u32[]{:S(2)}, u32[]{:S(2)}) collective-permute-start(bf16[128,2048]{1,0:T(8,128)(2,1)S(1)} %fusion.44), channel_id=1, source_target_pairs={{0,2},{1,3},{2,0},{3,1},{4,6},{5,7},{6,4},{7,5},{8,10},{9,11},{10,... | collective-permute-start | bytes 1572872 | tf_op jit(solution)/shard_map/ppermute | solution.py:20
  304.9 12.4 %collective-permute-start.24 = (bf16[128,2048]{1,0:T(8,128)(2,1)S(1)}, bf16[128,2048]{1,0:T(8,128)(2,1)S(1)}, u32[]{:S(2)}, u32[]{:S(2)}) collective-permute-start(bf16[128,2048]{1,0:T(8,128)(2,1)S(1)} %get-tuple-element.152), channel_id=1, source_target_pairs={{0,2},{1,3},{2,0},{3,1},{4,6},{5,7},{6,4},{7,5},{8,10},{9,11},{10,... | collective-permute-start | bytes 1572872 | tf_op jit(solution)/shard_map/ppermute | solution.py:20
  322.2 33.2 %collective-permute-start.26 = (bf16[16,64,512]{2,1,0:T(8,128)(2,1)}, bf16[16,64,512]{2,1,0:T(8,128)(2,1)}, u32[]{:S(2)}, u32[]{:S(2)}) collective-permute-start(bf16[16,64,512]{2,1,0:T(8,128)(2,1)} %select_bitcast_fusion.1), channel_id=1, source_target_pairs={{0,4},{1,5},{2,6},{3,7},{4,0},{5,1},{6,2},{7,3},{8,12},{9,13},{10,... | collective-permute-start | bytes 3145736 | tf_op jit(solution)/shard_map/ppermute | solution.py:20
  324.6 30.7 %collective-permute-start.27 = (bf16[128,512]{1,0:T(8,128)(2,1)S(1)}, bf16[128,512]{1,0:T(8,128)(2,1)S(1)}, u32[]{:S(2)}, u32[]{:S(2)}) collective-permute-start(bf16[128,512]{1,0:T(8,128)(2,1)S(1)} %get-tuple-element.214), channel_id=1, source_target_pairs={{0,1},{1,0},{2,3},{3,2},{4,5},{5,4},{6,7},{7,6},{8,9},{9,8},{10,11... | collective-permute-start | bytes 393224 | tf_op jit(solution)/shard_map/ppermute | solution.py:20
  325.3 30.0 %collective-permute-start.28 = (bf16[128,512]{1,0:T(8,128)(2,1)S(1)}, bf16[128,512]{1,0:T(8,128)(2,1)S(1)}, u32[]{:S(2)}, u32[]{:S(2)}) collective-permute-start(bf16[128,512]{1,0:T(8,128)(2,1)S(1)} %get-tuple-element.213), channel_id=1, source_target_pairs={{0,2},{1,3},{2,0},{3,1},{4,6},{5,7},{6,4},{7,5},{8,10},{9,11},{10,... | collective-permute-start | bytes 393224 | tf_op jit(solution)/shard_map/ppermute | solution.py:20
  328.8 26.5 %collective-permute-start.29 = (bf16[128,512]{1,0:T(8,128)(2,1)S(1)}, bf16[128,512]{1,0:T(8,128)(2,1)S(1)}, u32[]{:S(2)}, u32[]{:S(2)}) collective-permute-start(bf16[128,512]{1,0:T(8,128)(2,1)S(1)} %get-tuple-element.212), channel_id=1, source_target_pairs={{0,3},{1,2},{2,1},{3,0},{4,7},{5,6},{6,5},{7,4},{8,11},{9,10},{10,... | collective-permute-start | bytes 393224 | tf_op jit(solution)/shard_map/ppermute | solution.py:20
  412.1 13.1 %collective-permute-start.31 = (bf16[16,2,16,512]{3,2,1,0:T(8,128)(2,1)S(1)}, bf16[16,2,16,512]{3,2,1,0:T(8,128)(2,1)S(1)}, u32[]{:S(2)}, u32[]{:S(2)}) collective-permute-start(bf16[16,2,16,512]{3,2,1,0:T(8,128)(2,1)S(1)} %fusion.45), channel_id=1, source_target_pairs={{0,2},{1,3},{2,0},{3,1},{4,6},{5,7},{6,4},{7,5},{8,10},{9,11},{10,... | collective-permute-start | bytes 1572872 | tf_op jit(solution)/shard_map/ppermute | solution.py:20
  425.6 8.1 %collective-permute-start.34 = (bf16[16,16,512]{2,1,0:T(8,128)(2,1)S(1)}, bf16[16,16,512]{2,1,0:T(8,128)(2,1)S(1)}, u32[]{:S(2)}, u32[]{:S(2)}) collective-permute-start(bf16[16,16,512]{2,1,0:T(8,128)(2,1)S(1)} %fusion.49), channel_id=1, source_target_pairs={{0,4},{1,5},{2,6},{3,7},{4,0},{5,1},{6,2},{7,3},{8,12},{9,13},{10,... | collective-permute-start | bytes 786440 | tf_op jit(solution)/shard_map/ppermute | solution.py:20
  429.1 22.6 %collective-permute-start.33 = (bf16[128,2048]{1,0:T(8,128)(2,1)}, bf16[128,2048]{1,0:T(8,128)(2,1)}, u32[]{:S(2)}, u32[]{:S(2)}) collective-permute-start(bf16[128,2048]{1,0:T(8,128)(2,1)} %fusion.46), channel_id=1, source_target_pairs={{0,2},{1,3},{2,0},{3,1},{4,6},{5,7},{6,4},{7,5},{8,10},{9,11},{10,... | collective-permute-start | bytes 1572872 | tf_op jit(solution)/shard_map/ppermute | solution.py:20
  434.5 13.5 %all-to-all-start = ((bf16[16,16,512]{2,1,0:T(8,128)(2,1)}), bf16[16,16,512]{2,1,0:T(8,128)(2,1)}, u32[]{:S(2)}, u32[]{:S(2)}) async-start(bf16[16,16,512]{2,1,0:T(8,128)(2,1)} %fusion.48), calls=%async_computation.1 | async-start | bytes 524288 | tf_op jit(solution)/shard_map/all_to_all | solution.py:225
  441.2 13.6 %collective-permute-start.39 = (bf16[64,3584]{1,0:T(8,128)(2,1)}, bf16[64,3584]{1,0:T(8,128)(2,1)}, u32[]{:S(2)}, u32[]{:S(2)}) collective-permute-start(bf16[64,3584]{1,0:T(8,128)(2,1)} %broadcast_select_fusion.26), channel_id=1, source_target_pairs={{0,4},{1,5},{2,6},{3,7},{4,0},{5,1},{6,2},{7,3},{8,12},{9,13},{10,... | collective-permute-start | bytes 1376264 | tf_op jit(solution)/shard_map/ppermute | solution.py:20
  464.8 6.2 %collective-permute-start.36 = (bf16[16,512]{1,0:T(8,128)(2,1)S(1)}, bf16[16,512]{1,0:T(8,128)(2,1)S(1)}, u32[]{:S(2)}, u32[]{:S(2)}) collective-permute-start(bf16[16,512]{1,0:T(8,128)(2,1)S(1)} %get-tuple-element.238), channel_id=1, source_target_pairs={{0,1},{1,0},{2,3},{3,2},{4,5},{5,4},{6,7},{7,6},{8,9},{9,8},{10,11... | collective-permute-start | bytes 49160 | tf_op jit(solution)/shard_map/ppermute | solution.py:20
  468.6 10.7 %collective-permute-start.35 = (bf16[64,2560]{1,0:T(8,128)(2,1)S(1)}, bf16[64,2560]{1,0:T(8,128)(2,1)S(1)}, u32[]{:S(2)}, u32[]{:S(2)}) collective-permute-start(bf16[64,2560]{1,0:T(8,128)(2,1)S(1)} %broadcast_select_fusion.29), channel_id=1, source_target_pairs={{0,4},{1,5},{2,6},{3,7},{4,0},{5,1},{6,2},{7,3},{8,12},{9,13},{10,... | collective-permute-start | bytes 983048 | tf_op jit(solution)/shard_map/ppermute | solution.py:20
  (88 other events, 504.4 us)
Sparse Core Ops, SparseCore 0:
  30.4 91.5 all-gather.2
  124.2 100.2 all-gather.4
  269.3 99.4 reduce-scatter.2
  373.4 90.3 reduce-scatter.4

commit v5 on v4

--- a/solution.py
+++ b/solution.py
@@ -136,7 +136,7 @@
     result = jnp.zeros((4, *messages[0].shape), small.dtype)
     for bit, piece in enumerate(pieces):
         result = lax.dynamic_update_index_in_dim(result, piece, place ^ bit, 0)
-    return pieces[1], result.reshape(4 * small.shape[0], -1)
+    return result.reshape(4 * small.shape[0], -1)
 
 
 def split_columns(block):
@@ -257,7 +257,7 @@
 
 def head_ones():
     shape = (PACK, PACK)
-    same = iota2(shape, 0) // GROUP_DIMENSION == iota2(shape, 1) // GROUP_DIMENSION
+    same = (iota2(shape, 0) ^ iota2(shape, 1)) < GROUP_DIMENSION
     return jnp.where(same, 1.0, 0.0).astype(jnp.float32)
 
 
@@ -289,22 +289,23 @@
 
 def piece_factors(run, before):
     rows = iota2((CHUNK, PACK), 0)
-    t, i = iota2((CHUNK, PACK), 0), iota2((CHUNK, PACK), 1) % CHUNK
+    t, i = rows, iota2((CHUNK, PACK), 1) & (CHUNK - 1)
+    apart = t ^ i
     levels = []
     for half in (32, 16):
-        upper = rows % (2 * half) >= half
+        upper = (rows & half) != 0
         reference = jnp.broadcast_to(row_of(run, half - 1), run.shape)
         for start in range(2 * half, CHUNK, 2 * half):
             here = jnp.broadcast_to(row_of(run, start + half - 1), run.shape)
             reference = jnp.where(rows >= start, here, reference)
         scale = jnp.exp(jnp.where(upper, before - reference, reference - run))
-        pairs = (t // (2 * half) == i // (2 * half)) & (t % (2 * half) >= half) & (i % (2 * half) < half)
+        pairs = (apart < 2 * half) & upper & ((apart & half) != 0)
         levels.append((jnp.where(upper, scale, 0.0), jnp.where(upper, 0.0, scale), pairs))
     reference = jnp.broadcast_to(row_of(run, 7), run.shape)
     for start in range(16, CHUNK, 16):
         here = jnp.broadcast_to(row_of(run, start + 7), run.shape)
         reference = jnp.where(rows >= start, here, reference)
-    pairs = (t // 16 == i // 16) & (t > i)
+    pairs = (apart < 16) & (t > i)
     to_row = jnp.exp(jnp.minimum(before - reference, 80.0))
     to_prior = jnp.exp(jnp.minimum(reference - run, 80.0))
     levels.append((to_row, to_prior, pairs))
@@ -397,7 +398,7 @@
         ),
         cost_estimate=SOON,
         name="wkv_forward",
-    )(r, k, v, gate, low, up, par, first)
+    )(*[pltpu.with_memory_space_constraint(x, pltpu.HBM) for x in (r, k, v, gate)], low, up, par, first)
 
 
 def backward_heads(
@@ -547,27 +548,43 @@
     )(*operands)
 
 
-def copy_kernel(block_ref, into_ref, out_ref):
-    out_ref[...] = block_ref[...]
-
-
-def copy_into(block, at, into):
-    rows, columns = block.shape
-    shift = at // columns
+def grads_kernel(*refs):
+    count = len(refs) // 2
+    out_ref = refs[-1]
+    for n in range(count):
+
+        @pl.when(pl.program_id(0) == n)
+        def _(left_ref=refs[n], right_ref=refs[count + n]):
+            turned = left_ref[...].T
+            for at in range(0, out_ref.shape[1], GRAD_COLUMNS):
+                columns = slice(at, at + GRAD_COLUMNS)
+                out_ref[:, columns] = mxu(turned, right_ref[:, columns], NN).astype(jnp.bfloat16)
+
+
+def grads_side_by_side(lefts, rights, total):
+    rows, width = lefts[0].shape
+    columns = rights[0].shape[1]
+    blocks = width // GRAD_ROWS
+
+    def left_spec(n):
+        return pl.BlockSpec(
+            (rows, GRAD_ROWS),
+            lambda p, i: (0, jnp.where(p == n, i, jnp.where(p < n, 0, blocks - 1))),
+        )
+
     return pl.pallas_call(
-        copy_kernel,
-        grid=(rows // GRAD_ROWS,),
-        in_specs=[
-            pl.BlockSpec((GRAD_ROWS, columns), lambda i: (i, 0)),
-            pl.BlockSpec(memory_space=pltpu.HBM),
-        ],
-        out_specs=pl.BlockSpec((GRAD_ROWS, columns), lambda i: (i, shift)),
-        out_shape=pltpu.HBM(into.shape, into.dtype),
-        input_output_aliases={1: 0},
-        compiler_params=pltpu.CompilerParams(dimension_semantics=("arbitrary",)),
+        grads_kernel,
+        grid=(len(lefts), blocks),
+        in_specs=[left_spec(n) for n in range(len(lefts))]
+        + [pl.BlockSpec((rows, columns), lambda p, i: (0, 0))] * len(rights),
+        out_specs=pl.BlockSpec((GRAD_ROWS, columns), lambda p, i: (i, p)),
+        out_shape=pltpu.HBM((width, total), jnp.bfloat16),
+        compiler_params=pltpu.CompilerParams(
+            dimension_semantics=("arbitrary", "arbitrary"), vmem_limit_bytes=32 * 2**20
+        ),
         cost_estimate=SOON,
-        name="copy_into",
-    )(block, into)
+        name="time_mix_grads",
+    )(*lefts, *rights)
 
 
 LOW = 256
@@ -597,7 +614,7 @@
 
 
 def lane_group(shape):
-    return iota2(shape, 1) // SHIFT_RANK
+    return lax.shift_right_logical(iota2(shape, 1), 5)
 
 
 def mixes_forward_kernel(
@@ -674,7 +691,7 @@
         out_specs=[late] * 6 + [whole(LOW)] + [whole(own)] * 4,
         out_shape=[kept(width, jnp.bfloat16)] * 5
         + [kept(width, jnp.float32), kept(LOW, jnp.float32)]
-        + [kept(own, jnp.float32)] * 4,
+        + [pltpu.HBM((rows, own), jnp.float32)] * 4,
         scratch_shapes=[pltpu.VMEM((rows, LOW), jnp.float32), pltpu.VMEM((5, rows, LOW), jnp.bfloat16)],
         compiler_params=pltpu.CompilerParams(
             dimension_semantics=("arbitrary", "arbitrary"), vmem_limit_bytes=54 * 2**20
@@ -839,8 +856,7 @@
     small_rows = jnp.concatenate(
         [rank_down_weight, blank(LOW - LANES), rank_up_weight.T, vectors.T, blank(LOW - LANES - 16)], axis=1
     )
-    early, span_rows = gather_and_split(small_rows, channel_receptance_weight)
-    _, time_mix_weight = lax.optimization_barrier((early, time_mix_weight))
+    span_rows = gather_and_split(small_rows, channel_receptance_weight)
     weights = both_planes(lambda proj: [proj[g] for g in range(4)], time_mix_weight)
     small_pair = both_planes(lambda rows: [rows], span_rows[:, own_width:])
     late_pairs = [fill_pair(rows[None])[0] for rows in (output_weight.T, span_rows[:, :own_width])]
@@ -946,14 +962,14 @@
         g_first.reshape(GROUP_DIMENSION, local_heads, GROUP_DIMENSION), (1, 2, 0)
     )[None]
     tm_total = 5 * own_width + own_width // 2
-    tm_part = grad_into(g_att, mixed, tm_total, 0)
-    rec_got, g_recept = lax.optimization_barrier((rec_got, g_recept))
+    tm_part = grads_side_by_side(
+        (g_att, mixes[3], mixes[1], mixes[2], mixes[4]), (mixed, g_recept, g_key, g_val, g_gate), tm_total
+    )
+    rec_got, g_ww = lax.optimization_barrier((rec_got, g_ww))
     rec_sum = (rec_mine.astype(jnp.float32) + rec_got.astype(jnp.float32)).astype(jnp.bfloat16)
     tm_part = lax.dynamic_update_slice(
         tm_part, fill_pair(rec_sum).reshape(width, own_width // 2), (0, 5 * own_width)
     )
-    for at, mix, grad in ((1, 3, g_recept), (2, 1, g_key), (3, 2, g_val), (4, 4, g_gate)):
-        tm_part = grad_into(mixes[mix], grad, tm_total, at * own_width, tm_part)
     tm_part, cm_pair, gated_rows = lax.optimization_barrier((tm_part, cm_pair, gated_rows))
     output = (resid + gated_rows.astype(jnp.float32)).astype(jnp.bfloat16)
     tm_pair = plane_scatter(tm_part)

time: 496 us -> 492 us (level)
  local copies, waits for them, and re-layouts: 35.1 us -> 29.3 us
    pallas_call x8 -> x3, Pallas kernels: 32.1 us -> 15.7 us  [grad_into(): pl.pallas_call(grad_kernel, grid=(width // GRAD_ROWS,), in_specs=specs, o...]
    pallas_call x0 -> x1, Pallas kernels: none -> 15 us  [grads_side_by_side(): pl.pallas_call(grads_kernel, grid=(len(lefts), blocks), in_specs=[left_sp...]
    unnamed x153 -> x137, local copies, waits for them, and re-layouts: 14.5 us -> 9.3 us
where the time goes in v5:
time: 492 us; the launch traced here: 484 us
  waiting for transfers between devices  175 us (36%)
  Pallas kernels  119 us (24%)
  other arithmetic  58.1 us (12%)
  starting transfers between devices  52.2 us (11%)
  matrix products  34.7 us (7%)
  local copies, waits for them, and re-layouts  29.3 us (6%)
  between operations  15.7 us (3%)
    ppermute x40, waiting for transfers between devices, swap(): return lax.ppermute(block, ALL, [(i, i ^ bit) for i in range(count)])  110 us
    all_gather x2, waiting for transfers between devices, plane_gather(): lax.all_gather(pair, 'seg', axis=0, tiled=True, axis_index_groups=plane_g...  50.3 us
    ppermute x40, starting transfers between devices, swap(): return lax.ppermute(block, ALL, [(i, i ^ bit) for i in range(count)])  46.2 us
    pallas_call x1, Pallas kernels, mixes_back(): pl.pallas_call(mixes_back_kernel, grid=(2, tiles), in_specs=[whole(g_key)...  25.8 us
    pallas_call x1, Pallas kernels, mixes_forward(): pl.pallas_call(mixes_forward_kernel, grid=(2, tiles), in_specs=[across(ro...  21.8 us
    pallas_call x1, Pallas kernels, wkv_backward(): pl.pallas_call(wkv_backward_kernel, grid=(chunks,), in_specs=[block] * 4...  21.4 us
    pallas_call x1, Pallas kernels, wkv_forward(): pl.pallas_call(wkv_forward_kernel, grid=(chunks,), in_specs=[block] * 4 +...  19.3 us
    dot_general x5, matrix products, product_lower(): return jnp.dot(left_arg, right_arg, preferred_element_type=jnp.float32)  18 us
  transfers between devices with their start and end apart: 45, of which 24 were waited for; matrix products, arithmetic and copies ran while one was open for 22% of the time, Pallas kernels for 23%

profile of v5, /device:TPU:1, one launch (start us, length us, event | category | flops | bytes accessed | tf_op | source)
XLA Modules:
  0.0 484.1 jit_solution(10684402925900276792)
XLA Ops:
  14.4 3.0 collective-permute-start.7
  20.2 5.7 %collective-permute-done.11 = bf16[64,512]{1,0:T(8,128)(2,1)S(1)} collective-permute-done((bf16[64,512]{1,0:T(8,128)(2,1)S(1)}, bf16[64,512]{1,0:T(8,128)(2,1)S(1)}, u32[]{:S(2)}, u32[]{:S(2)}) %collective-permute-start.11) | collective-permute-done | bytes 65568 | tf_op jit(solution)/shard_map/ppermute | solution.py:20
  34.6 10.5 %collective-permute-done.5 = bf16[128,512]{1,0:T(8,128)(2,1)S(1)} collective-permute-done((bf16[128,512]{1,0:T(8,128)(2,1)S(1)}, bf16[128,512]{1,0:T(8,128)(2,1)S(1)}, u32[]{:S(2)}, u32[]{:S(2)}) %collective-permute-start.5) | collective-permute-done | bytes 131104 | tf_op jit(solution)/shard_map/ppermute | solution.py:20
  45.2 3.6 collective-permute-done.6
  51.1 3.7 collective-permute-done.1
  54.8 4.9 %collective-permute-done = bf16[64,1792]{1,0:T(8,128)(2,1)S(1)} collective-permute-done((bf16[64,1792]{1,0:T(8,128)(2,1)S(1)}, bf16[64,1792]{1,0:T(8,128)(2,1)S(1)}, u32[]{:S(2)}, u32[]{:S(2)}) %collective-permute-start) | collective-permute-done | bytes 229408 | tf_op jit(solution)/shard_map/ppermute | solution.py:20
  64.5 4.6 fusion.6.unit_ref
  69.2 50.3 %all-gather.3.cloned.1.call-done.w_ref.down_ref.up_ref = bf16[2048,3072]{1,0:T(8,128)(2,1)} async-done(((bf16[128,3072]{1,0:T(8,128)(2,1)}), bf16[2048,3072]{1,0:T(8,128)(2,1)}) %all-gather.3.cloned.1.call-update) | async-done | bytes 12582928 | tf_op jit(solution)/shard_map/all_gather | solution.py:102
  123.0 2.9 collective-permute-start.12
  128.1 21.8 %mixes_forward.1 = (bf16[512,2048]{1,0:T(8,128)(2,1)}, bf16[512,2048]{1,0:T(8,128)(2,1)}, bf16[512,2048]{1,0:T(8,128)(2,1)}, bf16[512,2048]{1,0:T(8,128)(2,1)}, ...) custom-call(f32[512,2048]{1,0:T(8,128)} %fusion.6.unit_ref, ...), custom_call_target="tpu_custom_call" | custom-call | flops 1048576 | bytes 65536 | tf_op jit(solution)/shard_map/mixes_forward/pallas_call | solution.py:681
  151.1 19.3 %wkv_forward.1 = (bf16[512,512]{1,0:T(8,128)(2,1)S(1)}, f32[512,512]{1,0:T(8,128)S(1)}, f32[512,512]{1,0:T(8,128)S(1)}) custom-call(f32[512,512]{1,0:T(8,128)} %get-tuple-element.66.refs_0_, f32[512,512]{1,0:T(8,128)} %get-tuple-element.67.refs_1_, f32[512,512]{1,0:T(8,128)} %get-tuple-element.68.refs_2_, f32[512,512]{1,0:T(8,128)} %get-tuple-element.69.refs_3_, ...), custom_call_target="tpu_custom_call" | custom-call | flops 1048576 | bytes 65536 | tf_op jit(solution)/shard_map/wkv_forward/pallas_call | solution.py:379
  171.5 3.8 select_bitcast_fusion.4
  183.8 11.0 %collective-permute-done.14 = bf16[128,2048]{1,0:T(8,128)(2,1)S(1)} collective-permute-done((bf16[128,2048]{1,0:T(8,128)(2,1)S(1)}, bf16[128,2048]{1,0:T(8,128)(2,1)S(1)}, u32[]{:S(2)}, u32[]{:S(2)}) %collective-permute-start.14) | collective-permute-done | bytes 524320 | tf_op jit(solution)/shard_map/ppermute | solution.py:20
  197.1 11.2 %collective-permute-done.15 = bf16[128,2048]{1,0:T(8,128)(2,1)S(1)} collective-permute-done((bf16[128,2048]{1,0:T(8,128)(2,1)S(1)}, bf16[128,2048]{1,0:T(8,128)(2,1)S(1)}, u32[]{:S(2)}, u32[]{:S(2)}) %collective-permute-start.15) | collective-permute-done | bytes 524320 | tf_op jit(solution)/shard_map/ppermute | solution.py:20
  225.9 7.2 %multiply_convert_fusion.1 = (bf16[512,1792]{1,0:T(8,128)(2,1)S(1)}, bf16[512,1792]{1,0:T(8,128)(2,1)S(1)}) fusion(bf16[512,2048]{1,0:T(8,128)(2,1)S(1)} %get-tuple-element.157.left_ref, bf16[2048,3584]{1,0:T(8,128)(2,1)} %all-gather.5.cloned.1.call-done), kind=kOutput, calls=%fused_computation.23 | convolution fusion | flops 3761766400 | bytes 13107200 | tf_op jit(solution)/shard_map/dot_general | solution.py:173
  245.7 4.0 multiply_convert_fusion.right_ref
  249.7 6.3 %weight_grad.3.rest_0_ = bf16[2048,3584]{1,0:T(8,128)(2,1)} custom-call(bf16[512,2048]{1,0:T(8,128)(2,1)S(1)} %pad_maximum_fusion.5.left_ref, bf16[512,1792]{1,0:T(8,128)(2,1)S(1)} %get-tuple-element.252.right_ref), custom_call_target="tpu_custom_call" | custom-call | flops 1048576 | bytes 65536 | tf_op jit(solution)/shard_map/weight_grad/pallas_call | solution.py:536
  258.4 6.2 %weight_grad.4 = bf16[2048,3584]{1,0:T(8,128)(2,1)} custom-call(bf16[512,2048]{1,0:T(8,128)(2,1)S(1)} %get-tuple-element.157.left_ref, bf16[512,1792]{1,0:T(8,128)(2,1)S(1)} %multiply_convert_fusion.right_ref, bf16[2048,3584]{1,0:T(8,128)(2,1)} %weight_grad.3.rest_0_), custom_call_target="tpu_custom_call", output_to_operand_aliasing={{}: (2, {})} | custom-call | flops 1048576 | bytes 65536 | tf_op jit(solution)/shard_map/weight_grad/pallas_call | solution.py:536
  269.0 6.4 %fusion.2 = f32[512,2048]{1,0:T(8,128)S(1)} fusion(bf16[512,1792]{1,0:T(8,128)(2,1)S(1)} %copy-done.15, bf16[2048,3584]{1,0:T(8,128)(2,1)} %all-gather.5.cloned.1.call-done), kind=kOutput, calls=%fused_computation.2 | convolution fusion | flops 3758096384 | bytes 13369344 | tf_op jit(solution)/shard_map/te,de->td/dot_general | solution.py:181
  286.2 3.2 weight_grad.5
  289.4 8.8 %collective-permute-done.23 = bf16[128,2048]{1,0:T(8,128)(2,1)S(1)} collective-permute-done((bf16[128,2048]{1,0:T(8,128)(2,1)S(1)}, bf16[128,2048]{1,0:T(8,128)(2,1)S(1)}, u32[]{:S(2)}, u32[]{:S(2)}) %collective-permute-start.23) | collective-permute-done | bytes 524320 | tf_op jit(solution)/shard_map/ppermute | solution.py:20
  301.7 11.2 %collective-permute-done.24 = bf16[128,2048]{1,0:T(8,128)(2,1)S(1)} collective-permute-done((bf16[128,2048]{1,0:T(8,128)(2,1)S(1)}, bf16[128,2048]{1,0:T(8,128)(2,1)S(1)}, u32[]{:S(2)}, u32[]{:S(2)}) %collective-permute-start.24) | collective-permute-done | bytes 524320 | tf_op jit(solution)/shard_map/ppermute | solution.py:20
  322.8 3.3 fusion.74.refs_9_
  328.2 21.4 %wkv_backward.1 = (bf16[512,512]{1,0:T(8,128)(2,1)S(1)}, bf16[512,512]{1,0:T(8,128)(2,1)S(1)}, bf16[512,512]{1,0:T(8,128)(2,1)S(1)}, bf16[512,512]{1,0:T(8,128)(...) custom-call(f32[512,512]{1,0:T(8,128)S(1)} %copy-done.2, ...), custom_call_target="tpu_custom_call" | custom-call | flops 1048576 | bytes 65536 | tf_op jit(solution)/shard_map/wkv_backward/pallas_call | solution.py:484
  349.8 15.0 %time_mix_grads.1 = bf16[2048,2816]{1,0:T(8,128)(2,1)} custom-call(bf16[512,2048]{1,0:T(8,128)(2,1)S(1)} %pad_maximum_fusion.6.refs_0_, bf16[512,2048]{1,0:T(8,128)(2,1)S(1)} %copy-done.12, bf16[512,2048]{1,0:T(8,128)(2,1)S(1)} %copy-done.10, bf16[512,2048]{1,0:T(8,128)(2,1)S(1)} %copy-done.11, bf16[512,2048]{1,0:T(8,128)(2,1)S(1)} %copy-done.13, ...), custom_call_target="tpu_custom_call" | custom-call | flops 1048576 | bytes 65536 | tf_op jit(solution)/shard_map/time_mix_grads/pallas_call | solution.py:575
  370.4 25.8 %mixes_back.1 = (bf16[512,2048]{1,0:T(8,128)(2,1)}, bf16[2048,512]{1,0:T(8,128)(2,1)}) custom-call(bf16[512,512]{1,0:T(8,128)(2,1)} %copy-done.7, bf16[512,512]{1,0:T(8,128)(2,1)} %copy-done.8, bf16[512,512]{1,0:T(8,128)(2,1)} %copy-done.6, bf16[512,512]{1,0:T(8,128)(2,1)} %copy-done.9, bf16[512,256]{1,0:T(8,128)(2,1)} %fusion.28.gd_ref, ...), custom_call_target="tpu_custom_call" | custom-call | flops 1048576 | bytes 65536 | tf_op jit(solution)/shard_map/mixes_back/pallas_call | solution.py:792
  407.6 12.4 %collective-permute-done.31 = bf16[16,2,16,512]{3,2,1,0:T(8,128)(2,1)S(1)} collective-permute-done((bf16[16,2,16,512]{3,2,1,0:T(8,128)(2,1)S(1)}, bf16[16,2,16,512]{3,2,1,0:T(8,128)(2,1)S(1)}, u32[]{:S(2)}, u32[]{:S(2)}) %collective-permute-start.31) | collective-permute-done | bytes 524320 | tf_op jit(solution)/shard_map/ppermute | solution.py:20
  422.1 6.5 %collective-permute-done.34 = bf16[16,16,512]{2,1,0:T(8,128)(2,1)S(1)} collective-permute-done((bf16[16,16,512]{2,1,0:T(8,128)(2,1)S(1)}, bf16[16,16,512]{2,1,0:T(8,128)(2,1)S(1)}, u32[]{:S(2)}, u32[]{:S(2)}) %collective-permute-start.34) | collective-permute-done | bytes 262176 | tf_op jit(solution)/shard_map/ppermute | solution.py:20
  429.5 5.9 %all-to-all-start = ((bf16[16,16,512]{2,1,0:T(8,128)(2,1)}), bf16[16,16,512]{2,1,0:T(8,128)(2,1)S(1)}, u32[]{:S(2)}, u32[]{:S(2)}) async-start(bf16[16,16,512]{2,1,0:T(8,128)(2,1)} %fusion.48), calls=%async_computation.1 | async-start | bytes 524288 | tf_op jit(solution)/shard_map/all_to_all | solution.py:225
  437.7 5.3 %all-to-all-done = bf16[16,16,512]{2,1,0:T(8,128)(2,1)S(1)} async-done(((bf16[16,16,512]{2,1,0:T(8,128)(2,1)}), bf16[16,16,512]{2,1,0:T(8,128)(2,1)S(1)}, u32[]{:S(2)}, u32[]{:S(2)}) %all-to-all-start) | async-done | bytes 262176 | tf_op jit(solution)/shard_map/all_to_all | solution.py:225
  450.4 9.5 %reduce-scatter.5.cloned.1.call-done = bf16[128,2816]{1,0:T(8,128)(2,1)} async-done(((bf16[2048,2816]{1,0:T(8,128)(2,1)}), bf16[128,2816]{1,0:T(8,128)(2,1)}) %reduce-scatter.5.cloned.1.call-update) | async-done | bytes 720912 | tf_op jit(solution)/shard_map/reduce_scatter | solution.py:113
  468.4 7.1 %collective-permute-done.35 = bf16[64,2560]{1,0:T(8,128)(2,1)S(1)} collective-permute-done((bf16[64,2560]{1,0:T(8,128)(2,1)S(1)}, bf16[64,2560]{1,0:T(8,128)(2,1)S(1)}, u32[]{:S(2)}, u32[]{:S(2)}) %collective-permute-start.35) | collective-permute-done | bytes 327712 | tf_op jit(solution)/shard_map/ppermute | solution.py:20
  (360 shorter events, 146.5 us)
Async XLA Ops:
  7.2 112.4 %all-gather.3.cloned.1.call-start = ((), (), s32[]{:S(2)}) async-start(), calls=%async_computation.3 | async-start | bytes 13369344 | tf_op jit(solution)/shard_map/all_gather | solution.py:102
  9.6 10.4 %collective-permute-start.8 = (bf16[16,1024]{1,0:T(8,128)(2,1)S(1)}, bf16[16,1024]{1,0:T(8,128)(2,1)S(1)}, u32[]{:S(2)}, u32[]{:S(2)}) collective-permute-start(bf16[16,1024]{1,0:T(8,128)(2,1)S(1)} %concatenate.95), channel_id=1, source_target_pairs={{0,1},{1,0},{2,3},{3,2},{4,5},{5,4},{6,7},{7,6},{8,9},{9,8},{10,11... | collective-permute-start | bytes 98312 | tf_op jit(solution)/shard_map/ppermute | solution.py:20
  11.9 8.2 %collective-permute-start.9 = (bf16[16,1024]{1,0:T(8,128)(2,1)S(1)}, bf16[16,1024]{1,0:T(8,128)(2,1)S(1)}, u32[]{:S(2)}, u32[]{:S(2)}) collective-permute-start(bf16[16,1024]{1,0:T(8,128)(2,1)S(1)} %concatenate.96), channel_id=1, source_target_pairs={{0,2},{1,3},{2,0},{3,1},{4,6},{5,7},{6,4},{7,5},{8,10},{9,11},{10,... | collective-permute-start | bytes 98312 | tf_op jit(solution)/shard_map/ppermute | solution.py:20
  14.4 11.6 %collective-permute-start.7 = (bf16[4,64,512]{2,1,0:T(8,128)(2,1)}, bf16[4,64,512]{2,1,0:T(8,128)(2,1)S(1)}, u32[]{:S(2)}, u32[]{:S(2)}) collective-permute-start(bf16[4,64,512]{2,1,0:T(8,128)(2,1)} %param.15), channel_id=1, source_target_pairs={{0,4},{1,5},{2,6},{3,7},{4,0},{5,1},{6,2},{7,3},{8,12},{9,13},{10,... | collective-permute-start | bytes 786440 | tf_op jit(solution)/shard_map/ppermute | solution.py:20
  27.1 197.6 %all-gather.5.cloned.1.call-start = ((), (), s32[]{:S(2)}) async-start(), calls=%async_computation.4 | async-start | bytes 15597568 | tf_op jit(solution)/shard_map/all_gather | solution.py:102
  27.9 6.3 %collective-permute-start.4 = (bf16[128,512]{1,0:T(8,128)(2,1)}, bf16[128,512]{1,0:T(8,128)(2,1)S(1)}, u32[]{:S(2)}, u32[]{:S(2)}) collective-permute-start(bf16[128,512]{1,0:T(8,128)(2,1)} %get-tuple-element.218), channel_id=1, source_target_pairs={{0,1},{1,0},{2,3},{3,2},{4,5},{5,4},{6,7},{7,6},{8,9},{9,8},{10,11... | collective-permute-start | bytes 393224 | tf_op jit(solution)/shard_map/ppermute | solution.py:20
  28.7 20.1 %collective-permute-start.2 = (bf16[128,2048]{1,0:T(8,128)(2,1)S(1)}, bf16[128,2048]{1,0:T(8,128)(2,1)S(1)}, u32[]{:S(2)}, u32[]{:S(2)}) collective-permute-start(bf16[128,2048]{1,0:T(8,128)(2,1)S(1)} %copy-done.31), channel_id=1, source_target_pairs={{0,2},{1,3},{2,0},{3,1},{4,6},{5,7},{6,4},{7,5},{8,10},{9,11},{10,... | collective-permute-start | bytes 1572872 | tf_op jit(solution)/shard_map/ppermute | solution.py:20
  29.6 15.6 %collective-permute-start.5 = (bf16[128,512]{1,0:T(8,128)(2,1)S(1)}, bf16[128,512]{1,0:T(8,128)(2,1)S(1)}, u32[]{:S(2)}, u32[]{:S(2)}) collective-permute-start(bf16[128,512]{1,0:T(8,128)(2,1)S(1)} %get-tuple-element.217), channel_id=1, source_target_pairs={{0,2},{1,3},{2,0},{3,1},{4,6},{5,7},{6,4},{7,5},{8,10},{9,11},{10,... | collective-permute-start | bytes 393224 | tf_op jit(solution)/shard_map/ppermute | solution.py:20
  30.2 18.6 %collective-permute-start.6 = (bf16[128,512]{1,0:T(8,128)(2,1)S(1)}, bf16[128,512]{1,0:T(8,128)(2,1)S(1)}, u32[]{:S(2)}, u32[]{:S(2)}) collective-permute-start(bf16[128,512]{1,0:T(8,128)(2,1)S(1)} %get-tuple-element.216), channel_id=1, source_target_pairs={{0,3},{1,2},{2,1},{3,0},{4,7},{5,6},{6,5},{7,4},{8,11},{9,10},{10,... | collective-permute-start | bytes 393224 | tf_op jit(solution)/shard_map/ppermute | solution.py:20
  31.5 23.3 %collective-permute-start.1 = (bf16[1792,64]{0,1:T(8,128)(2,1)S(1)}, bf16[1792,64]{0,1:T(8,128)(2,1)S(1)}, u32[]{:S(2)}, u32[]{:S(2)}) collective-permute-start(bf16[1792,64]{0,1:T(8,128)(2,1)S(1)} %copy-done.64), channel_id=1, source_target_pairs={{0,4},{1,5},{2,6},{3,7},{4,0},{5,1},{6,2},{7,3},{8,12},{9,13},{10,... | collective-permute-start | bytes 688136 | tf_op jit(solution)/shard_map/ppermute | solution.py:20
  34.2 25.5 %collective-permute-start = (bf16[64,1792]{1,0:T(8,128)(2,1)S(1)}, bf16[64,1792]{1,0:T(8,128)(2,1)S(1)}, u32[]{:S(2)}, u32[]{:S(2)}) collective-permute-start(bf16[64,1792]{1,0:T(8,128)(2,1)S(1)} %copy-done.65), channel_id=1, source_target_pairs={{0,4},{1,5},{2,6},{3,7},{4,0},{5,1},{6,2},{7,3},{8,12},{9,13},{10,... | collective-permute-start | bytes 688136 | tf_op jit(solution)/shard_map/ppermute | solution.py:20
  49.9 11.0 %collective-permute-start.3 = (bf16[2,128,2048]{2,1,0:T(8,128)(2,1)}, bf16[2,128,2048]{2,1,0:T(8,128)(2,1)}, u32[]{:S(2)}, u32[]{:S(2)}) collective-permute-start(bf16[2,128,2048]{2,1,0:T(8,128)(2,1)} %pad_maximum_fusion.7), channel_id=1, source_target_pairs={{0,1},{1,0},{2,3},{3,2},{4,5},{5,4},{6,7},{7,6},{8,9},{9,8},{10,11... | collective-permute-start | bytes 3145736 | tf_op jit(solution)/shard_map/ppermute | solution.py:20
  69.1 299.1 %reduce-scatter.3.cloned.1.call-start = ((), (), s32[]{:S(2)}) async-start(), calls=%async_computation.5 | async-start | bytes 15597568 | tf_op jit(solution)/shard_map/reduce_scatter | solution.py:113
  123.0 48.5 %collective-permute-start.12 = (bf16[16,64,1024]{2,1,0:T(8,128)(2,1)}, bf16[16,64,1024]{2,1,0:T(8,128)(2,1)}, u32[]{:S(2)}, u32[]{:S(2)}) collective-permute-start(bf16[16,64,1024]{2,1,0:T(8,128)(2,1)} %pad_maximum_fusion.1), channel_id=1, source_target_pairs={{0,4},{1,5},{2,6},{3,7},{4,0},{5,1},{6,2},{7,3},{8,12},{9,13},{10,... | collective-permute-start | bytes 6291464 | tf_op jit(solution)/shard_map/ppermute | solution.py:20
  181.5 13.3 %collective-permute-start.14 = (bf16[128,2048]{1,0:T(8,128)(2,1)S(1)}, bf16[128,2048]{1,0:T(8,128)(2,1)S(1)}, u32[]{:S(2)}, u32[]{:S(2)}) collective-permute-start(bf16[128,2048]{1,0:T(8,128)(2,1)S(1)} %fusion.43), channel_id=1, source_target_pairs={{0,2},{1,3},{2,0},{3,1},{4,6},{5,7},{6,4},{7,5},{8,10},{9,11},{10,... | collective-permute-start | bytes 1572872 | tf_op jit(solution)/shard_map/ppermute | solution.py:20
  195.8 12.5 %collective-permute-start.15 = (bf16[128,2048]{1,0:T(8,128)(2,1)S(1)}, bf16[128,2048]{1,0:T(8,128)(2,1)S(1)}, u32[]{:S(2)}, u32[]{:S(2)}) collective-permute-start(bf16[128,2048]{1,0:T(8,128)(2,1)S(1)} %add_convert_fusion.5), channel_id=1, source_target_pairs={{0,2},{1,3},{2,0},{3,1},{4,6},{5,7},{6,4},{7,5},{8,10},{9,11},{10,... | collective-permute-start | bytes 1572872 | tf_op jit(solution)/shard_map/ppermute | solution.py:20
  224.7 13.7 %collective-permute-start.18 = (bf16[512,512]{1,0:T(8,128)(2,1)}, bf16[512,512]{1,0:T(8,128)(2,1)S(1)}, u32[]{:S(2)}, u32[]{:S(2)}) collective-permute-start(bf16[512,512]{1,0:T(8,128)(2,1)} %get-tuple-element.75), channel_id=1, source_target_pairs={{0,2},{1,3},{2,0},{3,1},{4,6},{5,7},{6,4},{7,5},{8,10},{9,11},{10,... | collective-permute-start | bytes 1572872 | tf_op jit(solution)/shard_map/ppermute | solution.py:20
  244.3 13.4 %collective-permute-start.20 = (bf16[512,512]{1,0:T(8,128)(2,1)S(1)}, bf16[512,512]{1,0:T(8,128)(2,1)S(1)}, u32[]{:S(2)}, u32[]{:S(2)}) collective-permute-start(bf16[512,512]{1,0:T(8,128)(2,1)S(1)} %add_convert_fusion.4), channel_id=1, source_target_pairs={{0,2},{1,3},{2,0},{3,1},{4,6},{5,7},{6,4},{7,5},{8,10},{9,11},{10,... | collective-permute-start | bytes 1572872 | tf_op jit(solution)/shard_map/ppermute | solution.py:20
  264.7 195.3 %reduce-scatter.5.cloned.1.call-start = ((), (), s32[]{:S(2)}) async-start(), calls=%async_computation.6 | async-start | bytes 12255232 | tf_op jit(solution)/shard_map/reduce_scatter | solution.py:113
  284.9 13.3 %collective-permute-start.23 = (bf16[128,2048]{1,0:T(8,128)(2,1)S(1)}, bf16[128,2048]{1,0:T(8,128)(2,1)S(1)}, u32[]{:S(2)}, u32[]{:S(2)}) collective-permute-start(bf16[128,2048]{1,0:T(8,128)(2,1)S(1)} %fusion.44), channel_id=1, source_target_pairs={{0,2},{1,3},{2,0},{3,1},{4,6},{5,7},{6,4},{7,5},{8,10},{9,11},{10,... | collective-permute-start | bytes 1572872 | tf_op jit(solution)/shard_map/ppermute | solution.py:20
  300.5 12.4 %collective-permute-start.24 = (bf16[128,2048]{1,0:T(8,128)(2,1)S(1)}, bf16[128,2048]{1,0:T(8,128)(2,1)S(1)}, u32[]{:S(2)}, u32[]{:S(2)}) collective-permute-start(bf16[128,2048]{1,0:T(8,128)(2,1)S(1)} %get-tuple-element.150), channel_id=1, source_target_pairs={{0,2},{1,3},{2,0},{3,1},{4,6},{5,7},{6,4},{7,5},{8,10},{9,11},{10,... | collective-permute-start | bytes 1572872 | tf_op jit(solution)/shard_map/ppermute | solution.py:20
  317.6 47.3 %collective-permute-start.26 = (bf16[16,64,512]{2,1,0:T(8,128)(2,1)}, bf16[16,64,512]{2,1,0:T(8,128)(2,1)}, u32[]{:S(2)}, u32[]{:S(2)}) collective-permute-start(bf16[16,64,512]{2,1,0:T(8,128)(2,1)} %select_bitcast_fusion.1), channel_id=1, source_target_pairs={{0,4},{1,5},{2,6},{3,7},{4,0},{5,1},{6,2},{7,3},{8,12},{9,13},{10,... | collective-permute-start | bytes 3145736 | tf_op jit(solution)/shard_map/ppermute | solution.py:20
  321.8 43.0 %collective-permute-start.27 = (bf16[128,512]{1,0:T(8,128)(2,1)S(1)}, bf16[128,512]{1,0:T(8,128)(2,1)S(1)}, u32[]{:S(2)}, u32[]{:S(2)}) collective-permute-start(bf16[128,512]{1,0:T(8,128)(2,1)S(1)} %get-tuple-element.212), channel_id=1, source_target_pairs={{0,1},{1,0},{2,3},{3,2},{4,5},{5,4},{6,7},{7,6},{8,9},{9,8},{10,11... | collective-permute-start | bytes 393224 | tf_op jit(solution)/shard_map/ppermute | solution.py:20
  322.5 42.3 %collective-permute-start.28 = (bf16[128,512]{1,0:T(8,128)(2,1)S(1)}, bf16[128,512]{1,0:T(8,128)(2,1)S(1)}, u32[]{:S(2)}, u32[]{:S(2)}) collective-permute-start(bf16[128,512]{1,0:T(8,128)(2,1)S(1)} %get-tuple-element.211), channel_id=1, source_target_pairs={{0,2},{1,3},{2,0},{3,1},{4,6},{5,7},{6,4},{7,5},{8,10},{9,11},{10,... | collective-permute-start | bytes 393224 | tf_op jit(solution)/shard_map/ppermute | solution.py:20
  326.2 38.7 %collective-permute-start.29 = (bf16[128,512]{1,0:T(8,128)(2,1)S(1)}, bf16[128,512]{1,0:T(8,128)(2,1)S(1)}, u32[]{:S(2)}, u32[]{:S(2)}) collective-permute-start(bf16[128,512]{1,0:T(8,128)(2,1)S(1)} %get-tuple-element.210), channel_id=1, source_target_pairs={{0,3},{1,2},{2,1},{3,0},{4,7},{5,6},{6,5},{7,4},{8,11},{9,10},{10,... | collective-permute-start | bytes 393224 | tf_op jit(solution)/shard_map/ppermute | solution.py:20
  406.7 13.3 %collective-permute-start.31 = (bf16[16,2,16,512]{3,2,1,0:T(8,128)(2,1)S(1)}, bf16[16,2,16,512]{3,2,1,0:T(8,128)(2,1)S(1)}, u32[]{:S(2)}, u32[]{:S(2)}) collective-permute-start(bf16[16,2,16,512]{3,2,1,0:T(8,128)(2,1)S(1)} %fusion.45), channel_id=1, source_target_pairs={{0,2},{1,3},{2,0},{3,1},{4,6},{5,7},{6,4},{7,5},{8,10},{9,11},{10,... | collective-permute-start | bytes 1572872 | tf_op jit(solution)/shard_map/ppermute | solution.py:20
  420.4 8.3 %collective-permute-start.34 = (bf16[16,16,512]{2,1,0:T(8,128)(2,1)S(1)}, bf16[16,16,512]{2,1,0:T(8,128)(2,1)S(1)}, u32[]{:S(2)}, u32[]{:S(2)}) collective-permute-start(bf16[16,16,512]{2,1,0:T(8,128)(2,1)S(1)} %fusion.49), channel_id=1, source_target_pairs={{0,4},{1,5},{2,6},{3,7},{4,0},{5,1},{6,2},{7,3},{8,12},{9,13},{10,... | collective-permute-start | bytes 786440 | tf_op jit(solution)/shard_map/ppermute | solution.py:20
  421.3 23.0 %collective-permute-start.33 = (bf16[128,2048]{1,0:T(8,128)(2,1)}, bf16[128,2048]{1,0:T(8,128)(2,1)}, u32[]{:S(2)}, u32[]{:S(2)}) collective-permute-start(bf16[128,2048]{1,0:T(8,128)(2,1)} %fusion.46), channel_id=1, source_target_pairs={{0,2},{1,3},{2,0},{3,1},{4,6},{5,7},{6,4},{7,5},{8,10},{9,11},{10,... | collective-permute-start | bytes 1572872 | tf_op jit(solution)/shard_map/ppermute | solution.py:20
  429.5 13.5 %all-to-all-start = ((bf16[16,16,512]{2,1,0:T(8,128)(2,1)}), bf16[16,16,512]{2,1,0:T(8,128)(2,1)S(1)}, u32[]{:S(2)}, u32[]{:S(2)}) async-start(bf16[16,16,512]{2,1,0:T(8,128)(2,1)} %fusion.48), calls=%async_computation.1 | async-start | bytes 524288 | tf_op jit(solution)/shard_map/all_to_all | solution.py:225
  437.4 10.9 %collective-permute-start.39 = (bf16[64,3584]{1,0:T(8,128)(2,1)}, bf16[64,3584]{1,0:T(8,128)(2,1)}, u32[]{:S(2)}, u32[]{:S(2)}) collective-permute-start(bf16[64,3584]{1,0:T(8,128)(2,1)} %broadcast_select_fusion.26), channel_id=1, source_target_pairs={{0,4},{1,5},{2,6},{3,7},{4,0},{5,1},{6,2},{7,3},{8,12},{9,13},{10,... | collective-permute-start | bytes 1376264 | tf_op jit(solution)/shard_map/ppermute | solution.py:20
  460.9 6.7 %collective-permute-start.36 = (bf16[16,512]{1,0:T(8,128)(2,1)S(1)}, bf16[16,512]{1,0:T(8,128)(2,1)S(1)}, u32[]{:S(2)}, u32[]{:S(2)}) collective-permute-start(bf16[16,512]{1,0:T(8,128)(2,1)S(1)} %get-tuple-element.236), channel_id=1, source_target_pairs={{0,1},{1,0},{2,3},{3,2},{4,5},{5,4},{6,7},{7,6},{8,9},{9,8},{10,11... | collective-permute-start | bytes 49160 | tf_op jit(solution)/shard_map/ppermute | solution.py:20
  464.7 10.7 %collective-permute-start.35 = (bf16[64,2560]{1,0:T(8,128)(2,1)S(1)}, bf16[64,2560]{1,0:T(8,128)(2,1)S(1)}, u32[]{:S(2)}, u32[]{:S(2)}) collective-permute-start(bf16[64,2560]{1,0:T(8,128)(2,1)S(1)} %broadcast_select_fusion.29), channel_id=1, source_target_pairs={{0,4},{1,5},{2,6},{3,7},{4,0},{5,1},{6,2},{7,3},{8,12},{9,13},{10,... | collective-permute-start | bytes 983048 | tf_op jit(solution)/shard_map/ppermute | solution.py:20
  (80 other events, 504.9 us)
Sparse Core Ops, SparseCore 0:
  27.2 92.2 all-gather.2
  121.7 100.3 all-gather.4
  264.8 100.9 reduce-scatter.2
  369.1 90.7 reduce-scatter.4

commit v6 on v5

--- a/solution.py
+++ b/solution.py
@@ -289,27 +289,29 @@
 
 def piece_factors(run, before):
     rows = iota2((CHUNK, PACK), 0)
-    t, i = rows, iota2((CHUNK, PACK), 1) & (CHUNK - 1)
-    apart = t ^ i
+    apart = rows ^ (iota2((CHUNK, PACK), 1) & (CHUNK - 1))
     levels = []
-    for half in (32, 16):
+    for half in (32, 16, 8, 4, 2, 1):
         upper = (rows & half) != 0
-        reference = jnp.broadcast_to(row_of(run, half - 1), run.shape)
-        for start in range(2 * half, CHUNK, 2 * half):
-            here = jnp.broadcast_to(row_of(run, start + half - 1), run.shape)
-            reference = jnp.where(rows >= start, here, reference)
-        scale = jnp.exp(jnp.where(upper, before - reference, reference - run))
+        if half == 1:
+            scale = jnp.ones_like(run)
+        else:
+            if half == 2:
+                reference = run
+                for row, shift in ((0, CHUNK - 1), (2, 1), (3, 2)):
+                    reference = jnp.where((rows & 3) == row, pltpu.roll(run, shift, 0), reference)
+            else:
+                reference = jnp.broadcast_to(row_of(run, half - 1), run.shape)
+                for start in range(2 * half, CHUNK, 2 * half):
+                    here = jnp.broadcast_to(row_of(run, start + half - 1), run.shape)
+                    reference = jnp.where(rows >= start, here, reference)
+            scale = jnp.exp(jnp.minimum(jnp.where(upper, before - reference, reference - run), 0.0))
         pairs = (apart < 2 * half) & upper & ((apart & half) != 0)
         levels.append((jnp.where(upper, scale, 0.0), jnp.where(upper, 0.0, scale), pairs))
-    reference = jnp.broadcast_to(row_of(run, 7), run.shape)
-    for start in range(16, CHUNK, 16):
-        here = jnp.broadcast_to(row_of(run, start + 7), run.shape)
-        reference = jnp.where(rows >= start, here, reference)
-    pairs = (apart < 16) & (t > i)
-    to_row = jnp.exp(jnp.minimum(before - reference, 80.0))
-    to_prior = jnp.exp(jnp.minimum(reference - run, 80.0))
-    levels.append((to_row, to_prior, pairs))
     return levels
+
+
+NOTHING = -104.0
 
 
 def lower_ones():
@@ -318,8 +320,9 @@
 
 def decay_of(low_ref, up_ref, par_ref):
     log_decay = -jnp.exp(par_ref[0:1] + mxu(low_ref[...], up_ref[...], NT))
-    run = run_sum(lower_ones(), log_decay)
-    return log_decay, run, run - log_decay
+    kept = jnp.maximum(log_decay, NOTHING)
+    run = run_sum(lower_ones(), kept)
+    return jnp.where(log_decay <= NOTHING, 0.0, log_decay), run, run - kept
 
 
 def unit_heads(wkv, ones):
@@ -441,19 +444,25 @@
     score = jnp.zeros((CHUNK, PACK), jnp.float32)
     from_start = jnp.exp(before)
     g_r = from_start * mxu(g_out, start, NN)
+    g_before = r * g_r
     to_end = jnp.exp(last - run)
     g_end = to_end * mxu(v, end_grad, NN)
     g_k = g_end
+    g_after = k * g_end
     for to_row, to_prior, pairs in piece_factors(run, before):
         r_level = (r * to_row).astype(jnp.bfloat16)
-        k_level = spread(k * to_prior, ones).astype(jnp.bfloat16)
+        k_rows = (k * to_prior).astype(jnp.bfloat16)
+        k_level = spread(k_rows.astype(jnp.float32), ones).astype(jnp.bfloat16)
         score = jnp.where(pairs, mxu(r_level, k_level, NT), score)
         g_level = jnp.where(pairs, g_score, 0.0).astype(jnp.bfloat16)
-        g_r = g_r + to_row * mxu(g_level, k_level, NN)
-        g_k = g_k + to_prior * fold(mxu(g_level, r_level, TN), ones)
+        g_rows = mxu(g_level, k_level, NN)
+        g_prior = fold(mxu(g_level, r_level, TN), ones)
+        g_r = g_r + to_row * g_rows
+        g_k = g_k + to_prior * g_prior
+        g_before = g_before + r_level.astype(jnp.float32) * g_rows
+        g_after = g_after + k_rows.astype(jnp.float32) * g_prior
     g_v = fold(mxu(score, g_out, TN), ones) + mxu(k * to_end, end_grad, NT)
-    g_before = r * g_r
-    g_run = g_before - k * g_k
+    g_run = g_before - g_after
     g_last = jnp.sum(k * g_end, axis=0, keepdims=True) + jnp.exp(last) * jnp.sum(
         start * end_grad, axis=0, keepdims=True
     )

time: 492 us -> 496 us (level)
  Pallas kernels: 119 us -> 126 us
    pallas_call x1, Pallas kernels: 21.4 us -> 26.9 us  [wkv_backward(): pl.pallas_call(wkv_backward_kernel, grid=(chunks,), in_specs=[block] * 4...]
  transfers between devices with their start and end apart: 45 -> 45, of which waited for: 24 -> 23; matrix products, arithmetic and copies ran while one was open for 22% -> 22% of each run, Pallas kernels for 23% -> 25%
where the time goes in v6:
time: 496 us; the launch traced here: 488 us
  waiting for transfers between devices  174 us (35%)
  Pallas kernels  126 us (25%)
  other arithmetic  59.1 us (12%)
  starting transfers between devices  48.8 us (10%)
  matrix products  34.7 us (7%)
  local copies, waits for them, and re-layouts  29.6 us (6%)
  between operations  15.7 us (3%)
    ppermute x40, waiting for transfers between devices, swap(): return lax.ppermute(block, ALL, [(i, i ^ bit) for i in range(count)])  111 us
    all_gather x2, waiting for transfers between devices, plane_gather(): lax.all_gather(pair, 'seg', axis=0, tiled=True, axis_index_groups=plane_g...  50.3 us
    ppermute x40, starting transfers between devices, swap(): return lax.ppermute(block, ALL, [(i, i ^ bit) for i in range(count)])  43.2 us
    pallas_call x1, Pallas kernels, wkv_backward(): pl.pallas_call(wkv_backward_kernel, grid=(chunks,), in_specs=[block] * 4...  26.9 us
    pallas_call x1, Pallas kernels, mixes_back(): pl.pallas_call(mixes_back_kernel, grid=(2, tiles), in_specs=[whole(g_key)...  25.8 us
    pallas_call x1, Pallas kernels, mixes_forward(): pl.pallas_call(mixes_forward_kernel, grid=(2, tiles), in_specs=[across(ro...  21.8 us
    pallas_call x1, Pallas kernels, wkv_forward(): pl.pallas_call(wkv_forward_kernel, grid=(chunks,), in_specs=[block] * 4 +...  21 us
    dot_general x5, matrix products, product_lower(): return jnp.dot(left_arg, right_arg, preferred_element_type=jnp.float32)  18 us
  transfers between devices with their start and end apart: 45, of which 23 were waited for; matrix products, arithmetic and copies ran while one was open for 22% of the time, Pallas kernels for 25%

profile of v6, /device:TPU:1, one launch (start us, length us, event | category | flops | bytes accessed | tf_op | source)
XLA Modules:
  0.0 487.9 jit_solution(5177423830031742632)
XLA Ops:
  14.4 3.0 collective-permute-start.7
  20.2 5.7 %collective-permute-done.11 = bf16[64,512]{1,0:T(8,128)(2,1)S(1)} collective-permute-done((bf16[64,512]{1,0:T(8,128)(2,1)S(1)}, bf16[64,512]{1,0:T(8,128)(2,1)S(1)}, u32[]{:S(2)}, u32[]{:S(2)}) %collective-permute-start.11) | collective-permute-done | bytes 65568 | tf_op jit(solution)/shard_map/ppermute | solution.py:20
  34.6 10.5 %collective-permute-done.5 = bf16[128,512]{1,0:T(8,128)(2,1)S(1)} collective-permute-done((bf16[128,512]{1,0:T(8,128)(2,1)S(1)}, bf16[128,512]{1,0:T(8,128)(2,1)S(1)}, u32[]{:S(2)}, u32[]{:S(2)}) %collective-permute-start.5) | collective-permute-done | bytes 131104 | tf_op jit(solution)/shard_map/ppermute | solution.py:20
  45.2 3.6 collective-permute-done.6
  51.1 3.7 collective-permute-done.1
  54.8 4.9 %collective-permute-done = bf16[64,1792]{1,0:T(8,128)(2,1)S(1)} collective-permute-done((bf16[64,1792]{1,0:T(8,128)(2,1)S(1)}, bf16[64,1792]{1,0:T(8,128)(2,1)S(1)}, u32[]{:S(2)}, u32[]{:S(2)}) %collective-permute-start) | collective-permute-done | bytes 229408 | tf_op jit(solution)/shard_map/ppermute | solution.py:20
  64.5 4.6 fusion.6.unit_ref
  69.2 50.3 %all-gather.3.cloned.1.call-done.w_ref.down_ref.up_ref = bf16[2048,3072]{1,0:T(8,128)(2,1)} async-done(((bf16[128,3072]{1,0:T(8,128)(2,1)}), bf16[2048,3072]{1,0:T(8,128)(2,1)}) %all-gather.3.cloned.1.call-update) | async-done | bytes 12582928 | tf_op jit(solution)/shard_map/all_gather | solution.py:102
  123.0 2.9 collective-permute-start.12
  128.1 21.8 %mixes_forward.1 = (bf16[512,2048]{1,0:T(8,128)(2,1)}, bf16[512,2048]{1,0:T(8,128)(2,1)}, bf16[512,2048]{1,0:T(8,128)(2,1)}, bf16[512,2048]{1,0:T(8,128)(2,1)}, ...) custom-call(f32[512,2048]{1,0:T(8,128)} %fusion.6.unit_ref, ...), custom_call_target="tpu_custom_call" | custom-call | flops 1048576 | bytes 65536 | tf_op jit(solution)/shard_map/mixes_forward/pallas_call | solution.py:690
  151.1 21.0 %wkv_forward.1 = (bf16[512,512]{1,0:T(8,128)(2,1)S(1)}, f32[512,512]{1,0:T(8,128)S(1)}, f32[512,512]{1,0:T(8,128)S(1)}) custom-call(f32[512,512]{1,0:T(8,128)} %get-tuple-element.66.refs_0_, f32[512,512]{1,0:T(8,128)} %get-tuple-element.67.refs_1_, f32[512,512]{1,0:T(8,128)} %get-tuple-element.68.refs_2_, f32[512,512]{1,0:T(8,128)} %get-tuple-element.69.refs_3_, ...), custom_call_target="tpu_custom_call" | custom-call | flops 1048576 | bytes 65536 | tf_op jit(solution)/shard_map/wkv_forward/pallas_call | solution.py:382
  172.2 4.8 select_bitcast_fusion.4
  184.2 11.6 %collective-permute-done.14 = bf16[128,2048]{1,0:T(8,128)(2,1)S(1)} collective-permute-done((bf16[128,2048]{1,0:T(8,128)(2,1)S(1)}, bf16[128,2048]{1,0:T(8,128)(2,1)S(1)}, u32[]{:S(2)}, u32[]{:S(2)}) %collective-permute-start.14) | collective-permute-done | bytes 524320 | tf_op jit(solution)/shard_map/ppermute | solution.py:20
  197.4 11.9 %collective-permute-done.15 = bf16[128,2048]{1,0:T(8,128)(2,1)S(1)} collective-permute-done((bf16[128,2048]{1,0:T(8,128)(2,1)S(1)}, bf16[128,2048]{1,0:T(8,128)(2,1)S(1)}, u32[]{:S(2)}, u32[]{:S(2)}) %collective-permute-start.15) | collective-permute-done | bytes 524320 | tf_op jit(solution)/shard_map/ppermute | solution.py:20
  226.3 7.2 %multiply_convert_fusion.1 = (bf16[512,1792]{1,0:T(8,128)(2,1)S(1)}, bf16[512,1792]{1,0:T(8,128)(2,1)S(1)}) fusion(bf16[512,2048]{1,0:T(8,128)(2,1)S(1)} %get-tuple-element.157.left_ref, bf16[2048,3584]{1,0:T(8,128)(2,1)} %all-gather.5.cloned.1.call-done), kind=kOutput, calls=%fused_computation.23 | convolution fusion | flops 3761766400 | bytes 13107200 | tf_op jit(solution)/shard_map/dot_general | solution.py:173
  246.0 4.0 multiply_convert_fusion.right_ref
  250.0 6.3 %weight_grad.3.rest_0_ = bf16[2048,3584]{1,0:T(8,128)(2,1)} custom-call(bf16[512,2048]{1,0:T(8,128)(2,1)S(1)} %pad_maximum_fusion.5.left_ref, bf16[512,1792]{1,0:T(8,128)(2,1)S(1)} %get-tuple-element.252.right_ref), custom_call_target="tpu_custom_call" | custom-call | flops 1048576 | bytes 65536 | tf_op jit(solution)/shard_map/weight_grad/pallas_call | solution.py:545
  259.4 6.2 %weight_grad.4 = bf16[2048,3584]{1,0:T(8,128)(2,1)} custom-call(bf16[512,2048]{1,0:T(8,128)(2,1)S(1)} %get-tuple-element.157.left_ref, bf16[512,1792]{1,0:T(8,128)(2,1)S(1)} %multiply_convert_fusion.right_ref, bf16[2048,3584]{1,0:T(8,128)(2,1)} %weight_grad.3.rest_0_), custom_call_target="tpu_custom_call", output_to_operand_aliasing={{}: (2, {})} | custom-call | flops 1048576 | bytes 65536 | tf_op jit(solution)/shard_map/weight_grad/pallas_call | solution.py:545
  269.9 6.4 %fusion.2 = f32[512,2048]{1,0:T(8,128)S(1)} fusion(bf16[512,1792]{1,0:T(8,128)(2,1)S(1)} %copy-done.15, bf16[2048,3584]{1,0:T(8,128)(2,1)} %all-gather.5.cloned.1.call-done), kind=kOutput, calls=%fused_computation.2 | convolution fusion | flops 3758096384 | bytes 13369344 | tf_op jit(solution)/shard_map/te,de->td/dot_general | solution.py:181
  286.9 3.2 weight_grad.5
  290.1 9.1 %collective-permute-done.23 = bf16[128,2048]{1,0:T(8,128)(2,1)S(1)} collective-permute-done((bf16[128,2048]{1,0:T(8,128)(2,1)S(1)}, bf16[128,2048]{1,0:T(8,128)(2,1)S(1)}, u32[]{:S(2)}, u32[]{:S(2)}) %collective-permute-start.23) | collective-permute-done | bytes 524320 | tf_op jit(solution)/shard_map/ppermute | solution.py:20
  302.0 11.9 %collective-permute-done.24 = bf16[128,2048]{1,0:T(8,128)(2,1)S(1)} collective-permute-done((bf16[128,2048]{1,0:T(8,128)(2,1)S(1)}, bf16[128,2048]{1,0:T(8,128)(2,1)S(1)}, u32[]{:S(2)}, u32[]{:S(2)}) %collective-permute-start.24) | collective-permute-done | bytes 524320 | tf_op jit(solution)/shard_map/ppermute | solution.py:20
  322.8 3.3 fusion.74.refs_9_
  328.3 26.9 %wkv_backward.1 = (bf16[512,512]{1,0:T(8,128)(2,1)S(1)}, bf16[512,512]{1,0:T(8,128)(2,1)S(1)}, bf16[512,512]{1,0:T(8,128)(2,1)S(1)}, bf16[512,512]{1,0:T(8,128)(...) custom-call(f32[512,512]{1,0:T(8,128)S(1)} %copy-done.2, ...), custom_call_target="tpu_custom_call" | custom-call | flops 1048576 | bytes 65536 | tf_op jit(solution)/shard_map/wkv_backward/pallas_call | solution.py:493
  355.3 15.0 %time_mix_grads.1 = bf16[2048,2816]{1,0:T(8,128)(2,1)} custom-call(bf16[512,2048]{1,0:T(8,128)(2,1)S(1)} %pad_maximum_fusion.6.refs_0_, bf16[512,2048]{1,0:T(8,128)(2,1)S(1)} %copy-done.12, bf16[512,2048]{1,0:T(8,128)(2,1)S(1)} %copy-done.10, bf16[512,2048]{1,0:T(8,128)(2,1)S(1)} %copy-done.11, bf16[512,2048]{1,0:T(8,128)(2,1)S(1)} %copy-done.13, ...), custom_call_target="tpu_custom_call" | custom-call | flops 1048576 | bytes 65536 | tf_op jit(solution)/shard_map/time_mix_grads/pallas_call | solution.py:584
  375.9 25.8 %mixes_back.1 = (bf16[512,2048]{1,0:T(8,128)(2,1)}, bf16[2048,512]{1,0:T(8,128)(2,1)}) custom-call(bf16[512,512]{1,0:T(8,128)(2,1)} %copy-done.7, bf16[512,512]{1,0:T(8,128)(2,1)} %copy-done.8, bf16[512,512]{1,0:T(8,128)(2,1)} %copy-done.6, bf16[512,512]{1,0:T(8,128)(2,1)} %copy-done.9, bf16[512,256]{1,0:T(8,128)(2,1)} %fusion.28.gd_ref, ...), custom_call_target="tpu_custom_call" | custom-call | flops 1048576 | bytes 65536 | tf_op jit(solution)/shard_map/mixes_back/pallas_call | solution.py:801
  413.0 12.2 %collective-permute-done.31 = bf16[16,2,16,512]{3,2,1,0:T(8,128)(2,1)S(1)} collective-permute-done((bf16[16,2,16,512]{3,2,1,0:T(8,128)(2,1)S(1)}, bf16[16,2,16,512]{3,2,1,0:T(8,128)(2,1)S(1)}, u32[]{:S(2)}, u32[]{:S(2)}) %collective-permute-start.31) | collective-permute-done | bytes 524320 | tf_op jit(solution)/shard_map/ppermute | solution.py:20
  428.5 5.3 %collective-permute-done.34 = bf16[16,16,512]{2,1,0:T(8,128)(2,1)S(1)} collective-permute-done((bf16[16,16,512]{2,1,0:T(8,128)(2,1)S(1)}, bf16[16,16,512]{2,1,0:T(8,128)(2,1)S(1)}, u32[]{:S(2)}, u32[]{:S(2)}) %collective-permute-start.34) | collective-permute-done | bytes 262176 | tf_op jit(solution)/shard_map/ppermute | solution.py:20
  434.6 5.4 %all-to-all-start = ((bf16[16,16,512]{2,1,0:T(8,128)(2,1)}), bf16[16,16,512]{2,1,0:T(8,128)(2,1)S(1)}, u32[]{:S(2)}, u32[]{:S(2)}) async-start(bf16[16,16,512]{2,1,0:T(8,128)(2,1)} %fusion.48), calls=%async_computation.1 | async-start | bytes 524288 | tf_op jit(solution)/shard_map/all_to_all | solution.py:225
  444.2 3.4 all-to-all-done
  455.0 8.7 %reduce-scatter.5.cloned.1.call-done = bf16[128,2816]{1,0:T(8,128)(2,1)} async-done(((bf16[2048,2816]{1,0:T(8,128)(2,1)}), bf16[128,2816]{1,0:T(8,128)(2,1)}) %reduce-scatter.5.cloned.1.call-update) | async-done | bytes 720912 | tf_op jit(solution)/shard_map/reduce_scatter | solution.py:113
  471.7 7.5 %collective-permute-done.35 = bf16[64,2560]{1,0:T(8,128)(2,1)S(1)} collective-permute-done((bf16[64,2560]{1,0:T(8,128)(2,1)S(1)}, bf16[64,2560]{1,0:T(8,128)(2,1)S(1)}, u32[]{:S(2)}, u32[]{:S(2)}) %collective-permute-start.35) | collective-permute-done | bytes 327712 | tf_op jit(solution)/shard_map/ppermute | solution.py:20
  (360 shorter events, 144.1 us)
Async XLA Ops:
  7.2 112.4 %all-gather.3.cloned.1.call-start = ((), (), s32[]{:S(2)}) async-start(), calls=%async_computation.3 | async-start | bytes 13369344 | tf_op jit(solution)/shard_map/all_gather | solution.py:102
  9.6 10.4 %collective-permute-start.8 = (bf16[16,1024]{1,0:T(8,128)(2,1)S(1)}, bf16[16,1024]{1,0:T(8,128)(2,1)S(1)}, u32[]{:S(2)}, u32[]{:S(2)}) collective-permute-start(bf16[16,1024]{1,0:T(8,128)(2,1)S(1)} %concatenate.95), channel_id=1, source_target_pairs={{0,1},{1,0},{2,3},{3,2},{4,5},{5,4},{6,7},{7,6},{8,9},{9,8},{10,11... | collective-permute-start | bytes 98312 | tf_op jit(solution)/shard_map/ppermute | solution.py:20
  11.9 8.2 %collective-permute-start.9 = (bf16[16,1024]{1,0:T(8,128)(2,1)S(1)}, bf16[16,1024]{1,0:T(8,128)(2,1)S(1)}, u32[]{:S(2)}, u32[]{:S(2)}) collective-permute-start(bf16[16,1024]{1,0:T(8,128)(2,1)S(1)} %concatenate.96), channel_id=1, source_target_pairs={{0,2},{1,3},{2,0},{3,1},{4,6},{5,7},{6,4},{7,5},{8,10},{9,11},{10,... | collective-permute-start | bytes 98312 | tf_op jit(solution)/shard_map/ppermute | solution.py:20
  14.4 11.6 %collective-permute-start.7 = (bf16[4,64,512]{2,1,0:T(8,128)(2,1)}, bf16[4,64,512]{2,1,0:T(8,128)(2,1)S(1)}, u32[]{:S(2)}, u32[]{:S(2)}) collective-permute-start(bf16[4,64,512]{2,1,0:T(8,128)(2,1)} %param.15), channel_id=1, source_target_pairs={{0,4},{1,5},{2,6},{3,7},{4,0},{5,1},{6,2},{7,3},{8,12},{9,13},{10,... | collective-permute-start | bytes 786440 | tf_op jit(solution)/shard_map/ppermute | solution.py:20
  27.1 198.6 %all-gather.5.cloned.1.call-start = ((), (), s32[]{:S(2)}) async-start(), calls=%async_computation.4 | async-start | bytes 15597568 | tf_op jit(solution)/shard_map/all_gather | solution.py:102
  27.9 6.3 %collective-permute-start.4 = (bf16[128,512]{1,0:T(8,128)(2,1)}, bf16[128,512]{1,0:T(8,128)(2,1)S(1)}, u32[]{:S(2)}, u32[]{:S(2)}) collective-permute-start(bf16[128,512]{1,0:T(8,128)(2,1)} %get-tuple-element.218), channel_id=1, source_target_pairs={{0,1},{1,0},{2,3},{3,2},{4,5},{5,4},{6,7},{7,6},{8,9},{9,8},{10,11... | collective-permute-start | bytes 393224 | tf_op jit(solution)/shard_map/ppermute | solution.py:20
  28.7 20.1 %collective-permute-start.2 = (bf16[128,2048]{1,0:T(8,128)(2,1)S(1)}, bf16[128,2048]{1,0:T(8,128)(2,1)S(1)}, u32[]{:S(2)}, u32[]{:S(2)}) collective-permute-start(bf16[128,2048]{1,0:T(8,128)(2,1)S(1)} %copy-done.31), channel_id=1, source_target_pairs={{0,2},{1,3},{2,0},{3,1},{4,6},{5,7},{6,4},{7,5},{8,10},{9,11},{10,... | collective-permute-start | bytes 1572872 | tf_op jit(solution)/shard_map/ppermute | solution.py:20
  29.6 15.6 %collective-permute-start.5 = (bf16[128,512]{1,0:T(8,128)(2,1)S(1)}, bf16[128,512]{1,0:T(8,128)(2,1)S(1)}, u32[]{:S(2)}, u32[]{:S(2)}) collective-permute-start(bf16[128,512]{1,0:T(8,128)(2,1)S(1)} %get-tuple-element.217), channel_id=1, source_target_pairs={{0,2},{1,3},{2,0},{3,1},{4,6},{5,7},{6,4},{7,5},{8,10},{9,11},{10,... | collective-permute-start | bytes 393224 | tf_op jit(solution)/shard_map/ppermute | solution.py:20
  30.2 18.6 %collective-permute-start.6 = (bf16[128,512]{1,0:T(8,128)(2,1)S(1)}, bf16[128,512]{1,0:T(8,128)(2,1)S(1)}, u32[]{:S(2)}, u32[]{:S(2)}) collective-permute-start(bf16[128,512]{1,0:T(8,128)(2,1)S(1)} %get-tuple-element.216), channel_id=1, source_target_pairs={{0,3},{1,2},{2,1},{3,0},{4,7},{5,6},{6,5},{7,4},{8,11},{9,10},{10,... | collective-permute-start | bytes 393224 | tf_op jit(solution)/shard_map/ppermute | solution.py:20
  31.5 23.3 %collective-permute-start.1 = (bf16[1792,64]{0,1:T(8,128)(2,1)S(1)}, bf16[1792,64]{0,1:T(8,128)(2,1)S(1)}, u32[]{:S(2)}, u32[]{:S(2)}) collective-permute-start(bf16[1792,64]{0,1:T(8,128)(2,1)S(1)} %copy-done.64), channel_id=1, source_target_pairs={{0,4},{1,5},{2,6},{3,7},{4,0},{5,1},{6,2},{7,3},{8,12},{9,13},{10,... | collective-permute-start | bytes 688136 | tf_op jit(solution)/shard_map/ppermute | solution.py:20
  34.2 25.5 %collective-permute-start = (bf16[64,1792]{1,0:T(8,128)(2,1)S(1)}, bf16[64,1792]{1,0:T(8,128)(2,1)S(1)}, u32[]{:S(2)}, u32[]{:S(2)}) collective-permute-start(bf16[64,1792]{1,0:T(8,128)(2,1)S(1)} %copy-done.65), channel_id=1, source_target_pairs={{0,4},{1,5},{2,6},{3,7},{4,0},{5,1},{6,2},{7,3},{8,12},{9,13},{10,... | collective-permute-start | bytes 688136 | tf_op jit(solution)/shard_map/ppermute | solution.py:20
  49.9 11.0 %collective-permute-start.3 = (bf16[2,128,2048]{2,1,0:T(8,128)(2,1)}, bf16[2,128,2048]{2,1,0:T(8,128)(2,1)}, u32[]{:S(2)}, u32[]{:S(2)}) collective-permute-start(bf16[2,128,2048]{2,1,0:T(8,128)(2,1)} %pad_maximum_fusion.7), channel_id=1, source_target_pairs={{0,1},{1,0},{2,3},{3,2},{4,5},{5,4},{6,7},{7,6},{8,9},{9,8},{10,11... | collective-permute-start | bytes 3145736 | tf_op jit(solution)/shard_map/ppermute | solution.py:20
  69.1 304.6 %reduce-scatter.3.cloned.1.call-start = ((), (), s32[]{:S(2)}) async-start(), calls=%async_computation.5 | async-start | bytes 15597568 | tf_op jit(solution)/shard_map/reduce_scatter | solution.py:113
  123.0 49.2 %collective-permute-start.12 = (bf16[16,64,1024]{2,1,0:T(8,128)(2,1)}, bf16[16,64,1024]{2,1,0:T(8,128)(2,1)}, u32[]{:S(2)}, u32[]{:S(2)}) collective-permute-start(bf16[16,64,1024]{2,1,0:T(8,128)(2,1)} %pad_maximum_fusion.1), channel_id=1, source_target_pairs={{0,4},{1,5},{2,6},{3,7},{4,0},{5,1},{6,2},{7,3},{8,12},{9,13},{10,... | collective-permute-start | bytes 6291464 | tf_op jit(solution)/shard_map/ppermute | solution.py:20
  182.4 13.3 %collective-permute-start.14 = (bf16[128,2048]{1,0:T(8,128)(2,1)S(1)}, bf16[128,2048]{1,0:T(8,128)(2,1)S(1)}, u32[]{:S(2)}, u32[]{:S(2)}) collective-permute-start(bf16[128,2048]{1,0:T(8,128)(2,1)S(1)} %fusion.43), channel_id=1, source_target_pairs={{0,2},{1,3},{2,0},{3,1},{4,6},{5,7},{6,4},{7,5},{8,10},{9,11},{10,... | collective-permute-start | bytes 1572872 | tf_op jit(solution)/shard_map/ppermute | solution.py:20
  196.8 12.5 %collective-permute-start.15 = (bf16[128,2048]{1,0:T(8,128)(2,1)S(1)}, bf16[128,2048]{1,0:T(8,128)(2,1)S(1)}, u32[]{:S(2)}, u32[]{:S(2)}) collective-permute-start(bf16[128,2048]{1,0:T(8,128)(2,1)S(1)} %add_convert_fusion.5), channel_id=1, source_target_pairs={{0,2},{1,3},{2,0},{3,1},{4,6},{5,7},{6,4},{7,5},{8,10},{9,11},{10,... | collective-permute-start | bytes 1572872 | tf_op jit(solution)/shard_map/ppermute | solution.py:20
  225.7 13.7 %collective-permute-start.18 = (bf16[512,512]{1,0:T(8,128)(2,1)}, bf16[512,512]{1,0:T(8,128)(2,1)S(1)}, u32[]{:S(2)}, u32[]{:S(2)}) collective-permute-start(bf16[512,512]{1,0:T(8,128)(2,1)} %get-tuple-element.75), channel_id=1, source_target_pairs={{0,2},{1,3},{2,0},{3,1},{4,6},{5,7},{6,4},{7,5},{8,10},{9,11},{10,... | collective-permute-start | bytes 1572872 | tf_op jit(solution)/shard_map/ppermute | solution.py:20
  245.2 13.4 %collective-permute-start.20 = (bf16[512,512]{1,0:T(8,128)(2,1)S(1)}, bf16[512,512]{1,0:T(8,128)(2,1)S(1)}, u32[]{:S(2)}, u32[]{:S(2)}) collective-permute-start(bf16[512,512]{1,0:T(8,128)(2,1)S(1)} %add_convert_fusion.4), channel_id=1, source_target_pairs={{0,2},{1,3},{2,0},{3,1},{4,6},{5,7},{6,4},{7,5},{8,10},{9,11},{10,... | collective-permute-start | bytes 1572872 | tf_op jit(solution)/shard_map/ppermute | solution.py:20
  265.6 198.0 %reduce-scatter.5.cloned.1.call-start = ((), (), s32[]{:S(2)}) async-start(), calls=%async_computation.6 | async-start | bytes 12255232 | tf_op jit(solution)/shard_map/reduce_scatter | solution.py:113
  285.9 13.3 %collective-permute-start.23 = (bf16[128,2048]{1,0:T(8,128)(2,1)S(1)}, bf16[128,2048]{1,0:T(8,128)(2,1)S(1)}, u32[]{:S(2)}, u32[]{:S(2)}) collective-permute-start(bf16[128,2048]{1,0:T(8,128)(2,1)S(1)} %fusion.44), channel_id=1, source_target_pairs={{0,2},{1,3},{2,0},{3,1},{4,6},{5,7},{6,4},{7,5},{8,10},{9,11},{10,... | collective-permute-start | bytes 1572872 | tf_op jit(solution)/shard_map/ppermute | solution.py:20
  301.4 12.4 %collective-permute-start.24 = (bf16[128,2048]{1,0:T(8,128)(2,1)S(1)}, bf16[128,2048]{1,0:T(8,128)(2,1)S(1)}, u32[]{:S(2)}, u32[]{:S(2)}) collective-permute-start(bf16[128,2048]{1,0:T(8,128)(2,1)S(1)} %get-tuple-element.150), channel_id=1, source_target_pairs={{0,2},{1,3},{2,0},{3,1},{4,6},{5,7},{6,4},{7,5},{8,10},{9,11},{10,... | collective-permute-start | bytes 1572872 | tf_op jit(solution)/shard_map/ppermute | solution.py:20
  318.6 51.8 %collective-permute-start.26 = (bf16[16,64,512]{2,1,0:T(8,128)(2,1)}, bf16[16,64,512]{2,1,0:T(8,128)(2,1)}, u32[]{:S(2)}, u32[]{:S(2)}) collective-permute-start(bf16[16,64,512]{2,1,0:T(8,128)(2,1)} %select_bitcast_fusion.1), channel_id=1, source_target_pairs={{0,4},{1,5},{2,6},{3,7},{4,0},{5,1},{6,2},{7,3},{8,12},{9,13},{10,... | collective-permute-start | bytes 3145736 | tf_op jit(solution)/shard_map/ppermute | solution.py:20
  321.8 48.6 %collective-permute-start.27 = (bf16[128,512]{1,0:T(8,128)(2,1)S(1)}, bf16[128,512]{1,0:T(8,128)(2,1)S(1)}, u32[]{:S(2)}, u32[]{:S(2)}) collective-permute-start(bf16[128,512]{1,0:T(8,128)(2,1)S(1)} %get-tuple-element.212), channel_id=1, source_target_pairs={{0,1},{1,0},{2,3},{3,2},{4,5},{5,4},{6,7},{7,6},{8,9},{9,8},{10,11... | collective-permute-start | bytes 393224 | tf_op jit(solution)/shard_map/ppermute | solution.py:20
  322.5 47.8 %collective-permute-start.28 = (bf16[128,512]{1,0:T(8,128)(2,1)S(1)}, bf16[128,512]{1,0:T(8,128)(2,1)S(1)}, u32[]{:S(2)}, u32[]{:S(2)}) collective-permute-start(bf16[128,512]{1,0:T(8,128)(2,1)S(1)} %get-tuple-element.211), channel_id=1, source_target_pairs={{0,2},{1,3},{2,0},{3,1},{4,6},{5,7},{6,4},{7,5},{8,10},{9,11},{10,... | collective-permute-start | bytes 393224 | tf_op jit(solution)/shard_map/ppermute | solution.py:20
  326.1 44.3 %collective-permute-start.29 = (bf16[128,512]{1,0:T(8,128)(2,1)S(1)}, bf16[128,512]{1,0:T(8,128)(2,1)S(1)}, u32[]{:S(2)}, u32[]{:S(2)}) collective-permute-start(bf16[128,512]{1,0:T(8,128)(2,1)S(1)} %get-tuple-element.210), channel_id=1, source_target_pairs={{0,3},{1,2},{2,1},{3,0},{4,7},{5,6},{6,5},{7,4},{8,11},{9,10},{10,... | collective-permute-start | bytes 393224 | tf_op jit(solution)/shard_map/ppermute | solution.py:20
  412.1 13.1 %collective-permute-start.31 = (bf16[16,2,16,512]{3,2,1,0:T(8,128)(2,1)S(1)}, bf16[16,2,16,512]{3,2,1,0:T(8,128)(2,1)S(1)}, u32[]{:S(2)}, u32[]{:S(2)}) collective-permute-start(bf16[16,2,16,512]{3,2,1,0:T(8,128)(2,1)S(1)} %fusion.45), channel_id=1, source_target_pairs={{0,2},{1,3},{2,0},{3,1},{4,6},{5,7},{6,4},{7,5},{8,10},{9,11},{10,... | collective-permute-start | bytes 1572872 | tf_op jit(solution)/shard_map/ppermute | solution.py:20
  425.7 8.1 %collective-permute-start.34 = (bf16[16,16,512]{2,1,0:T(8,128)(2,1)S(1)}, bf16[16,16,512]{2,1,0:T(8,128)(2,1)S(1)}, u32[]{:S(2)}, u32[]{:S(2)}) collective-permute-start(bf16[16,16,512]{2,1,0:T(8,128)(2,1)S(1)} %fusion.49), channel_id=1, source_target_pairs={{0,4},{1,5},{2,6},{3,7},{4,0},{5,1},{6,2},{7,3},{8,12},{9,13},{10,... | collective-permute-start | bytes 786440 | tf_op jit(solution)/shard_map/ppermute | solution.py:20
  428.3 20.7 %collective-permute-start.33 = (bf16[128,2048]{1,0:T(8,128)(2,1)}, bf16[128,2048]{1,0:T(8,128)(2,1)}, u32[]{:S(2)}, u32[]{:S(2)}) collective-permute-start(bf16[128,2048]{1,0:T(8,128)(2,1)} %fusion.46), channel_id=1, source_target_pairs={{0,2},{1,3},{2,0},{3,1},{4,6},{5,7},{6,4},{7,5},{8,10},{9,11},{10,... | collective-permute-start | bytes 1572872 | tf_op jit(solution)/shard_map/ppermute | solution.py:20
  434.6 13.0 %all-to-all-start = ((bf16[16,16,512]{2,1,0:T(8,128)(2,1)}), bf16[16,16,512]{2,1,0:T(8,128)(2,1)S(1)}, u32[]{:S(2)}, u32[]{:S(2)}) async-start(bf16[16,16,512]{2,1,0:T(8,128)(2,1)} %fusion.48), calls=%async_computation.1 | async-start | bytes 524288 | tf_op jit(solution)/shard_map/all_to_all | solution.py:225
  442.1 10.8 %collective-permute-start.39 = (bf16[64,3584]{1,0:T(8,128)(2,1)}, bf16[64,3584]{1,0:T(8,128)(2,1)}, u32[]{:S(2)}, u32[]{:S(2)}) collective-permute-start(bf16[64,3584]{1,0:T(8,128)(2,1)} %broadcast_select_fusion.26), channel_id=1, source_target_pairs={{0,4},{1,5},{2,6},{3,7},{4,0},{5,1},{6,2},{7,3},{8,12},{9,13},{10,... | collective-permute-start | bytes 1376264 | tf_op jit(solution)/shard_map/ppermute | solution.py:20
  464.6 6.4 %collective-permute-start.36 = (bf16[16,512]{1,0:T(8,128)(2,1)S(1)}, bf16[16,512]{1,0:T(8,128)(2,1)S(1)}, u32[]{:S(2)}, u32[]{:S(2)}) collective-permute-start(bf16[16,512]{1,0:T(8,128)(2,1)S(1)} %get-tuple-element.236), channel_id=1, source_target_pairs={{0,1},{1,0},{2,3},{3,2},{4,5},{5,4},{6,7},{7,6},{8,9},{9,8},{10,11... | collective-permute-start | bytes 49160 | tf_op jit(solution)/shard_map/ppermute | solution.py:20
  468.5 10.7 %collective-permute-start.35 = (bf16[64,2560]{1,0:T(8,128)(2,1)S(1)}, bf16[64,2560]{1,0:T(8,128)(2,1)S(1)}, u32[]{:S(2)}, u32[]{:S(2)}) collective-permute-start(bf16[64,2560]{1,0:T(8,128)(2,1)S(1)} %broadcast_select_fusion.29), channel_id=1, source_target_pairs={{0,4},{1,5},{2,6},{3,7},{4,0},{5,1},{6,2},{7,3},{8,12},{9,13},{10,... | collective-permute-start | bytes 983048 | tf_op jit(solution)/shard_map/ppermute | solution.py:20
  (80 other events, 533.3 us)
Sparse Core Ops, SparseCore 0:
  27.2 92.2 all-gather.2
  121.7 100.2 all-gather.4
  265.8 100.3 reduce-scatter.2
  373.9 89.7 reduce-scatter.4

commit v7 on v6

--- a/solution.py
+++ b/solution.py
@@ -340,24 +340,40 @@
 
 
 def wkv_forward_kernel(*refs):
-    for group in lane_groups(refs, "ccccwrcccccs"):
-        forward_heads(*group)
+    groups = list(lane_groups(refs, "ccccwrcccccs"))
+    ones = head_ones()
+
+    @pl.when(pl.program_id(0) == 0)
+    def _():
+        for *_, first_ref, _, _, _, state in groups:
+            state[...] = spread(first_ref[...], ones)
+
+    for group in groups:
+        forward_heads(ones, *group)
 
 
 def wkv_backward_kernel(*refs):
-    for group in lane_groups(refs, "ccccwrccccccccccc" + "s"):
-        backward_heads(*group)
+    groups = list(lane_groups(refs, "ccccwrccccccccccc" + "s"))
+    ones = head_ones()
+
+    @pl.when(pl.program_id(0) == 0)
+    def _():
+        for *_, sums_ref, _, state in groups:
+            state[...] = jnp.zeros_like(state)
+            sums_ref[...] = jnp.zeros_like(sums_ref)
+
+    for group in groups:
+        backward_heads(ones, *group)
+
+    @pl.when(pl.program_id(0) == pl.num_programs(0) - 1)
+    def _():
+        for *_, first_ref, state in groups:
+            first_ref[...] = fold(state[...], ones)
 
 
 def forward_heads(
-    r_ref, k_ref, v_ref, gate_ref, low_ref, up_ref, par_ref, first_ref, mixed_ref, wkv_ref, held_ref, state
+    ones, r_ref, k_ref, v_ref, gate_ref, low_ref, up_ref, par_ref, first_ref, mixed_ref, wkv_ref, held_ref, state
 ):
-    ones = head_ones()
-
-    @pl.when(pl.program_id(0) == 0)
-    def _():
-        state[...] = spread(first_ref[...], ones)
-
     r, k, v = r_ref[...], k_ref[...], v_ref[...]
     _, run, before = decay_of(low_ref, up_ref, par_ref)
     held_ref[...] = fold(state[...], ones)
@@ -405,16 +421,9 @@
 
 
 def backward_heads(
-    r_ref, k_ref, v_ref, gate_ref, low_ref, up_ref, par_ref, wkv_ref, held_ref, gm_ref,
+    ones, r_ref, k_ref, v_ref, gate_ref, low_ref, up_ref, par_ref, wkv_ref, held_ref, gm_ref,
     gr_ref, gk_ref, gv_ref, gg_ref, gw_ref, sums_ref, first_ref, state,
 ):
-    ones = head_ones()
-
-    @pl.when(pl.program_id(0) == 0)
-    def _():
-        state[...] = jnp.zeros_like(state)
-        sums_ref[...] = jnp.zeros_like(sums_ref)
-
     r, k, v, gate = r_ref[...], k_ref[...], v_ref[...], gate_ref[...]
     bonus, gain = par_ref[1:2], par_ref[2:3]
 
@@ -477,10 +486,6 @@
     gk_ref[...] = (g_k + bonus * r * g_diag).astype(jnp.bfloat16)
     gv_ref[...] = (g_v + head_sum(r * bonus * k, ones) * g_out).astype(jnp.bfloat16)
     state[...] = jnp.exp(last) * end_grad + mxu(g_out, r * from_start, TN) * ones
-
-    @pl.when(pl.program_id(0) == pl.num_programs(0) - 1)
-    def _():
-        first_ref[...] = fold(state[...], ones)
 
 
 def wkv_backward(r, k, v, gate, low, up, par, wkv, held, g_mixed):

time: 496 us -> 495 us (level)
  transfers between devices with their start and end apart: 45 -> 45, of which waited for: 23 -> 24; matrix products, arithmetic and copies ran while one was open for 22% -> 22% of each run, Pallas kernels for 25% -> 24%
where the time goes in v7:
time: 495 us; the launch traced here: 487 us
  waiting for transfers between devices  175 us (35%)
  Pallas kernels  123 us (25%)
  other arithmetic  58.1 us (12%)
  starting transfers between devices  50.8 us (10%)
  matrix products  34.7 us (7%)
  local copies, waits for them, and re-layouts  29.3 us (6%)
  between operations  15.8 us (3%)
    ppermute x40, waiting for transfers between devices, swap(): return lax.ppermute(block, ALL, [(i, i ^ bit) for i in range(count)])  112 us
    all_gather x2, waiting for transfers between devices, plane_gather(): lax.all_gather(pair, 'seg', axis=0, tiled=True, axis_index_groups=plane_g...  50.3 us
    ppermute x40, starting transfers between devices, swap(): return lax.ppermute(block, ALL, [(i, i ^ bit) for i in range(count)])  45.4 us
    pallas_call x1, Pallas kernels, wkv_backward(): pl.pallas_call(wkv_backward_kernel, grid=(chunks,), in_specs=[block] * 4...  25.9 us
    pallas_call x1, Pallas kernels, mixes_back(): pl.pallas_call(mixes_back_kernel, grid=(2, tiles), in_specs=[whole(g_key)...  25.7 us
    pallas_call x1, Pallas kernels, mixes_forward(): pl.pallas_call(mixes_forward_kernel, grid=(2, tiles), in_specs=[across(ro...  21.8 us
    pallas_call x1, Pallas kernels, wkv_forward(): pl.pallas_call(wkv_forward_kernel, grid=(chunks,), in_specs=[block] * 4 +...  18.7 us
    dot_general x5, matrix products, product_lower(): return jnp.dot(left_arg, right_arg, preferred_element_type=jnp.float32)  17.9 us
  transfers between devices with their start and end apart: 45, of which 24 were waited for; matrix products, arithmetic and copies ran while one was open for 22% of the time, Pallas kernels for 24%

profile of v7, /device:TPU:1, one launch (start us, length us, event | category | flops | bytes accessed | tf_op | source)
XLA Modules:
  0.0 486.7 jit_solution(16444642163288571588)
XLA Ops:
  14.4 3.0 collective-permute-start.7
  20.2 5.7 %collective-permute-done.11 = bf16[64,512]{1,0:T(8,128)(2,1)S(1)} collective-permute-done((bf16[64,512]{1,0:T(8,128)(2,1)S(1)}, bf16[64,512]{1,0:T(8,128)(2,1)S(1)}, u32[]{:S(2)}, u32[]{:S(2)}) %collective-permute-start.11) | collective-permute-done | bytes 65568 | tf_op jit(solution)/shard_map/ppermute | solution.py:20
  34.6 10.5 %collective-permute-done.5 = bf16[128,512]{1,0:T(8,128)(2,1)S(1)} collective-permute-done((bf16[128,512]{1,0:T(8,128)(2,1)S(1)}, bf16[128,512]{1,0:T(8,128)(2,1)S(1)}, u32[]{:S(2)}, u32[]{:S(2)}) %collective-permute-start.5) | collective-permute-done | bytes 131104 | tf_op jit(solution)/shard_map/ppermute | solution.py:20
  45.2 3.6 collective-permute-done.6
  51.1 3.7 collective-permute-done.1
  54.8 4.9 %collective-permute-done = bf16[64,1792]{1,0:T(8,128)(2,1)S(1)} collective-permute-done((bf16[64,1792]{1,0:T(8,128)(2,1)S(1)}, bf16[64,1792]{1,0:T(8,128)(2,1)S(1)}, u32[]{:S(2)}, u32[]{:S(2)}) %collective-permute-start) | collective-permute-done | bytes 229408 | tf_op jit(solution)/shard_map/ppermute | solution.py:20
  64.5 4.6 fusion.6.unit_ref
  69.2 50.3 %all-gather.3.cloned.1.call-done.w_ref.down_ref.up_ref = bf16[2048,3072]{1,0:T(8,128)(2,1)} async-done(((bf16[128,3072]{1,0:T(8,128)(2,1)}), bf16[2048,3072]{1,0:T(8,128)(2,1)}) %all-gather.3.cloned.1.call-update) | async-done | bytes 12582928 | tf_op jit(solution)/shard_map/all_gather | solution.py:102
  123.0 2.9 collective-permute-start.12
  128.1 21.8 %mixes_forward.1 = (bf16[512,2048]{1,0:T(8,128)(2,1)}, bf16[512,2048]{1,0:T(8,128)(2,1)}, bf16[512,2048]{1,0:T(8,128)(2,1)}, bf16[512,2048]{1,0:T(8,128)(2,1)}, ...) custom-call(f32[512,2048]{1,0:T(8,128)} %fusion.6.unit_ref, ...), custom_call_target="tpu_custom_call" | custom-call | flops 1048576 | bytes 65536 | tf_op jit(solution)/shard_map/mixes_forward/pallas_call | solution.py:695
  151.1 18.7 %wkv_forward.1 = (bf16[512,512]{1,0:T(8,128)(2,1)S(1)}, f32[512,512]{1,0:T(8,128)S(1)}, f32[512,512]{1,0:T(8,128)S(1)}) custom-call(f32[512,512]{1,0:T(8,128)} %get-tuple-element.66.refs_0_, f32[512,512]{1,0:T(8,128)} %get-tuple-element.67.refs_1_, f32[512,512]{1,0:T(8,128)} %get-tuple-element.68.refs_2_, f32[512,512]{1,0:T(8,128)} %get-tuple-element.69.refs_3_, ...), custom_call_target="tpu_custom_call" | custom-call | flops 1048576 | bytes 65536 | tf_op jit(solution)/shard_map/wkv_forward/pallas_call | solution.py:398
  171.5 3.8 select_bitcast_fusion.4
  183.8 11.0 %collective-permute-done.14 = bf16[128,2048]{1,0:T(8,128)(2,1)S(1)} collective-permute-done((bf16[128,2048]{1,0:T(8,128)(2,1)S(1)}, bf16[128,2048]{1,0:T(8,128)(2,1)S(1)}, u32[]{:S(2)}, u32[]{:S(2)}) %collective-permute-start.14) | collective-permute-done | bytes 524320 | tf_op jit(solution)/shard_map/ppermute | solution.py:20
  197.1 11.2 %collective-permute-done.15 = bf16[128,2048]{1,0:T(8,128)(2,1)S(1)} collective-permute-done((bf16[128,2048]{1,0:T(8,128)(2,1)S(1)}, bf16[128,2048]{1,0:T(8,128)(2,1)S(1)}, u32[]{:S(2)}, u32[]{:S(2)}) %collective-permute-start.15) | collective-permute-done | bytes 524320 | tf_op jit(solution)/shard_map/ppermute | solution.py:20
  225.9 7.2 %multiply_convert_fusion.1 = (bf16[512,1792]{1,0:T(8,128)(2,1)S(1)}, bf16[512,1792]{1,0:T(8,128)(2,1)S(1)}) fusion(bf16[512,2048]{1,0:T(8,128)(2,1)S(1)} %get-tuple-element.157.left_ref, bf16[2048,3584]{1,0:T(8,128)(2,1)} %all-gather.5.cloned.1.call-done), kind=kOutput, calls=%fused_computation.23 | convolution fusion | flops 3761766400 | bytes 13107200 | tf_op jit(solution)/shard_map/dot_general | solution.py:173
  245.7 4.0 multiply_convert_fusion.right_ref
  249.7 6.3 %weight_grad.3.rest_0_ = bf16[2048,3584]{1,0:T(8,128)(2,1)} custom-call(bf16[512,2048]{1,0:T(8,128)(2,1)S(1)} %pad_maximum_fusion.5.left_ref, bf16[512,1792]{1,0:T(8,128)(2,1)S(1)} %get-tuple-element.252.right_ref), custom_call_target="tpu_custom_call" | custom-call | flops 1048576 | bytes 65536 | tf_op jit(solution)/shard_map/weight_grad/pallas_call | solution.py:550
  258.4 6.2 %weight_grad.4 = bf16[2048,3584]{1,0:T(8,128)(2,1)} custom-call(bf16[512,2048]{1,0:T(8,128)(2,1)S(1)} %get-tuple-element.157.left_ref, bf16[512,1792]{1,0:T(8,128)(2,1)S(1)} %multiply_convert_fusion.right_ref, bf16[2048,3584]{1,0:T(8,128)(2,1)} %weight_grad.3.rest_0_), custom_call_target="tpu_custom_call", output_to_operand_aliasing={{}: (2, {})} | custom-call | flops 1048576 | bytes 65536 | tf_op jit(solution)/shard_map/weight_grad/pallas_call | solution.py:550
  269.0 6.4 %fusion.2 = f32[512,2048]{1,0:T(8,128)S(1)} fusion(bf16[512,1792]{1,0:T(8,128)(2,1)S(1)} %copy-done.15, bf16[2048,3584]{1,0:T(8,128)(2,1)} %all-gather.5.cloned.1.call-done), kind=kOutput, calls=%fused_computation.2 | convolution fusion | flops 3758096384 | bytes 13369344 | tf_op jit(solution)/shard_map/te,de->td/dot_general | solution.py:181
  286.2 3.2 weight_grad.5
  289.4 8.8 %collective-permute-done.23 = bf16[128,2048]{1,0:T(8,128)(2,1)S(1)} collective-permute-done((bf16[128,2048]{1,0:T(8,128)(2,1)S(1)}, bf16[128,2048]{1,0:T(8,128)(2,1)S(1)}, u32[]{:S(2)}, u32[]{:S(2)}) %collective-permute-start.23) | collective-permute-done | bytes 524320 | tf_op jit(solution)/shard_map/ppermute | solution.py:20
  301.7 11.2 %collective-permute-done.24 = bf16[128,2048]{1,0:T(8,128)(2,1)S(1)} collective-permute-done((bf16[128,2048]{1,0:T(8,128)(2,1)S(1)}, bf16[128,2048]{1,0:T(8,128)(2,1)S(1)}, u32[]{:S(2)}, u32[]{:S(2)}) %collective-permute-start.24) | collective-permute-done | bytes 524320 | tf_op jit(solution)/shard_map/ppermute | solution.py:20
  322.8 3.2 fusion.74.refs_9_
  328.4 25.9 %wkv_backward.1 = (bf16[512,512]{1,0:T(8,128)(2,1)S(1)}, bf16[512,512]{1,0:T(8,128)(2,1)S(1)}, bf16[512,512]{1,0:T(8,128)(2,1)S(1)}, bf16[512,512]{1,0:T(8,128)(...) custom-call(f32[512,512]{1,0:T(8,128)S(1)} %copy-done.2, ...), custom_call_target="tpu_custom_call" | custom-call | flops 1048576 | bytes 65536 | tf_op jit(solution)/shard_map/wkv_backward/pallas_call | solution.py:498
  354.4 15.0 %time_mix_grads.1 = bf16[2048,2816]{1,0:T(8,128)(2,1)} custom-call(bf16[512,2048]{1,0:T(8,128)(2,1)S(1)} %pad_maximum_fusion.6.refs_0_, bf16[512,2048]{1,0:T(8,128)(2,1)S(1)} %copy-done.12, bf16[512,2048]{1,0:T(8,128)(2,1)S(1)} %copy-done.10, bf16[512,2048]{1,0:T(8,128)(2,1)S(1)} %copy-done.11, bf16[512,2048]{1,0:T(8,128)(2,1)S(1)} %copy-done.13, ...), custom_call_target="tpu_custom_call" | custom-call | flops 1048576 | bytes 65536 | tf_op jit(solution)/shard_map/time_mix_grads/pallas_call | solution.py:589
  375.0 25.7 %mixes_back.1 = (bf16[512,2048]{1,0:T(8,128)(2,1)}, bf16[2048,512]{1,0:T(8,128)(2,1)}) custom-call(bf16[512,512]{1,0:T(8,128)(2,1)} %copy-done.7, bf16[512,512]{1,0:T(8,128)(2,1)} %copy-done.8, bf16[512,512]{1,0:T(8,128)(2,1)} %copy-done.6, bf16[512,512]{1,0:T(8,128)(2,1)} %copy-done.9, bf16[512,256]{1,0:T(8,128)(2,1)} %fusion.28.gd_ref, ...), custom_call_target="tpu_custom_call" | custom-call | flops 1048576 | bytes 65536 | tf_op jit(solution)/shard_map/mixes_back/pallas_call | solution.py:806
  412.0 12.6 %collective-permute-done.31 = bf16[16,2,16,512]{3,2,1,0:T(8,128)(2,1)S(1)} collective-permute-done((bf16[16,2,16,512]{3,2,1,0:T(8,128)(2,1)S(1)}, bf16[16,2,16,512]{3,2,1,0:T(8,128)(2,1)S(1)}, u32[]{:S(2)}, u32[]{:S(2)}) %collective-permute-start.31) | collective-permute-done | bytes 524320 | tf_op jit(solution)/shard_map/ppermute | solution.py:20
  426.8 6.3 %collective-permute-done.34 = bf16[16,16,512]{2,1,0:T(8,128)(2,1)S(1)} collective-permute-done((bf16[16,16,512]{2,1,0:T(8,128)(2,1)S(1)}, bf16[16,16,512]{2,1,0:T(8,128)(2,1)S(1)}, u32[]{:S(2)}, u32[]{:S(2)}) %collective-permute-start.34) | collective-permute-done | bytes 262176 | tf_op jit(solution)/shard_map/ppermute | solution.py:20
  433.9 5.2 %all-to-all-start = ((bf16[16,16,512]{2,1,0:T(8,128)(2,1)}), bf16[16,16,512]{2,1,0:T(8,128)(2,1)S(1)}, u32[]{:S(2)}, u32[]{:S(2)}) async-start(bf16[16,16,512]{2,1,0:T(8,128)(2,1)} %fusion.48), calls=%async_computation.1 | async-start | bytes 524288 | tf_op jit(solution)/shard_map/all_to_all | solution.py:225
  441.7 4.9 %all-to-all-done = bf16[16,16,512]{2,1,0:T(8,128)(2,1)S(1)} async-done(((bf16[16,16,512]{2,1,0:T(8,128)(2,1)}), bf16[16,16,512]{2,1,0:T(8,128)(2,1)S(1)}, u32[]{:S(2)}, u32[]{:S(2)}) %all-to-all-start) | async-done | bytes 262176 | tf_op jit(solution)/shard_map/all_to_all | solution.py:225
  454.4 8.2 %reduce-scatter.5.cloned.1.call-done = bf16[128,2816]{1,0:T(8,128)(2,1)} async-done(((bf16[2048,2816]{1,0:T(8,128)(2,1)}), bf16[128,2816]{1,0:T(8,128)(2,1)}) %reduce-scatter.5.cloned.1.call-update) | async-done | bytes 720912 | tf_op jit(solution)/shard_map/reduce_scatter | solution.py:113
  469.8 8.2 %collective-permute-done.35 = bf16[64,2560]{1,0:T(8,128)(2,1)S(1)} collective-permute-done((bf16[64,2560]{1,0:T(8,128)(2,1)S(1)}, bf16[64,2560]{1,0:T(8,128)(2,1)S(1)}, u32[]{:S(2)}, u32[]{:S(2)}) %collective-permute-start.35) | collective-permute-done | bytes 327712 | tf_op jit(solution)/shard_map/ppermute | solution.py:20
  (360 shorter events, 146.7 us)
Async XLA Ops:
  7.2 112.4 %all-gather.3.cloned.1.call-start = ((), (), s32[]{:S(2)}) async-start(), calls=%async_computation.3 | async-start | bytes 13369344 | tf_op jit(solution)/shard_map/all_gather | solution.py:102
  9.6 10.4 %collective-permute-start.8 = (bf16[16,1024]{1,0:T(8,128)(2,1)S(1)}, bf16[16,1024]{1,0:T(8,128)(2,1)S(1)}, u32[]{:S(2)}, u32[]{:S(2)}) collective-permute-start(bf16[16,1024]{1,0:T(8,128)(2,1)S(1)} %concatenate.95), channel_id=1, source_target_pairs={{0,1},{1,0},{2,3},{3,2},{4,5},{5,4},{6,7},{7,6},{8,9},{9,8},{10,11... | collective-permute-start | bytes 98312 | tf_op jit(solution)/shard_map/ppermute | solution.py:20
  11.9 8.2 %collective-permute-start.9 = (bf16[16,1024]{1,0:T(8,128)(2,1)S(1)}, bf16[16,1024]{1,0:T(8,128)(2,1)S(1)}, u32[]{:S(2)}, u32[]{:S(2)}) collective-permute-start(bf16[16,1024]{1,0:T(8,128)(2,1)S(1)} %concatenate.96), channel_id=1, source_target_pairs={{0,2},{1,3},{2,0},{3,1},{4,6},{5,7},{6,4},{7,5},{8,10},{9,11},{10,... | collective-permute-start | bytes 98312 | tf_op jit(solution)/shard_map/ppermute | solution.py:20
  14.1 6.0 %collective-permute-start.10 = (bf16[16,1024]{1,0:T(8,128)(2,1)S(1)}, bf16[16,1024]{1,0:T(8,128)(2,1)S(1)}, u32[]{:S(2)}, u32[]{:S(2)}) collective-permute-start(bf16[16,1024]{1,0:T(8,128)(2,1)S(1)} %concatenate.97), channel_id=1, source_target_pairs={{0,3},{1,2},{2,1},{3,0},{4,7},{5,6},{6,5},{7,4},{8,11},{9,10},{10,... | collective-permute-start | bytes 98312 | tf_op jit(solution)/shard_map/ppermute | solution.py:20
  14.4 11.6 %collective-permute-start.7 = (bf16[4,64,512]{2,1,0:T(8,128)(2,1)}, bf16[4,64,512]{2,1,0:T(8,128)(2,1)S(1)}, u32[]{:S(2)}, u32[]{:S(2)}) collective-permute-start(bf16[4,64,512]{2,1,0:T(8,128)(2,1)} %param.15), channel_id=1, source_target_pairs={{0,4},{1,5},{2,6},{3,7},{4,0},{5,1},{6,2},{7,3},{8,12},{9,13},{10,... | collective-permute-start | bytes 786440 | tf_op jit(solution)/shard_map/ppermute | solution.py:20
  27.1 197.6 %all-gather.5.cloned.1.call-start = ((), (), s32[]{:S(2)}) async-start(), calls=%async_computation.4 | async-start | bytes 15597568 | tf_op jit(solution)/shard_map/all_gather | solution.py:102
  27.9 6.3 %collective-permute-start.4 = (bf16[128,512]{1,0:T(8,128)(2,1)}, bf16[128,512]{1,0:T(8,128)(2,1)S(1)}, u32[]{:S(2)}, u32[]{:S(2)}) collective-permute-start(bf16[128,512]{1,0:T(8,128)(2,1)} %get-tuple-element.218), channel_id=1, source_target_pairs={{0,1},{1,0},{2,3},{3,2},{4,5},{5,4},{6,7},{7,6},{8,9},{9,8},{10,11... | collective-permute-start | bytes 393224 | tf_op jit(solution)/shard_map/ppermute | solution.py:20
  28.7 20.1 %collective-permute-start.2 = (bf16[128,2048]{1,0:T(8,128)(2,1)S(1)}, bf16[128,2048]{1,0:T(8,128)(2,1)S(1)}, u32[]{:S(2)}, u32[]{:S(2)}) collective-permute-start(bf16[128,2048]{1,0:T(8,128)(2,1)S(1)} %copy-done.31), channel_id=1, source_target_pairs={{0,2},{1,3},{2,0},{3,1},{4,6},{5,7},{6,4},{7,5},{8,10},{9,11},{10,... | collective-permute-start | bytes 1572872 | tf_op jit(solution)/shard_map/ppermute | solution.py:20
  29.6 15.6 %collective-permute-start.5 = (bf16[128,512]{1,0:T(8,128)(2,1)S(1)}, bf16[128,512]{1,0:T(8,128)(2,1)S(1)}, u32[]{:S(2)}, u32[]{:S(2)}) collective-permute-start(bf16[128,512]{1,0:T(8,128)(2,1)S(1)} %get-tuple-element.217), channel_id=1, source_target_pairs={{0,2},{1,3},{2,0},{3,1},{4,6},{5,7},{6,4},{7,5},{8,10},{9,11},{10,... | collective-permute-start | bytes 393224 | tf_op jit(solution)/shard_map/ppermute | solution.py:20
  30.2 18.6 %collective-permute-start.6 = (bf16[128,512]{1,0:T(8,128)(2,1)S(1)}, bf16[128,512]{1,0:T(8,128)(2,1)S(1)}, u32[]{:S(2)}, u32[]{:S(2)}) collective-permute-start(bf16[128,512]{1,0:T(8,128)(2,1)S(1)} %get-tuple-element.216), channel_id=1, source_target_pairs={{0,3},{1,2},{2,1},{3,0},{4,7},{5,6},{6,5},{7,4},{8,11},{9,10},{10,... | collective-permute-start | bytes 393224 | tf_op jit(solution)/shard_map/ppermute | solution.py:20
  31.5 23.3 %collective-permute-start.1 = (bf16[1792,64]{0,1:T(8,128)(2,1)S(1)}, bf16[1792,64]{0,1:T(8,128)(2,1)S(1)}, u32[]{:S(2)}, u32[]{:S(2)}) collective-permute-start(bf16[1792,64]{0,1:T(8,128)(2,1)S(1)} %copy-done.64), channel_id=1, source_target_pairs={{0,4},{1,5},{2,6},{3,7},{4,0},{5,1},{6,2},{7,3},{8,12},{9,13},{10,... | collective-permute-start | bytes 688136 | tf_op jit(solution)/shard_map/ppermute | solution.py:20
  34.2 25.5 %collective-permute-start = (bf16[64,1792]{1,0:T(8,128)(2,1)S(1)}, bf16[64,1792]{1,0:T(8,128)(2,1)S(1)}, u32[]{:S(2)}, u32[]{:S(2)}) collective-permute-start(bf16[64,1792]{1,0:T(8,128)(2,1)S(1)} %copy-done.65), channel_id=1, source_target_pairs={{0,4},{1,5},{2,6},{3,7},{4,0},{5,1},{6,2},{7,3},{8,12},{9,13},{10,... | collective-permute-start | bytes 688136 | tf_op jit(solution)/shard_map/ppermute | solution.py:20
  49.9 11.0 %collective-permute-start.3 = (bf16[2,128,2048]{2,1,0:T(8,128)(2,1)}, bf16[2,128,2048]{2,1,0:T(8,128)(2,1)}, u32[]{:S(2)}, u32[]{:S(2)}) collective-permute-start(bf16[2,128,2048]{2,1,0:T(8,128)(2,1)} %pad_maximum_fusion.7), channel_id=1, source_target_pairs={{0,1},{1,0},{2,3},{3,2},{4,5},{5,4},{6,7},{7,6},{8,9},{9,8},{10,11... | collective-permute-start | bytes 3145736 | tf_op jit(solution)/shard_map/ppermute | solution.py:20
  69.1 303.6 %reduce-scatter.3.cloned.1.call-start = ((), (), s32[]{:S(2)}) async-start(), calls=%async_computation.5 | async-start | bytes 15597568 | tf_op jit(solution)/shard_map/reduce_scatter | solution.py:113
  123.0 48.5 %collective-permute-start.12 = (bf16[16,64,1024]{2,1,0:T(8,128)(2,1)}, bf16[16,64,1024]{2,1,0:T(8,128)(2,1)}, u32[]{:S(2)}, u32[]{:S(2)}) collective-permute-start(bf16[16,64,1024]{2,1,0:T(8,128)(2,1)} %pad_maximum_fusion.1), channel_id=1, source_target_pairs={{0,4},{1,5},{2,6},{3,7},{4,0},{5,1},{6,2},{7,3},{8,12},{9,13},{10,... | collective-permute-start | bytes 6291464 | tf_op jit(solution)/shard_map/ppermute | solution.py:20
  181.5 13.3 %collective-permute-start.14 = (bf16[128,2048]{1,0:T(8,128)(2,1)S(1)}, bf16[128,2048]{1,0:T(8,128)(2,1)S(1)}, u32[]{:S(2)}, u32[]{:S(2)}) collective-permute-start(bf16[128,2048]{1,0:T(8,128)(2,1)S(1)} %fusion.43), channel_id=1, source_target_pairs={{0,2},{1,3},{2,0},{3,1},{4,6},{5,7},{6,4},{7,5},{8,10},{9,11},{10,... | collective-permute-start | bytes 1572872 | tf_op jit(solution)/shard_map/ppermute | solution.py:20
  195.8 12.5 %collective-permute-start.15 = (bf16[128,2048]{1,0:T(8,128)(2,1)S(1)}, bf16[128,2048]{1,0:T(8,128)(2,1)S(1)}, u32[]{:S(2)}, u32[]{:S(2)}) collective-permute-start(bf16[128,2048]{1,0:T(8,128)(2,1)S(1)} %add_convert_fusion.5), channel_id=1, source_target_pairs={{0,2},{1,3},{2,0},{3,1},{4,6},{5,7},{6,4},{7,5},{8,10},{9,11},{10,... | collective-permute-start | bytes 1572872 | tf_op jit(solution)/shard_map/ppermute | solution.py:20
  224.7 13.7 %collective-permute-start.18 = (bf16[512,512]{1,0:T(8,128)(2,1)}, bf16[512,512]{1,0:T(8,128)(2,1)S(1)}, u32[]{:S(2)}, u32[]{:S(2)}) collective-permute-start(bf16[512,512]{1,0:T(8,128)(2,1)} %get-tuple-element.75), channel_id=1, source_target_pairs={{0,2},{1,3},{2,0},{3,1},{4,6},{5,7},{6,4},{7,5},{8,10},{9,11},{10,... | collective-permute-start | bytes 1572872 | tf_op jit(solution)/shard_map/ppermute | solution.py:20
  244.3 13.4 %collective-permute-start.20 = (bf16[512,512]{1,0:T(8,128)(2,1)S(1)}, bf16[512,512]{1,0:T(8,128)(2,1)S(1)}, u32[]{:S(2)}, u32[]{:S(2)}) collective-permute-start(bf16[512,512]{1,0:T(8,128)(2,1)S(1)} %add_convert_fusion.4), channel_id=1, source_target_pairs={{0,2},{1,3},{2,0},{3,1},{4,6},{5,7},{6,4},{7,5},{8,10},{9,11},{10,... | collective-permute-start | bytes 1572872 | tf_op jit(solution)/shard_map/ppermute | solution.py:20
  264.7 197.9 %reduce-scatter.5.cloned.1.call-start = ((), (), s32[]{:S(2)}) async-start(), calls=%async_computation.6 | async-start | bytes 12255232 | tf_op jit(solution)/shard_map/reduce_scatter | solution.py:113
  284.9 13.3 %collective-permute-start.23 = (bf16[128,2048]{1,0:T(8,128)(2,1)S(1)}, bf16[128,2048]{1,0:T(8,128)(2,1)S(1)}, u32[]{:S(2)}, u32[]{:S(2)}) collective-permute-start(bf16[128,2048]{1,0:T(8,128)(2,1)S(1)} %fusion.44), channel_id=1, source_target_pairs={{0,2},{1,3},{2,0},{3,1},{4,6},{5,7},{6,4},{7,5},{8,10},{9,11},{10,... | collective-permute-start | bytes 1572872 | tf_op jit(solution)/shard_map/ppermute | solution.py:20
  300.5 12.4 %collective-permute-start.24 = (bf16[128,2048]{1,0:T(8,128)(2,1)S(1)}, bf16[128,2048]{1,0:T(8,128)(2,1)S(1)}, u32[]{:S(2)}, u32[]{:S(2)}) collective-permute-start(bf16[128,2048]{1,0:T(8,128)(2,1)S(1)} %get-tuple-element.150), channel_id=1, source_target_pairs={{0,2},{1,3},{2,0},{3,1},{4,6},{5,7},{6,4},{7,5},{8,10},{9,11},{10,... | collective-permute-start | bytes 1572872 | tf_op jit(solution)/shard_map/ppermute | solution.py:20
  317.6 51.9 %collective-permute-start.26 = (bf16[16,64,512]{2,1,0:T(8,128)(2,1)}, bf16[16,64,512]{2,1,0:T(8,128)(2,1)}, u32[]{:S(2)}, u32[]{:S(2)}) collective-permute-start(bf16[16,64,512]{2,1,0:T(8,128)(2,1)} %select_bitcast_fusion.1), channel_id=1, source_target_pairs={{0,4},{1,5},{2,6},{3,7},{4,0},{5,1},{6,2},{7,3},{8,12},{9,13},{10,... | collective-permute-start | bytes 3145736 | tf_op jit(solution)/shard_map/ppermute | solution.py:20
  321.8 47.6 %collective-permute-start.27 = (bf16[128,512]{1,0:T(8,128)(2,1)S(1)}, bf16[128,512]{1,0:T(8,128)(2,1)S(1)}, u32[]{:S(2)}, u32[]{:S(2)}) collective-permute-start(bf16[128,512]{1,0:T(8,128)(2,1)S(1)} %get-tuple-element.212), channel_id=1, source_target_pairs={{0,1},{1,0},{2,3},{3,2},{4,5},{5,4},{6,7},{7,6},{8,9},{9,8},{10,11... | collective-permute-start | bytes 393224 | tf_op jit(solution)/shard_map/ppermute | solution.py:20
  322.5 46.9 %collective-permute-start.28 = (bf16[128,512]{1,0:T(8,128)(2,1)S(1)}, bf16[128,512]{1,0:T(8,128)(2,1)S(1)}, u32[]{:S(2)}, u32[]{:S(2)}) collective-permute-start(bf16[128,512]{1,0:T(8,128)(2,1)S(1)} %get-tuple-element.211), channel_id=1, source_target_pairs={{0,2},{1,3},{2,0},{3,1},{4,6},{5,7},{6,4},{7,5},{8,10},{9,11},{10,... | collective-permute-start | bytes 393224 | tf_op jit(solution)/shard_map/ppermute | solution.py:20
  326.1 43.4 %collective-permute-start.29 = (bf16[128,512]{1,0:T(8,128)(2,1)S(1)}, bf16[128,512]{1,0:T(8,128)(2,1)S(1)}, u32[]{:S(2)}, u32[]{:S(2)}) collective-permute-start(bf16[128,512]{1,0:T(8,128)(2,1)S(1)} %get-tuple-element.210), channel_id=1, source_target_pairs={{0,3},{1,2},{2,1},{3,0},{4,7},{5,6},{6,5},{7,4},{8,11},{9,10},{10,... | collective-permute-start | bytes 393224 | tf_op jit(solution)/shard_map/ppermute | solution.py:20
  411.3 13.2 %collective-permute-start.31 = (bf16[16,2,16,512]{3,2,1,0:T(8,128)(2,1)S(1)}, bf16[16,2,16,512]{3,2,1,0:T(8,128)(2,1)S(1)}, u32[]{:S(2)}, u32[]{:S(2)}) collective-permute-start(bf16[16,2,16,512]{3,2,1,0:T(8,128)(2,1)S(1)} %fusion.45), channel_id=1, source_target_pairs={{0,2},{1,3},{2,0},{3,1},{4,6},{5,7},{6,4},{7,5},{8,10},{9,11},{10,... | collective-permute-start | bytes 1572872 | tf_op jit(solution)/shard_map/ppermute | solution.py:20
  424.9 8.2 %collective-permute-start.34 = (bf16[16,16,512]{2,1,0:T(8,128)(2,1)S(1)}, bf16[16,16,512]{2,1,0:T(8,128)(2,1)S(1)}, u32[]{:S(2)}, u32[]{:S(2)}) collective-permute-start(bf16[16,16,512]{2,1,0:T(8,128)(2,1)S(1)} %fusion.49), channel_id=1, source_target_pairs={{0,4},{1,5},{2,6},{3,7},{4,0},{5,1},{6,2},{7,3},{8,12},{9,13},{10,... | collective-permute-start | bytes 786440 | tf_op jit(solution)/shard_map/ppermute | solution.py:20
  426.3 21.7 %collective-permute-start.33 = (bf16[128,2048]{1,0:T(8,128)(2,1)}, bf16[128,2048]{1,0:T(8,128)(2,1)}, u32[]{:S(2)}, u32[]{:S(2)}) collective-permute-start(bf16[128,2048]{1,0:T(8,128)(2,1)} %fusion.46), channel_id=1, source_target_pairs={{0,2},{1,3},{2,0},{3,1},{4,6},{5,7},{6,4},{7,5},{8,10},{9,11},{10,... | collective-permute-start | bytes 1572872 | tf_op jit(solution)/shard_map/ppermute | solution.py:20
  433.9 12.7 %all-to-all-start = ((bf16[16,16,512]{2,1,0:T(8,128)(2,1)}), bf16[16,16,512]{2,1,0:T(8,128)(2,1)S(1)}, u32[]{:S(2)}, u32[]{:S(2)}) async-start(bf16[16,16,512]{2,1,0:T(8,128)(2,1)} %fusion.48), calls=%async_computation.1 | async-start | bytes 524288 | tf_op jit(solution)/shard_map/all_to_all | solution.py:225
  441.1 11.2 %collective-permute-start.39 = (bf16[64,3584]{1,0:T(8,128)(2,1)}, bf16[64,3584]{1,0:T(8,128)(2,1)}, u32[]{:S(2)}, u32[]{:S(2)}) collective-permute-start(bf16[64,3584]{1,0:T(8,128)(2,1)} %broadcast_select_fusion.26), channel_id=1, source_target_pairs={{0,4},{1,5},{2,6},{3,7},{4,0},{5,1},{6,2},{7,3},{8,12},{9,13},{10,... | collective-permute-start | bytes 1376264 | tf_op jit(solution)/shard_map/ppermute | solution.py:20
  467.3 10.7 %collective-permute-start.35 = (bf16[64,2560]{1,0:T(8,128)(2,1)S(1)}, bf16[64,2560]{1,0:T(8,128)(2,1)S(1)}, u32[]{:S(2)}, u32[]{:S(2)}) collective-permute-start(bf16[64,2560]{1,0:T(8,128)(2,1)S(1)} %broadcast_select_fusion.29), channel_id=1, source_target_pairs={{0,4},{1,5},{2,6},{3,7},{4,0},{5,1},{6,2},{7,3},{8,12},{9,13},{10,... | collective-permute-start | bytes 983048 | tf_op jit(solution)/shard_map/ppermute | solution.py:20
  (80 other events, 528.0 us)
Sparse Core Ops, SparseCore 0:
  27.2 92.2 all-gather.2
  121.7 100.4 all-gather.4
  264.8 101.4 reduce-scatter.2
  372.9 89.6 reduce-scatter.4

commit v8 on v7

--- a/solution.py
+++ b/solution.py
@@ -339,6 +339,12 @@
         yield [ref if kind == "w" else part[kind](ref) for ref, kind in zip(refs, kinds)]
 
 
+def in_turns(*bodies):
+    bodies = list(bodies)
+    while bodies:
+        bodies = [body for body in bodies if next(body, body) is not body]
+
+
 def wkv_forward_kernel(*refs):
     groups = list(lane_groups(refs, "ccccwrcccccs"))
     ones = head_ones()
@@ -348,8 +354,7 @@
         for *_, first_ref, _, _, _, state in groups:
             state[...] = spread(first_ref[...], ones)
 
-    for group in groups:
-        forward_heads(ones, *group)
+    in_turns(*(forward_heads(ones, *group) for group in groups))
 
 
 def wkv_backward_kernel(*refs):
@@ -362,8 +367,7 @@
             state[...] = jnp.zeros_like(state)
             sums_ref[...] = jnp.zeros_like(sums_ref)
 
-    for group in groups:
-        backward_heads(ones, *group)
+    in_turns(*(backward_heads(ones, *group) for group in groups))
 
     @pl.when(pl.program_id(0) == pl.num_programs(0) - 1)
     def _():
@@ -376,16 +380,21 @@
 ):
     r, k, v = r_ref[...], k_ref[...], v_ref[...]
     _, run, before = decay_of(low_ref, up_ref, par_ref)
+    yield
     held_ref[...] = fold(state[...], ones)
     score = jnp.zeros((CHUNK, PACK), jnp.float32)
     for to_row, to_prior, pairs in piece_factors(run, before):
         score = jnp.where(pairs, mxu(r * to_row, spread(k * to_prior, ones), NT), score)
+        yield
     out = mxu(score, spread(v, ones), NN) + mxu(r * jnp.exp(before), state[...], NT)
     out = out + head_sum(r * par_ref[1:2] * k, ones) * v
+    yield
     wkv_ref[...] = out
     last = row_of(run, CHUNK - 1)
     state[...] = jnp.exp(last) * state[...] + mxu(v, k * jnp.exp(last - run), TN) * ones
+    yield
     unit, _ = unit_heads(out, ones)
+    yield
     gate = gate_ref[...]
     mixed_ref[...] = ((unit * par_ref[2:3] + par_ref[3:4]) * gate * jax.nn.sigmoid(gate)).astype(jnp.bfloat16)
 
@@ -431,6 +440,7 @@
         sums_ref[row : row + 1] = sums_ref[row : row + 1] + jnp.sum(values, axis=0, keepdims=True)
 
     unit, rstd = unit_heads(wkv_ref[...], ones)
+    yield
     sig = jax.nn.sigmoid(gate)
     g_mixed = gm_ref[...].astype(jnp.float32)
     g_grouped = g_mixed * gate * sig
@@ -444,7 +454,9 @@
         g_unit - head_sum(g_unit, ones) * scale - unit * (head_sum(g_unit * unit, ones) * scale)
     )
 
+    yield
     log_decay, run, before = decay_of(low_ref, up_ref, par_ref)
+    yield
     last = row_of(run, CHUNK - 1)
     start = spread(held_ref[...], ones)
     end_grad = state[...]
@@ -470,6 +482,7 @@
         g_k = g_k + to_prior * g_prior
         g_before = g_before + r_level.astype(jnp.float32) * g_rows
         g_after = g_after + k_rows.astype(jnp.float32) * g_prior
+        yield
     g_v = fold(mxu(score, g_out, TN), ones) + mxu(k * to_end, end_grad, NT)
     g_run = g_before - g_after
     g_last = jnp.sum(k * g_end, axis=0, keepdims=True) + jnp.exp(last) * jnp.sum(
@@ -477,6 +490,7 @@
     )
     upper = jnp.where(iota2((CHUNK, CHUNK), 0) <= iota2((CHUNK, CHUNK), 1), 1.0, 0.0).astype(jnp.float32)
     g_decay = run_sum(upper, g_run) - g_before + g_last
+    yield
     g_expo = g_decay * log_decay
     gw_ref[...] = g_expo.astype(jnp.bfloat16)
     add_to(0, g_expo)

time: 495 us -> 492 us (level)
  Pallas kernels: 123 us -> 116 us
  transfers between devices with their start and end apart: 45 -> 45, of which waited for: 24 -> 24; matrix products, arithmetic and copies ran while one was open for 22% -> 22% of each run, Pallas kernels for 24% -> 23%
where the time goes in v8:
time: 492 us; the launch traced here: 484 us
  waiting for transfers between devices  178 us (36%)
  Pallas kernels  116 us (24%)
  other arithmetic  58 us (12%)
  starting transfers between devices  53.1 us (11%)
  matrix products  34.7 us (7%)
  local copies, waits for them, and re-layouts  29.2 us (6%)
  between operations  15.7 us (3%)
    ppermute x40, waiting for transfers between devices, swap(): return lax.ppermute(block, ALL, [(i, i ^ bit) for i in range(count)])  113 us
    all_gather x2, waiting for transfers between devices, plane_gather(): lax.all_gather(pair, 'seg', axis=0, tiled=True, axis_index_groups=plane_g...  50.3 us
    ppermute x40, starting transfers between devices, swap(): return lax.ppermute(block, ALL, [(i, i ^ bit) for i in range(count)])  47.3 us
    pallas_call x1, Pallas kernels, mixes_back(): pl.pallas_call(mixes_back_kernel, grid=(2, tiles), in_specs=[whole(g_key)...  25.7 us
    pallas_call x1, Pallas kernels, wkv_backward(): pl.pallas_call(wkv_backward_kernel, grid=(chunks,), in_specs=[block] * 4...  22.2 us
    pallas_call x1, Pallas kernels, mixes_forward(): pl.pallas_call(mixes_forward_kernel, grid=(2, tiles), in_specs=[across(ro...  21.8 us
    dot_general x5, matrix products, product_lower(): return jnp.dot(left_arg, right_arg, preferred_element_type=jnp.float32)  17.9 us
    pallas_call x3, Pallas kernels, grad_into(): pl.pallas_call(grad_kernel, grid=(width // GRAD_ROWS,), in_specs=specs, o...  15.7 us
  transfers between devices with their start and end apart: 45, of which 24 were waited for; matrix products, arithmetic and copies ran while one was open for 22% of the time, Pallas kernels for 23%

profile of v8, /device:TPU:1, one launch (start us, length us, event | category | flops | bytes accessed | tf_op | source)
XLA Modules:
  0.0 484.4 jit_solution(18327266452590789738)
XLA Ops:
  14.4 3.0 collective-permute-start.7
  20.2 5.7 %collective-permute-done.11 = bf16[64,512]{1,0:T(8,128)(2,1)S(1)} collective-permute-done((bf16[64,512]{1,0:T(8,128)(2,1)S(1)}, bf16[64,512]{1,0:T(8,128)(2,1)S(1)}, u32[]{:S(2)}, u32[]{:S(2)}) %collective-permute-start.11) | collective-permute-done | bytes 65568 | tf_op jit(solution)/shard_map/ppermute | solution.py:20
  34.6 10.5 %collective-permute-done.5 = bf16[128,512]{1,0:T(8,128)(2,1)S(1)} collective-permute-done((bf16[128,512]{1,0:T(8,128)(2,1)S(1)}, bf16[128,512]{1,0:T(8,128)(2,1)S(1)}, u32[]{:S(2)}, u32[]{:S(2)}) %collective-permute-start.5) | collective-permute-done | bytes 131104 | tf_op jit(solution)/shard_map/ppermute | solution.py:20
  45.2 3.6 collective-permute-done.6
  51.1 3.7 collective-permute-done.1
  54.8 4.9 %collective-permute-done = bf16[64,1792]{1,0:T(8,128)(2,1)S(1)} collective-permute-done((bf16[64,1792]{1,0:T(8,128)(2,1)S(1)}, bf16[64,1792]{1,0:T(8,128)(2,1)S(1)}, u32[]{:S(2)}, u32[]{:S(2)}) %collective-permute-start) | collective-permute-done | bytes 229408 | tf_op jit(solution)/shard_map/ppermute | solution.py:20
  64.5 4.6 fusion.6.unit_ref
  69.2 50.3 %all-gather.3.cloned.1.call-done.w_ref.down_ref.up_ref = bf16[2048,3072]{1,0:T(8,128)(2,1)} async-done(((bf16[128,3072]{1,0:T(8,128)(2,1)}), bf16[2048,3072]{1,0:T(8,128)(2,1)}) %all-gather.3.cloned.1.call-update) | async-done | bytes 12582928 | tf_op jit(solution)/shard_map/all_gather | solution.py:102
  128.1 21.8 %mixes_forward.1 = (bf16[512,2048]{1,0:T(8,128)(2,1)}, bf16[512,2048]{1,0:T(8,128)(2,1)}, bf16[512,2048]{1,0:T(8,128)(2,1)}, bf16[512,2048]{1,0:T(8,128)(2,1)}, ...) custom-call(f32[512,2048]{1,0:T(8,128)} %fusion.6.unit_ref, ...), custom_call_target="tpu_custom_call" | custom-call | flops 1048576 | bytes 65536 | tf_op jit(solution)/shard_map/mixes_forward/pallas_call | solution.py:709
  151.1 15.5 %wkv_forward.1 = (bf16[512,512]{1,0:T(8,128)(2,1)S(1)}, f32[512,512]{1,0:T(8,128)S(1)}, f32[512,512]{1,0:T(8,128)S(1)}) custom-call(f32[512,512]{1,0:T(8,128)} %get-tuple-element.66.refs_0_, f32[512,512]{1,0:T(8,128)} %get-tuple-element.67.refs_1_, f32[512,512]{1,0:T(8,128)} %get-tuple-element.68.refs_2_, f32[512,512]{1,0:T(8,128)} %get-tuple-element.69.refs_3_, ...), custom_call_target="tpu_custom_call" | custom-call | flops 1048576 | bytes 65536 | tf_op jit(solution)/shard_map/wkv_forward/pallas_call | solution.py:407
  166.7 4.8 collective-permute-done.12
  171.5 3.8 select_bitcast_fusion.4
  183.8 11.0 %collective-permute-done.14 = bf16[128,2048]{1,0:T(8,128)(2,1)S(1)} collective-permute-done((bf16[128,2048]{1,0:T(8,128)(2,1)S(1)}, bf16[128,2048]{1,0:T(8,128)(2,1)S(1)}, u32[]{:S(2)}, u32[]{:S(2)}) %collective-permute-start.14) | collective-permute-done | bytes 524320 | tf_op jit(solution)/shard_map/ppermute | solution.py:20
  197.1 11.2 %collective-permute-done.15 = bf16[128,2048]{1,0:T(8,128)(2,1)S(1)} collective-permute-done((bf16[128,2048]{1,0:T(8,128)(2,1)S(1)}, bf16[128,2048]{1,0:T(8,128)(2,1)S(1)}, u32[]{:S(2)}, u32[]{:S(2)}) %collective-permute-start.15) | collective-permute-done | bytes 524320 | tf_op jit(solution)/shard_map/ppermute | solution.py:20
  225.9 7.2 %multiply_convert_fusion.1 = (bf16[512,1792]{1,0:T(8,128)(2,1)S(1)}, bf16[512,1792]{1,0:T(8,128)(2,1)S(1)}) fusion(bf16[512,2048]{1,0:T(8,128)(2,1)S(1)} %get-tuple-element.157.left_ref, bf16[2048,3584]{1,0:T(8,128)(2,1)} %all-gather.5.cloned.1.call-done), kind=kOutput, calls=%fused_computation.23 | convolution fusion | flops 3761766400 | bytes 13107200 | tf_op jit(solution)/shard_map/dot_general | solution.py:173
  245.7 4.0 multiply_convert_fusion.right_ref
  249.7 6.3 %weight_grad.3.rest_0_ = bf16[2048,3584]{1,0:T(8,128)(2,1)} custom-call(bf16[512,2048]{1,0:T(8,128)(2,1)S(1)} %pad_maximum_fusion.5.left_ref, bf16[512,1792]{1,0:T(8,128)(2,1)S(1)} %get-tuple-element.252.right_ref), custom_call_target="tpu_custom_call" | custom-call | flops 1048576 | bytes 65536 | tf_op jit(solution)/shard_map/weight_grad/pallas_call | solution.py:564
  258.4 6.2 %weight_grad.4 = bf16[2048,3584]{1,0:T(8,128)(2,1)} custom-call(bf16[512,2048]{1,0:T(8,128)(2,1)S(1)} %get-tuple-element.157.left_ref, bf16[512,1792]{1,0:T(8,128)(2,1)S(1)} %multiply_convert_fusion.right_ref, bf16[2048,3584]{1,0:T(8,128)(2,1)} %weight_grad.3.rest_0_), custom_call_target="tpu_custom_call", output_to_operand_aliasing={{}: (2, {})} | custom-call | flops 1048576 | bytes 65536 | tf_op jit(solution)/shard_map/weight_grad/pallas_call | solution.py:564
  269.0 6.4 %fusion.2 = f32[512,2048]{1,0:T(8,128)S(1)} fusion(bf16[512,1792]{1,0:T(8,128)(2,1)S(1)} %copy-done.15, bf16[2048,3584]{1,0:T(8,128)(2,1)} %all-gather.5.cloned.1.call-done), kind=kOutput, calls=%fused_computation.2 | convolution fusion | flops 3758096384 | bytes 13369344 | tf_op jit(solution)/shard_map/te,de->td/dot_general | solution.py:181
  286.2 3.2 weight_grad.5
  289.4 8.8 %collective-permute-done.23 = bf16[128,2048]{1,0:T(8,128)(2,1)S(1)} collective-permute-done((bf16[128,2048]{1,0:T(8,128)(2,1)S(1)}, bf16[128,2048]{1,0:T(8,128)(2,1)S(1)}, u32[]{:S(2)}, u32[]{:S(2)}) %collective-permute-start.23) | collective-permute-done | bytes 524320 | tf_op jit(solution)/shard_map/ppermute | solution.py:20
  301.7 11.2 %collective-permute-done.24 = bf16[128,2048]{1,0:T(8,128)(2,1)S(1)} collective-permute-done((bf16[128,2048]{1,0:T(8,128)(2,1)S(1)}, bf16[128,2048]{1,0:T(8,128)(2,1)S(1)}, u32[]{:S(2)}, u32[]{:S(2)}) %collective-permute-start.24) | collective-permute-done | bytes 524320 | tf_op jit(solution)/shard_map/ppermute | solution.py:20
  322.8 3.3 fusion.74.refs_9_
  328.3 22.2 %wkv_backward.1 = (bf16[512,512]{1,0:T(8,128)(2,1)S(1)}, bf16[512,512]{1,0:T(8,128)(2,1)S(1)}, bf16[512,512]{1,0:T(8,128)(2,1)S(1)}, bf16[512,512]{1,0:T(8,128)(...) custom-call(f32[512,512]{1,0:T(8,128)S(1)} %copy-done.2, ...), custom_call_target="tpu_custom_call" | custom-call | flops 1048576 | bytes 65536 | tf_op jit(solution)/shard_map/wkv_backward/pallas_call | solution.py:512
  350.6 15.0 %time_mix_grads.1 = bf16[2048,2816]{1,0:T(8,128)(2,1)} custom-call(bf16[512,2048]{1,0:T(8,128)(2,1)S(1)} %pad_maximum_fusion.6.refs_0_, bf16[512,2048]{1,0:T(8,128)(2,1)S(1)} %copy-done.12, bf16[512,2048]{1,0:T(8,128)(2,1)S(1)} %copy-done.10, bf16[512,2048]{1,0:T(8,128)(2,1)S(1)} %copy-done.11, bf16[512,2048]{1,0:T(8,128)(2,1)S(1)} %copy-done.13, ...), custom_call_target="tpu_custom_call" | custom-call | flops 1048576 | bytes 65536 | tf_op jit(solution)/shard_map/time_mix_grads/pallas_call | solution.py:603
  371.2 25.7 %mixes_back.1 = (bf16[512,2048]{1,0:T(8,128)(2,1)}, bf16[2048,512]{1,0:T(8,128)(2,1)}) custom-call(bf16[512,512]{1,0:T(8,128)(2,1)} %copy-done.7, bf16[512,512]{1,0:T(8,128)(2,1)} %copy-done.8, bf16[512,512]{1,0:T(8,128)(2,1)} %copy-done.6, bf16[512,512]{1,0:T(8,128)(2,1)} %copy-done.9, bf16[512,256]{1,0:T(8,128)(2,1)} %fusion.28.gd_ref, ...), custom_call_target="tpu_custom_call" | custom-call | flops 1048576 | bytes 65536 | tf_op jit(solution)/shard_map/mixes_back/pallas_call | solution.py:820
  408.2 12.4 %collective-permute-done.31 = bf16[16,2,16,512]{3,2,1,0:T(8,128)(2,1)S(1)} collective-permute-done((bf16[16,2,16,512]{3,2,1,0:T(8,128)(2,1)S(1)}, bf16[16,2,16,512]{3,2,1,0:T(8,128)(2,1)S(1)}, u32[]{:S(2)}, u32[]{:S(2)}) %collective-permute-start.31) | collective-permute-done | bytes 524320 | tf_op jit(solution)/shard_map/ppermute | solution.py:20
  423.1 6.1 %collective-permute-done.34 = bf16[16,16,512]{2,1,0:T(8,128)(2,1)S(1)} collective-permute-done((bf16[16,16,512]{2,1,0:T(8,128)(2,1)S(1)}, bf16[16,16,512]{2,1,0:T(8,128)(2,1)S(1)}, u32[]{:S(2)}, u32[]{:S(2)}) %collective-permute-start.34) | collective-permute-done | bytes 262176 | tf_op jit(solution)/shard_map/ppermute | solution.py:20
  430.0 5.7 %all-to-all-start = ((bf16[16,16,512]{2,1,0:T(8,128)(2,1)}), bf16[16,16,512]{2,1,0:T(8,128)(2,1)S(1)}, u32[]{:S(2)}, u32[]{:S(2)}) async-start(bf16[16,16,512]{2,1,0:T(8,128)(2,1)} %fusion.48), calls=%async_computation.1 | async-start | bytes 524288 | tf_op jit(solution)/shard_map/all_to_all | solution.py:225
  438.6 4.7 all-to-all-done
  450.1 10.0 %reduce-scatter.5.cloned.1.call-done = bf16[128,2816]{1,0:T(8,128)(2,1)} async-done(((bf16[2048,2816]{1,0:T(8,128)(2,1)}), bf16[128,2816]{1,0:T(8,128)(2,1)}) %reduce-scatter.5.cloned.1.call-update) | async-done | bytes 720912 | tf_op jit(solution)/shard_map/reduce_scatter | solution.py:113
  468.6 7.2 %collective-permute-done.35 = bf16[64,2560]{1,0:T(8,128)(2,1)S(1)} collective-permute-done((bf16[64,2560]{1,0:T(8,128)(2,1)S(1)}, bf16[64,2560]{1,0:T(8,128)(2,1)S(1)}, u32[]{:S(2)}, u32[]{:S(2)}) %collective-permute-start.35) | collective-permute-done | bytes 327712 | tf_op jit(solution)/shard_map/ppermute | solution.py:20
  (360 shorter events, 148.7 us)
Async XLA Ops:
  7.2 112.4 %all-gather.3.cloned.1.call-start = ((), (), s32[]{:S(2)}) async-start(), calls=%async_computation.3 | async-start | bytes 13369344 | tf_op jit(solution)/shard_map/all_gather | solution.py:102
  9.6 10.4 %collective-permute-start.8 = (bf16[16,1024]{1,0:T(8,128)(2,1)S(1)}, bf16[16,1024]{1,0:T(8,128)(2,1)S(1)}, u32[]{:S(2)}, u32[]{:S(2)}) collective-permute-start(bf16[16,1024]{1,0:T(8,128)(2,1)S(1)} %concatenate.95), channel_id=1, source_target_pairs={{0,1},{1,0},{2,3},{3,2},{4,5},{5,4},{6,7},{7,6},{8,9},{9,8},{10,11... | collective-permute-start | bytes 98312 | tf_op jit(solution)/shard_map/ppermute | solution.py:20
  11.9 8.2 %collective-permute-start.9 = (bf16[16,1024]{1,0:T(8,128)(2,1)S(1)}, bf16[16,1024]{1,0:T(8,128)(2,1)S(1)}, u32[]{:S(2)}, u32[]{:S(2)}) collective-permute-start(bf16[16,1024]{1,0:T(8,128)(2,1)S(1)} %concatenate.96), channel_id=1, source_target_pairs={{0,2},{1,3},{2,0},{3,1},{4,6},{5,7},{6,4},{7,5},{8,10},{9,11},{10,... | collective-permute-start | bytes 98312 | tf_op jit(solution)/shard_map/ppermute | solution.py:20
  14.4 11.6 %collective-permute-start.7 = (bf16[4,64,512]{2,1,0:T(8,128)(2,1)}, bf16[4,64,512]{2,1,0:T(8,128)(2,1)S(1)}, u32[]{:S(2)}, u32[]{:S(2)}) collective-permute-start(bf16[4,64,512]{2,1,0:T(8,128)(2,1)} %param.15), channel_id=1, source_target_pairs={{0,4},{1,5},{2,6},{3,7},{4,0},{5,1},{6,2},{7,3},{8,12},{9,13},{10,... | collective-permute-start | bytes 786440 | tf_op jit(solution)/shard_map/ppermute | solution.py:20
  27.1 197.6 %all-gather.5.cloned.1.call-start = ((), (), s32[]{:S(2)}) async-start(), calls=%async_computation.4 | async-start | bytes 15597568 | tf_op jit(solution)/shard_map/all_gather | solution.py:102
  27.9 6.3 %collective-permute-start.4 = (bf16[128,512]{1,0:T(8,128)(2,1)}, bf16[128,512]{1,0:T(8,128)(2,1)S(1)}, u32[]{:S(2)}, u32[]{:S(2)}) collective-permute-start(bf16[128,512]{1,0:T(8,128)(2,1)} %get-tuple-element.218), channel_id=1, source_target_pairs={{0,1},{1,0},{2,3},{3,2},{4,5},{5,4},{6,7},{7,6},{8,9},{9,8},{10,11... | collective-permute-start | bytes 393224 | tf_op jit(solution)/shard_map/ppermute | solution.py:20
  28.7 20.1 %collective-permute-start.2 = (bf16[128,2048]{1,0:T(8,128)(2,1)S(1)}, bf16[128,2048]{1,0:T(8,128)(2,1)S(1)}, u32[]{:S(2)}, u32[]{:S(2)}) collective-permute-start(bf16[128,2048]{1,0:T(8,128)(2,1)S(1)} %copy-done.31), channel_id=1, source_target_pairs={{0,2},{1,3},{2,0},{3,1},{4,6},{5,7},{6,4},{7,5},{8,10},{9,11},{10,... | collective-permute-start | bytes 1572872 | tf_op jit(solution)/shard_map/ppermute | solution.py:20
  29.6 15.6 %collective-permute-start.5 = (bf16[128,512]{1,0:T(8,128)(2,1)S(1)}, bf16[128,512]{1,0:T(8,128)(2,1)S(1)}, u32[]{:S(2)}, u32[]{:S(2)}) collective-permute-start(bf16[128,512]{1,0:T(8,128)(2,1)S(1)} %get-tuple-element.217), channel_id=1, source_target_pairs={{0,2},{1,3},{2,0},{3,1},{4,6},{5,7},{6,4},{7,5},{8,10},{9,11},{10,... | collective-permute-start | bytes 393224 | tf_op jit(solution)/shard_map/ppermute | solution.py:20
  30.2 18.6 %collective-permute-start.6 = (bf16[128,512]{1,0:T(8,128)(2,1)S(1)}, bf16[128,512]{1,0:T(8,128)(2,1)S(1)}, u32[]{:S(2)}, u32[]{:S(2)}) collective-permute-start(bf16[128,512]{1,0:T(8,128)(2,1)S(1)} %get-tuple-element.216), channel_id=1, source_target_pairs={{0,3},{1,2},{2,1},{3,0},{4,7},{5,6},{6,5},{7,4},{8,11},{9,10},{10,... | collective-permute-start | bytes 393224 | tf_op jit(solution)/shard_map/ppermute | solution.py:20
  31.5 23.3 %collective-permute-start.1 = (bf16[1792,64]{0,1:T(8,128)(2,1)S(1)}, bf16[1792,64]{0,1:T(8,128)(2,1)S(1)}, u32[]{:S(2)}, u32[]{:S(2)}) collective-permute-start(bf16[1792,64]{0,1:T(8,128)(2,1)S(1)} %copy-done.64), channel_id=1, source_target_pairs={{0,4},{1,5},{2,6},{3,7},{4,0},{5,1},{6,2},{7,3},{8,12},{9,13},{10,... | collective-permute-start | bytes 688136 | tf_op jit(solution)/shard_map/ppermute | solution.py:20
  34.2 25.5 %collective-permute-start = (bf16[64,1792]{1,0:T(8,128)(2,1)S(1)}, bf16[64,1792]{1,0:T(8,128)(2,1)S(1)}, u32[]{:S(2)}, u32[]{:S(2)}) collective-permute-start(bf16[64,1792]{1,0:T(8,128)(2,1)S(1)} %copy-done.65), channel_id=1, source_target_pairs={{0,4},{1,5},{2,6},{3,7},{4,0},{5,1},{6,2},{7,3},{8,12},{9,13},{10,... | collective-permute-start | bytes 688136 | tf_op jit(solution)/shard_map/ppermute | solution.py:20
  49.9 11.0 %collective-permute-start.3 = (bf16[2,128,2048]{2,1,0:T(8,128)(2,1)}, bf16[2,128,2048]{2,1,0:T(8,128)(2,1)}, u32[]{:S(2)}, u32[]{:S(2)}) collective-permute-start(bf16[2,128,2048]{2,1,0:T(8,128)(2,1)} %pad_maximum_fusion.7), channel_id=1, source_target_pairs={{0,1},{1,0},{2,3},{3,2},{4,5},{5,4},{6,7},{7,6},{8,9},{9,8},{10,11... | collective-permute-start | bytes 3145736 | tf_op jit(solution)/shard_map/ppermute | solution.py:20
  69.1 299.9 %reduce-scatter.3.cloned.1.call-start = ((), (), s32[]{:S(2)}) async-start(), calls=%async_computation.5 | async-start | bytes 15597568 | tf_op jit(solution)/shard_map/reduce_scatter | solution.py:113
  123.0 48.5 %collective-permute-start.12 = (bf16[16,64,1024]{2,1,0:T(8,128)(2,1)}, bf16[16,64,1024]{2,1,0:T(8,128)(2,1)}, u32[]{:S(2)}, u32[]{:S(2)}) collective-permute-start(bf16[16,64,1024]{2,1,0:T(8,128)(2,1)} %pad_maximum_fusion.1), channel_id=1, source_target_pairs={{0,4},{1,5},{2,6},{3,7},{4,0},{5,1},{6,2},{7,3},{8,12},{9,13},{10,... | collective-permute-start | bytes 6291464 | tf_op jit(solution)/shard_map/ppermute | solution.py:20
  181.5 13.3 %collective-permute-start.14 = (bf16[128,2048]{1,0:T(8,128)(2,1)S(1)}, bf16[128,2048]{1,0:T(8,128)(2,1)S(1)}, u32[]{:S(2)}, u32[]{:S(2)}) collective-permute-start(bf16[128,2048]{1,0:T(8,128)(2,1)S(1)} %fusion.43), channel_id=1, source_target_pairs={{0,2},{1,3},{2,0},{3,1},{4,6},{5,7},{6,4},{7,5},{8,10},{9,11},{10,... | collective-permute-start | bytes 1572872 | tf_op jit(solution)/shard_map/ppermute | solution.py:20
  195.8 12.5 %collective-permute-start.15 = (bf16[128,2048]{1,0:T(8,128)(2,1)S(1)}, bf16[128,2048]{1,0:T(8,128)(2,1)S(1)}, u32[]{:S(2)}, u32[]{:S(2)}) collective-permute-start(bf16[128,2048]{1,0:T(8,128)(2,1)S(1)} %add_convert_fusion.5), channel_id=1, source_target_pairs={{0,2},{1,3},{2,0},{3,1},{4,6},{5,7},{6,4},{7,5},{8,10},{9,11},{10,... | collective-permute-start | bytes 1572872 | tf_op jit(solution)/shard_map/ppermute | solution.py:20
  224.7 13.7 %collective-permute-start.18 = (bf16[512,512]{1,0:T(8,128)(2,1)}, bf16[512,512]{1,0:T(8,128)(2,1)S(1)}, u32[]{:S(2)}, u32[]{:S(2)}) collective-permute-start(bf16[512,512]{1,0:T(8,128)(2,1)} %get-tuple-element.75), channel_id=1, source_target_pairs={{0,2},{1,3},{2,0},{3,1},{4,6},{5,7},{6,4},{7,5},{8,10},{9,11},{10,... | collective-permute-start | bytes 1572872 | tf_op jit(solution)/shard_map/ppermute | solution.py:20
  244.3 13.4 %collective-permute-start.20 = (bf16[512,512]{1,0:T(8,128)(2,1)S(1)}, bf16[512,512]{1,0:T(8,128)(2,1)S(1)}, u32[]{:S(2)}, u32[]{:S(2)}) collective-permute-start(bf16[512,512]{1,0:T(8,128)(2,1)S(1)} %add_convert_fusion.4), channel_id=1, source_target_pairs={{0,2},{1,3},{2,0},{3,1},{4,6},{5,7},{6,4},{7,5},{8,10},{9,11},{10,... | collective-permute-start | bytes 1572872 | tf_op jit(solution)/shard_map/ppermute | solution.py:20
  264.7 195.5 %reduce-scatter.5.cloned.1.call-start = ((), (), s32[]{:S(2)}) async-start(), calls=%async_computation.6 | async-start | bytes 12255232 | tf_op jit(solution)/shard_map/reduce_scatter | solution.py:113
  284.9 13.3 %collective-permute-start.23 = (bf16[128,2048]{1,0:T(8,128)(2,1)S(1)}, bf16[128,2048]{1,0:T(8,128)(2,1)S(1)}, u32[]{:S(2)}, u32[]{:S(2)}) collective-permute-start(bf16[128,2048]{1,0:T(8,128)(2,1)S(1)} %fusion.44), channel_id=1, source_target_pairs={{0,2},{1,3},{2,0},{3,1},{4,6},{5,7},{6,4},{7,5},{8,10},{9,11},{10,... | collective-permute-start | bytes 1572872 | tf_op jit(solution)/shard_map/ppermute | solution.py:20
  300.5 12.4 %collective-permute-start.24 = (bf16[128,2048]{1,0:T(8,128)(2,1)S(1)}, bf16[128,2048]{1,0:T(8,128)(2,1)S(1)}, u32[]{:S(2)}, u32[]{:S(2)}) collective-permute-start(bf16[128,2048]{1,0:T(8,128)(2,1)S(1)} %get-tuple-element.150), channel_id=1, source_target_pairs={{0,2},{1,3},{2,0},{3,1},{4,6},{5,7},{6,4},{7,5},{8,10},{9,11},{10,... | collective-permute-start | bytes 1572872 | tf_op jit(solution)/shard_map/ppermute | solution.py:20
  317.6 48.1 %collective-permute-start.26 = (bf16[16,64,512]{2,1,0:T(8,128)(2,1)}, bf16[16,64,512]{2,1,0:T(8,128)(2,1)}, u32[]{:S(2)}, u32[]{:S(2)}) collective-permute-start(bf16[16,64,512]{2,1,0:T(8,128)(2,1)} %select_bitcast_fusion.1), channel_id=1, source_target_pairs={{0,4},{1,5},{2,6},{3,7},{4,0},{5,1},{6,2},{7,3},{8,12},{9,13},{10,... | collective-permute-start | bytes 3145736 | tf_op jit(solution)/shard_map/ppermute | solution.py:20
  321.7 43.9 %collective-permute-start.27 = (bf16[128,512]{1,0:T(8,128)(2,1)S(1)}, bf16[128,512]{1,0:T(8,128)(2,1)S(1)}, u32[]{:S(2)}, u32[]{:S(2)}) collective-permute-start(bf16[128,512]{1,0:T(8,128)(2,1)S(1)} %get-tuple-element.212), channel_id=1, source_target_pairs={{0,1},{1,0},{2,3},{3,2},{4,5},{5,4},{6,7},{7,6},{8,9},{9,8},{10,11... | collective-permute-start | bytes 393224 | tf_op jit(solution)/shard_map/ppermute | solution.py:20
  322.5 43.1 %collective-permute-start.28 = (bf16[128,512]{1,0:T(8,128)(2,1)S(1)}, bf16[128,512]{1,0:T(8,128)(2,1)S(1)}, u32[]{:S(2)}, u32[]{:S(2)}) collective-permute-start(bf16[128,512]{1,0:T(8,128)(2,1)S(1)} %get-tuple-element.211), channel_id=1, source_target_pairs={{0,2},{1,3},{2,0},{3,1},{4,6},{5,7},{6,4},{7,5},{8,10},{9,11},{10,... | collective-permute-start | bytes 393224 | tf_op jit(solution)/shard_map/ppermute | solution.py:20
  326.1 39.6 %collective-permute-start.29 = (bf16[128,512]{1,0:T(8,128)(2,1)S(1)}, bf16[128,512]{1,0:T(8,128)(2,1)S(1)}, u32[]{:S(2)}, u32[]{:S(2)}) collective-permute-start(bf16[128,512]{1,0:T(8,128)(2,1)S(1)} %get-tuple-element.210), channel_id=1, source_target_pairs={{0,3},{1,2},{2,1},{3,0},{4,7},{5,6},{6,5},{7,4},{8,11},{9,10},{10,... | collective-permute-start | bytes 393224 | tf_op jit(solution)/shard_map/ppermute | solution.py:20
  407.4 13.2 %collective-permute-start.31 = (bf16[16,2,16,512]{3,2,1,0:T(8,128)(2,1)S(1)}, bf16[16,2,16,512]{3,2,1,0:T(8,128)(2,1)S(1)}, u32[]{:S(2)}, u32[]{:S(2)}) collective-permute-start(bf16[16,2,16,512]{3,2,1,0:T(8,128)(2,1)S(1)} %fusion.45), channel_id=1, source_target_pairs={{0,2},{1,3},{2,0},{3,1},{4,6},{5,7},{6,4},{7,5},{8,10},{9,11},{10,... | collective-permute-start | bytes 1572872 | tf_op jit(solution)/shard_map/ppermute | solution.py:20
  421.0 8.2 %collective-permute-start.34 = (bf16[16,16,512]{2,1,0:T(8,128)(2,1)S(1)}, bf16[16,16,512]{2,1,0:T(8,128)(2,1)S(1)}, u32[]{:S(2)}, u32[]{:S(2)}) collective-permute-start(bf16[16,16,512]{2,1,0:T(8,128)(2,1)S(1)} %fusion.49), channel_id=1, source_target_pairs={{0,4},{1,5},{2,6},{3,7},{4,0},{5,1},{6,2},{7,3},{8,12},{9,13},{10,... | collective-permute-start | bytes 786440 | tf_op jit(solution)/shard_map/ppermute | solution.py:20
  422.5 22.2 %collective-permute-start.33 = (bf16[128,2048]{1,0:T(8,128)(2,1)}, bf16[128,2048]{1,0:T(8,128)(2,1)}, u32[]{:S(2)}, u32[]{:S(2)}) collective-permute-start(bf16[128,2048]{1,0:T(8,128)(2,1)} %fusion.46), channel_id=1, source_target_pairs={{0,2},{1,3},{2,0},{3,1},{4,6},{5,7},{6,4},{7,5},{8,10},{9,11},{10,... | collective-permute-start | bytes 1572872 | tf_op jit(solution)/shard_map/ppermute | solution.py:20
  430.0 13.3 %all-to-all-start = ((bf16[16,16,512]{2,1,0:T(8,128)(2,1)}), bf16[16,16,512]{2,1,0:T(8,128)(2,1)S(1)}, u32[]{:S(2)}, u32[]{:S(2)}) async-start(bf16[16,16,512]{2,1,0:T(8,128)(2,1)} %fusion.48), calls=%async_computation.1 | async-start | bytes 524288 | tf_op jit(solution)/shard_map/all_to_all | solution.py:225
  437.7 10.3 %collective-permute-start.39 = (bf16[64,3584]{1,0:T(8,128)(2,1)}, bf16[64,3584]{1,0:T(8,128)(2,1)}, u32[]{:S(2)}, u32[]{:S(2)}) collective-permute-start(bf16[64,3584]{1,0:T(8,128)(2,1)} %broadcast_select_fusion.26), channel_id=1, source_target_pairs={{0,4},{1,5},{2,6},{3,7},{4,0},{5,1},{6,2},{7,3},{8,12},{9,13},{10,... | collective-permute-start | bytes 1376264 | tf_op jit(solution)/shard_map/ppermute | solution.py:20
  461.1 6.7 %collective-permute-start.36 = (bf16[16,512]{1,0:T(8,128)(2,1)S(1)}, bf16[16,512]{1,0:T(8,128)(2,1)S(1)}, u32[]{:S(2)}, u32[]{:S(2)}) collective-permute-start(bf16[16,512]{1,0:T(8,128)(2,1)S(1)} %get-tuple-element.236), channel_id=1, source_target_pairs={{0,1},{1,0},{2,3},{3,2},{4,5},{5,4},{6,7},{7,6},{8,9},{9,8},{10,11... | collective-permute-start | bytes 49160 | tf_op jit(solution)/shard_map/ppermute | solution.py:20
  465.0 10.7 %collective-permute-start.35 = (bf16[64,2560]{1,0:T(8,128)(2,1)S(1)}, bf16[64,2560]{1,0:T(8,128)(2,1)S(1)}, u32[]{:S(2)}, u32[]{:S(2)}) collective-permute-start(bf16[64,2560]{1,0:T(8,128)(2,1)S(1)} %broadcast_select_fusion.29), channel_id=1, source_target_pairs={{0,4},{1,5},{2,6},{3,7},{4,0},{5,1},{6,2},{7,3},{8,12},{9,13},{10,... | collective-permute-start | bytes 983048 | tf_op jit(solution)/shard_map/ppermute | solution.py:20
  (80 other events, 519.4 us)
Sparse Core Ops, SparseCore 0:
  27.2 92.2 all-gather.2
  121.7 100.3 all-gather.4
  264.8 101.3 reduce-scatter.2
  369.5 90.5 reduce-scatter.4

commit v9 on v8

--- a/solution.py
+++ b/solution.py
@@ -460,6 +460,7 @@
     last = row_of(run, CHUNK - 1)
     start = spread(held_ref[...], ones)
     end_grad = state[...]
+    yield
     v_wide = spread(v, ones)
     g_score = mxu(g_out, v_wide, NT)
     score = jnp.zeros((CHUNK, PACK), jnp.float32)
@@ -475,8 +476,10 @@
         k_rows = (k * to_prior).astype(jnp.bfloat16)
         k_level = spread(k_rows.astype(jnp.float32), ones).astype(jnp.bfloat16)
         score = jnp.where(pairs, mxu(r_level, k_level, NT), score)
+        yield
         g_level = jnp.where(pairs, g_score, 0.0).astype(jnp.bfloat16)
         g_rows = mxu(g_level, k_level, NN)
+        yield
         g_prior = fold(mxu(g_level, r_level, TN), ones)
         g_r = g_r + to_row * g_rows
         g_k = g_k + to_prior * g_prior
@@ -494,6 +497,7 @@
     g_expo = g_decay * log_decay
     gw_ref[...] = g_expo.astype(jnp.bfloat16)
     add_to(0, g_expo)
+    yield
     g_diag = head_sum(g_out * v, ones)
     add_to(1, r * k * g_diag)
     gr_ref[...] = (g_r + bonus * k * g_diag).astype(jnp.bfloat16)

time: 492 us -> 492 us (level)
  transfers between devices with their start and end apart: 45 -> 45, of which waited for: 24 -> 24; matrix products, arithmetic and copies ran while one was open for 22% -> 22% of each run, Pallas kernels for 23% -> 22%
where the time goes in v9:
time: 492 us; the launch traced here: 485 us
  waiting for transfers between devices  180 us (37%)
  Pallas kernels  115 us (23%)
  other arithmetic  58.1 us (12%)
  starting transfers between devices  52.5 us (11%)
  matrix products  34.7 us (7%)
  local copies, waits for them, and re-layouts  29.2 us (6%)
  between operations  15.7 us (3%)
    ppermute x40, waiting for transfers between devices, swap(): return lax.ppermute(block, ALL, [(i, i ^ bit) for i in range(count)])  114 us
    all_gather x2, waiting for transfers between devices, plane_gather(): lax.all_gather(pair, 'seg', axis=0, tiled=True, axis_index_groups=plane_g...  50.3 us
    ppermute x40, starting transfers between devices, swap(): return lax.ppermute(block, ALL, [(i, i ^ bit) for i in range(count)])  46.2 us
    pallas_call x1, Pallas kernels, mixes_back(): pl.pallas_call(mixes_back_kernel, grid=(2, tiles), in_specs=[whole(g_key)...  25.7 us
    pallas_call x1, Pallas kernels, mixes_forward(): pl.pallas_call(mixes_forward_kernel, grid=(2, tiles), in_specs=[across(ro...  21.8 us
    pallas_call x1, Pallas kernels, wkv_backward(): pl.pallas_call(wkv_backward_kernel, grid=(chunks,), in_specs=[block] * 4...  21.1 us
    dot_general x5, matrix products, product_lower(): return jnp.dot(left_arg, right_arg, preferred_element_type=jnp.float32)  18 us
    pallas_call x3, Pallas kernels, grad_into(): pl.pallas_call(grad_kernel, grid=(width // GRAD_ROWS,), in_specs=specs, o...  15.7 us
  transfers between devices with their start and end apart: 45, of which 24 were waited for; matrix products, arithmetic and copies ran while one was open for 22% of the time, Pallas kernels for 22%

profile of v9, /device:TPU:1, one launch (start us, length us, event | category | flops | bytes accessed | tf_op | source)
XLA Modules:
  0.0 484.5 jit_solution(3931501818179513753)
XLA Ops:
  14.4 3.0 collective-permute-start.7
  20.2 5.7 %collective-permute-done.11 = bf16[64,512]{1,0:T(8,128)(2,1)S(1)} collective-permute-done((bf16[64,512]{1,0:T(8,128)(2,1)S(1)}, bf16[64,512]{1,0:T(8,128)(2,1)S(1)}, u32[]{:S(2)}, u32[]{:S(2)}) %collective-permute-start.11) | collective-permute-done | bytes 65568 | tf_op jit(solution)/shard_map/ppermute | solution.py:20
  34.6 10.5 %collective-permute-done.5 = bf16[128,512]{1,0:T(8,128)(2,1)S(1)} collective-permute-done((bf16[128,512]{1,0:T(8,128)(2,1)S(1)}, bf16[128,512]{1,0:T(8,128)(2,1)S(1)}, u32[]{:S(2)}, u32[]{:S(2)}) %collective-permute-start.5) | collective-permute-done | bytes 131104 | tf_op jit(solution)/shard_map/ppermute | solution.py:20
  45.2 3.6 collective-permute-done.6
  51.1 3.7 collective-permute-done.1
  54.8 4.9 %collective-permute-done = bf16[64,1792]{1,0:T(8,128)(2,1)S(1)} collective-permute-done((bf16[64,1792]{1,0:T(8,128)(2,1)S(1)}, bf16[64,1792]{1,0:T(8,128)(2,1)S(1)}, u32[]{:S(2)}, u32[]{:S(2)}) %collective-permute-start) | collective-permute-done | bytes 229408 | tf_op jit(solution)/shard_map/ppermute | solution.py:20
  64.5 4.6 fusion.6.unit_ref
  69.2 50.3 %all-gather.3.cloned.1.call-done.w_ref.down_ref.up_ref = bf16[2048,3072]{1,0:T(8,128)(2,1)} async-done(((bf16[128,3072]{1,0:T(8,128)(2,1)}), bf16[2048,3072]{1,0:T(8,128)(2,1)}) %all-gather.3.cloned.1.call-update) | async-done | bytes 12582928 | tf_op jit(solution)/shard_map/all_gather | solution.py:102
  128.1 21.8 %mixes_forward.1 = (bf16[512,2048]{1,0:T(8,128)(2,1)}, bf16[512,2048]{1,0:T(8,128)(2,1)}, bf16[512,2048]{1,0:T(8,128)(2,1)}, bf16[512,2048]{1,0:T(8,128)(2,1)}, ...) custom-call(f32[512,2048]{1,0:T(8,128)} %fusion.6.unit_ref, ...), custom_call_target="tpu_custom_call" | custom-call | flops 1048576 | bytes 65536 | tf_op jit(solution)/shard_map/mixes_forward/pallas_call | solution.py:713
  151.1 15.5 %wkv_forward.1 = (bf16[512,512]{1,0:T(8,128)(2,1)S(1)}, f32[512,512]{1,0:T(8,128)S(1)}, f32[512,512]{1,0:T(8,128)S(1)}) custom-call(f32[512,512]{1,0:T(8,128)} %get-tuple-element.66.refs_0_, f32[512,512]{1,0:T(8,128)} %get-tuple-element.67.refs_1_, f32[512,512]{1,0:T(8,128)} %get-tuple-element.68.refs_2_, f32[512,512]{1,0:T(8,128)} %get-tuple-element.69.refs_3_, ...), custom_call_target="tpu_custom_call" | custom-call | flops 1048576 | bytes 65536 | tf_op jit(solution)/shard_map/wkv_forward/pallas_call | solution.py:407
  166.7 4.8 collective-permute-done.12
  171.5 3.8 select_bitcast_fusion.4
  183.8 11.0 %collective-permute-done.14 = bf16[128,2048]{1,0:T(8,128)(2,1)S(1)} collective-permute-done((bf16[128,2048]{1,0:T(8,128)(2,1)S(1)}, bf16[128,2048]{1,0:T(8,128)(2,1)S(1)}, u32[]{:S(2)}, u32[]{:S(2)}) %collective-permute-start.14) | collective-permute-done | bytes 524320 | tf_op jit(solution)/shard_map/ppermute | solution.py:20
  197.1 11.2 %collective-permute-done.15 = bf16[128,2048]{1,0:T(8,128)(2,1)S(1)} collective-permute-done((bf16[128,2048]{1,0:T(8,128)(2,1)S(1)}, bf16[128,2048]{1,0:T(8,128)(2,1)S(1)}, u32[]{:S(2)}, u32[]{:S(2)}) %collective-permute-start.15) | collective-permute-done | bytes 524320 | tf_op jit(solution)/shard_map/ppermute | solution.py:20
  225.9 7.2 %multiply_convert_fusion.1 = (bf16[512,1792]{1,0:T(8,128)(2,1)S(1)}, bf16[512,1792]{1,0:T(8,128)(2,1)S(1)}) fusion(bf16[512,2048]{1,0:T(8,128)(2,1)S(1)} %get-tuple-element.157.left_ref, bf16[2048,3584]{1,0:T(8,128)(2,1)} %all-gather.5.cloned.1.call-done), kind=kOutput, calls=%fused_computation.23 | convolution fusion | flops 3761766400 | bytes 13107200 | tf_op jit(solution)/shard_map/dot_general | solution.py:173
  245.7 4.0 multiply_convert_fusion.right_ref
  249.7 6.3 %weight_grad.3.rest_0_ = bf16[2048,3584]{1,0:T(8,128)(2,1)} custom-call(bf16[512,2048]{1,0:T(8,128)(2,1)S(1)} %pad_maximum_fusion.5.left_ref, bf16[512,1792]{1,0:T(8,128)(2,1)S(1)} %get-tuple-element.252.right_ref), custom_call_target="tpu_custom_call" | custom-call | flops 1048576 | bytes 65536 | tf_op jit(solution)/shard_map/weight_grad/pallas_call | solution.py:568
  258.4 6.2 %weight_grad.4 = bf16[2048,3584]{1,0:T(8,128)(2,1)} custom-call(bf16[512,2048]{1,0:T(8,128)(2,1)S(1)} %get-tuple-element.157.left_ref, bf16[512,1792]{1,0:T(8,128)(2,1)S(1)} %multiply_convert_fusion.right_ref, bf16[2048,3584]{1,0:T(8,128)(2,1)} %weight_grad.3.rest_0_), custom_call_target="tpu_custom_call", output_to_operand_aliasing={{}: (2, {})} | custom-call | flops 1048576 | bytes 65536 | tf_op jit(solution)/shard_map/weight_grad/pallas_call | solution.py:568
  269.0 6.4 %fusion.2 = f32[512,2048]{1,0:T(8,128)S(1)} fusion(bf16[512,1792]{1,0:T(8,128)(2,1)S(1)} %copy-done.15, bf16[2048,3584]{1,0:T(8,128)(2,1)} %all-gather.5.cloned.1.call-done), kind=kOutput, calls=%fused_computation.2 | convolution fusion | flops 3758096384 | bytes 13369344 | tf_op jit(solution)/shard_map/te,de->td/dot_general | solution.py:181
  286.2 3.2 weight_grad.5
  289.4 8.8 %collective-permute-done.23 = bf16[128,2048]{1,0:T(8,128)(2,1)S(1)} collective-permute-done((bf16[128,2048]{1,0:T(8,128)(2,1)S(1)}, bf16[128,2048]{1,0:T(8,128)(2,1)S(1)}, u32[]{:S(2)}, u32[]{:S(2)}) %collective-permute-start.23) | collective-permute-done | bytes 524320 | tf_op jit(solution)/shard_map/ppermute | solution.py:20
  301.7 11.2 %collective-permute-done.24 = bf16[128,2048]{1,0:T(8,128)(2,1)S(1)} collective-permute-done((bf16[128,2048]{1,0:T(8,128)(2,1)S(1)}, bf16[128,2048]{1,0:T(8,128)(2,1)S(1)}, u32[]{:S(2)}, u32[]{:S(2)}) %collective-permute-start.24) | collective-permute-done | bytes 524320 | tf_op jit(solution)/shard_map/ppermute | solution.py:20
  322.8 3.3 fusion.74.refs_9_
  328.3 21.1 %wkv_backward.1 = (bf16[512,512]{1,0:T(8,128)(2,1)S(1)}, bf16[512,512]{1,0:T(8,128)(2,1)S(1)}, bf16[512,512]{1,0:T(8,128)(2,1)S(1)}, bf16[512,512]{1,0:T(8,128)(...) custom-call(f32[512,512]{1,0:T(8,128)S(1)} %copy-done.2, ...), custom_call_target="tpu_custom_call" | custom-call | flops 1048576 | bytes 65536 | tf_op jit(solution)/shard_map/wkv_backward/pallas_call | solution.py:516
  349.5 15.0 %time_mix_grads.1 = bf16[2048,2816]{1,0:T(8,128)(2,1)} custom-call(bf16[512,2048]{1,0:T(8,128)(2,1)S(1)} %pad_maximum_fusion.6.refs_0_, bf16[512,2048]{1,0:T(8,128)(2,1)S(1)} %copy-done.12, bf16[512,2048]{1,0:T(8,128)(2,1)S(1)} %copy-done.10, bf16[512,2048]{1,0:T(8,128)(2,1)S(1)} %copy-done.11, bf16[512,2048]{1,0:T(8,128)(2,1)S(1)} %copy-done.13, ...), custom_call_target="tpu_custom_call" | custom-call | flops 1048576 | bytes 65536 | tf_op jit(solution)/shard_map/time_mix_grads/pallas_call | solution.py:607
  370.1 25.7 %mixes_back.1 = (bf16[512,2048]{1,0:T(8,128)(2,1)}, bf16[2048,512]{1,0:T(8,128)(2,1)}) custom-call(bf16[512,512]{1,0:T(8,128)(2,1)} %copy-done.7, bf16[512,512]{1,0:T(8,128)(2,1)} %copy-done.8, bf16[512,512]{1,0:T(8,128)(2,1)} %copy-done.6, bf16[512,512]{1,0:T(8,128)(2,1)} %copy-done.9, bf16[512,256]{1,0:T(8,128)(2,1)} %fusion.28.gd_ref, ...), custom_call_target="tpu_custom_call" | custom-call | flops 1048576 | bytes 65536 | tf_op jit(solution)/shard_map/mixes_back/pallas_call | solution.py:824
  406.9 12.7 %collective-permute-done.31 = bf16[16,2,16,512]{3,2,1,0:T(8,128)(2,1)S(1)} collective-permute-done((bf16[16,2,16,512]{3,2,1,0:T(8,128)(2,1)S(1)}, bf16[16,2,16,512]{3,2,1,0:T(8,128)(2,1)S(1)}, u32[]{:S(2)}, u32[]{:S(2)}) %collective-permute-start.31) | collective-permute-done | bytes 524320 | tf_op jit(solution)/shard_map/ppermute | solution.py:20
  422.0 6.3 %collective-permute-done.34 = bf16[16,16,512]{2,1,0:T(8,128)(2,1)S(1)} collective-permute-done((bf16[16,16,512]{2,1,0:T(8,128)(2,1)S(1)}, bf16[16,16,512]{2,1,0:T(8,128)(2,1)S(1)}, u32[]{:S(2)}, u32[]{:S(2)}) %collective-permute-start.34) | collective-permute-done | bytes 262176 | tf_op jit(solution)/shard_map/ppermute | solution.py:20
  429.1 6.1 %all-to-all-start = ((bf16[16,16,512]{2,1,0:T(8,128)(2,1)}), bf16[16,16,512]{2,1,0:T(8,128)(2,1)S(1)}, u32[]{:S(2)}, u32[]{:S(2)}) async-start(bf16[16,16,512]{2,1,0:T(8,128)(2,1)} %fusion.48), calls=%async_computation.1 | async-start | bytes 524288 | tf_op jit(solution)/shard_map/all_to_all | solution.py:225
  437.5 5.3 %all-to-all-done = bf16[16,16,512]{2,1,0:T(8,128)(2,1)S(1)} async-done(((bf16[16,16,512]{2,1,0:T(8,128)(2,1)}), bf16[16,16,512]{2,1,0:T(8,128)(2,1)S(1)}, u32[]{:S(2)}, u32[]{:S(2)}) %all-to-all-start) | async-done | bytes 262176 | tf_op jit(solution)/shard_map/all_to_all | solution.py:225
  450.2 10.1 %reduce-scatter.5.cloned.1.call-done = bf16[128,2816]{1,0:T(8,128)(2,1)} async-done(((bf16[2048,2816]{1,0:T(8,128)(2,1)}), bf16[128,2816]{1,0:T(8,128)(2,1)}) %reduce-scatter.5.cloned.1.call-update) | async-done | bytes 720912 | tf_op jit(solution)/shard_map/reduce_scatter | solution.py:113
  468.8 7.1 %collective-permute-done.35 = bf16[64,2560]{1,0:T(8,128)(2,1)S(1)} collective-permute-done((bf16[64,2560]{1,0:T(8,128)(2,1)S(1)}, bf16[64,2560]{1,0:T(8,128)(2,1)S(1)}, u32[]{:S(2)}, u32[]{:S(2)}) %collective-permute-start.35) | collective-permute-done | bytes 327712 | tf_op jit(solution)/shard_map/ppermute | solution.py:20
  (360 shorter events, 148.4 us)
Async XLA Ops:
  7.2 112.4 %all-gather.3.cloned.1.call-start = ((), (), s32[]{:S(2)}) async-start(), calls=%async_computation.3 | async-start | bytes 13369344 | tf_op jit(solution)/shard_map/all_gather | solution.py:102
  9.6 10.4 %collective-permute-start.8 = (bf16[16,1024]{1,0:T(8,128)(2,1)S(1)}, bf16[16,1024]{1,0:T(8,128)(2,1)S(1)}, u32[]{:S(2)}, u32[]{:S(2)}) collective-permute-start(bf16[16,1024]{1,0:T(8,128)(2,1)S(1)} %concatenate.95), channel_id=1, source_target_pairs={{0,1},{1,0},{2,3},{3,2},{4,5},{5,4},{6,7},{7,6},{8,9},{9,8},{10,11... | collective-permute-start | bytes 98312 | tf_op jit(solution)/shard_map/ppermute | solution.py:20
  11.9 8.2 %collective-permute-start.9 = (bf16[16,1024]{1,0:T(8,128)(2,1)S(1)}, bf16[16,1024]{1,0:T(8,128)(2,1)S(1)}, u32[]{:S(2)}, u32[]{:S(2)}) collective-permute-start(bf16[16,1024]{1,0:T(8,128)(2,1)S(1)} %concatenate.96), channel_id=1, source_target_pairs={{0,2},{1,3},{2,0},{3,1},{4,6},{5,7},{6,4},{7,5},{8,10},{9,11},{10,... | collective-permute-start | bytes 98312 | tf_op jit(solution)/shard_map/ppermute | solution.py:20
  14.4 11.6 %collective-permute-start.7 = (bf16[4,64,512]{2,1,0:T(8,128)(2,1)}, bf16[4,64,512]{2,1,0:T(8,128)(2,1)S(1)}, u32[]{:S(2)}, u32[]{:S(2)}) collective-permute-start(bf16[4,64,512]{2,1,0:T(8,128)(2,1)} %param.15), channel_id=1, source_target_pairs={{0,4},{1,5},{2,6},{3,7},{4,0},{5,1},{6,2},{7,3},{8,12},{9,13},{10,... | collective-permute-start | bytes 786440 | tf_op jit(solution)/shard_map/ppermute | solution.py:20
  27.1 197.6 %all-gather.5.cloned.1.call-start = ((), (), s32[]{:S(2)}) async-start(), calls=%async_computation.4 | async-start | bytes 15597568 | tf_op jit(solution)/shard_map/all_gather | solution.py:102
  27.9 6.3 %collective-permute-start.4 = (bf16[128,512]{1,0:T(8,128)(2,1)}, bf16[128,512]{1,0:T(8,128)(2,1)S(1)}, u32[]{:S(2)}, u32[]{:S(2)}) collective-permute-start(bf16[128,512]{1,0:T(8,128)(2,1)} %get-tuple-element.218), channel_id=1, source_target_pairs={{0,1},{1,0},{2,3},{3,2},{4,5},{5,4},{6,7},{7,6},{8,9},{9,8},{10,11... | collective-permute-start | bytes 393224 | tf_op jit(solution)/shard_map/ppermute | solution.py:20
  28.7 20.1 %collective-permute-start.2 = (bf16[128,2048]{1,0:T(8,128)(2,1)S(1)}, bf16[128,2048]{1,0:T(8,128)(2,1)S(1)}, u32[]{:S(2)}, u32[]{:S(2)}) collective-permute-start(bf16[128,2048]{1,0:T(8,128)(2,1)S(1)} %copy-done.31), channel_id=1, source_target_pairs={{0,2},{1,3},{2,0},{3,1},{4,6},{5,7},{6,4},{7,5},{8,10},{9,11},{10,... | collective-permute-start | bytes 1572872 | tf_op jit(solution)/shard_map/ppermute | solution.py:20
  29.6 15.6 %collective-permute-start.5 = (bf16[128,512]{1,0:T(8,128)(2,1)S(1)}, bf16[128,512]{1,0:T(8,128)(2,1)S(1)}, u32[]{:S(2)}, u32[]{:S(2)}) collective-permute-start(bf16[128,512]{1,0:T(8,128)(2,1)S(1)} %get-tuple-element.217), channel_id=1, source_target_pairs={{0,2},{1,3},{2,0},{3,1},{4,6},{5,7},{6,4},{7,5},{8,10},{9,11},{10,... | collective-permute-start | bytes 393224 | tf_op jit(solution)/shard_map/ppermute | solution.py:20
  30.2 18.6 %collective-permute-start.6 = (bf16[128,512]{1,0:T(8,128)(2,1)S(1)}, bf16[128,512]{1,0:T(8,128)(2,1)S(1)}, u32[]{:S(2)}, u32[]{:S(2)}) collective-permute-start(bf16[128,512]{1,0:T(8,128)(2,1)S(1)} %get-tuple-element.216), channel_id=1, source_target_pairs={{0,3},{1,2},{2,1},{3,0},{4,7},{5,6},{6,5},{7,4},{8,11},{9,10},{10,... | collective-permute-start | bytes 393224 | tf_op jit(solution)/shard_map/ppermute | solution.py:20
  31.5 23.3 %collective-permute-start.1 = (bf16[1792,64]{0,1:T(8,128)(2,1)S(1)}, bf16[1792,64]{0,1:T(8,128)(2,1)S(1)}, u32[]{:S(2)}, u32[]{:S(2)}) collective-permute-start(bf16[1792,64]{0,1:T(8,128)(2,1)S(1)} %copy-done.64), channel_id=1, source_target_pairs={{0,4},{1,5},{2,6},{3,7},{4,0},{5,1},{6,2},{7,3},{8,12},{9,13},{10,... | collective-permute-start | bytes 688136 | tf_op jit(solution)/shard_map/ppermute | solution.py:20
  34.2 25.5 %collective-permute-start = (bf16[64,1792]{1,0:T(8,128)(2,1)S(1)}, bf16[64,1792]{1,0:T(8,128)(2,1)S(1)}, u32[]{:S(2)}, u32[]{:S(2)}) collective-permute-start(bf16[64,1792]{1,0:T(8,128)(2,1)S(1)} %copy-done.65), channel_id=1, source_target_pairs={{0,4},{1,5},{2,6},{3,7},{4,0},{5,1},{6,2},{7,3},{8,12},{9,13},{10,... | collective-permute-start | bytes 688136 | tf_op jit(solution)/shard_map/ppermute | solution.py:20
  49.9 11.0 %collective-permute-start.3 = (bf16[2,128,2048]{2,1,0:T(8,128)(2,1)}, bf16[2,128,2048]{2,1,0:T(8,128)(2,1)}, u32[]{:S(2)}, u32[]{:S(2)}) collective-permute-start(bf16[2,128,2048]{2,1,0:T(8,128)(2,1)} %pad_maximum_fusion.7), channel_id=1, source_target_pairs={{0,1},{1,0},{2,3},{3,2},{4,5},{5,4},{6,7},{7,6},{8,9},{9,8},{10,11... | collective-permute-start | bytes 3145736 | tf_op jit(solution)/shard_map/ppermute | solution.py:20
  69.1 298.7 %reduce-scatter.3.cloned.1.call-start = ((), (), s32[]{:S(2)}) async-start(), calls=%async_computation.5 | async-start | bytes 15597568 | tf_op jit(solution)/shard_map/reduce_scatter | solution.py:113
  123.0 48.5 %collective-permute-start.12 = (bf16[16,64,1024]{2,1,0:T(8,128)(2,1)}, bf16[16,64,1024]{2,1,0:T(8,128)(2,1)}, u32[]{:S(2)}, u32[]{:S(2)}) collective-permute-start(bf16[16,64,1024]{2,1,0:T(8,128)(2,1)} %pad_maximum_fusion.1), channel_id=1, source_target_pairs={{0,4},{1,5},{2,6},{3,7},{4,0},{5,1},{6,2},{7,3},{8,12},{9,13},{10,... | collective-permute-start | bytes 6291464 | tf_op jit(solution)/shard_map/ppermute | solution.py:20
  181.5 13.3 %collective-permute-start.14 = (bf16[128,2048]{1,0:T(8,128)(2,1)S(1)}, bf16[128,2048]{1,0:T(8,128)(2,1)S(1)}, u32[]{:S(2)}, u32[]{:S(2)}) collective-permute-start(bf16[128,2048]{1,0:T(8,128)(2,1)S(1)} %fusion.43), channel_id=1, source_target_pairs={{0,2},{1,3},{2,0},{3,1},{4,6},{5,7},{6,4},{7,5},{8,10},{9,11},{10,... | collective-permute-start | bytes 1572872 | tf_op jit(solution)/shard_map/ppermute | solution.py:20
  195.8 12.5 %collective-permute-start.15 = (bf16[128,2048]{1,0:T(8,128)(2,1)S(1)}, bf16[128,2048]{1,0:T(8,128)(2,1)S(1)}, u32[]{:S(2)}, u32[]{:S(2)}) collective-permute-start(bf16[128,2048]{1,0:T(8,128)(2,1)S(1)} %add_convert_fusion.5), channel_id=1, source_target_pairs={{0,2},{1,3},{2,0},{3,1},{4,6},{5,7},{6,4},{7,5},{8,10},{9,11},{10,... | collective-permute-start | bytes 1572872 | tf_op jit(solution)/shard_map/ppermute | solution.py:20
  224.7 13.7 %collective-permute-start.18 = (bf16[512,512]{1,0:T(8,128)(2,1)}, bf16[512,512]{1,0:T(8,128)(2,1)S(1)}, u32[]{:S(2)}, u32[]{:S(2)}) collective-permute-start(bf16[512,512]{1,0:T(8,128)(2,1)} %get-tuple-element.75), channel_id=1, source_target_pairs={{0,2},{1,3},{2,0},{3,1},{4,6},{5,7},{6,4},{7,5},{8,10},{9,11},{10,... | collective-permute-start | bytes 1572872 | tf_op jit(solution)/shard_map/ppermute | solution.py:20
  244.3 13.4 %collective-permute-start.20 = (bf16[512,512]{1,0:T(8,128)(2,1)S(1)}, bf16[512,512]{1,0:T(8,128)(2,1)S(1)}, u32[]{:S(2)}, u32[]{:S(2)}) collective-permute-start(bf16[512,512]{1,0:T(8,128)(2,1)S(1)} %add_convert_fusion.4), channel_id=1, source_target_pairs={{0,2},{1,3},{2,0},{3,1},{4,6},{5,7},{6,4},{7,5},{8,10},{9,11},{10,... | collective-permute-start | bytes 1572872 | tf_op jit(solution)/shard_map/ppermute | solution.py:20
  264.7 195.7 %reduce-scatter.5.cloned.1.call-start = ((), (), s32[]{:S(2)}) async-start(), calls=%async_computation.6 | async-start | bytes 12255232 | tf_op jit(solution)/shard_map/reduce_scatter | solution.py:113
  284.9 13.3 %collective-permute-start.23 = (bf16[128,2048]{1,0:T(8,128)(2,1)S(1)}, bf16[128,2048]{1,0:T(8,128)(2,1)S(1)}, u32[]{:S(2)}, u32[]{:S(2)}) collective-permute-start(bf16[128,2048]{1,0:T(8,128)(2,1)S(1)} %fusion.44), channel_id=1, source_target_pairs={{0,2},{1,3},{2,0},{3,1},{4,6},{5,7},{6,4},{7,5},{8,10},{9,11},{10,... | collective-permute-start | bytes 1572872 | tf_op jit(solution)/shard_map/ppermute | solution.py:20
  300.5 12.4 %collective-permute-start.24 = (bf16[128,2048]{1,0:T(8,128)(2,1)S(1)}, bf16[128,2048]{1,0:T(8,128)(2,1)S(1)}, u32[]{:S(2)}, u32[]{:S(2)}) collective-permute-start(bf16[128,2048]{1,0:T(8,128)(2,1)S(1)} %get-tuple-element.150), channel_id=1, source_target_pairs={{0,2},{1,3},{2,0},{3,1},{4,6},{5,7},{6,4},{7,5},{8,10},{9,11},{10,... | collective-permute-start | bytes 1572872 | tf_op jit(solution)/shard_map/ppermute | solution.py:20
  317.6 47.0 %collective-permute-start.26 = (bf16[16,64,512]{2,1,0:T(8,128)(2,1)}, bf16[16,64,512]{2,1,0:T(8,128)(2,1)}, u32[]{:S(2)}, u32[]{:S(2)}) collective-permute-start(bf16[16,64,512]{2,1,0:T(8,128)(2,1)} %select_bitcast_fusion.1), channel_id=1, source_target_pairs={{0,4},{1,5},{2,6},{3,7},{4,0},{5,1},{6,2},{7,3},{8,12},{9,13},{10,... | collective-permute-start | bytes 3145736 | tf_op jit(solution)/shard_map/ppermute | solution.py:20
  321.7 42.7 %collective-permute-start.27 = (bf16[128,512]{1,0:T(8,128)(2,1)S(1)}, bf16[128,512]{1,0:T(8,128)(2,1)S(1)}, u32[]{:S(2)}, u32[]{:S(2)}) collective-permute-start(bf16[128,512]{1,0:T(8,128)(2,1)S(1)} %get-tuple-element.212), channel_id=1, source_target_pairs={{0,1},{1,0},{2,3},{3,2},{4,5},{5,4},{6,7},{7,6},{8,9},{9,8},{10,11... | collective-permute-start | bytes 393224 | tf_op jit(solution)/shard_map/ppermute | solution.py:20
  322.5 42.0 %collective-permute-start.28 = (bf16[128,512]{1,0:T(8,128)(2,1)S(1)}, bf16[128,512]{1,0:T(8,128)(2,1)S(1)}, u32[]{:S(2)}, u32[]{:S(2)}) collective-permute-start(bf16[128,512]{1,0:T(8,128)(2,1)S(1)} %get-tuple-element.211), channel_id=1, source_target_pairs={{0,2},{1,3},{2,0},{3,1},{4,6},{5,7},{6,4},{7,5},{8,10},{9,11},{10,... | collective-permute-start | bytes 393224 | tf_op jit(solution)/shard_map/ppermute | solution.py:20
  326.1 38.4 %collective-permute-start.29 = (bf16[128,512]{1,0:T(8,128)(2,1)S(1)}, bf16[128,512]{1,0:T(8,128)(2,1)S(1)}, u32[]{:S(2)}, u32[]{:S(2)}) collective-permute-start(bf16[128,512]{1,0:T(8,128)(2,1)S(1)} %get-tuple-element.210), channel_id=1, source_target_pairs={{0,3},{1,2},{2,1},{3,0},{4,7},{5,6},{6,5},{7,4},{8,11},{9,10},{10,... | collective-permute-start | bytes 393224 | tf_op jit(solution)/shard_map/ppermute | solution.py:20
  406.3 13.3 %collective-permute-start.31 = (bf16[16,2,16,512]{3,2,1,0:T(8,128)(2,1)S(1)}, bf16[16,2,16,512]{3,2,1,0:T(8,128)(2,1)S(1)}, u32[]{:S(2)}, u32[]{:S(2)}) collective-permute-start(bf16[16,2,16,512]{3,2,1,0:T(8,128)(2,1)S(1)} %fusion.45), channel_id=1, source_target_pairs={{0,2},{1,3},{2,0},{3,1},{4,6},{5,7},{6,4},{7,5},{8,10},{9,11},{10,... | collective-permute-start | bytes 1572872 | tf_op jit(solution)/shard_map/ppermute | solution.py:20
  420.0 8.3 %collective-permute-start.34 = (bf16[16,16,512]{2,1,0:T(8,128)(2,1)S(1)}, bf16[16,16,512]{2,1,0:T(8,128)(2,1)S(1)}, u32[]{:S(2)}, u32[]{:S(2)}) collective-permute-start(bf16[16,16,512]{2,1,0:T(8,128)(2,1)S(1)} %fusion.49), channel_id=1, source_target_pairs={{0,4},{1,5},{2,6},{3,7},{4,0},{5,1},{6,2},{7,3},{8,12},{9,13},{10,... | collective-permute-start | bytes 786440 | tf_op jit(solution)/shard_map/ppermute | solution.py:20
  421.6 22.5 %collective-permute-start.33 = (bf16[128,2048]{1,0:T(8,128)(2,1)}, bf16[128,2048]{1,0:T(8,128)(2,1)}, u32[]{:S(2)}, u32[]{:S(2)}) collective-permute-start(bf16[128,2048]{1,0:T(8,128)(2,1)} %fusion.46), channel_id=1, source_target_pairs={{0,2},{1,3},{2,0},{3,1},{4,6},{5,7},{6,4},{7,5},{8,10},{9,11},{10,... | collective-permute-start | bytes 1572872 | tf_op jit(solution)/shard_map/ppermute | solution.py:20
  429.1 13.6 %all-to-all-start = ((bf16[16,16,512]{2,1,0:T(8,128)(2,1)}), bf16[16,16,512]{2,1,0:T(8,128)(2,1)S(1)}, u32[]{:S(2)}, u32[]{:S(2)}) async-start(bf16[16,16,512]{2,1,0:T(8,128)(2,1)} %fusion.48), calls=%async_computation.1 | async-start | bytes 524288 | tf_op jit(solution)/shard_map/all_to_all | solution.py:225
  437.2 10.9 %collective-permute-start.39 = (bf16[64,3584]{1,0:T(8,128)(2,1)}, bf16[64,3584]{1,0:T(8,128)(2,1)}, u32[]{:S(2)}, u32[]{:S(2)}) collective-permute-start(bf16[64,3584]{1,0:T(8,128)(2,1)} %broadcast_select_fusion.26), channel_id=1, source_target_pairs={{0,4},{1,5},{2,6},{3,7},{4,0},{5,1},{6,2},{7,3},{8,12},{9,13},{10,... | collective-permute-start | bytes 1376264 | tf_op jit(solution)/shard_map/ppermute | solution.py:20
  461.3 6.7 %collective-permute-start.36 = (bf16[16,512]{1,0:T(8,128)(2,1)S(1)}, bf16[16,512]{1,0:T(8,128)(2,1)S(1)}, u32[]{:S(2)}, u32[]{:S(2)}) collective-permute-start(bf16[16,512]{1,0:T(8,128)(2,1)S(1)} %get-tuple-element.236), channel_id=1, source_target_pairs={{0,1},{1,0},{2,3},{3,2},{4,5},{5,4},{6,7},{7,6},{8,9},{9,8},{10,11... | collective-permute-start | bytes 49160 | tf_op jit(solution)/shard_map/ppermute | solution.py:20
  465.2 10.7 %collective-permute-start.35 = (bf16[64,2560]{1,0:T(8,128)(2,1)S(1)}, bf16[64,2560]{1,0:T(8,128)(2,1)S(1)}, u32[]{:S(2)}, u32[]{:S(2)}) collective-permute-start(bf16[64,2560]{1,0:T(8,128)(2,1)S(1)} %broadcast_select_fusion.29), channel_id=1, source_target_pairs={{0,4},{1,5},{2,6},{3,7},{4,0},{5,1},{6,2},{7,3},{8,12},{9,13},{10,... | collective-permute-start | bytes 983048 | tf_op jit(solution)/shard_map/ppermute | solution.py:20
  (80 other events, 514.0 us)
Sparse Core Ops, SparseCore 0:
  27.2 92.2 all-gather.2
  121.7 100.3 all-gather.4
  264.8 101.2 reduce-scatter.2
  369.4 90.9 reduce-scatter.4
